TPU v7x, 32 devices: a whole 2x2x4 slice. The times are simulated.
32 devices in a mesh: veh: 8 (over z, y), row: 4 (over x, core).
Axes of the slice: x: 2, y: 2, z: 4, core: 2. Of those that a mesh axis runs over, the one named last changes fastest.
Arguments:
- bev_maps: bfloat16 [64, 32, 64, 128], P('veh', 'row'), may hold values from -6 to 6
- senders: int32 [64, 4], replicated, may hold values from 0 to 63, as said below
- shifts: int32 [64, 4], replicated, may hold values from -1 to 1
- counts: int32 [64], replicated, may hold values from 1 to 4, as said below
- agent_query: bfloat16 [128, 128], replicated, may hold values from -0.5 to 0.5
- agent_keyvalue: bfloat16 [128, 256], replicated, may hold values from -0.5 to 0.5
- agent_out: bfloat16 [128, 128], replicated, may hold values from -0.5 to 0.5
- agent_scale: float32 [4], replicated, may hold values from 1 to 600
- conv_weight: float32 [3, 3, 256], replicated, may hold values from -1.5 to 1.5
- gain_first: float32 [256], replicated, may hold values from 0.1 to 1.9
- window_in: bfloat16 [256, 768], replicated, may hold values from -0.375 to 0.375
- window_out: bfloat16 [256, 256], replicated, may hold values from -0.375 to 0.375
- window_scale: float32 [8], replicated, may hold values from 1 to 600
- gain_second: float32 [256], replicated, may hold values from 0.1 to 1.9
- hidden_up: bfloat16 [256, 512], replicated, may hold values from -0.375 to 0.375
- hidden_down: bfloat16 [512, 256], replicated, may hold values from -0.25 to 0.25
Outputs:
- joined_map: bfloat16 [64, 32, 64, 256], P('veh', 'row')
Inputs may be any that keep to these rules, and one draw needn't show every extreme that they name: `senders`: never the receiver itself. Blocks are aligned runs of 8 vehicles; over the live pairs whose receiver lies in one block and whose sender lies in one block, the intersecting tiles (2 - |shift| a pair) number at most 8. Slots a < counts[r] of receiver r are live.
All inputs are finite; a program needn't handle non-finite values.
Results may differ from a plain program's by a relative error of at most 0.0095.
The roundings to bfloat16 on the way count: a program that leaves them out, or rounds other values in their place, can miss the bound.
Values may be sent and summed in bfloat16 or wider, within the bound.
No kernel may reach another device: no remote copies, remote signals or barrier semaphores. Data moves between devices by JAX's collectives and lax.ppermute only.
A program may use at most 128 MiB of HBM per device.

v0:
```python
import jax
import jax.numpy as jnp
from jax import lax
from jax.sharding import PartitionSpec as P

TILE = 32
WIN = 8


exact_dot = lax.Precision.HIGHEST
norm_eps = 1e-05
unit_eps = 1e-06


def padded_2(cells, sides, width):
    for axis, dim in sides:
        count = lax.axis_size(axis)
        ends = count - 1
        head = lax.slice_in_dim(cells, 0, width, axis=dim)
        tail = lax.slice_in_dim(cells, cells.shape[dim] - width, cells.shape[dim], axis=dim)
        cells = jnp.concatenate(
            [
                lax.ppermute(tail, axis, [(i, (i + 1) % count) for i in range(ends)]),
                cells,
                lax.ppermute(head, axis, [((i + 1) % count, i) for i in range(ends)]),
            ],
            axis=dim,
        )
    return cells


def head_spread(tensor, head_count):
    feature_width = tensor.shape[-1]
    member = (
        jnp.arange(feature_width)[:, None] // (feature_width // head_count)
        == jnp.arange(head_count)[None, :]
    ).astype(jnp.float32)
    summed = jnp.dot(tensor, member, precision=exact_dot)
    return jnp.dot(summed, member.T, precision=exact_dot)


def unit_heads(tensor, head_count):
    return tensor / jnp.sqrt(head_spread(tensor * tensor, head_count) + unit_eps)


def join_agents(ego_map, own_keyvalue, sent_keyvalue, covered, agent_query, agent_out, agent_scale):
    channels = ego_map.shape[-1]
    head_count = agent_scale.shape[0]
    queries = unit_heads(
        jnp.dot(ego_map, agent_query, preferred_element_type=jnp.float32), head_count
    )
    all_kv = jnp.concatenate([own_keyvalue[:, None], sent_keyvalue], axis=1).astype(jnp.float32)
    key_part = unit_heads(all_kv[..., :channels], head_count)
    values = all_kv[..., channels:]
    scale_row = jnp.repeat(agent_scale, channels // head_count)
    scores = head_spread(queries[:, None] * key_part, head_count) * scale_row
    present = jnp.concatenate([jnp.ones_like(covered[:, :1]), covered], axis=1)[..., None]
    scores = jnp.where(present, scores, -1e30)
    row_top = jnp.max(scores, axis=1, keepdims=True)
    weight = jnp.where(present, jnp.exp(scores - row_top), 0.0)
    weight = weight / jnp.sum(weight, axis=1, keepdims=True)
    agent_mix = jnp.sum(weight * values, axis=1).astype(jnp.bfloat16)
    joined = jnp.dot(agent_mix, agent_out, preferred_element_type=jnp.float32).astype(jnp.bfloat16)
    return jnp.concatenate([ego_map, joined], axis=-1)


def layer_norm(tensor, gain):
    average = jnp.mean(tensor, axis=-1, keepdims=True)
    centred = tensor - average
    spread = jnp.mean(centred * centred, axis=-1, keepdims=True)
    return centred * lax.rsqrt(spread + norm_eps) * gain


def to_windows(tensor, head_count):
    batch_size, height, width_cells, feature_width = tensor.shape
    tensor = tensor.reshape(
        batch_size,
        height // WIN,
        WIN,
        width_cells // WIN,
        WIN,
        head_count,
        feature_width // head_count,
    )
    tensor = tensor.transpose(0, 1, 3, 5, 2, 4, 6)
    return tensor.reshape(
        batch_size,
        height // WIN,
        width_cells // WIN,
        head_count,
        WIN * WIN,
        feature_width // head_count,
    )


def from_windows(tensor, height, width_cells):
    batch_size = tensor.shape[0]
    head_count = tensor.shape[3]
    head_width = tensor.shape[-1]
    tensor = tensor.reshape(
        batch_size, height // WIN, width_cells // WIN, head_count, WIN, WIN, head_width
    )
    tensor = tensor.transpose(0, 1, 4, 2, 5, 3, 6)
    return tensor.reshape(batch_size, height, width_cells, head_count * head_width)


def window_layer(
    padded,
    conv_weight,
    gain_first,
    window_in,
    window_out,
    window_scale,
    gain_second,
    hidden_up,
    hidden_down,
):
    batch_size, height, width_cells, feature_width = padded.shape
    height = height - 2
    widened = jnp.pad(padded, ((0, 0), (0, 0), (1, 1), (0, 0))).astype(jnp.float32)
    mixed_sum = widened[:, 1 : height + 1, 1 : width_cells + 1]
    for row_step in range(3):
        for col_step in range(3):
            mixed_sum = (
                mixed_sum
                + widened[:, row_step : row_step + height, col_step : col_step + width_cells]
                * conv_weight[row_step, col_step]
            )
    hidden = layer_norm(mixed_sum, gain_first).astype(jnp.bfloat16)
    projected = jnp.dot(hidden, window_in, preferred_element_type=jnp.float32)
    head_count = window_scale.shape[0]
    queries = to_windows(unit_heads(projected[..., :feature_width], head_count), head_count)
    key_part = to_windows(
        unit_heads(projected[..., feature_width : 2 * feature_width], head_count), head_count
    )
    values = to_windows(projected[..., 2 * feature_width :].astype(jnp.bfloat16), head_count)
    scores = (
        jnp.einsum("bxyhqd,bxyhkd->bxyhqk", queries, key_part, precision=exact_dot)
        * window_scale[:, None, None]
    )
    row_top = jnp.max(scores, axis=-1, keepdims=True)
    weight = jnp.exp(scores - row_top)
    weight = (weight / jnp.sum(weight, axis=-1, keepdims=True)).astype(jnp.bfloat16)
    attended = jnp.einsum(
        "bxyhqk,bxyhkd->bxyhqd", weight, values, preferred_element_type=jnp.float32
    )
    attended = from_windows(attended, height, width_cells).astype(jnp.bfloat16)
    mixed_sum = mixed_sum + jnp.dot(attended, window_out, preferred_element_type=jnp.float32)
    hidden = layer_norm(mixed_sum, gain_second).astype(jnp.bfloat16)
    inner_act = jax.nn.silu(jnp.dot(hidden, hidden_up, preferred_element_type=jnp.float32)).astype(
        jnp.bfloat16
    )
    return (mixed_sum + jnp.dot(inner_act, hidden_down, preferred_element_type=jnp.float32)).astype(
        jnp.bfloat16
    )


def on_device(
    bev_maps,
    senders,
    shifts,
    counts,
    agent_query,
    agent_keyvalue,
    agent_out,
    agent_scale,
    conv_weight,
    gain_first,
    window_in,
    window_out,
    window_scale,
    gain_second,
    hidden_up,
    hidden_down,
):
    vehicles_here, height, width_cells, channels = bev_maps.shape
    agents = senders.shape[1]
    devices = lax.axis_size("veh")
    myself = lax.axis_index("veh")
    tile_cols = width_cells // TILE
    pair_count = vehicles_here * agents
    per_link = max(1, pair_count // devices)
    capacity = tile_cols * per_link
    cell_count = height * width_cells
    send_all = senders.reshape(devices, pair_count)
    shift_all = shifts.reshape(devices, pair_count)
    live_all = (jnp.arange(agents)[None, :] < counts[:, None]).reshape(devices, pair_count)
    tiles_all = jnp.where(live_all, tile_cols - jnp.abs(shift_all), 0)
    source_all = send_all // vehicles_here
    tile_step = jnp.arange(tile_cols, dtype=jnp.int32)
    outgoing = jnp.where(source_all == myself, tiles_all, 0)
    slot_start = jnp.cumsum(outgoing, axis=1) - outgoing
    occupied = tile_step[None, None, :] < outgoing[:, :, None]
    target = jnp.where(
        occupied,
        jnp.arange(devices, dtype=jnp.int32)[:, None, None] * capacity
        + slot_start[:, :, None]
        + tile_step,
        devices * capacity,
    )
    anchor = (
        (send_all % vehicles_here)[:, :, None] * tile_cols
        + jnp.maximum(shift_all, 0)[:, :, None]
        + tile_step
    )
    slot_table = (
        jnp.full((devices * capacity,), -1, jnp.int32)
        .at[target.reshape(-1)]
        .set(anchor.reshape(-1), mode="drop")
    )
    filled = slot_table >= 0
    chosen = jnp.maximum(slot_table, 0)
    row_index = jnp.arange(height)[None, :]
    own_keyvalue = jnp.dot(bev_maps, agent_keyvalue, preferred_element_type=jnp.float32).astype(
        jnp.bfloat16
    )
    feature_width = bev_maps.shape[-1]
    tiled_map = bev_maps.reshape(vehicles_here, height, tile_cols, TILE, feature_width)
    packed = tiled_map[(chosen // tile_cols)[:, None], row_index, (chosen % tile_cols)[:, None]]
    packed = jnp.where(filled[:, None, None, None], packed, jnp.zeros((), bev_maps.dtype))
    arrived = jnp.dot(
        lax.all_to_all(
            packed.reshape(devices, capacity, height, TILE, feature_width),
            "veh",
            split_axis=0,
            concat_axis=0,
            tiled=True,
        ),
        agent_keyvalue,
        preferred_element_type=jnp.float32,
    ).astype(jnp.bfloat16)
    arrived = arrived.reshape(devices * capacity, height, TILE, 2 * channels)
    my_senders = send_all[myself]
    my_shifts = shift_all[myself]
    my_tiles = tiles_all[myself]
    my_live = live_all[myself]
    my_sources = my_senders // vehicles_here
    position = jnp.arange(pair_count)
    earlier = (my_sources[None, :] == my_sources[:, None]) & (position[None, :] < position[:, None])
    offset = jnp.sum(jnp.where(earlier, my_tiles[None, :], 0), axis=1)
    shifted = tile_step[None, :] + my_shifts[:, None]
    inside = (shifted >= 0) & (shifted < tile_cols) & my_live[:, None]
    slot_of = (
        my_sources[:, None] * capacity
        + offset[:, None]
        + tile_step[None, :]
        - jnp.maximum(-my_shifts, 0)[:, None]
    )
    slot_of = jnp.where(inside, slot_of, 0)
    covered_cols = jnp.repeat(inside, TILE, axis=1)
    group_size = min(vehicles_here, max(1, 1024 // cell_count))
    block_count = vehicles_here // group_size
    band_rows = jnp.arange(height)[None, :, None]

    def agent_group(operands):
        ego_map, self_kv, group_slots, group_cover = operands
        sent_keyvalue = arrived[group_slots[:, None, :], band_rows]
        sent_keyvalue = sent_keyvalue.reshape(group_size, agents, cell_count, 2 * channels)
        covered = jnp.broadcast_to(
            group_cover.reshape(group_size, agents, 1, width_cells),
            (group_size, agents, height, width_cells),
        ).reshape(group_size, agents, cell_count)
        mixed_in = join_agents(
            ego_map.reshape(group_size, cell_count, channels),
            self_kv.reshape(group_size, cell_count, 2 * channels),
            sent_keyvalue,
            covered,
            agent_query,
            agent_out,
            agent_scale,
        )
        return mixed_in.reshape(group_size, height, width_cells, 2 * channels)

    layer_input = lax.map(
        agent_group,
        (
            bev_maps.reshape(block_count, group_size, height, width_cells, channels),
            own_keyvalue.reshape(block_count, group_size, height, width_cells, 2 * channels),
            slot_of.reshape(block_count, group_size * agents, tile_cols),
            covered_cols.reshape(block_count, group_size * agents, width_cells),
        ),
    )
    layer_input = layer_input.reshape(vehicles_here, height, width_cells, 2 * channels)
    padded = padded_2(layer_input, (("row", 1),), 1)

    def layer_group(padded_group):
        return window_layer(
            padded_group,
            conv_weight,
            gain_first,
            window_in,
            window_out,
            window_scale,
            gain_second,
            hidden_up,
            hidden_down,
        )

    result = lax.map(
        layer_group, padded.reshape(block_count, group_size, height + 2, width_cells, 2 * channels)
    )
    return result.reshape(vehicles_here, height, width_cells, 2 * channels)


def solution(mesh):
    in_specs = (
        P("veh", "row", None, None),
        P(),
        P(),
        P(),
        P(),
        P(),
        P(),
        P(),
        P(),
        P(),
        P(),
        P(),
        P(),
        P(),
        P(),
        P(),
    )
    out_specs = P("veh", "row", None, None)
    return jax.shard_map(
        on_device, mesh=mesh, in_specs=in_specs, out_specs=out_specs, check_vma=False
    )
```

profile of v0, /device:TPU:1, one launch (start us, length us, event | category | flops | bytes accessed | tf_op | source)
XLA Modules:
  0.0 431.3 jit_solution(1812687231458971583)
XLA Ops:
  6.2 5.6 %gather_fusion.1 = bf16[512,32,128]{2,1,0:T(8,128)(2,1)} fusion(bf16[8,8,2,32,128]{4,3,2,1,0:T(8,128)(2,1)} %bitcast.259, s32[512]{0:T(512)S(1)} %reshape.673), kind=kCustom, calls=%fused_computation.1 | custom fusion | bytes 8394752 | tf_op jit(solution)/shard_map/gather | solution.py:219
  11.9 4.5 %broadcast_select_fusion = bf16[8,8,8,32,128]{4,3,2,1,0:T(8,128)(2,1)} fusion(bf16[8,8,8,32,128]{4,3,2,1,0:T(8,128)(2,1)} %bitcast.263, pred[8,8]{1,0:T(8,128)(4,1)S(1)} %broadcast_in_dim.191), kind=kLoop, calls=%fused_computation.141 | loop fusion | flops 2097152 | bytes 8388672 | tf_op jit(solution)/shard_map/jit(_where)/select_n | solution.py:220
  16.3 6.5 %all-to-all-start = ((bf16[8,8,8,32,128]{4,3,2,1,0:T(8,128)(2,1)}), bf16[8,8,8,32,128]{4,3,2,1,0:T(8,128)(2,1)}, u32[]{:S(2)}, u32[]{:S(2)}) async-start(bf16[8,8,8,32,128]{4,3,2,1,0:T(8,128)(2,1)} %broadcast_select_fusion), calls=%async_computation | async-start | bytes 8388608 | tf_op jit(solution)/shard_map/all_to_all | solution.py:222
  25.8 89.4 %all-to-all-done = bf16[8,8,8,32,128]{4,3,2,1,0:T(8,128)(2,1)} async-done(((bf16[8,8,8,32,128]{4,3,2,1,0:T(8,128)(2,1)}), bf16[8,8,8,32,128]{4,3,2,1,0:T(8,128)(2,1)}, u32[]{:S(2)}, u32[]{:S(2)}) %all-to-all-start) | async-done | bytes 4194336 | tf_op jit(solution)/shard_map/all_to_all | solution.py:222
  115.3 7.7 %convolution_convert_fusion.1 = bf16[8,8,8,32,256]{4,3,2,1,0:T(8,128)(2,1)} fusion(bf16[8,8,8,32,128]{4,3,2,1,0:T(8,128)(2,1)} %all-to-all-done, bf16[128,256]{1,0:T(8,128)(2,1)S(1)} %copy-done), kind=kOutput, calls=%fused_computation.140 | convolution fusion | flops 1077936128 | bytes 12648448 | tf_op jit(solution)/shard_map/dot_general | solution.py:221
  124.6 76.9 %while.26 = (s32[]{:T(128)}, bf16[4,2,8,64,256]{4,3,2,1,0:T(8,128)(2,1)}, bf16[4,2,8,64,128]{4,3,2,1,0:T(8,128)(2,1)S(1)}, pred[4,8,64]{2,1,0:T(8,128)(4,1)S(1)}...) while((s32[]{:T(128)}, ...), condition=%wide.region_7.8_spmd.clone, body=%wide.region_3.7_spmd.clone.sunk | while | flops 221778144 | bytes 88555112 | solution.py:274
  126.4 4.2 gather_fusion
  137.7 2.8 fusion.250
  145.6 4.2 gather_fusion
  156.9 2.8 fusion.250
  164.7 4.2 gather_fusion
  176.0 2.8 fusion.250
  183.9 4.2 gather_fusion
  195.2 2.8 fusion.250
  202.6 4.8 %collective-permute-start = (bf16[8,1,64,256]{3,2,1,0:T(8,128)(2,1)S(1)}, bf16[8,1,64,256]{3,2,1,0:T(8,128)(2,1)S(1)}, u32[]{:S(2)}, u32[]{:S(2)}) collective-permute-start(bf16[8,1,64,256]{3,2,1,0:T(8,128)(2,1)S(1)} %get-tuple-element.368), channel_id=1, source_target_pairs={{0,1},{1,2},{2,3},{4,5},{5,6},{6,7},{8,9},{9,10},{10,11},{12,13},{... | collective-permute-start | bytes 786440 | tf_op jit(solution)/shard_map/ppermute | solution.py:23
  210.7 4.4 %collective-permute-done.1 = bf16[8,1,64,256]{3,2,1,0:T(8,128)(2,1)S(1)} collective-permute-done((bf16[8,1,64,256]{3,2,1,0:T(8,128)(2,1)S(1)}, bf16[8,1,64,256]{3,2,1,0:T(8,128)(2,1)S(1)}, u32[]{:S(2)}, u32[]{:S(2)}) %collective-permute-start.1) | collective-permute-done | bytes 262176 | tf_op jit(solution)/shard_map/ppermute | solution.py:25
  215.1 3.6 pad_maximum_fusion
  220.3 210.0 %while.25 = (s32[]{:T(128)}, bf16[4,2,8,64,256]{4,3,2,1,0:T(8,128)(2,1)}, bf16[4,2,10,64,256]{4,3,2,1,0:T(8,128)(2,1)}, f32[3,3,256]{2,1,0:T(4,128)S(1)}, f32[25...) while((s32[]{:T(128)}, ...), condition=%wide.region_15.16_spmd, body=%wide.region_8.15_spmd.sunk | while | flops 1426937856 | bytes 66022180 | solution.py:299
  239.0 3.7 reshape.738
  245.1 3.7 reshape.737
  248.8 11.4 %fusion.222 = f32[2,8,8,64,64]{3,4,2,1,0:T(8,128)S(1)} fusion(f32[2,1,8,8,8,8,32]{6,5,4,3,2,0,1:T(8,128)} %reshape.737, f32[2,1,8,8,8,8,32]{6,5,4,3,2,0,1:T(8,128)} %reshape.738), kind=kOutput, calls=%fused_computation.5.clone.1 | convolution fusion | flops 201326592 | bytes 4194304 | tf_op jit(solution)/shard_map/while/body/eval_jaxpr/bxyhqd,bxyhkd->bxyhqk/dot_general | solution.py:138
  260.2 3.2 fusion.223
  264.2 2.6 reshape.736
  266.9 3.9 fusion.224
  272.8 3.8 copy.118
  276.6 3.2 convert_element_type.136
  288.3 3.7 reshape.738
  294.4 3.7 reshape.737
  298.2 11.4 %fusion.222 = f32[2,8,8,64,64]{3,4,2,1,0:T(8,128)S(1)} fusion(f32[2,1,8,8,8,8,32]{6,5,4,3,2,0,1:T(8,128)} %reshape.737, f32[2,1,8,8,8,8,32]{6,5,4,3,2,0,1:T(8,128)} %reshape.738), kind=kOutput, calls=%fused_computation.5.clone.1 | convolution fusion | flops 201326592 | bytes 4194304 | tf_op jit(solution)/shard_map/while/body/eval_jaxpr/bxyhqd,bxyhkd->bxyhqk/dot_general | solution.py:138
  309.5 3.2 fusion.223
  313.6 2.6 reshape.736
  316.2 3.9 fusion.224
  322.1 3.8 copy.118
  325.9 3.2 convert_element_type.136
  337.6 3.7 reshape.738
  343.8 3.7 reshape.737
  347.5 11.4 %fusion.222 = f32[2,8,8,64,64]{3,4,2,1,0:T(8,128)S(1)} fusion(f32[2,1,8,8,8,8,32]{6,5,4,3,2,0,1:T(8,128)} %reshape.737, f32[2,1,8,8,8,8,32]{6,5,4,3,2,0,1:T(8,128)} %reshape.738), kind=kOutput, calls=%fused_computation.5.clone.1 | convolution fusion | flops 201326592 | bytes 4194304 | tf_op jit(solution)/shard_map/while/body/eval_jaxpr/bxyhqd,bxyhkd->bxyhqk/dot_general | solution.py:138
  358.9 3.2 fusion.223
  365.6 3.9 fusion.224
  371.5 3.8 copy.118
  375.3 3.2 convert_element_type.136
  387.0 3.7 reshape.738
  393.1 3.7 reshape.737
  396.8 11.4 %fusion.222 = f32[2,8,8,64,64]{3,4,2,1,0:T(8,128)S(1)} fusion(f32[2,1,8,8,8,8,32]{6,5,4,3,2,0,1:T(8,128)} %reshape.737, f32[2,1,8,8,8,8,32]{6,5,4,3,2,0,1:T(8,128)} %reshape.738), kind=kOutput, calls=%fused_computation.5.clone.1 | convolution fusion | flops 201326592 | bytes 4194304 | tf_op jit(solution)/shard_map/while/body/eval_jaxpr/bxyhqd,bxyhkd->bxyhqk/dot_general | solution.py:138
  408.2 3.2 fusion.223
  414.9 3.9 fusion.224
  420.8 3.8 copy.118
  424.6 3.2 convert_element_type.136
  (315 shorter events, 125.3 us)
Async XLA Ops:
  0.0 23.8 %copy-start = (bf16[128,256]{1,0:T(8,128)(2,1)S(1)}, bf16[128,256]{1,0:T(8,128)(2,1)}, u32[]{:S(2)}) copy-start(bf16[128,256]{1,0:T(8,128)(2,1)} %param.25) | copy-start | bytes 196612
  16.3 7.5 %copy-start.6 = (bf16[8,8,64,128]{3,2,1,0:T(8,128)(2,1)S(1)}, bf16[8,8,64,128]{3,2,1,0:T(8,128)(2,1)}, u32[]{:S(2)}) copy-start(bf16[8,8,64,128]{3,2,1,0:T(8,128)(2,1)} %param.20) | copy-start | bytes 3145732
  16.3 98.9 %all-to-all-start = ((bf16[8,8,8,32,128]{4,3,2,1,0:T(8,128)(2,1)}), bf16[8,8,8,32,128]{4,3,2,1,0:T(8,128)(2,1)}, u32[]{:S(2)}, u32[]{:S(2)}) async-start(bf16[8,8,8,32,128]{4,3,2,1,0:T(8,128)(2,1)} %broadcast_select_fusion), calls=%async_computation | async-start | bytes 8388608 | tf_op jit(solution)/shard_map/all_to_all | solution.py:222
  25.8 98.8 %copy-start.10 = (bf16[128,128]{1,0:T(8,128)(2,1)S(1)}, bf16[128,128]{1,0:T(8,128)(2,1)}, u32[]{:S(2)}) copy-start(bf16[128,128]{1,0:T(8,128)(2,1)} %param.24) | copy-start | bytes 98308
  25.8 98.8 %copy-start.11 = (bf16[128,128]{1,0:T(8,128)(2,1)S(1)}, bf16[128,128]{1,0:T(8,128)(2,1)}, u32[]{:S(2)}) copy-start(bf16[128,128]{1,0:T(8,128)(2,1)} %param.26) | copy-start | bytes 98308
  25.8 98.8 %copy-start.15 = (f32[4]{0:T(128)S(1)}, f32[4]{0:T(128)}, u32[]{:S(2)}) copy-start(f32[4]{0:T(128)} %param.27) | copy-start | bytes 52
  132.1 3.6 copy-start.2
  137.7 3.9 copy-start.3
  141.6 2.4 copy-start.7
  151.3 3.6 copy-start.2
  156.9 3.9 copy-start.3
  160.8 2.4 copy-start.7
  170.4 3.6 copy-start.2
  176.0 3.9 copy-start.3
  179.9 2.4 copy-start.7
  189.6 3.6 copy-start.2
  195.2 3.9 copy-start.3
  199.1 2.4 copy-start.7
  202.6 8.1 %collective-permute-start = (bf16[8,1,64,256]{3,2,1,0:T(8,128)(2,1)S(1)}, bf16[8,1,64,256]{3,2,1,0:T(8,128)(2,1)S(1)}, u32[]{:S(2)}, u32[]{:S(2)}) collective-permute-start(bf16[8,1,64,256]{3,2,1,0:T(8,128)(2,1)S(1)} %get-tuple-element.368), channel_id=1, source_target_pairs={{0,1},{1,2},{2,3},{4,5},{5,6},{6,7},{8,9},{9,10},{10,11},{12,13},{... | collective-permute-start | bytes 786440 | tf_op jit(solution)/shard_map/ppermute | solution.py:23
  207.4 7.7 %collective-permute-start.1 = (bf16[8,1,64,256]{3,2,1,0:T(8,128)(2,1)S(1)}, bf16[8,1,64,256]{3,2,1,0:T(8,128)(2,1)S(1)}, u32[]{:S(2)}, u32[]{:S(2)}) collective-permute-start(bf16[8,1,64,256]{3,2,1,0:T(8,128)(2,1)S(1)} %get-tuple-element.369), channel_id=1, source_target_pairs={{1,0},{2,1},{3,2},{5,4},{6,5},{7,6},{9,8},{10,9},{11,10},{13,12},{... | collective-permute-start | bytes 786440 | tf_op jit(solution)/shard_map/ppermute | solution.py:25
  215.1 5.2 %copy-start.9 = (bf16[256,256]{1,0:T(8,128)(2,1)S(1)}, bf16[256,256]{1,0:T(8,128)(2,1)}, u32[]{:S(2)}) copy-start(bf16[256,256]{1,0:T(8,128)(2,1)} %param.31) | copy-start | bytes 393220
  215.1 5.2 %copy-start.12 = (f32[3,3,256]{2,1,0:T(4,128)S(1)}, f32[3,3,256]{2,1,0:T(4,128)}, u32[]{:S(2)}) copy-start(f32[3,3,256]{2,1,0:T(4,128)} %param.28) | copy-start | bytes 27652
  215.1 5.2 %copy-start.13 = (f32[256]{0:T(256)S(1)}, f32[256]{0:T(256)}, u32[]{:S(2)}) copy-start(f32[256]{0:T(256)} %param.29) | copy-start | bytes 3076
  215.1 5.2 %copy-start.14 = (f32[8]{0:T(128)S(1)}, f32[8]{0:T(128)}, u32[]{:S(2)}) copy-start(f32[8]{0:T(128)} %param.32) | copy-start | bytes 100
  215.1 5.2 %copy-start.18 = (f32[256]{0:T(256)S(1)}, f32[256]{0:T(256)}, u32[]{:S(2)}) copy-start(f32[256]{0:T(256)} %param.33) | copy-start | bytes 3076
  234.3 1.5 copy-start.8
  235.4 1.2 copy-start.4
  272.8 7.0 %copy-start.5 = (f32[2,8,64,256]{3,2,1,0:T(8,128)S(1)}, f32[2,8,64,256]{3,2,1,0:T(8,128)}, u32[]{:S(2)}) copy-start(f32[2,8,64,256]{3,2,1,0:T(8,128)} %copy-done.4) | copy-start | bytes 3145732 | tf_op jit(solution)/shard_map/while
  276.6 4.0 copy-start.16
  276.6 4.0 copy-start.17
  283.6 1.5 copy-start.8
  284.7 1.2 copy-start.4
  322.1 7.0 %copy-start.5 = (f32[2,8,64,256]{3,2,1,0:T(8,128)S(1)}, f32[2,8,64,256]{3,2,1,0:T(8,128)}, u32[]{:S(2)}) copy-start(f32[2,8,64,256]{3,2,1,0:T(8,128)} %copy-done.4) | copy-start | bytes 3145732 | tf_op jit(solution)/shard_map/while
  325.9 4.0 copy-start.16
  325.9 4.0 copy-start.17
  333.0 1.5 copy-start.8
  334.0 1.2 copy-start.4
  371.5 7.0 %copy-start.5 = (f32[2,8,64,256]{3,2,1,0:T(8,128)S(1)}, f32[2,8,64,256]{3,2,1,0:T(8,128)}, u32[]{:S(2)}) copy-start(f32[2,8,64,256]{3,2,1,0:T(8,128)} %copy-done.4) | copy-start | bytes 3145732 | tf_op jit(solution)/shard_map/while
  375.3 4.0 copy-start.16
  375.3 4.0 copy-start.17
  382.3 1.5 copy-start.8
  383.4 1.2 copy-start.4
  420.8 7.0 %copy-start.5 = (f32[2,8,64,256]{3,2,1,0:T(8,128)S(1)}, f32[2,8,64,256]{3,2,1,0:T(8,128)}, u32[]{:S(2)}) copy-start(f32[2,8,64,256]{3,2,1,0:T(8,128)} %copy-done.4) | copy-start | bytes 3145732 | tf_op jit(solution)/shard_map/while
  424.6 4.0 copy-start.16
  424.6 4.0 copy-start.17
  430.3 0.8 copy-start.1
where the time goes:
time: 433 us; the launch traced here: 431 us
  matrix products  139 us (32%)
  local copies, waits for them, and re-layouts  125 us (29%)
  waiting for transfers between devices  95.2 us (22%)
  other arithmetic  44.3 us (10%)
  loops' own time  14.1 us (3%)
  starting transfers between devices  13.3 us (3%)
    all_to_all x1, waiting for transfers between devices, on_device(): lax.all_to_all(packed.reshape(devices, capacity, height, TILE, feature_wi...  89.4 us
    dot_general x4, matrix products, window_layer(): jnp.einsum('bxyhqd,bxyhkd->bxyhqk', queries, key_part, precision=exact_dot)  45.5 us
    reshape x12, local copies, waits for them, and re-layouts, to_windows(): tensor.reshape(batch_size, height // WIN, WIN, width_cells // WIN, WIN, h...  40.4 us
    convert_element_type x12, local copies, waits for them, and re-layouts, window_layer(): attended = from_windows(attended, height, width_cells).astype(jnp.bfloat16)  35.8 us
    dot_general x20, matrix products, head_spread(): return jnp.dot(summed, member.T, precision=exact_dot)  35.7 us
    dot_general x20, matrix products, head_spread(): summed = jnp.dot(tensor, member, precision=exact_dot)  19.7 us
    gather x4, local copies, waits for them, and re-layouts, agent_group(): sent_keyvalue = arrived[group_slots[:, None, :], band_rows]  17 us
    dot_general x4, matrix products, window_layer(): jnp.einsum('bxyhqk,bxyhkd->bxyhqd', weight, values, preferred_element_typ...  15.6 us
  transfers between devices with their start and end apart: 3, of which 3 were waited for; matrix products, arithmetic and copies ran while one was open for 1% of the time, Pallas kernels for 0%

commit v1 on v0

v1 whole, which is shorter than its diff:
```python
import functools
import math

import jax
import jax.numpy as jnp
from jax import lax
from jax.experimental import pallas as pl
from jax.experimental.pallas import tpu as pltpu
from jax.sharding import PartitionSpec as P

TILE = 32
WIN = 8
HEAD = 32

norm_eps = 1e-05
unit_eps = 1e-06
LOG2E = math.log2(math.e)
VMEM_BYTES = 48 * 2**20

NN = (((1,), (0,)), ((), ()))
NT = (((1,), (1,)), ((), ()))
TN = (((0,), (0,)), ((), ()))


def dot(a, b, dims=NN):
    return lax.dot_general(a, b, dims, preferred_element_type=jnp.float32)


def split(x):
    high = x.astype(jnp.bfloat16)
    return high, (x - high.astype(jnp.float32)).astype(jnp.bfloat16)


def head_sums(x):
    return jnp.sum(x.reshape(x.shape[0] // HEAD, HEAD, x.shape[1]), axis=1, keepdims=True)


def by_head(x, factor):
    return (x.reshape(x.shape[0] // HEAD, HEAD, x.shape[1]) * factor).reshape(x.shape)


def join_kernel(agents, tile_cols, buffers, place, live, ego, *refs):
    bufs, refs = refs[:buffers], refs[buffers:]
    wq, wkv, wout, scale, out, landed, sems = refs
    r = pl.program_id(0)
    height, _, channels = ego.shape[1:]
    slots = agents * tile_cols
    sizes = [b.shape[0] for b in bufs]

    def fetch(i, _):
        @pl.when(live[i] > 0)
        def _():
            start = 0
            for b, size in zip(bufs, sizes):
                here = place[i] - start

                @pl.when((here >= 0) & (here < size))
                def _(b=b, here=here):
                    pltpu.make_async_copy(b.at[here], landed.at[i], sems.at[i]).start()

                start += size

        return 0

    @pl.when(r == 0)
    def _():
        lax.fori_loop(0, landed.shape[0], fetch, 0)

    heads = channels // HEAD
    scale_col = scale[...].reshape(heads, 1, 1)
    for t in range(tile_cols):
        cells = ego[0, :, t * TILE : (t + 1) * TILE, :].reshape(height * TILE, channels)
        queries = dot(wq[...], cells, NT)
        factor = lax.rsqrt(head_sums(queries * queries) + unit_eps) * scale_col

        def agent(x):
            kv = dot(wkv[...], x, NT).astype(jnp.bfloat16).astype(jnp.float32)
            keys, values = kv[:channels], kv[channels:]
            score = head_sums(queries * keys) * factor
            return score * lax.rsqrt(head_sums(keys * keys) + unit_eps), values

        scores, values = [], []
        s, v = agent(cells)
        scores.append(s)
        values.append(v)
        for a in range(agents):
            i = r * slots + a * tile_cols + t

            @pl.when(live[i] > 0)
            def _(i=i):
                pltpu.make_async_copy(bufs[0].at[0], landed.at[i], sems.at[i]).wait()

            x = landed[i].reshape(height * TILE, channels)
            x = jnp.where(live[i] > 0, x, jnp.zeros_like(x))
            s, v = agent(x)
            scores.append(jnp.where(live[i] > 0, s, -1e30))
            values.append(v)
        top = functools.reduce(jnp.maximum, scores)
        weights = [jnp.exp(s - top) for s in scores]
        total = functools.reduce(jnp.add, weights)
        inverse = 1.0 / total
        mix = by_head(values[0], weights[0] * inverse)
        for w, v in zip(weights[1:], values[1:]):
            mix = mix + by_head(v, w * inverse)
        joined = dot(mix.astype(jnp.bfloat16), wout[...], TN)
        out[0, :, t * TILE : (t + 1) * TILE, :] = joined.astype(jnp.bfloat16).reshape(
            height, TILE, channels
        )


def join_agents(maps, bufs, place, live, wq, wkv, wout, scale):
    vehicles, height, width, channels = maps.shape
    tile_cols = width // TILE
    agents = place.shape[0] // (vehicles * tile_cols)
    whole = lambda x: pl.BlockSpec(x.shape, lambda r, *_: (0,) * x.ndim)
    block = pl.BlockSpec((1, height, width, channels), lambda r, *_: (r, 0, 0, 0))
    weights = (wq.T, wkv.T, wout, scale.reshape(-1, 1))
    cells = vehicles * height * width
    return pl.pallas_call(
        functools.partial(join_kernel, agents, tile_cols, len(bufs)),
        out_shape=jax.ShapeDtypeStruct(maps.shape, jnp.bfloat16),
        grid_spec=pltpu.PrefetchScalarGridSpec(
            num_scalar_prefetch=2,
            grid=(vehicles,),
            in_specs=[block]
            + [pl.BlockSpec(memory_space=pl.ANY)] * len(bufs)
            + [whole(w) for w in weights],
            out_specs=block,
            scratch_shapes=[
                pltpu.VMEM((place.shape[0], height, TILE, channels), jnp.bfloat16),
                pltpu.SemaphoreType.DMA((place.shape[0],)),
            ],
        ),
        compiler_params=pltpu.CompilerParams(vmem_limit_bytes=VMEM_BYTES),
        cost_estimate=pl.CostEstimate(
            flops=cells * channels * channels * 20, bytes_accessed=cells * channels * 12, transcendentals=cells * 20
        ),
    )(place, live, maps, *bufs, *weights)


def norm(x, gain):
    average = jnp.mean(x, axis=-1, keepdims=True)
    centred = x - average
    spread = jnp.mean(centred * centred, axis=-1, keepdims=True)
    return (centred * lax.rsqrt(spread + norm_eps) * gain).astype(jnp.bfloat16)


def mixed_half(x, above, below, taps):
    rows, cols, channels = x.shape
    tall = jnp.concatenate([above, x, below], axis=0)

    def column(at):
        part = tall[0:rows] * taps[at]
        part = part + tall[1 : rows + 1] * taps[3 + at]
        return part + tall[2 : rows + 2] * taps[6 + at]

    total = x + column(1)
    place = lax.broadcasted_iota(jnp.int32, (cols, channels), 0)[None]
    flat = (rows * cols, channels)
    left = pltpu.roll(column(0).reshape(flat), 1, 0).reshape(x.shape)
    total = total + jnp.where(place == 0, 0.0, left)
    right = pltpu.roll(column(2).reshape(flat), rows * cols - 1, 0).reshape(x.shape)
    return total + jnp.where(place == cols - 1, 0.0, right)


def window_kernel(ego, joined, ego_up, ego_down, join_up, join_down, taps, gain_one, wq, wk, wv, wo,
                  scale, gain_two, up, down, out, mixed_ref):
    rows, cols, channels = ego.shape[1:]
    width = 2 * channels
    windows = cols // WIN
    in_window = rows * WIN
    cells = rows * cols
    heads = width // HEAD
    f32 = jnp.float32
    for half, (x, above, below) in enumerate(((ego, ego_up, ego_down), (joined, join_up, join_down))):
        lanes = slice(half * channels, (half + 1) * channels)
        part = mixed_half(x[0].astype(f32), above[0].astype(f32), below[0].astype(f32),
                          [taps[i : i + 1, lanes].reshape(1, 1, channels) for i in range(9)])
        part = jnp.swapaxes(part.reshape(rows, windows, WIN, channels), 0, 1)
        mixed_ref[:, lanes] = part.reshape(cells, channels)
    hidden = norm(mixed_ref[...], gain_one[...])
    queries = dot(wq[...], hidden, NT)
    values = dot(wv[...], hidden, NT).astype(jnp.bfloat16)
    keys = dot(hidden, wk[...])
    factor = lax.rsqrt(head_sums(queries * queries) + unit_eps) * scale[...].reshape(heads, 1, 1)
    queries = by_head(queries, factor)
    member = (
        lax.broadcasted_iota(jnp.int32, (width, width), 0) // HEAD
        == lax.broadcasted_iota(jnp.int32, (width, width), 1) // HEAD
    ).astype(f32).astype(jnp.bfloat16)
    square_high, square_low = split(keys * keys)
    keys = keys * lax.rsqrt(dot(square_high, member) + dot(square_low, member) + unit_eps)
    key_high, key_low = split(keys)

    pair = 2 * in_window
    group = 4 * HEAD
    lane = lax.broadcasted_iota(jnp.int32, (width, pair), 1) < in_window
    even = (lax.broadcasted_iota(jnp.int32, (width, pair), 0) // HEAD) % 2 == 0
    blank = jnp.zeros((2 * HEAD, pair), jnp.bfloat16)
    blank_p = jnp.zeros((in_window, 4 * in_window), jnp.bfloat16)
    lane_head = lax.broadcasted_iota(jnp.int32, (HEAD, pair), 1) < in_window
    attended = []
    for p in range(windows // 2):
        straight = queries[:, p * pair : (p + 1) * pair]
        turned = pltpu.roll(straight, in_window, 1)
        blocks = []
        for w in range(2):
            low, high = (straight, turned) if w == 0 else (turned, straight)
            blocks.append(split(jnp.where(even, jnp.where(lane, low, 0.0), jnp.where(lane, 0.0, high))))
        parts = []
        for g in range(width // group):
            channels_of = slice(g * group, (g + 1) * group)
            probs = []
            for w in range(2):
                at = (2 * p + w) * in_window
                k_high = key_high[at : at + in_window, channels_of]
                k_low = key_low[at : at + in_window, channels_of]

                def right(block):
                    block = block[channels_of]
                    return jnp.concatenate(
                        [
                            jnp.concatenate([block[: 2 * HEAD], blank], axis=1),
                            jnp.concatenate([blank, block[2 * HEAD :]], axis=1),
                        ],
                        axis=0,
                    )

                first = dot(jnp.concatenate([k_high, k_low], axis=0), right(blocks[w][0]))
                score = first[:in_window] + first[in_window:] + dot(k_high, right(blocks[w][1]))
                weight = jnp.exp2(score - jnp.max(score, axis=0, keepdims=True))
                weight = weight * (1.0 / jnp.sum(weight, axis=0, keepdims=True))
                weight = weight.astype(jnp.bfloat16)
                probs.append(
                    jnp.concatenate([weight, blank_p] if w == 0 else [blank_p, weight], axis=0)
                )
            v = values[channels_of, p * pair : (p + 1) * pair]
            first, second = dot(v, probs[0]), dot(v, probs[1])
            for h in range(4):
                rows_of = slice(h * HEAD, (h + 1) * HEAD)
                cols_of = slice((h // 2) * pair, (h // 2 + 1) * pair)
                a, b = first[rows_of, cols_of], second[rows_of, cols_of]
                if h % 2 == 0:
                    b = pltpu.roll(b, in_window, 1)
                else:
                    a = pltpu.roll(a, in_window, 1)
                parts.append(jnp.where(lane_head, a, b))
        attended.append(jnp.concatenate(parts, axis=0).astype(jnp.bfloat16))
    attended = jnp.concatenate(attended, axis=1)
    mixed = mixed_ref[...] + dot(attended, wo[...], TN)
    hidden = norm(mixed, gain_two[...])
    inner = dot(hidden, up[...])
    inner = (0.5 * inner * (1.0 + jnp.tanh(0.5 * inner))).astype(jnp.bfloat16)
    result = mixed + dot(inner, down[...])
    result = jnp.swapaxes(result.reshape(windows, rows, WIN, width), 0, 1)
    out[0] = result.reshape(rows, cols, width).astype(jnp.bfloat16)


def window_layer(maps, joined, edges, conv_weight, gain_first, window_in, window_out, window_scale,
                 gain_second, hidden_up, hidden_down):
    vehicles, height, cols, channels = maps.shape
    width = 2 * channels
    whole = lambda x: pl.BlockSpec(x.shape, lambda r: (0,) * x.ndim)
    block = lambda n, c: pl.BlockSpec((1, n, cols, c), lambda r: (r, 0, 0, 0))
    weights = (
        conv_weight.reshape(9, width),
        gain_first[None],
        window_in[:, :width].T,
        window_in[:, width : 2 * width],
        window_in[:, 2 * width :].T,
        window_out,
        (window_scale * LOG2E).reshape(-1, 1),
        gain_second[None],
        hidden_up,
        hidden_down,
    )
    cells = vehicles * height * cols
    return pl.pallas_call(
        window_kernel,
        out_shape=jax.ShapeDtypeStruct((vehicles, height, cols, width), jnp.bfloat16),
        grid=(vehicles,),
        in_specs=[block(height, channels)] * 2 + [block(1, channels)] * 4 + [whole(w) for w in weights],
        out_specs=block(height, width),
        scratch_shapes=[pltpu.VMEM((height * cols, width), jnp.float32)],
        compiler_params=pltpu.CompilerParams(vmem_limit_bytes=VMEM_BYTES),
        cost_estimate=pl.CostEstimate(
            flops=cells * width * width * 30, bytes_accessed=cells * width * 6, transcendentals=cells * width * 4
        ),
    )(maps, joined, *edges, *weights)


def edges_of(x):
    count = lax.axis_size("row")
    rows = x.shape[1]
    above = lax.ppermute(x[:, rows - 1 :], "row", [(i, i + 1) for i in range(count - 1)])
    below = lax.ppermute(x[:, :1], "row", [(i + 1, i) for i in range(count - 1)])
    return above, below


def pack_kernel(tile_cols, chosen, maps, packed, sems):
    def start(i, _):
        column = pl.multiple_of(chosen[i] % tile_cols * TILE, TILE)
        pltpu.make_async_copy(
            maps.at[chosen[i] // tile_cols, :, pl.ds(column, TILE), :], packed.at[i], sems.at[i]
        ).start()
        return 0

    def finish(i, _):
        pltpu.make_async_copy(maps.at[0, :, pl.ds(0, TILE), :], packed.at[i], sems.at[i]).wait()
        return 0

    count = packed.shape[0]
    lax.fori_loop(0, count, start, 0)
    lax.fori_loop(0, count, finish, 0)


def pack_tiles(maps, chosen):
    _, height, width, channels = maps.shape
    count = chosen.shape[0]
    return pl.pallas_call(
        functools.partial(pack_kernel, width // TILE),
        out_shape=jax.ShapeDtypeStruct((count, height, TILE, channels), maps.dtype),
        grid_spec=pltpu.PrefetchScalarGridSpec(
            num_scalar_prefetch=1,
            grid=(1,),
            in_specs=[pl.BlockSpec(maps.shape, lambda i, *_: (0, 0, 0, 0))],
            out_specs=pl.BlockSpec(memory_space=pl.ANY),
            scratch_shapes=[pltpu.SemaphoreType.DMA((count,))],
        ),
        compiler_params=pltpu.CompilerParams(vmem_limit_bytes=VMEM_BYTES),
        cost_estimate=pl.CostEstimate(flops=0, bytes_accessed=4 * maps.size, transcendentals=0),
    )(chosen.astype(jnp.int32), maps)


def exchange(bev_maps, senders, shifts, counts):
    vehicles_here, height, width_cells, channels = bev_maps.shape
    agents = senders.shape[1]
    devices = lax.axis_size("veh")
    myself = lax.axis_index("veh")
    tile_cols = width_cells // TILE
    pairs = vehicles_here * agents
    capacity = tile_cols * max(1, pairs // devices)
    send_all = senders.reshape(devices, pairs)
    shift_all = shifts.reshape(devices, pairs)
    live_all = (jnp.arange(agents)[None, :] < counts[:, None]).reshape(devices, pairs)
    tiles_all = jnp.where(live_all, tile_cols - jnp.abs(shift_all), 0)
    source_all = send_all // vehicles_here
    same = source_all[:, :, None] == source_all[:, None, :]
    before = jnp.arange(pairs)[None, :] < jnp.arange(pairs)[:, None]
    start_all = jnp.sum(jnp.where(same & before[None], tiles_all[:, None, :], 0), axis=2)
    step = jnp.arange(tile_cols, dtype=jnp.int32)
    tile_of = (
        (send_all % vehicles_here * tile_cols + jnp.maximum(shift_all, 0))[:, :, None] + step
    ).reshape(devices, pairs * tile_cols)
    slot_of = jnp.where(
        ((source_all == myself)[:, :, None]) & (step < tiles_all[:, :, None]),
        start_all[:, :, None] + step,
        -1,
    ).reshape(devices, pairs * tile_cols)
    hit = slot_of[:, None, :] == jnp.arange(capacity)[None, :, None]
    chosen = jnp.sum(jnp.where(hit, tile_of[:, None, :], 0), axis=2).reshape(-1)
    packed = pack_tiles(bev_maps, chosen)
    arrived = lax.all_to_all(
        packed.reshape(devices, capacity, height, TILE, channels), "veh", 0, 0, tiled=True
    ).reshape(devices * capacity, height, TILE, channels)
    shifted = step + shift_all[myself][:, None]
    inside = (shifted >= 0) & (shifted < tile_cols) & live_all[myself][:, None]
    place = (
        (source_all[myself] * capacity + start_all[myself])[:, None]
        + step
        - jnp.maximum(-shift_all[myself], 0)[:, None]
    )
    place = jnp.where(inside, place, 0)
    return [arrived], place.reshape(-1).astype(jnp.int32), inside.reshape(-1).astype(jnp.int32)


def on_device(
    bev_maps,
    senders,
    shifts,
    counts,
    agent_query,
    agent_keyvalue,
    agent_out,
    agent_scale,
    conv_weight,
    gain_first,
    window_in,
    window_out,
    window_scale,
    gain_second,
    hidden_up,
    hidden_down,
):
    ego_up, ego_down = edges_of(bev_maps)
    bufs, place, live = exchange(bev_maps, senders, shifts, counts)
    joined = join_agents(
        bev_maps, bufs, place, live, agent_query, agent_keyvalue, agent_out, agent_scale
    )
    join_up, join_down = edges_of(joined)
    return window_layer(
        bev_maps,
        joined,
        (ego_up, ego_down, join_up, join_down),
        conv_weight,
        gain_first,
        window_in,
        window_out,
        window_scale,
        gain_second,
        hidden_up,
        hidden_down,
    )


def solution(mesh):
    split_maps = P("veh", "row", None, None)
    return jax.shard_map(
        on_device,
        mesh=mesh,
        in_specs=(split_maps,) + (P(),) * 15,
        out_specs=split_maps,
        check_vma=False,
    )
```

time: 433 us -> 181 us (0.42)
  matrix products: 139 us -> 0 us
  local copies, waits for them, and re-layouts: 125 us -> 9.49 us
  Pallas kernels: 0 us -> 62 us
  other arithmetic: 44.3 us -> 0.69 us
  loops' own time: 14.1 us -> 0 us
  waiting for transfers between devices: 95.2 us -> 88.9 us
  starting transfers between devices: 13.3 us -> 19.1 us
    dot_general x70 -> x0, matrix products: 139 us -> none  [the longest x4 45.5 us: window_layer(): jnp.einsum('bxyhqd,bxyhkd->bxyhqk', queries, key_part, precision=exact_dot)]
    pallas_call x0 -> x3, Pallas kernels: none -> 62 us  [the longest x1 36 us: window_layer(): pl.pallas_call(window_kernel, out_shape=jax.ShapeDtypeStruct((vehicles, h...]
    reshape x18 -> x6, local copies, waits for them, and re-layouts: 40.9 us -> 0.42 us  [the longest x1 0.09 us: join_agents(): weights = (wq.T, wkv.T, wout, scale.reshape(-1, 1))]
    convert_element_type x12 -> x0, local copies, waits for them, and re-layouts: 35.8 us -> none  [window_layer(): attended = from_windows(attended, height, width_cells).astype(jnp.bfloat16)]
    gather x5 -> x0, local copies, waits for them, and re-layouts: 22.6 us -> none  [the longest x4 17 us: agent_group(): sent_keyvalue = arrived[group_slots[:, None, :], band_rows]]
    reduce_sum x21 -> x2, other arithmetic: 17.1 us -> 0.53 us  [the longest x1 0.29 us: exchange(): jnp.sum(jnp.where(same & before[None], tiles_all[:, None, :], 0), axis=2)]
    another operation x2 -> x0, loops' own time: 14.1 us -> none  [the longest x1 13.3 us: on_device(): lax.map(layer_group, padded.reshape(block_count, group_size, height + 2,...]
    sub x4 -> x0, other arithmetic: 12.7 us -> none  [window_layer(): weight = jnp.exp(scores - row_top)]
  transfers between devices with their start and end apart: 3 -> 5, of which waited for: 3 -> 3; matrix products, arithmetic and copies ran while one was open for 1% -> 2% of each run, Pallas kernels for 0% -> 13%
where the time goes in v1:
time: 181 us
  waiting for transfers between devices  88.9 us (49%)
  Pallas kernels  62 us (34%)
  starting transfers between devices  19.1 us (11%)
  local copies, waits for them, and re-layouts  9.49 us (5%)
    all_to_all x1, waiting for transfers between devices, exchange(): lax.all_to_all(packed.reshape(devices, capacity, height, TILE, channels),...  84.3 us
    pallas_call x1, Pallas kernels, window_layer(): pl.pallas_call(window_kernel, out_shape=jax.ShapeDtypeStruct((vehicles, h...  36 us
    pallas_call x1, Pallas kernels, join_agents(): pl.pallas_call(functools.partial(join_kernel, agents, tile_cols, len(bufs...  22.7 us
    ppermute x2, starting transfers between devices, edges_of(): lax.ppermute(x[:, rows - 1:], 'row', [(i, i + 1) for i in range(count - 1)])  8.76 us
    all_to_all x1, starting transfers between devices, exchange(): lax.all_to_all(packed.reshape(devices, capacity, height, TILE, channels),...  6.53 us
    unnamed x36, local copies, waits for them, and re-layouts  5.28 us
    ppermute x2, waiting for transfers between devices, edges_of(): lax.ppermute(x[:, :1], 'row', [(i + 1, i) for i in range(count - 1)])  4.36 us
    ppermute x2, starting transfers between devices, edges_of(): lax.ppermute(x[:, :1], 'row', [(i + 1, i) for i in range(count - 1)])  3.84 us
  transfers between devices with their start and end apart: 5, of which 3 were waited for; matrix products, arithmetic and copies ran while one was open for 2% of the time, Pallas kernels for 13%

profile of v1, /device:TPU:1, one launch (start us, length us, event | category | flops | bytes accessed | tf_op | source)
XLA Modules:
  0.0 180.6 jit_solution(17230660186911292349)
XLA Ops:
  0.0 0.8 copy.39
  0.8 0.1 reshape.269
  0.9 0.7 lt.97
  1.6 0.1 copy.40
  1.7 0.1 copy.41
  1.7 0.1 lt.95
  1.8 0.8 copy.42
  2.6 0.1 reshape.270
  2.7 0.1 add.132
  2.8 0.1 copy.44
  2.9 0.3 select_reduce_fusion
  3.2 0.1 copy.45
  3.3 0.1 copy.43
  3.4 0.1 copy.47
  3.6 0.1 add_select_fusion
  3.7 0.1 copy.48
  3.7 0.1 copy.46
  3.8 0.2 select_reduce_fusion.1
  4.0 0.1 reshape.271.chosen
  4.1 1.2 copy-done.1
  5.3 3.4 %shard_map.154 = bf16[64,8,32,128]{3,2,1,0:T(8,128)(2,1)S(1)} custom-call(s32[64]{0:T(128)S(1)} %reshape.271.chosen, bf16[8,8,64,128]{3,2,1,0:T(8,128)(2,1)S(1)} %copy-done.1), custom_call_target="tpu_custom_call" | custom-call | bytes 2097152 | tf_op jit(solution)/shard_map/pallas_call | solution.py:320
  8.7 2.0 %copy-done = bf16[64,8,32,128]{3,2,1,0:T(8,128)(2,1)} copy-done((bf16[64,8,32,128]{3,2,1,0:T(8,128)(2,1)}, bf16[64,8,32,128]{3,2,1,0:T(8,128)(2,1)S(1)}, u32[]{:S(2)}) %copy-start) | copy-done | bytes 4194328
  10.8 6.5 %all-to-all-start = ((bf16[8,8,8,32,128]{4,3,2,1,0:T(8,128)(2,1)}), bf16[8,8,8,32,128]{4,3,2,1,0:T(8,128)(2,1)}, u32[]{:S(2)}, u32[]{:S(2)}) async-start(bf16[8,8,8,32,128]{4,3,2,1,0:T(8,128)(2,1)} %bitcast.24), calls=%async_computation | async-start | bytes 8388608 | tf_op jit(solution)/shard_map/all_to_all | solution.py:363
  17.3 0.7 fusion.11
  18.0 3.9 %collective-permute-start = (bf16[8,1,64,128]{3,2,1,0:T(8,128)(2,1)}, bf16[8,1,64,128]{3,2,1,0:T(8,128)(2,1)S(1)}, u32[]{:S(2)}, u32[]{:S(2)}) collective-permute-start(bf16[8,1,64,128]{3,2,1,0:T(8,128)(2,1)} %get-tuple-element.16), channel_id=1, source_target_pairs={{0,1},{1,2},{2,3},{4,5},{5,6},{6,7},{8,9},{9,10},{10,11},{12,13},{... | collective-permute-start | bytes 393224 | tf_op jit(solution)/shard_map/ppermute | solution.py:295
  22.0 1.9 %collective-permute-start.1 = (bf16[8,1,64,128]{3,2,1,0:T(8,128)(2,1)}, bf16[8,1,64,128]{3,2,1,0:T(8,128)(2,1)}, u32[]{:S(2)}, u32[]{:S(2)}) collective-permute-start(bf16[8,1,64,128]{3,2,1,0:T(8,128)(2,1)} %get-tuple-element.15), channel_id=1, source_target_pairs={{1,0},{2,1},{3,2},{5,4},{6,5},{7,6},{9,8},{10,9},{11,10},{13,12},{... | collective-permute-start | bytes 393224 | tf_op jit(solution)/shard_map/ppermute | solution.py:296
  23.9 0.1 and.83
  24.0 0.1 and.84
  24.1 0.1 add.135
  24.2 0.1 add.136
  24.3 0.1 sub.30
  24.4 0.1 sub.31
  24.5 0.1 add.140
  24.6 0.1 add.141
  24.7 0.1 copy.49
  24.8 0.1 copy.50
  25.0 0.1 copy.51.refs_4_
  25.2 0.1 copy.55
  25.3 0.1 copy.56
  25.4 84.3 %all-to-all-done = bf16[8,8,8,32,128]{4,3,2,1,0:T(8,128)(2,1)} async-done(((bf16[8,8,8,32,128]{4,3,2,1,0:T(8,128)(2,1)}), bf16[8,8,8,32,128]{4,3,2,1,0:T(8,128)(2,1)}, u32[]{:S(2)}, u32[]{:S(2)}) %all-to-all-start) | async-done | bytes 4194336 | tf_op jit(solution)/shard_map/all_to_all | solution.py:363
  109.7 22.7 %shard_map.155.joined = bf16[8,8,64,128]{3,2,1,0:T(8,128)(2,1)S(1)} custom-call(s32[64]{0:T(128)S(1)} %subtract_select_fusion.1.place, s32[64]{0:T(128)S(1)} %get-tuple-element.7.live, bf16[8,8,64,128]{3,2,1,0:T(8,128)(2,1)S(1)} %copy-done.2, bf16[64,8,32,128]{3,2,1,0:T(8,128)(2,1)} %bitcast.8.refs_0_, bf16[128,128]{1,0:T(8,128)(2,1)S(1)} %bitcast.26, ...), custom_call_target="tpu_custom_call" | custom-call | flops 1342177280 | bytes 6291456 | tf_op jit(solution)/shard_map/pallas_call | solution.py:119
  132.4 0.7 fusion.10
  133.1 4.8 %collective-permute-start.2 = (bf16[8,1,64,128]{3,2,1,0:T(8,128)(2,1)}, bf16[8,1,64,128]{3,2,1,0:T(8,128)(2,1)}, u32[]{:S(2)}, u32[]{:S(2)}) collective-permute-start(bf16[8,1,64,128]{3,2,1,0:T(8,128)(2,1)} %get-tuple-element.14), channel_id=1, source_target_pairs={{0,1},{1,2},{2,3},{4,5},{5,6},{6,7},{8,9},{9,10},{10,11},{12,13},{... | collective-permute-start | bytes 393224 | tf_op jit(solution)/shard_map/ppermute | solution.py:295
  138.0 1.9 %collective-permute-start.3 = (bf16[8,1,64,128]{3,2,1,0:T(8,128)(2,1)}, bf16[8,1,64,128]{3,2,1,0:T(8,128)(2,1)}, u32[]{:S(2)}, u32[]{:S(2)}) collective-permute-start(bf16[8,1,64,128]{3,2,1,0:T(8,128)(2,1)} %get-tuple-element.13), channel_id=1, source_target_pairs={{1,0},{2,1},{3,2},{5,4},{6,5},{7,6},{9,8},{10,9},{11,10},{13,12},{... | collective-permute-start | bytes 393224 | tf_op jit(solution)/shard_map/ppermute | solution.py:296
  139.9 0.1 copy.54.scale
  140.0 0.2 collective-permute-done.2.join_up
  140.2 4.4 %collective-permute-done.3.join_down = bf16[8,1,64,128]{3,2,1,0:T(8,128)(2,1)} collective-permute-done((bf16[8,1,64,128]{3,2,1,0:T(8,128)(2,1)}, bf16[8,1,64,128]{3,2,1,0:T(8,128)(2,1)}, u32[]{:S(2)}, u32[]{:S(2)}) %collective-permute-start.3) | collective-permute-done | bytes 131104 | tf_op jit(solution)/shard_map/ppermute | solution.py:296
  144.6 36.0 %shard_map.156 = bf16[8,8,64,256]{3,2,1,0:T(8,128)(2,1)} custom-call(bf16[8,8,64,128]{3,2,1,0:T(8,128)(2,1)S(1)} %copy-done.2, bf16[8,8,64,128]{3,2,1,0:T(8,128)(2,1)S(1)} %shard_map.155.joined, bf16[8,1,64,128]{3,2,1,0:T(8,128)(2,1)S(1)} %collective-permute-done.ego_up, bf16[8,1,64,128]{3,2,1,0:T(8,128)(2,1)} %collective-permute-done.1.ego_down, ...), custom_call_target="tpu_custom_call" | custom-call | flops 8053063680 | bytes 6291456 | tf_op jit(solution)/shard_map/pallas_call | solution.py:278
  (49 shorter events, 0.3 us)
Async XLA Ops:
  4.1 1.2 copy-start.1
  8.7 2.0 %copy-start = (bf16[64,8,32,128]{3,2,1,0:T(8,128)(2,1)}, bf16[64,8,32,128]{3,2,1,0:T(8,128)(2,1)S(1)}, u32[]{:S(2)}) copy-start(bf16[64,8,32,128]{3,2,1,0:T(8,128)(2,1)S(1)} %shard_map.154) | copy-start | bytes 12582916
  10.7 6.6 %copy-start.2 = (bf16[8,8,64,128]{3,2,1,0:T(8,128)(2,1)S(1)}, bf16[8,8,64,128]{3,2,1,0:T(8,128)(2,1)}, u32[]{:S(2)}) copy-start(bf16[8,8,64,128]{3,2,1,0:T(8,128)(2,1)} %ego.3) | copy-start | bytes 3145732
  10.7 14.0 %copy-start.11 = (bf16[128,128]{1,0:T(8,128)(2,1)S(1)}, bf16[128,128]{1,0:T(8,128)(2,1)}, u32[]{:S(2)}) copy-start(bf16[128,128]{1,0:T(8,128)(2,1)} %param.20) | copy-start | bytes 98308
  10.7 14.1 %copy-start.10 = (bf16[128,256]{1,0:T(8,128)(2,1)S(1)}, bf16[128,256]{1,0:T(8,128)(2,1)}, u32[]{:S(2)}) copy-start(bf16[128,256]{1,0:T(8,128)(2,1)} %param.21) | copy-start | bytes 196612
  10.7 14.3 %copy-start.13 = (f32[4]{0:T(128)S(1)}, f32[4]{0:T(128)}, u32[]{:S(2)}) copy-start(f32[4]{0:T(128)} %param.23) | copy-start | bytes 52
  10.7 14.4 %copy-start.12 = (f32[3,3,256]{2,1,0:T(4,128)S(1)}, f32[3,3,256]{2,1,0:T(4,128)}, u32[]{:S(2)}) copy-start(f32[3,3,256]{2,1,0:T(4,128)} %param.24) | copy-start | bytes 27652
  10.7 14.4 %copy-start.9 = (bf16[256,768]{1,0:T(8,128)(2,1)S(1)}, bf16[256,768]{1,0:T(8,128)(2,1)}, u32[]{:S(2)}) copy-start(bf16[256,768]{1,0:T(8,128)(2,1)} %param.26) | copy-start | bytes 1179652
  10.7 99.0 %copy-start.3 = (bf16[128,128]{1,0:T(8,128)(2,1)S(1)}, bf16[128,128]{1,0:T(8,128)(2,1)}, u32[]{:S(2)}) copy-start(bf16[128,128]{1,0:T(8,128)(2,1)} %refs_3_.1) | copy-start | bytes 98308
  10.8 98.9 %all-to-all-start = ((bf16[8,8,8,32,128]{4,3,2,1,0:T(8,128)(2,1)}), bf16[8,8,8,32,128]{4,3,2,1,0:T(8,128)(2,1)}, u32[]{:S(2)}, u32[]{:S(2)}) async-start(bf16[8,8,8,32,128]{4,3,2,1,0:T(8,128)(2,1)} %bitcast.24), calls=%async_computation | async-start | bytes 8388608 | tf_op jit(solution)/shard_map/all_to_all | solution.py:363
  18.0 122.0 %collective-permute-start = (bf16[8,1,64,128]{3,2,1,0:T(8,128)(2,1)}, bf16[8,1,64,128]{3,2,1,0:T(8,128)(2,1)S(1)}, u32[]{:S(2)}, u32[]{:S(2)}) collective-permute-start(bf16[8,1,64,128]{3,2,1,0:T(8,128)(2,1)} %get-tuple-element.16), channel_id=1, source_target_pairs={{0,1},{1,2},{2,3},{4,5},{5,6},{6,7},{8,9},{9,10},{10,11},{12,13},{... | collective-permute-start | bytes 393224 | tf_op jit(solution)/shard_map/ppermute | solution.py:295
  22.0 118.0 %collective-permute-start.1 = (bf16[8,1,64,128]{3,2,1,0:T(8,128)(2,1)}, bf16[8,1,64,128]{3,2,1,0:T(8,128)(2,1)}, u32[]{:S(2)}, u32[]{:S(2)}) collective-permute-start(bf16[8,1,64,128]{3,2,1,0:T(8,128)(2,1)} %get-tuple-element.15), channel_id=1, source_target_pairs={{1,0},{2,1},{3,2},{5,4},{6,5},{7,6},{9,8},{10,9},{11,10},{13,12},{... | collective-permute-start | bytes 393224 | tf_op jit(solution)/shard_map/ppermute | solution.py:296
  24.8 115.1 %copy-start.14 = (f32[8]{0:T(128)S(1)}, f32[8]{0:T(128)}, u32[]{:S(2)}) copy-start(f32[8]{0:T(128)} %param.28) | copy-start | bytes 100
  24.9 119.6 %copy-start.4 = (bf16[256,512]{1,0:T(8,128)(2,1)S(1)}, bf16[256,512]{1,0:T(8,128)(2,1)}, u32[]{:S(2)}) copy-start(bf16[256,512]{1,0:T(8,128)(2,1)} %up.1) | copy-start | bytes 786436
  25.0 119.6 %copy-start.5 = (bf16[512,256]{1,0:T(8,128)(2,1)S(1)}, bf16[512,256]{1,0:T(8,128)(2,1)}, u32[]{:S(2)}) copy-start(bf16[512,256]{1,0:T(8,128)(2,1)} %down.1) | copy-start | bytes 786436
  25.0 119.6 %copy-start.6 = (bf16[256,256]{1,0:T(8,128)(2,1)S(1)}, bf16[256,256]{1,0:T(8,128)(2,1)}, u32[]{:S(2)}) copy-start(bf16[256,256]{1,0:T(8,128)(2,1)} %wo.1) | copy-start | bytes 393220
  25.0 119.6 %copy-start.7 = (f32[256]{0:T(256)S(1)}, f32[256]{0:T(256)}, u32[]{:S(2)}) copy-start(f32[256]{0:T(256)} %param.25) | copy-start | bytes 3076
  25.0 119.6 %copy-start.8 = (f32[256]{0:T(256)S(1)}, f32[256]{0:T(256)}, u32[]{:S(2)}) copy-start(f32[256]{0:T(256)} %param.29) | copy-start | bytes 3076
  133.1 7.1 %collective-permute-start.2 = (bf16[8,1,64,128]{3,2,1,0:T(8,128)(2,1)}, bf16[8,1,64,128]{3,2,1,0:T(8,128)(2,1)}, u32[]{:S(2)}, u32[]{:S(2)}) collective-permute-start(bf16[8,1,64,128]{3,2,1,0:T(8,128)(2,1)} %get-tuple-element.14), channel_id=1, source_target_pairs={{0,1},{1,2},{2,3},{4,5},{5,6},{6,7},{8,9},{9,10},{10,11},{12,13},{... | collective-permute-start | bytes 393224 | tf_op jit(solution)/shard_map/ppermute | solution.py:295
  138.0 6.6 %collective-permute-start.3 = (bf16[8,1,64,128]{3,2,1,0:T(8,128)(2,1)}, bf16[8,1,64,128]{3,2,1,0:T(8,128)(2,1)}, u32[]{:S(2)}, u32[]{:S(2)}) collective-permute-start(bf16[8,1,64,128]{3,2,1,0:T(8,128)(2,1)} %get-tuple-element.13), channel_id=1, source_target_pairs={{1,0},{2,1},{3,2},{5,4},{6,5},{7,6},{9,8},{10,9},{11,10},{13,12},{... | collective-permute-start | bytes 393224 | tf_op jit(solution)/shard_map/ppermute | solution.py:296

commit v2 on v1

v2 whole, which is shorter than its diff:
```python
import functools
import math

import jax
import jax.numpy as jnp
from jax import lax
from jax.experimental import pallas as pl
from jax.experimental.pallas import tpu as pltpu
from jax.sharding import PartitionSpec as P

TILE = 32
WIN = 8
HEAD = 32

norm_eps = 1e-05
unit_eps = 1e-06
LOG2E = math.log2(math.e)
VMEM_BYTES = 48 * 2**20
PHASES = 2

NN = (((1,), (0,)), ((), ()))
NT = (((1,), (1,)), ((), ()))
TN = (((0,), (0,)), ((), ()))


def dot(a, b, dims=NN):
    return lax.dot_general(a, b, dims, preferred_element_type=jnp.float32)


def split(x):
    high = x.astype(jnp.bfloat16)
    return high, (x - high.astype(jnp.float32)).astype(jnp.bfloat16)


def head_sums(x):
    return jnp.sum(x.reshape(x.shape[0] // HEAD, HEAD, x.shape[1]), axis=1, keepdims=True)


def by_head(x, factor):
    return (x.reshape(x.shape[0] // HEAD, HEAD, x.shape[1]) * factor).reshape(x.shape)


def phase_columns(phase):
    run = TILE // PHASES
    return [TILE - 1] + list(range(run + 1)) if phase == 0 else list(range(run + 1, TILE - 1))


def copy_tiles(chosen, pieces, packed, sems):
    def start(i, _):
        pltpu.make_async_copy(pieces.at[chosen[i]], packed.at[i], sems.at[i]).start()
        return 0

    def finish(i, _):
        pltpu.make_async_copy(pieces.at[0], packed.at[i], sems.at[i]).wait()
        return 0

    count = packed.shape[0]
    lax.fori_loop(0, count, start, 0)
    lax.fori_loop(0, count, finish, 0)


def turn_kernel(chosen, maps, turned, first, second, packed, scratch, sems):
    vehicles, rows, cols, channels = maps.shape
    tile_cols = cols // TILE
    run = TILE // PHASES

    def vehicle(v, _):
        for i in range(rows):
            scratch[pl.ds(i, cols, stride=rows), :] = maps[v, i].astype(jnp.float32)
        x = scratch[...].astype(jnp.bfloat16).reshape(cols, rows, channels)
        turned[v] = x
        for t in range(tile_cols):
            at = v * tile_cols + t
            tile = x[t * TILE : (t + 1) * TILE]
            first[at] = jnp.concatenate([tile[TILE - 1 :], tile[: run + 1]], axis=0)
            second[at] = tile[run + 1 : TILE - 1]
        return 0

    lax.fori_loop(0, vehicles, vehicle, 0)
    copy_tiles(chosen, first, packed, sems)


def turn_maps(maps, chosen):
    vehicles, rows, cols, channels = maps.shape
    tiles = vehicles * (cols // TILE)
    count = chosen.shape[0]
    pieces = [(tiles, len(phase_columns(p)), rows, channels) for p in range(PHASES)]
    shapes = [(vehicles, cols, rows, channels), *pieces, (count, *pieces[0][1:])]
    whole = lambda shape: pl.BlockSpec(shape, lambda i, *_: (0,) * len(shape))
    return pl.pallas_call(
        turn_kernel,
        out_shape=[jax.ShapeDtypeStruct(shape, maps.dtype) for shape in shapes],
        grid_spec=pltpu.PrefetchScalarGridSpec(
            num_scalar_prefetch=1,
            grid=(1,),
            in_specs=[whole(maps.shape)],
            out_specs=[whole(shape) for shape in shapes[:3]] + [pl.BlockSpec(memory_space=pl.ANY)],
            scratch_shapes=[
                pltpu.VMEM((rows * cols, channels), jnp.float32),
                pltpu.SemaphoreType.DMA((count,)),
            ],
        ),
        compiler_params=pltpu.CompilerParams(vmem_limit_bytes=VMEM_BYTES),
        cost_estimate=pl.CostEstimate(flops=0, bytes_accessed=10 * maps.size, transcendentals=0),
    )(chosen, maps)


def pack_tiles(pieces, chosen):
    count = chosen.shape[0]
    return pl.pallas_call(
        copy_tiles,
        out_shape=jax.ShapeDtypeStruct((count, *pieces.shape[1:]), pieces.dtype),
        grid_spec=pltpu.PrefetchScalarGridSpec(
            num_scalar_prefetch=1,
            grid=(1,),
            in_specs=[pl.BlockSpec(pieces.shape, lambda i, *_: (0,) * pieces.ndim)],
            out_specs=pl.BlockSpec(memory_space=pl.ANY),
            scratch_shapes=[pltpu.SemaphoreType.DMA((count,))],
        ),
        compiler_params=pltpu.CompilerParams(vmem_limit_bytes=VMEM_BYTES),
        cost_estimate=pl.CostEstimate(flops=0, bytes_accessed=8 * pieces.size, transcendentals=0),
    )(chosen, pieces)


LANES = 128


def join_kernel(steps, place, ego, arrived, present, wq, wkv, wout, scale, out, top_row, low_row, landed, joined, sems):
    step = pl.program_id(0)
    agents, total, channels = landed.shape
    here = total // steps
    cells = arrived.shape[1]
    pieces = total // cells
    part = pieces // steps

    def copy(i, source):
        a, q = i // pieces, i % pieces
        start = pl.multiple_of(q * cells, 16)
        return pltpu.make_async_copy(arrived.at[source], landed.at[a, pl.ds(start, cells), :], sems.at[i])

    @pl.when(step == 0)
    def _():
        lax.fori_loop(0, agents * pieces, lambda i, _: (copy(i, place[i]).start(), 0)[1], 0)

    def wait(i, _):
        copy(i // part * pieces + step * part + i % part, 0).wait()
        return 0

    lax.fori_loop(0, agents * part, wait, 0)
    heads = channels // HEAD
    scale_col = scale[...].reshape(heads, 1, 1)
    for c in range(here // LANES):
        span = pl.ds(c * LANES, LANES)
        cells_here = ego[span, :]
        queries = dot(wq[...], cells_here, NT)
        factor = lax.rsqrt(head_sums(queries * queries) + unit_eps) * scale_col

        def agent(x):
            kv = dot(wkv[...], x, NT).astype(jnp.bfloat16).astype(jnp.float32)
            keys, values = kv[:channels], kv[channels:]
            score = head_sums(queries * keys) * factor
            return score * lax.rsqrt(head_sums(keys * keys) + unit_eps), values

        scores, values = zip(
            agent(cells_here),
            *(
                agent(landed[a, pl.ds(pl.multiple_of(step * here + c * LANES, LANES), LANES), :])
                for a in range(agents)
            ),
        )
        scores = [scores[0]] + [
            jnp.where(present[a : a + 1, c * LANES : (c + 1) * LANES].reshape(1, 1, LANES) > 0, s, -1e30)
            for a, s in enumerate(scores[1:])
        ]
        top = functools.reduce(jnp.maximum, scores)
        weights = [jnp.exp(s - top) for s in scores]
        inverse = 1.0 / functools.reduce(jnp.add, weights)
        mix = functools.reduce(jnp.add, [by_head(v, w * inverse) for w, v in zip(weights, values)])
        joined[span, :] = dot(mix.astype(jnp.bfloat16), wout[...], TN)
    out[...] = joined[...].astype(jnp.bfloat16)
    rows = here // top_row.shape[0]
    top_row[...] = joined[pl.ds(0, here // rows, stride=rows), :].astype(jnp.bfloat16)
    low_row[...] = joined[pl.ds(rows - 1, here // rows, stride=rows), :].astype(jnp.bfloat16)


def join_agents(pieces, arrived, place, live, wq, wkv, wout, scale):
    count, cols, rows, channels = pieces.shape
    agents = live.shape[0]
    cells = cols * rows
    total = count * cells
    steps = 2
    whole = lambda x: pl.BlockSpec(x.shape, lambda r, *_: (0,) * x.ndim)
    block = lambda n: pl.BlockSpec((n // steps, channels), lambda r, *_: (r, 0))
    weights = (wq.T, wkv.T, wout, scale.reshape(-1, 1))
    present = jnp.repeat(live.astype(jnp.float32), cells, axis=1)
    like = lambda n: jax.ShapeDtypeStruct((n, channels), jnp.bfloat16)
    return pl.pallas_call(
        functools.partial(join_kernel, steps),
        out_shape=[like(total), like(total // rows), like(total // rows)],
        grid_spec=pltpu.PrefetchScalarGridSpec(
            num_scalar_prefetch=1,
            grid=(steps,),
            in_specs=[
                block(total),
                pl.BlockSpec(memory_space=pl.ANY),
                pl.BlockSpec((agents, total // steps), lambda r, *_: (0, r)),
            ]
            + [whole(w) for w in weights],
            out_specs=[block(total), block(total // rows), block(total // rows)],
            scratch_shapes=[
                pltpu.VMEM((agents, total, channels), jnp.bfloat16),
                pltpu.VMEM((total // steps, channels), jnp.float32),
                pltpu.SemaphoreType.DMA((agents * count,)),
            ],
        ),
        compiler_params=pltpu.CompilerParams(vmem_limit_bytes=VMEM_BYTES),
        cost_estimate=pl.CostEstimate(
            flops=total * channels * channels * 40, bytes_accessed=total * channels * 12, transcendentals=total * 20
        ),
    )(
        place.reshape(-1),
        pieces.reshape(total, channels),
        arrived.reshape(-1, cells, channels),
        present,
        *weights,
    )


def norm(x, gain):
    average = jnp.mean(x, axis=-1, keepdims=True)
    centred = x - average
    spread = jnp.mean(centred * centred, axis=-1, keepdims=True)
    return (centred * lax.rsqrt(spread + norm_eps) * gain).astype(jnp.bfloat16)


def spread_rows(ref, rows_of, at, rows):
    count, channels = rows_of.shape
    ref[pl.ds(at, count, stride=rows), :] = rows_of.astype(jnp.float32)
    return ref[: count * rows].reshape(count, rows, channels)


def runs_of(phase, tile_cols, whole_map, pieces):
    run = TILE // PHASES
    out = []
    for t in range(tile_cols):
        first = t * TILE + phase * run - 1
        if pieces is None:
            last = first + run + 2
            blank = jnp.zeros_like(whole_map[:1])
            body = whole_map[max(first, 0) : min(last, tile_cols * TILE)]
            parts = ([blank] if first < 0 else []) + [body] + ([blank] if last > tile_cols * TILE else [])
        else:
            size = run + 2
            one = pieces[0]
            blank = jnp.zeros_like(one[:1])
            if phase == 0:
                left = one[(t - 1) * size : (t - 1) * size + 1] if t else blank
                parts = [left, one[t * size + 1 : (t + 1) * size]]
            else:
                rest = TILE - size
                right = one[(t + 1) * size + 1 : (t + 1) * size + 2] if t + 1 < tile_cols else blank
                parts = [
                    one[t * size + run : (t + 1) * size],
                    pieces[1][t * rest : (t + 1) * rest],
                    one[t * size : t * size + 1],
                    right,
                ]
        out.append(jnp.concatenate(parts, axis=0))
    return out


def taps_of(runs, above, below, taps):
    out = []
    for x, first, last in zip(runs, above, below):
        cols, rows, channels = x.shape
        row = lax.broadcasted_iota(jnp.int32, (rows, channels), 0)[None]
        flat = x.reshape(cols * rows, channels)
        over = jnp.where(row == 0, first, pltpu.roll(flat, 1, 0).reshape(x.shape))
        under = jnp.where(row == rows - 1, last, pltpu.roll(flat, cols * rows - 1, 0).reshape(x.shape))
        total = x[1 : cols - 1]
        for j in range(3):
            span = slice(j, cols - 2 + j)
            total = total + over[span] * taps[j] + x[span] * taps[3 + j] + under[span] * taps[6 + j]
        out.append(total.reshape((cols - 2) * rows, channels))
    return out


def window_kernel(phase, rows, *refs):
    ego, ego_up, ego_down, refs = *refs[:3], refs[3:]
    pieces, refs = [refs[3 * p : 3 * p + 3] for p in range(phase + 1)], refs[3 * phase + 3 :]
    taps, gain_one, wq, wk, wv, wo, scale, gain_two, up, down = refs[:10]
    out, mixed_ref, result_ref, halo = refs[10 + phase :]
    group_size, cols, _, channels = ego.shape
    tile_cols = cols // TILE
    run = TILE // PHASES
    width = 2 * channels
    in_window = rows * WIN
    here = tile_cols * run * rows
    cells = group_size * here
    windows = cells // in_window
    heads = width // HEAD
    f32 = jnp.float32
    for v in range(group_size):
        for half in range(2):
            lanes = slice(half * channels, (half + 1) * channels)
            weights = [taps[i : i + 1, lanes].reshape(1, 1, channels) for i in range(9)]
            if half == 0:
                centre = runs_of(phase, tile_cols, ego[v].astype(f32), None)
                above = runs_of(phase, tile_cols, spread_rows(halo.at[0], ego_up[v, 0], 0, rows), None)
                below = runs_of(phase, tile_cols, spread_rows(halo.at[1], ego_down[v, 0], rows - 1, rows), None)
            else:
                centre, above, below = [], [], []
                for p, (x, first, last) in enumerate(pieces):
                    centre.append(x[v].astype(f32).reshape(-1, rows, channels))
                    above.append(spread_rows(halo.at[2 + 2 * p], first[v], 0, rows))
                    below.append(spread_rows(halo.at[3 + 2 * p], last[v], rows - 1, rows))
                centre, above, below = (runs_of(phase, tile_cols, None, x) for x in (centre, above, below))
            for t, part in enumerate(taps_of(centre, above, below, weights)):
                at = v * here + t * run * rows
                mixed_ref[at : at + run * rows, lanes] = part
    hidden = norm(mixed_ref[...], gain_one[...])
    queries = dot(wq[...], hidden, NT)
    values = dot(wv[...], hidden, NT).astype(jnp.bfloat16)
    keys = dot(hidden, wk[...])
    factor = lax.rsqrt(head_sums(queries * queries) + unit_eps) * scale[...].reshape(heads, 1, 1)
    queries = by_head(queries, factor)
    member = (
        lax.broadcasted_iota(jnp.int32, (width, width), 0) // HEAD
        == lax.broadcasted_iota(jnp.int32, (width, width), 1) // HEAD
    ).astype(f32).astype(jnp.bfloat16)
    square_high, square_low = split(keys * keys)
    keys = keys * lax.rsqrt(dot(square_high, member) + dot(square_low, member) + unit_eps)
    key_high, key_low = split(keys)

    pair = 2 * in_window
    group = 4 * HEAD
    lane = lax.broadcasted_iota(jnp.int32, (width, pair), 1) < in_window
    even = (lax.broadcasted_iota(jnp.int32, (width, pair), 0) // HEAD) % 2 == 0
    blank = jnp.zeros((2 * HEAD, pair), jnp.bfloat16)
    blank_p = jnp.zeros((in_window, 4 * in_window), jnp.bfloat16)
    lane_head = lax.broadcasted_iota(jnp.int32, (HEAD, pair), 1) < in_window
    attended = []
    for p in range(windows // 2):
        straight = queries[:, p * pair : (p + 1) * pair]
        turned = pltpu.roll(straight, in_window, 1)
        blocks = []
        for w in range(2):
            low, high = (straight, turned) if w == 0 else (turned, straight)
            blocks.append(split(jnp.where(even, jnp.where(lane, low, 0.0), jnp.where(lane, 0.0, high))))
        parts = []
        for g in range(width // group):
            channels_of = slice(g * group, (g + 1) * group)
            probs = []
            for w in range(2):
                at = (2 * p + w) * in_window
                k_high = key_high[at : at + in_window, channels_of]
                k_low = key_low[at : at + in_window, channels_of]

                def right(block):
                    block = block[channels_of]
                    return jnp.concatenate(
                        [
                            jnp.concatenate([block[: 2 * HEAD], blank], axis=1),
                            jnp.concatenate([blank, block[2 * HEAD :]], axis=1),
                        ],
                        axis=0,
                    )

                first = dot(jnp.concatenate([k_high, k_low], axis=0), right(blocks[w][0]))
                score = first[:in_window] + first[in_window:] + dot(k_high, right(blocks[w][1]))
                weight = jnp.exp2(score - jnp.max(score, axis=0, keepdims=True))
                weight = weight * (1.0 / jnp.sum(weight, axis=0, keepdims=True))
                weight = weight.astype(jnp.bfloat16)
                probs.append(
                    jnp.concatenate([weight, blank_p] if w == 0 else [blank_p, weight], axis=0)
                )
            v = values[channels_of, p * pair : (p + 1) * pair]
            first, second = dot(v, probs[0]), dot(v, probs[1])
            for h in range(4):
                rows_of = slice(h * HEAD, (h + 1) * HEAD)
                cols_of = slice((h // 2) * pair, (h // 2 + 1) * pair)
                a, b = first[rows_of, cols_of], second[rows_of, cols_of]
                if h % 2 == 0:
                    b = pltpu.roll(b, in_window, 1)
                else:
                    a = pltpu.roll(a, in_window, 1)
                parts.append(jnp.where(lane_head, a, b))
        attended.append(jnp.concatenate(parts, axis=0).astype(jnp.bfloat16))
    attended = jnp.concatenate(attended, axis=1)
    mixed = mixed_ref[...] + dot(attended, wo[...], TN)
    hidden = norm(mixed, gain_two[...])
    inner = dot(hidden, up[...])
    inner = (0.5 * inner * (1.0 + jnp.tanh(0.5 * inner))).astype(jnp.bfloat16)
    result = mixed + dot(inner, down[...])
    for half in range(2):
        result_ref[half] = result[:, half * channels : (half + 1) * channels]
    for v in range(group_size):
        for t in range(tile_cols):
            for i in range(rows):
                at = v * here + t * run * rows + i
                for half in range(2):
                    lanes = slice(half * channels, (half + 1) * channels)
                    line = result_ref[half, pl.ds(at, run, stride=rows), :]
                    out[v, i, t, :, lanes] = line.astype(jnp.bfloat16)


def window_layer(phase, turned, ego_edges, pieces, before, conv_weight, gain_first, window_in, window_out,
                 window_scale, gain_second, hidden_up, hidden_down):
    vehicles, cols, rows, channels = turned.shape
    width = 2 * channels
    tile_cols = cols // TILE
    run = TILE // PHASES
    group = 2
    whole = lambda x: pl.BlockSpec(x.shape, lambda r: (0,) * x.ndim)
    block = lambda *shape: pl.BlockSpec((group, *shape), lambda r: (r,) + (0,) * len(shape))
    weights = (
        conv_weight.reshape(9, width),
        gain_first[None],
        window_in[:, :width].T,
        window_in[:, width : 2 * width],
        window_in[:, 2 * width :].T,
        window_out,
        (window_scale * LOG2E).reshape(-1, 1),
        gain_second[None],
        hidden_up,
        hidden_down,
    )
    pieces = [x.reshape(vehicles, -1, channels) for three in pieces for x in three]
    cells = vehicles * rows * tile_cols * run
    most = cols * rows
    operands = (turned, *ego_edges, *pieces, *weights)
    in_specs = (
        [block(cols, rows, channels)]
        + [block(1, cols, channels)] * 2
        + [block(*x.shape[1:]) for x in pieces]
        + [whole(w) for w in weights]
    )
    aliases = {}
    if before is not None:
        aliases = {len(operands): 0}
        operands += (before,)
        in_specs += [pl.BlockSpec(memory_space=pl.ANY)]
    return pl.pallas_call(
        functools.partial(window_kernel, phase, rows),
        out_shape=jax.ShapeDtypeStruct((vehicles, rows, tile_cols, PHASES, run, width), jnp.bfloat16),
        grid=(vehicles // group,),
        in_specs=in_specs,
        out_specs=pl.BlockSpec(
            (group, rows, tile_cols, None, run, width), lambda r: (r, 0, 0, phase, 0, 0)
        ),
        scratch_shapes=[
            pltpu.VMEM((group * rows * tile_cols * run, width), jnp.float32),
            pltpu.VMEM((2, group * rows * tile_cols * run, channels), jnp.float32),
            pltpu.VMEM((2 * PHASES + 2, most, channels), jnp.float32),
        ],
        input_output_aliases=aliases,
        compiler_params=pltpu.CompilerParams(vmem_limit_bytes=VMEM_BYTES),
        cost_estimate=pl.CostEstimate(
            flops=cells * width * width * 60, bytes_accessed=cells * width * 6, transcendentals=cells * width * 4
        ),
    )(*operands)


def beside(last, first):
    count = lax.axis_size("row")
    above = lax.ppermute(last, "row", [(i, i + 1) for i in range(count - 1)])
    below = lax.ppermute(first, "row", [(i + 1, i) for i in range(count - 1)])
    return above, below


def tables(vehicles_here, tile_cols, senders, shifts, counts):
    agents = senders.shape[1]
    devices = lax.axis_size("veh")
    myself = lax.axis_index("veh")
    pairs = vehicles_here * agents
    capacity = tile_cols * max(1, pairs // devices)
    send_all = senders.reshape(devices, pairs)
    shift_all = shifts.reshape(devices, pairs)
    live_all = (jnp.arange(agents)[None, :] < counts[:, None]).reshape(devices, pairs)
    tiles_all = jnp.where(live_all, tile_cols - jnp.abs(shift_all), 0)
    source_all = send_all // vehicles_here
    same = source_all[:, :, None] == source_all[:, None, :]
    before = jnp.arange(pairs)[None, :] < jnp.arange(pairs)[:, None]
    start_all = jnp.sum(jnp.where(same & before[None], tiles_all[:, None, :], 0), axis=2)
    step = jnp.arange(tile_cols, dtype=jnp.int32)
    tile_of = (
        (send_all % vehicles_here * tile_cols + jnp.maximum(shift_all, 0))[:, :, None] + step
    ).reshape(devices, pairs * tile_cols)
    slot_of = jnp.where(
        ((source_all == myself)[:, :, None]) & (step < tiles_all[:, :, None]),
        start_all[:, :, None] + step,
        -1,
    ).reshape(devices, pairs * tile_cols)
    hit = slot_of[:, None, :] == jnp.arange(capacity)[None, :, None]
    chosen = jnp.sum(jnp.where(hit, tile_of[:, None, :], 0), axis=2).reshape(-1)
    shifted = step + shift_all[myself][:, None]
    inside = (shifted >= 0) & (shifted < tile_cols) & live_all[myself][:, None]
    place = (
        (source_all[myself] * capacity + start_all[myself])[:, None]
        + step
        - jnp.maximum(-shift_all[myself], 0)[:, None]
    )
    place = jnp.where(inside, place, 0)
    by_agent = lambda x: jnp.swapaxes(x.reshape(vehicles_here, agents, tile_cols), 0, 1).reshape(agents, -1)
    return chosen.astype(jnp.int32), by_agent(place.astype(jnp.int32)), by_agent(inside)


def on_device(
    bev_maps,
    senders,
    shifts,
    counts,
    agent_query,
    agent_keyvalue,
    agent_out,
    agent_scale,
    conv_weight,
    gain_first,
    window_in,
    window_out,
    window_scale,
    gain_second,
    hidden_up,
    hidden_down,
):
    vehicles_here, rows, cols, channels = bev_maps.shape
    devices = lax.axis_size("veh")
    chosen, place, live = tables(vehicles_here, cols // TILE, senders, shifts, counts)
    turned, first, second, packed = turn_maps(bev_maps, chosen)
    ego_edges = beside(bev_maps[:, rows - 1 :], bev_maps[:, :1])

    def travel(x):
        x = x.reshape(devices, -1, *x.shape[1:])
        x = lax.all_to_all(x, "veh", 0, 0, tiled=True)
        return x.reshape(-1, *x.shape[2:])

    arrived = [travel(packed)]
    later = pack_tiles(second, chosen)
    arrived[0], later = lax.optimization_barrier((arrived[0], later))
    arrived.append(travel(later))
    result, pieces = None, []
    for phase, own in enumerate((first, second)):
        joined, top, low = join_agents(
            own, arrived[phase], place, live, agent_query, agent_keyvalue, agent_out, agent_scale
        )
        pieces.append((joined, *beside(low, top)))
        result = window_layer(
            phase,
            turned,
            ego_edges,
            pieces,
            result,
            conv_weight,
            gain_first,
            window_in,
            window_out,
            window_scale,
            gain_second,
            hidden_up,
            hidden_down,
        )
    return result.reshape(vehicles_here, rows, cols, 2 * channels)


def solution(mesh):
    split_maps = P("veh", "row", None, None)
    return jax.shard_map(
        on_device,
        mesh=mesh,
        in_specs=(split_maps,) + (P(),) * 15,
        out_specs=split_maps,
        check_vma=False,
    )
```

time: 181 us -> 176 us (0.972)
  waiting for transfers between devices: 88.9 us -> 57.8 us
  starting transfers between devices: 19.1 us -> 30.5 us
  local copies, waits for them, and re-layouts: 9.49 us -> 19.2 us
  Pallas kernels: 62 us -> 66.7 us
    all_to_all x1 -> x2, waiting for transfers between devices: 84.3 us -> 56.4 us  [travel(): x = lax.all_to_all(x, 'veh', 0, 0, tiled=True)]
    unnamed x36 -> x50, local copies, waits for them, and re-layouts: 5.28 us -> 12.3 us
    ppermute x4 -> x6, starting transfers between devices: 12.6 us -> 19.3 us  [the longest x3 13.3 us: beside(): above = lax.ppermute(last, 'row', [(i, i + 1) for i in range(count - 1)])]
    all_to_all x1 -> x2, starting transfers between devices: 6.53 us -> 11.2 us  [travel(): x = lax.all_to_all(x, 'veh', 0, 0, tiled=True)]
    pallas_call x3 -> x6, Pallas kernels: 62 us -> 66.7 us  [the longest x2 36.6 us: window_layer(): pl.pallas_call(functools.partial(window_kernel, phase, rows), out_shape=j...]
    ppermute x4 -> x6, waiting for transfers between devices: 4.57 us -> 1.41 us  [the longest x3 1.4 us: beside(): below = lax.ppermute(first, 'row', [(i + 1, i) for i in range(count - 1)])]
  transfers between devices with their start and end apart: 5 -> 8, of which waited for: 3 -> 3; matrix products, arithmetic and copies ran while one was open for 2% -> 4% of each run, Pallas kernels for 13% -> 24%
where the time goes in v2:
time: 176 us; the launch traced here: 175 us
  Pallas kernels  66.7 us (38%)
  waiting for transfers between devices  57.8 us (33%)
  starting transfers between devices  30.5 us (17%)
  local copies, waits for them, and re-layouts  19.2 us (11%)
    all_to_all x2, waiting for transfers between devices, travel(): x = lax.all_to_all(x, 'veh', 0, 0, tiled=True)  56.4 us
    pallas_call x2, Pallas kernels, window_layer(): pl.pallas_call(functools.partial(window_kernel, phase, rows), out_shape=j...  36.6 us
    pallas_call x2, Pallas kernels, join_agents(): pl.pallas_call(functools.partial(join_kernel, steps), out_shape=[like(tot...  22 us
    ppermute x3, starting transfers between devices, beside(): above = lax.ppermute(last, 'row', [(i, i + 1) for i in range(count - 1)])  13.3 us
    unnamed x50, local copies, waits for them, and re-layouts  12.3 us
    all_to_all x2, starting transfers between devices, travel(): x = lax.all_to_all(x, 'veh', 0, 0, tiled=True)  11.2 us
    ppermute x3, starting transfers between devices, beside(): below = lax.ppermute(first, 'row', [(i + 1, i) for i in range(count - 1)])  5.94 us
    pallas_call x1, Pallas kernels, turn_maps(): pl.pallas_call(turn_kernel, out_shape=[jax.ShapeDtypeStruct(shape, maps.d...  5.76 us
  transfers between devices with their start and end apart: 8, of which 3 were waited for; matrix products, arithmetic and copies ran while one was open for 4% of the time, Pallas kernels for 24%

profile of v2, /device:TPU:1, one launch (start us, length us, event | category | flops | bytes accessed | tf_op | source)
XLA Modules:
  0.0 175.5 jit_solution(9672813770000093308)
XLA Ops:
  0.0 0.8 copy.90
  0.9 0.7 lt.118
  1.8 0.8 copy.86
  2.8 0.3 select_reduce_fusion
  3.2 0.1 copy.87
  3.3 0.1 lt.113
  3.8 0.2 select_reduce_fusion.1
  4.1 1.2 copy-done.1
  5.3 5.8 %shard_map.154 = (bf16[8,64,8,128]{3,2,1,0:T(8,128)(2,1)S(1)}, bf16[16,18,8,128]{3,2,1,0:T(8,128)(2,1)S(1)}, bf16[16,14,8,128]{3,2,1,0:T(8,128)(2,1)S(1)}, bf16[64,18,8,128]{3,2,1,0:T(8,128)(2,1)S(1)}) custom-call(s32[64]{0:T(128)S(1)} %reshape.365.chosen, bf16[8,8,64,128]{3,2,1,0:T(8,128)(2,1)S(1)} %copy-done.1), custom_call_target="tpu_custom_call" | custom-call | bytes 5242880 | tf_op jit(solution)/shard_map/pallas_call | solution.py:90
  11.1 1.4 copy-done
  12.6 1.0 copy-done.2
  13.6 0.8 copy-done.4
  14.4 6.4 %all-to-all-start = ((bf16[8,8,18,8,128]{4,3,2,1,0:T(8,128)(2,1)}), bf16[8,8,18,8,128]{4,3,2,1,0:T(8,128)(2,1)S(1)}, u32[]{:S(2)}, u32[]{:S(2)}) async-start(bf16[8,8,18,8,128]{4,3,2,1,0:T(8,128)(2,1)} %bitcast.32), calls=%async_computation | async-start | bytes 4718592 | tf_op jit(solution)/shard_map/all_to_all | solution.py:534
  20.8 2.3 %shard_map.155 = bf16[64,14,8,128]{3,2,1,0:T(8,128)(2,1)} custom-call(s32[64]{0:T(128)S(1)} %reshape.365.chosen, bf16[16,14,8,128]{3,2,1,0:T(8,128)(2,1)S(1)} %get-tuple-element.20.pieces), custom_call_target="tpu_custom_call" | custom-call | bytes 1835008 | tf_op jit(solution)/shard_map/pallas_call | solution.py:110
  23.1 50.7 %all-to-all-done = bf16[8,8,18,8,128]{4,3,2,1,0:T(8,128)(2,1)S(1)} async-done(((bf16[8,8,18,8,128]{4,3,2,1,0:T(8,128)(2,1)}), bf16[8,8,18,8,128]{4,3,2,1,0:T(8,128)(2,1)S(1)}, u32[]{:S(2)}, u32[]{:S(2)}) %all-to-all-start) | async-done | bytes 2359328 | tf_op jit(solution)/shard_map/all_to_all | solution.py:534
  73.8 4.8 %all-to-all-start.1 = ((bf16[8,8,14,8,128]{4,3,2,1,0:T(8,128)(2,1)}), bf16[8,8,14,8,128]{4,3,2,1,0:T(8,128)(2,1)}, u32[]{:S(2)}, u32[]{:S(2)}) async-start(bf16[8,8,14,8,128]{4,3,2,1,0:T(8,128)(2,1)} %bitcast.18), calls=%async_computation.1 | async-start | bytes 3670016 | tf_op jit(solution)/shard_map/all_to_all | solution.py:534
  78.6 1.7 fusion.12
  80.3 4.5 %collective-permute-start = (bf16[8,1,64,128]{3,2,1,0:T(8,128)(2,1)}, bf16[8,1,64,128]{3,2,1,0:T(8,128)(2,1)S(1)}, u32[]{:S(2)}, u32[]{:S(2)}) collective-permute-start(bf16[8,1,64,128]{3,2,1,0:T(8,128)(2,1)} %get-tuple-element.34), channel_id=1, source_target_pairs={{0,1},{1,2},{2,3},{4,5},{5,6},{6,7},{8,9},{9,10},{10,11},{12,13},{... | collective-permute-start | bytes 393224 | tf_op jit(solution)/shard_map/ppermute | solution.py:466
  84.8 1.9 %collective-permute-start.1 = (bf16[8,1,64,128]{3,2,1,0:T(8,128)(2,1)}, bf16[8,1,64,128]{3,2,1,0:T(8,128)(2,1)S(1)}, u32[]{:S(2)}, u32[]{:S(2)}) collective-permute-start(bf16[8,1,64,128]{3,2,1,0:T(8,128)(2,1)} %get-tuple-element.33), channel_id=1, source_target_pairs={{1,0},{2,1},{3,2},{5,4},{6,5},{7,6},{9,8},{10,9},{11,10},{13,12},{... | collective-permute-start | bytes 393224 | tf_op jit(solution)/shard_map/ppermute | solution.py:467
  86.8 0.1 copy.99
  87.0 0.1 copy.98
  87.1 0.1 and.107
  87.2 0.1 copy.97
  87.3 0.1 subtract_select_fusion
  87.4 0.1 reshape.385.place
  87.6 0.1 and.113
  88.0 0.1 reshape.370.present
  88.1 0.1 copy.102
  88.2 0.1 copy.103
  88.4 0.1 copy.104.scale
  88.5 1.8 %fusion.13 = (bf16[256,256]{1,0:T(8,128)(2,1)}, bf16[256,256]{1,0:T(8,128)(2,1)}, bf16[256,256]{1,0:T(8,128)(2,1)S(1)}) fusion(bf16[256,768]{1,0:T(8,128)(2,1)} %param.26), kind=kLoop, calls=%fused_computation.37 | loop fusion | bytes 786432 | tf_op jit(solution)/shard_map/slice | solution.py:421
  90.2 1.1 copy-done.5
  91.3 12.9 %shard_map.156 = (bf16[2304,128]{1,0:T(8,128)(2,1)S(1)}, bf16[288,128]{1,0:T(8,128)(2,1)S(1)}, bf16[288,128]{1,0:T(8,128)(2,1)S(1)}) custom-call(s32[64]{0:T(128)S(1)} %reshape.385.place, bf16[2304,128]{1,0:T(8,128)(2,1)S(1)} %bitcast.42, bf16[64,144,128]{2,1,0:T(8,128)(2,1)S(1)} %bitcast.31, f32[4,2304]{1,0:T(4,128)S(1)} %reshape.370.present, ...), custom_call_target="tpu_custom_call" | custom-call | flops 1509949440 | bytes 3538944 | tf_op jit(solution)/shard_map/pallas_call | solution.py:197
  104.2 0.8 copy-done.12
  105.0 3.6 %collective-permute-start.2 = (bf16[288,128]{1,0:T(8,128)(2,1)S(1)}, bf16[288,128]{1,0:T(8,128)(2,1)S(1)}, u32[]{:S(2)}, u32[]{:S(2)}) collective-permute-start(bf16[288,128]{1,0:T(8,128)(2,1)S(1)} %get-tuple-element.23), channel_id=1, source_target_pairs={{0,1},{1,2},{2,3},{4,5},{5,6},{6,7},{8,9},{9,10},{10,11},{12,13},{... | collective-permute-start | bytes 221192 | tf_op jit(solution)/shard_map/ppermute | solution.py:466
  108.6 1.9 %collective-permute-start.3 = (bf16[288,128]{1,0:T(8,128)(2,1)S(1)}, bf16[288,128]{1,0:T(8,128)(2,1)S(1)}, u32[]{:S(2)}, u32[]{:S(2)}) collective-permute-start(bf16[288,128]{1,0:T(8,128)(2,1)S(1)} %get-tuple-element.24), channel_id=1, source_target_pairs={{1,0},{2,1},{3,2},{5,4},{6,5},{7,6},{9,8},{10,9},{11,10},{13,12},{... | collective-permute-start | bytes 221192 | tf_op jit(solution)/shard_map/ppermute | solution.py:467
  110.6 0.1 reshape.377.present
  110.8 1.0 copy.110
  111.8 1.0 copy.111
  112.9 1.4 collective-permute-done.3
  114.3 5.7 %all-to-all-done.1 = bf16[8,8,14,8,128]{4,3,2,1,0:T(8,128)(2,1)} async-done(((bf16[8,8,14,8,128]{4,3,2,1,0:T(8,128)(2,1)}), bf16[8,8,14,8,128]{4,3,2,1,0:T(8,128)(2,1)}, u32[]{:S(2)}, u32[]{:S(2)}) %all-to-all-start.1) | async-done | bytes 1835040 | tf_op jit(solution)/shard_map/all_to_all | solution.py:534
  120.1 9.1 %shard_map.157 = (bf16[1792,128]{1,0:T(8,128)(2,1)S(1)}, bf16[224,128]{1,0:T(8,128)(2,1)S(1)}, bf16[224,128]{1,0:T(8,128)(2,1)S(1)}) custom-call(s32[64]{0:T(128)S(1)} %reshape.385.place, bf16[1792,128]{1,0:T(8,128)(2,1)S(1)} %bitcast.33, bf16[64,112,128]{2,1,0:T(8,128)(2,1)} %bitcast.19.arrived, f32[4,1792]{1,0:T(4,128)S(1)} %reshape.377.present, ...), custom_call_target="tpu_custom_call" | custom-call | flops 1174405120 | bytes 2752512 | tf_op jit(solution)/shard_map/pallas_call | solution.py:197
  129.3 5.2 %collective-permute-start.4 = (bf16[224,128]{1,0:T(8,128)(2,1)S(1)}, bf16[224,128]{1,0:T(8,128)(2,1)S(1)}, u32[]{:S(2)}, u32[]{:S(2)}) collective-permute-start(bf16[224,128]{1,0:T(8,128)(2,1)S(1)} %get-tuple-element.27), channel_id=1, source_target_pairs={{0,1},{1,2},{2,3},{4,5},{5,6},{6,7},{8,9},{9,10},{10,11},{12,13},{... | collective-permute-start | bytes 172040 | tf_op jit(solution)/shard_map/ppermute | solution.py:466
  134.5 2.1 %collective-permute-start.5 = (bf16[224,128]{1,0:T(8,128)(2,1)S(1)}, bf16[224,128]{1,0:T(8,128)(2,1)S(1)}, u32[]{:S(2)}, u32[]{:S(2)}) collective-permute-start(bf16[224,128]{1,0:T(8,128)(2,1)S(1)} %get-tuple-element.28), channel_id=1, source_target_pairs={{1,0},{2,1},{3,2},{5,4},{6,5},{7,6},{9,8},{10,9},{11,10},{13,12},{... | collective-permute-start | bytes 172040 | tf_op jit(solution)/shard_map/ppermute | solution.py:467
  136.7 18.3 %shard_map.158.refs_19_ = bf16[8,8,2,2,16,256]{5,4,3,2,1,0:T(8,128)(2,1)} custom-call(bf16[8,64,8,128]{3,2,1,0:T(8,128)(2,1)S(1)} %copy-done.3, bf16[8,1,64,128]{3,2,1,0:T(8,128)(2,1)S(1)} %collective-permute-done.refs_1_, bf16[8,1,64,128]{3,2,1,0:T(8,128)(2,1)S(1)} %collective-permute-done.1.refs_2_, bf16[8,288,128]{2,1,0:T(8,128)(2,1)S(1)} %bitcast.47, ...), custom_call_target="tpu_custom_call" | custom-call | flops 8053063680 | bytes 3145728 | tf_op jit(solution)/shard_map/pallas_call | solution.py:443
  155.1 1.1 copy-done.14
  156.1 1.0 copy-done.16
  157.2 18.3 %shard_map.159 = bf16[8,8,2,2,16,256]{5,4,3,2,1,0:T(8,128)(2,1)} custom-call(bf16[8,64,8,128]{3,2,1,0:T(8,128)(2,1)S(1)} %copy-done.3, bf16[8,1,64,128]{3,2,1,0:T(8,128)(2,1)S(1)} %collective-permute-done.refs_1_, bf16[8,1,64,128]{3,2,1,0:T(8,128)(2,1)S(1)} %collective-permute-done.1.refs_2_, ...), custom_call_target="tpu_custom_call", output_to_operand_aliasing={{}: (19, {})} | custom-call | flops 8053063680 | bytes 3145728 | tf_op jit(solution)/shard_map/pallas_call | solution.py:443
  (85 shorter events, 2.0 us)
Async XLA Ops:
  4.1 1.2 copy-start.1
  11.1 1.4 copy-start
  12.6 1.0 copy-start.2
  13.6 0.8 copy-start.4
  14.4 59.4 %all-to-all-start = ((bf16[8,8,18,8,128]{4,3,2,1,0:T(8,128)(2,1)}), bf16[8,8,18,8,128]{4,3,2,1,0:T(8,128)(2,1)S(1)}, u32[]{:S(2)}, u32[]{:S(2)}) async-start(bf16[8,8,18,8,128]{4,3,2,1,0:T(8,128)(2,1)} %bitcast.32), calls=%async_computation | async-start | bytes 4718592 | tf_op jit(solution)/shard_map/all_to_all | solution.py:534
  73.7 14.4 %copy-start.18 = (bf16[128,128]{1,0:T(8,128)(2,1)S(1)}, bf16[128,128]{1,0:T(8,128)(2,1)}, u32[]{:S(2)}) copy-start(bf16[128,128]{1,0:T(8,128)(2,1)} %param.20) | copy-start | bytes 98308
  73.7 14.5 %copy-start.17 = (bf16[128,256]{1,0:T(8,128)(2,1)S(1)}, bf16[128,256]{1,0:T(8,128)(2,1)}, u32[]{:S(2)}) copy-start(bf16[128,256]{1,0:T(8,128)(2,1)} %param.21) | copy-start | bytes 196612
  73.8 14.6 %copy-start.20 = (f32[4]{0:T(128)S(1)}, f32[4]{0:T(128)}, u32[]{:S(2)}) copy-start(f32[4]{0:T(128)} %param.23) | copy-start | bytes 52
  73.8 16.5 %copy-start.9 = (bf16[128,128]{1,0:T(8,128)(2,1)S(1)}, bf16[128,128]{1,0:T(8,128)(2,1)}, u32[]{:S(2)}) copy-start(bf16[128,128]{1,0:T(8,128)(2,1)} %wout.3) | copy-start | bytes 98308
  73.8 46.3 %all-to-all-start.1 = ((bf16[8,8,14,8,128]{4,3,2,1,0:T(8,128)(2,1)}), bf16[8,8,14,8,128]{4,3,2,1,0:T(8,128)(2,1)}, u32[]{:S(2)}, u32[]{:S(2)}) async-start(bf16[8,8,14,8,128]{4,3,2,1,0:T(8,128)(2,1)} %bitcast.18), calls=%async_computation.1 | async-start | bytes 3670016 | tf_op jit(solution)/shard_map/all_to_all | solution.py:534
  80.3 56.3 %collective-permute-start = (bf16[8,1,64,128]{3,2,1,0:T(8,128)(2,1)}, bf16[8,1,64,128]{3,2,1,0:T(8,128)(2,1)S(1)}, u32[]{:S(2)}, u32[]{:S(2)}) collective-permute-start(bf16[8,1,64,128]{3,2,1,0:T(8,128)(2,1)} %get-tuple-element.34), channel_id=1, source_target_pairs={{0,1},{1,2},{2,3},{4,5},{5,6},{6,7},{8,9},{9,10},{10,11},{12,13},{... | collective-permute-start | bytes 393224 | tf_op jit(solution)/shard_map/ppermute | solution.py:466
  84.8 51.9 %collective-permute-start.1 = (bf16[8,1,64,128]{3,2,1,0:T(8,128)(2,1)}, bf16[8,1,64,128]{3,2,1,0:T(8,128)(2,1)S(1)}, u32[]{:S(2)}, u32[]{:S(2)}) collective-permute-start(bf16[8,1,64,128]{3,2,1,0:T(8,128)(2,1)} %get-tuple-element.33), channel_id=1, source_target_pairs={{1,0},{2,1},{3,2},{5,4},{6,5},{7,6},{9,8},{10,9},{11,10},{13,12},{... | collective-permute-start | bytes 393224 | tf_op jit(solution)/shard_map/ppermute | solution.py:467
  90.2 1.1 copy-start.5
  91.3 19.3 %copy-start.21 = (f32[8]{0:T(128)S(1)}, f32[8]{0:T(128)}, u32[]{:S(2)}) copy-start(f32[8]{0:T(128)} %param.28) | copy-start | bytes 100
  91.3 19.5 %copy-start.19 = (f32[3,3,256]{2,1,0:T(4,128)S(1)}, f32[3,3,256]{2,1,0:T(4,128)}, u32[]{:S(2)}) copy-start(f32[3,3,256]{2,1,0:T(4,128)} %param.24) | copy-start | bytes 27652
  104.2 0.8 copy-start.12
  105.0 7.9 %collective-permute-start.2 = (bf16[288,128]{1,0:T(8,128)(2,1)S(1)}, bf16[288,128]{1,0:T(8,128)(2,1)S(1)}, u32[]{:S(2)}, u32[]{:S(2)}) collective-permute-start(bf16[288,128]{1,0:T(8,128)(2,1)S(1)} %get-tuple-element.23), channel_id=1, source_target_pairs={{0,1},{1,2},{2,3},{4,5},{5,6},{6,7},{8,9},{9,10},{10,11},{12,13},{... | collective-permute-start | bytes 221192 | tf_op jit(solution)/shard_map/ppermute | solution.py:466
  108.6 5.7 %collective-permute-start.3 = (bf16[288,128]{1,0:T(8,128)(2,1)S(1)}, bf16[288,128]{1,0:T(8,128)(2,1)S(1)}, u32[]{:S(2)}, u32[]{:S(2)}) collective-permute-start(bf16[288,128]{1,0:T(8,128)(2,1)S(1)} %get-tuple-element.24), channel_id=1, source_target_pairs={{1,0},{2,1},{3,2},{5,4},{6,5},{7,6},{9,8},{10,9},{11,10},{13,12},{... | collective-permute-start | bytes 221192 | tf_op jit(solution)/shard_map/ppermute | solution.py:467
  120.0 16.6 %copy-start.3 = (bf16[8,64,8,128]{3,2,1,0:T(8,128)(2,1)S(1)}, bf16[8,64,8,128]{3,2,1,0:T(8,128)(2,1)}, u32[]{:S(2)}) copy-start(bf16[8,64,8,128]{3,2,1,0:T(8,128)(2,1)} %copy-done.2) | copy-start | bytes 3145732
  120.0 16.6 %copy-start.6 = (bf16[256,512]{1,0:T(8,128)(2,1)S(1)}, bf16[256,512]{1,0:T(8,128)(2,1)}, u32[]{:S(2)}) copy-start(bf16[256,512]{1,0:T(8,128)(2,1)} %refs_17_.1) | copy-start | bytes 786436
  120.0 16.6 %copy-start.7 = (bf16[512,256]{1,0:T(8,128)(2,1)S(1)}, bf16[512,256]{1,0:T(8,128)(2,1)}, u32[]{:S(2)}) copy-start(bf16[512,256]{1,0:T(8,128)(2,1)} %refs_18_.1) | copy-start | bytes 786436
  120.1 16.6 %copy-start.8 = (bf16[256,256]{1,0:T(8,128)(2,1)S(1)}, bf16[256,256]{1,0:T(8,128)(2,1)}, u32[]{:S(2)}) copy-start(bf16[256,256]{1,0:T(8,128)(2,1)} %refs_14_.3) | copy-start | bytes 393220
  120.1 16.6 %copy-start.10 = (f32[256]{0:T(256)S(1)}, f32[256]{0:T(256)}, u32[]{:S(2)}) copy-start(f32[256]{0:T(256)} %param.25) | copy-start | bytes 3076
  120.1 16.6 %copy-start.11 = (f32[256]{0:T(256)S(1)}, f32[256]{0:T(256)}, u32[]{:S(2)}) copy-start(f32[256]{0:T(256)} %param.29) | copy-start | bytes 3076
  120.1 16.6 %copy-start.13 = (bf16[2304,128]{1,0:T(8,128)(2,1)S(1)}, bf16[2304,128]{1,0:T(8,128)(2,1)}, u32[]{:S(2)}) copy-start(bf16[2304,128]{1,0:T(8,128)(2,1)} %copy-done.12) | copy-start | bytes 1769476
  129.2 25.8 %copy-start.15 = (bf16[1792,128]{1,0:T(8,128)(2,1)}, bf16[1792,128]{1,0:T(8,128)(2,1)S(1)}, u32[]{:S(2)}) copy-start(bf16[1792,128]{1,0:T(8,128)(2,1)S(1)} %get-tuple-element.26) | copy-start | bytes 1376260
  129.3 25.8 %collective-permute-start.4 = (bf16[224,128]{1,0:T(8,128)(2,1)S(1)}, bf16[224,128]{1,0:T(8,128)(2,1)S(1)}, u32[]{:S(2)}, u32[]{:S(2)}) collective-permute-start(bf16[224,128]{1,0:T(8,128)(2,1)S(1)} %get-tuple-element.27), channel_id=1, source_target_pairs={{0,1},{1,2},{2,3},{4,5},{5,6},{6,7},{8,9},{9,10},{10,11},{12,13},{... | collective-permute-start | bytes 172040 | tf_op jit(solution)/shard_map/ppermute | solution.py:466
  134.5 20.5 %collective-permute-start.5 = (bf16[224,128]{1,0:T(8,128)(2,1)S(1)}, bf16[224,128]{1,0:T(8,128)(2,1)S(1)}, u32[]{:S(2)}, u32[]{:S(2)}) collective-permute-start(bf16[224,128]{1,0:T(8,128)(2,1)S(1)} %get-tuple-element.28), channel_id=1, source_target_pairs={{1,0},{2,1},{3,2},{5,4},{6,5},{7,6},{9,8},{10,9},{11,10},{13,12},{... | collective-permute-start | bytes 172040 | tf_op jit(solution)/shard_map/ppermute | solution.py:467
  155.1 1.1 copy-start.14
  156.1 1.0 copy-start.16

commit v3 on v2

--- a/solution.py
+++ b/solution.py
@@ -540,6 +540,8 @@
     arrived.append(travel(later))
     result, pieces = None, []
     for phase, own in enumerate((first, second)):
+        if phase:
+            place, result = lax.optimization_barrier((place, result))
         joined, top, low = join_agents(
             own, arrived[phase], place, live, agent_query, agent_keyvalue, agent_out, agent_scale
         )

time: 176 us -> 175 us (level)
  starting transfers between devices: 30.5 us -> 27 us
  local copies, waits for them, and re-layouts: 19.2 us -> 22 us
  waiting for transfers between devices: 57.8 us -> 55.3 us
  Pallas kernels: 66.7 us -> 68.6 us
    all_to_all x2, waiting for transfers between devices: 56.4 us -> 50.6 us  [travel(): x = lax.all_to_all(x, 'veh', 0, 0, tiled=True)]
    ppermute x3, starting transfers between devices: 13.3 us -> 8.11 us  [beside(): above = lax.ppermute(last, 'row', [(i, i + 1) for i in range(count - 1)])]
    unnamed x50 -> x56, local copies, waits for them, and re-layouts: 12.3 us -> 16.2 us
    ppermute x3, waiting for transfers between devices: 1.4 us -> 4.63 us  [beside(): below = lax.ppermute(first, 'row', [(i + 1, i) for i in range(count - 1)])]
    ppermute x3, starting transfers between devices: 5.94 us -> 7.72 us  [beside(): below = lax.ppermute(first, 'row', [(i + 1, i) for i in range(count - 1)])]
  transfers between devices with their start and end apart: 8 -> 8, of which waited for: 3 -> 3; matrix products, arithmetic and copies ran while one was open for 4% -> 4% of each run, Pallas kernels for 24% -> 20%
where the time goes in v3:
time: 175 us; the launch traced here: 174 us
  Pallas kernels  68.6 us (39%)
  waiting for transfers between devices  55.3 us (32%)
  starting transfers between devices  27 us (15%)
  local copies, waits for them, and re-layouts  22 us (13%)
    all_to_all x2, waiting for transfers between devices, travel(): x = lax.all_to_all(x, 'veh', 0, 0, tiled=True)  50.6 us
    pallas_call x2, Pallas kernels, window_layer(): pl.pallas_call(functools.partial(window_kernel, phase, rows), out_shape=j...  38.3 us
    pallas_call x2, Pallas kernels, join_agents(): pl.pallas_call(functools.partial(join_kernel, steps), out_shape=[like(tot...  22.2 us
    unnamed x56, local copies, waits for them, and re-layouts  16.2 us
    all_to_all x2, starting transfers between devices, travel(): x = lax.all_to_all(x, 'veh', 0, 0, tiled=True)  11.2 us
    ppermute x3, starting transfers between devices, beside(): above = lax.ppermute(last, 'row', [(i, i + 1) for i in range(count - 1)])  8.11 us
    ppermute x3, starting transfers between devices, beside(): below = lax.ppermute(first, 'row', [(i + 1, i) for i in range(count - 1)])  7.72 us
    pallas_call x1, Pallas kernels, turn_maps(): pl.pallas_call(turn_kernel, out_shape=[jax.ShapeDtypeStruct(shape, maps.d...  5.76 us
  transfers between devices with their start and end apart: 8, of which 3 were waited for; matrix products, arithmetic and copies ran while one was open for 4% of the time, Pallas kernels for 20%

profile of v3, /device:TPU:1, one launch (start us, length us, event | category | flops | bytes accessed | tf_op | source)
XLA Modules:
  0.0 174.2 jit_solution(1570076100458059760)
XLA Ops:
  0.0 0.7 lt.119
  1.0 0.1 lt.114
  1.1 0.8 copy.56
  2.0 0.1 copy.57
  2.1 0.8 copy.60
  3.1 0.3 select_reduce_fusion
  3.8 0.2 select_reduce_fusion.1
  4.1 1.2 copy-done.1
  5.3 5.8 %shard_map.154 = (bf16[8,64,8,128]{3,2,1,0:T(8,128)(2,1)S(1)}, bf16[16,18,8,128]{3,2,1,0:T(8,128)(2,1)S(1)}, bf16[16,14,8,128]{3,2,1,0:T(8,128)(2,1)S(1)}, bf16[64,18,8,128]{3,2,1,0:T(8,128)(2,1)S(1)}) custom-call(s32[64]{0:T(128)S(1)} %reshape.375.chosen, bf16[8,8,64,128]{3,2,1,0:T(8,128)(2,1)S(1)} %copy-done.1), custom_call_target="tpu_custom_call" | custom-call | bytes 5242880 | tf_op jit(solution)/shard_map/pallas_call | solution.py:90
  11.1 1.4 copy-done
  12.5 1.0 copy-done.2
  13.5 0.8 copy-done.5
  14.4 6.4 %all-to-all-start = ((bf16[8,8,18,8,128]{4,3,2,1,0:T(8,128)(2,1)}), bf16[8,8,18,8,128]{4,3,2,1,0:T(8,128)(2,1)S(1)}, u32[]{:S(2)}, u32[]{:S(2)}) async-start(bf16[8,8,18,8,128]{4,3,2,1,0:T(8,128)(2,1)} %bitcast.36), calls=%async_computation | async-start | bytes 4718592 | tf_op jit(solution)/shard_map/all_to_all | solution.py:534
  20.7 2.3 %shard_map.155 = bf16[64,14,8,128]{3,2,1,0:T(8,128)(2,1)} custom-call(s32[64]{0:T(128)S(1)} %reshape.375.chosen, bf16[16,14,8,128]{3,2,1,0:T(8,128)(2,1)S(1)} %get-tuple-element.22.pieces), custom_call_target="tpu_custom_call" | custom-call | bytes 1835008 | tf_op jit(solution)/shard_map/pallas_call | solution.py:110
  23.1 50.6 %all-to-all-done = bf16[8,8,18,8,128]{4,3,2,1,0:T(8,128)(2,1)S(1)} async-done(((bf16[8,8,18,8,128]{4,3,2,1,0:T(8,128)(2,1)}), bf16[8,8,18,8,128]{4,3,2,1,0:T(8,128)(2,1)S(1)}, u32[]{:S(2)}, u32[]{:S(2)}) %all-to-all-start) | async-done | bytes 2359328 | tf_op jit(solution)/shard_map/all_to_all | solution.py:534
  73.8 4.8 %all-to-all-start.1 = ((bf16[8,8,14,8,128]{4,3,2,1,0:T(8,128)(2,1)}), bf16[8,8,14,8,128]{4,3,2,1,0:T(8,128)(2,1)}, u32[]{:S(2)}, u32[]{:S(2)}) async-start(bf16[8,8,14,8,128]{4,3,2,1,0:T(8,128)(2,1)} %bitcast.25), calls=%async_computation.1 | async-start | bytes 3670016 | tf_op jit(solution)/shard_map/all_to_all | solution.py:534
  78.6 1.7 fusion.8
  80.3 3.4 %collective-permute-start.1 = (bf16[8,1,64,128]{3,2,1,0:T(8,128)(2,1)}, bf16[8,1,64,128]{3,2,1,0:T(8,128)(2,1)}, u32[]{:S(2)}, u32[]{:S(2)}) collective-permute-start(bf16[8,1,64,128]{3,2,1,0:T(8,128)(2,1)} %get-tuple-element.39), channel_id=1, source_target_pairs={{1,0},{2,1},{3,2},{5,4},{6,5},{7,6},{9,8},{10,9},{11,10},{13,12},{... | collective-permute-start | bytes 393224 | tf_op jit(solution)/shard_map/ppermute | solution.py:467
  83.7 3.0 %collective-permute-start = (bf16[8,1,64,128]{3,2,1,0:T(8,128)(2,1)}, bf16[8,1,64,128]{3,2,1,0:T(8,128)(2,1)}, u32[]{:S(2)}, u32[]{:S(2)}) collective-permute-start(bf16[8,1,64,128]{3,2,1,0:T(8,128)(2,1)} %get-tuple-element.40), channel_id=1, source_target_pairs={{0,1},{1,2},{2,3},{4,5},{5,6},{6,7},{8,9},{9,10},{10,11},{12,13},{... | collective-permute-start | bytes 393224 | tf_op jit(solution)/shard_map/ppermute | solution.py:466
  86.7 0.1 copy.72.scale
  86.9 0.1 and.109
  87.4 0.1 copy.66
  87.6 0.1 reshape.396.place
  87.7 0.1 copy.70
  87.9 0.1 reshape.380.present
  88.0 0.1 copy.71
  88.1 0.7 fusion.9
  88.9 1.1 copy-done.6
  90.0 13.5 %shard_map.156 = (bf16[2304,128]{1,0:T(8,128)(2,1)S(1)}, bf16[288,128]{1,0:T(8,128)(2,1)}, bf16[288,128]{1,0:T(8,128)(2,1)}) custom-call(s32[64]{0:T(128)S(1)} %reshape.396.place, bf16[2304,128]{1,0:T(8,128)(2,1)S(1)} %bitcast.46, bf16[64,144,128]{2,1,0:T(8,128)(2,1)S(1)} %bitcast.35, f32[4,2304]{1,0:T(4,128)S(1)} %reshape.380.present, ...), custom_call_target="tpu_custom_call" | custom-call | flops 1509949440 | bytes 3538944 | tf_op jit(solution)/shard_map/pallas_call | solution.py:197
  103.5 0.8 copy-done.14
  104.3 3.0 %collective-permute-start.2 = (bf16[288,128]{1,0:T(8,128)(2,1)}, bf16[288,128]{1,0:T(8,128)(2,1)S(1)}, u32[]{:S(2)}, u32[]{:S(2)}) collective-permute-start(bf16[288,128]{1,0:T(8,128)(2,1)} %get-tuple-element.25), channel_id=1, source_target_pairs={{0,1},{1,2},{2,3},{4,5},{5,6},{6,7},{8,9},{9,10},{10,11},{12,13},{... | collective-permute-start | bytes 221192 | tf_op jit(solution)/shard_map/ppermute | solution.py:466
  107.4 1.9 %collective-permute-start.3 = (bf16[288,128]{1,0:T(8,128)(2,1)}, bf16[288,128]{1,0:T(8,128)(2,1)S(1)}, u32[]{:S(2)}, u32[]{:S(2)}) collective-permute-start(bf16[288,128]{1,0:T(8,128)(2,1)} %get-tuple-element.26), channel_id=1, source_target_pairs={{1,0},{2,1},{3,2},{5,4},{6,5},{7,6},{9,8},{10,9},{11,10},{13,12},{... | collective-permute-start | bytes 221192 | tf_op jit(solution)/shard_map/ppermute | solution.py:467
  109.5 0.1 reshape.390.present
  109.6 1.0 copy.82
  110.6 1.0 copy.81
  111.6 1.6 collective-permute-done.3
  113.3 1.2 copy-done.3
  114.6 0.9 copy-done.8
  115.5 1.1 copy-done.15
  116.6 19.1 %shard_map.157.refs_19_ = bf16[8,8,2,2,16,256]{5,4,3,2,1,0:T(8,128)(2,1)} custom-call(bf16[8,64,8,128]{3,2,1,0:T(8,128)(2,1)S(1)} %copy-done.3, bf16[8,1,64,128]{3,2,1,0:T(8,128)(2,1)} %collective-permute-done.refs_1_, bf16[8,1,64,128]{3,2,1,0:T(8,128)(2,1)} %collective-permute-done.1.refs_2_, bf16[8,288,128]{2,1,0:T(8,128)(2,1)S(1)} %bitcast.51, ...), custom_call_target="tpu_custom_call" | custom-call | flops 8053063680 | bytes 3145728 | tf_op jit(solution)/shard_map/pallas_call | solution.py:443
  135.9 8.7 %shard_map.158 = (bf16[1792,128]{1,0:T(8,128)(2,1)S(1)}, bf16[224,128]{1,0:T(8,128)(2,1)S(1)}, bf16[224,128]{1,0:T(8,128)(2,1)S(1)}) custom-call(s32[64]{0:T(128)S(1)} %reshape.387.place, bf16[1792,128]{1,0:T(8,128)(2,1)S(1)} %bitcast.37, bf16[64,112,128]{2,1,0:T(8,128)(2,1)} %bitcast.26.arrived, f32[4,1792]{1,0:T(4,128)S(1)} %reshape.390.present, ...), custom_call_target="tpu_custom_call" | custom-call | flops 1174405120 | bytes 2752512 | tf_op jit(solution)/shard_map/pallas_call | solution.py:197
  144.6 0.8 copy-done.17
  145.3 2.1 %collective-permute-start.4 = (bf16[224,128]{1,0:T(8,128)(2,1)S(1)}, bf16[224,128]{1,0:T(8,128)(2,1)S(1)}, u32[]{:S(2)}, u32[]{:S(2)}) collective-permute-start(bf16[224,128]{1,0:T(8,128)(2,1)S(1)} %get-tuple-element.30), channel_id=1, source_target_pairs={{0,1},{1,2},{2,3},{4,5},{5,6},{6,7},{8,9},{9,10},{10,11},{12,13},{... | collective-permute-start | bytes 172040 | tf_op jit(solution)/shard_map/ppermute | solution.py:466
  147.4 2.4 %collective-permute-start.5 = (bf16[224,128]{1,0:T(8,128)(2,1)S(1)}, bf16[224,128]{1,0:T(8,128)(2,1)S(1)}, u32[]{:S(2)}, u32[]{:S(2)}) collective-permute-start(bf16[224,128]{1,0:T(8,128)(2,1)S(1)} %get-tuple-element.31), channel_id=1, source_target_pairs={{1,0},{2,1},{3,2},{5,4},{6,5},{7,6},{9,8},{10,9},{11,10},{13,12},{... | collective-permute-start | bytes 172040 | tf_op jit(solution)/shard_map/ppermute | solution.py:467
  149.9 3.0 %collective-permute-done.5 = bf16[224,128]{1,0:T(8,128)(2,1)S(1)} collective-permute-done((bf16[224,128]{1,0:T(8,128)(2,1)S(1)}, bf16[224,128]{1,0:T(8,128)(2,1)S(1)}, u32[]{:S(2)}, u32[]{:S(2)}) %collective-permute-start.5) | collective-permute-done | bytes 57376 | tf_op jit(solution)/shard_map/ppermute | solution.py:467
  152.9 1.1 copy-done.16
  154.0 1.0 copy-done.18
  155.0 19.2 %shard_map.159 = bf16[8,8,2,2,16,256]{5,4,3,2,1,0:T(8,128)(2,1)} custom-call(bf16[8,64,8,128]{3,2,1,0:T(8,128)(2,1)S(1)} %copy-done.4, bf16[8,1,64,128]{3,2,1,0:T(8,128)(2,1)} %collective-permute-done.refs_1_, bf16[8,1,64,128]{3,2,1,0:T(8,128)(2,1)} %collective-permute-done.1.refs_2_, ...), custom_call_target="tpu_custom_call", output_to_operand_aliasing={{}: (19, {})} | custom-call | flops 8053063680 | bytes 3145728 | tf_op jit(solution)/shard_map/pallas_call | solution.py:443
  (93 shorter events, 2.1 us)
Async XLA Ops:
  4.1 1.2 copy-start.1
  11.1 1.4 copy-start
  12.5 1.0 copy-start.2
  13.5 0.8 copy-start.5
  14.4 59.4 %all-to-all-start = ((bf16[8,8,18,8,128]{4,3,2,1,0:T(8,128)(2,1)}), bf16[8,8,18,8,128]{4,3,2,1,0:T(8,128)(2,1)S(1)}, u32[]{:S(2)}, u32[]{:S(2)}) async-start(bf16[8,8,18,8,128]{4,3,2,1,0:T(8,128)(2,1)} %bitcast.36), calls=%async_computation | async-start | bytes 4718592 | tf_op jit(solution)/shard_map/all_to_all | solution.py:534
  73.7 13.0 %copy-start.23 = (f32[4]{0:T(128)S(1)}, f32[4]{0:T(128)}, u32[]{:S(2)}) copy-start(f32[4]{0:T(128)} %param.23) | copy-start | bytes 52
  73.7 14.0 %copy-start.21 = (bf16[128,128]{1,0:T(8,128)(2,1)S(1)}, bf16[128,128]{1,0:T(8,128)(2,1)}, u32[]{:S(2)}) copy-start(bf16[128,128]{1,0:T(8,128)(2,1)} %param.20) | copy-start | bytes 98308
  73.7 14.3 %copy-start.20 = (bf16[128,256]{1,0:T(8,128)(2,1)S(1)}, bf16[128,256]{1,0:T(8,128)(2,1)}, u32[]{:S(2)}) copy-start(bf16[128,256]{1,0:T(8,128)(2,1)} %param.21) | copy-start | bytes 196612
  73.7 14.4 %copy-start.19 = (bf16[256,768]{1,0:T(8,128)(2,1)S(1)}, bf16[256,768]{1,0:T(8,128)(2,1)}, u32[]{:S(2)}) copy-start(bf16[256,768]{1,0:T(8,128)(2,1)} %param.26) | copy-start | bytes 1179652
  73.7 15.1 %copy-start.11 = (bf16[128,128]{1,0:T(8,128)(2,1)S(1)}, bf16[128,128]{1,0:T(8,128)(2,1)}, u32[]{:S(2)}) copy-start(bf16[128,128]{1,0:T(8,128)(2,1)} %wout.3) | copy-start | bytes 98308
  73.8 62.1 %all-to-all-start.1 = ((bf16[8,8,14,8,128]{4,3,2,1,0:T(8,128)(2,1)}), bf16[8,8,14,8,128]{4,3,2,1,0:T(8,128)(2,1)}, u32[]{:S(2)}, u32[]{:S(2)}) async-start(bf16[8,8,14,8,128]{4,3,2,1,0:T(8,128)(2,1)} %bitcast.25), calls=%async_computation.1 | async-start | bytes 3670016 | tf_op jit(solution)/shard_map/all_to_all | solution.py:534
  80.3 33.0 %collective-permute-start.1 = (bf16[8,1,64,128]{3,2,1,0:T(8,128)(2,1)}, bf16[8,1,64,128]{3,2,1,0:T(8,128)(2,1)}, u32[]{:S(2)}, u32[]{:S(2)}) collective-permute-start(bf16[8,1,64,128]{3,2,1,0:T(8,128)(2,1)} %get-tuple-element.39), channel_id=1, source_target_pairs={{1,0},{2,1},{3,2},{5,4},{6,5},{7,6},{9,8},{10,9},{11,10},{13,12},{... | collective-permute-start | bytes 393224 | tf_op jit(solution)/shard_map/ppermute | solution.py:467
  83.7 29.6 %collective-permute-start = (bf16[8,1,64,128]{3,2,1,0:T(8,128)(2,1)}, bf16[8,1,64,128]{3,2,1,0:T(8,128)(2,1)}, u32[]{:S(2)}, u32[]{:S(2)}) collective-permute-start(bf16[8,1,64,128]{3,2,1,0:T(8,128)(2,1)} %get-tuple-element.40), channel_id=1, source_target_pairs={{0,1},{1,2},{2,3},{4,5},{5,6},{6,7},{8,9},{9,10},{10,11},{12,13},{... | collective-permute-start | bytes 393224 | tf_op jit(solution)/shard_map/ppermute | solution.py:466
  88.9 1.1 copy-start.6
  89.9 19.4 %copy-start.24 = (f32[8]{0:T(128)S(1)}, f32[8]{0:T(128)}, u32[]{:S(2)}) copy-start(f32[8]{0:T(128)} %param.28) | copy-start | bytes 100
  90.0 19.5 %copy-start.22 = (f32[3,3,256]{2,1,0:T(4,128)S(1)}, f32[3,3,256]{2,1,0:T(4,128)}, u32[]{:S(2)}) copy-start(f32[3,3,256]{2,1,0:T(4,128)} %param.24) | copy-start | bytes 27652
  90.0 23.3 %copy-start.7 = (bf16[256,512]{1,0:T(8,128)(2,1)S(1)}, bf16[256,512]{1,0:T(8,128)(2,1)}, u32[]{:S(2)}) copy-start(bf16[256,512]{1,0:T(8,128)(2,1)} %refs_17_.1) | copy-start | bytes 786436
  90.0 23.4 %copy-start.10 = (bf16[256,256]{1,0:T(8,128)(2,1)S(1)}, bf16[256,256]{1,0:T(8,128)(2,1)}, u32[]{:S(2)}) copy-start(bf16[256,256]{1,0:T(8,128)(2,1)} %refs_14_.3) | copy-start | bytes 393220
  90.0 23.4 %copy-start.12 = (f32[256]{0:T(256)S(1)}, f32[256]{0:T(256)}, u32[]{:S(2)}) copy-start(f32[256]{0:T(256)} %param.25) | copy-start | bytes 3076
  90.0 23.4 %copy-start.13 = (f32[256]{0:T(256)S(1)}, f32[256]{0:T(256)}, u32[]{:S(2)}) copy-start(f32[256]{0:T(256)} %param.29) | copy-start | bytes 3076
  103.5 0.8 copy-start.14
  104.3 7.3 %collective-permute-start.2 = (bf16[288,128]{1,0:T(8,128)(2,1)}, bf16[288,128]{1,0:T(8,128)(2,1)S(1)}, u32[]{:S(2)}, u32[]{:S(2)}) collective-permute-start(bf16[288,128]{1,0:T(8,128)(2,1)} %get-tuple-element.25), channel_id=1, source_target_pairs={{0,1},{1,2},{2,3},{4,5},{5,6},{6,7},{8,9},{9,10},{10,11},{12,13},{... | collective-permute-start | bytes 221192 | tf_op jit(solution)/shard_map/ppermute | solution.py:466
  107.4 5.9 %collective-permute-start.3 = (bf16[288,128]{1,0:T(8,128)(2,1)}, bf16[288,128]{1,0:T(8,128)(2,1)S(1)}, u32[]{:S(2)}, u32[]{:S(2)}) collective-permute-start(bf16[288,128]{1,0:T(8,128)(2,1)} %get-tuple-element.26), channel_id=1, source_target_pairs={{1,0},{2,1},{3,2},{5,4},{6,5},{7,6},{9,8},{10,9},{11,10},{13,12},{... | collective-permute-start | bytes 221192 | tf_op jit(solution)/shard_map/ppermute | solution.py:467
  113.3 1.2 copy-start.3
  114.6 0.9 copy-start.8
  115.5 1.1 copy-start.15
  135.9 17.0 %copy-start.4 = (bf16[8,64,8,128]{3,2,1,0:T(8,128)(2,1)S(1)}, bf16[8,64,8,128]{3,2,1,0:T(8,128)(2,1)}, u32[]{:S(2)}) copy-start(bf16[8,64,8,128]{3,2,1,0:T(8,128)(2,1)} %copy-done.2) | copy-start | bytes 3145732
  135.9 17.1 %copy-start.9 = (bf16[512,256]{1,0:T(8,128)(2,1)S(1)}, bf16[512,256]{1,0:T(8,128)(2,1)}, u32[]{:S(2)}) copy-start(bf16[512,256]{1,0:T(8,128)(2,1)} %refs_18_.1) | copy-start | bytes 786436
  144.6 0.8 copy-start.17
  145.3 4.5 %collective-permute-start.4 = (bf16[224,128]{1,0:T(8,128)(2,1)S(1)}, bf16[224,128]{1,0:T(8,128)(2,1)S(1)}, u32[]{:S(2)}, u32[]{:S(2)}) collective-permute-start(bf16[224,128]{1,0:T(8,128)(2,1)S(1)} %get-tuple-element.30), channel_id=1, source_target_pairs={{0,1},{1,2},{2,3},{4,5},{5,6},{6,7},{8,9},{9,10},{10,11},{12,13},{... | collective-permute-start | bytes 172040 | tf_op jit(solution)/shard_map/ppermute | solution.py:466
  147.4 5.5 %collective-permute-start.5 = (bf16[224,128]{1,0:T(8,128)(2,1)S(1)}, bf16[224,128]{1,0:T(8,128)(2,1)S(1)}, u32[]{:S(2)}, u32[]{:S(2)}) collective-permute-start(bf16[224,128]{1,0:T(8,128)(2,1)S(1)} %get-tuple-element.31), channel_id=1, source_target_pairs={{1,0},{2,1},{3,2},{5,4},{6,5},{7,6},{9,8},{10,9},{11,10},{13,12},{... | collective-permute-start | bytes 172040 | tf_op jit(solution)/shard_map/ppermute | solution.py:467
  152.9 1.1 copy-start.16
  154.0 1.0 copy-start.18

commit v4 on v3

--- a/solution.py
+++ b/solution.py
@@ -15,7 +15,7 @@
 norm_eps = 1e-05
 unit_eps = 1e-06
 LOG2E = math.log2(math.e)
-VMEM_BYTES = 48 * 2**20
+VMEM_BYTES = 24 * 2**20
 PHASES = 2
 
 NN = (((1,), (0,)), ((), ()))
@@ -45,105 +45,197 @@
     return [TILE - 1] + list(range(run + 1)) if phase == 0 else list(range(run + 1, TILE - 1))
 
 
-def copy_tiles(chosen, pieces, packed, sems):
-    def start(i, _):
-        pltpu.make_async_copy(pieces.at[chosen[i]], packed.at[i], sems.at[i]).start()
-        return 0
-
-    def finish(i, _):
-        pltpu.make_async_copy(pieces.at[0], packed.at[i], sems.at[i]).wait()
-        return 0
-
-    count = packed.shape[0]
-    lax.fori_loop(0, count, start, 0)
-    lax.fori_loop(0, count, finish, 0)
-
-
-def turn_kernel(chosen, maps, turned, first, second, packed, scratch, sems):
+def half_size():
+    return max(1, lax.axis_size("veh") // 2)
+
+
+def turn_kernel(maps, turned, first, second, scratch):
+    rows, cols, channels = maps.shape[1:]
+    run = TILE // PHASES
+    for i in range(rows):
+        scratch[pl.ds(i, cols, stride=rows), :] = maps[0, i].astype(jnp.float32)
+    x = scratch[...].astype(jnp.bfloat16).reshape(cols, rows, channels)
+    turned[0] = x
+    for t in range(cols // TILE):
+        tile = x[t * TILE : (t + 1) * TILE]
+        first[t] = jnp.concatenate([tile[TILE - 1 :], tile[: run + 1]], axis=0)
+        second[t] = tile[run + 1 : TILE - 1]
+
+
+def turn_maps(maps):
     vehicles, rows, cols, channels = maps.shape
     tile_cols = cols // TILE
-    run = TILE // PHASES
-
-    def vehicle(v, _):
-        for i in range(rows):
-            scratch[pl.ds(i, cols, stride=rows), :] = maps[v, i].astype(jnp.float32)
-        x = scratch[...].astype(jnp.bfloat16).reshape(cols, rows, channels)
-        turned[v] = x
-        for t in range(tile_cols):
-            at = v * tile_cols + t
-            tile = x[t * TILE : (t + 1) * TILE]
-            first[at] = jnp.concatenate([tile[TILE - 1 :], tile[: run + 1]], axis=0)
-            second[at] = tile[run + 1 : TILE - 1]
-        return 0
-
-    lax.fori_loop(0, vehicles, vehicle, 0)
-    copy_tiles(chosen, first, packed, sems)
-
-
-def turn_maps(maps, chosen):
-    vehicles, rows, cols, channels = maps.shape
-    tiles = vehicles * (cols // TILE)
-    count = chosen.shape[0]
-    pieces = [(tiles, len(phase_columns(p)), rows, channels) for p in range(PHASES)]
-    shapes = [(vehicles, cols, rows, channels), *pieces, (count, *pieces[0][1:])]
-    whole = lambda shape: pl.BlockSpec(shape, lambda i, *_: (0,) * len(shape))
+    pieces = [(tile_cols, len(phase_columns(p)), rows, channels) for p in range(PHASES)]
+    blocks = [(1, cols, rows, channels), *pieces]
+    block = lambda shape: pl.BlockSpec(shape, lambda v: (v, 0, 0, 0))
     return pl.pallas_call(
         turn_kernel,
-        out_shape=[jax.ShapeDtypeStruct(shape, maps.dtype) for shape in shapes],
+        out_shape=[jax.ShapeDtypeStruct((vehicles * n[0], *n[1:]), maps.dtype) for n in blocks],
+        grid=(vehicles,),
+        in_specs=[block((1, rows, cols, channels))],
+        out_specs=[block(n) for n in blocks],
+        scratch_shapes=[pltpu.VMEM((rows * cols, channels), jnp.float32)],
+        compiler_params=pltpu.CompilerParams(vmem_limit_bytes=VMEM_BYTES),
+        cost_estimate=pl.CostEstimate(flops=0, bytes_accessed=10 * maps.size, transcendentals=0),
+    )(maps)
+
+
+def send_kernel(sizes, senders, shifts, counts, ids, *refs):
+    vehicles, agents, tile_cols, group, capacity, sources = sizes
+    bufs, messages, sems = refs[:sources], refs[sources:-1], refs[-1]
+    me = ids[0]
+    base = me // group * group
+    filled = []
+    for k in range(1, group):
+        target = base + (me - base + k) % group
+        for b in range(sources):
+
+            def pair(i, n):
+                r, a = target * vehicles + i // agents, i % agents
+                sender, shift = senders[r, a], shifts[r, a]
+                tiles = tile_cols - jnp.abs(shift)
+                fits = (a < counts[r]) & (sender // vehicles == ids[b + 1]) & (n + tiles <= capacity)
+                tile = sender % vehicles * tile_cols + jnp.maximum(shift, 0)
+                for t in range(tile_cols):
+
+                    @pl.when(fits & (t < tiles))
+                    def _():
+                        slot = b * capacity + n + t
+                        pltpu.make_async_copy(
+                            bufs[b].at[tile + t], messages[k - 1].at[slot], sems.at[k - 1, slot]
+                        ).start()
+
+                return n + jnp.where(fits, tiles, 0)
+
+            filled.append((k, b, lax.fori_loop(0, vehicles * agents, pair, 0)))
+    for k, b, n in filled:
+
+        def finish(i, _):
+            slot = b * capacity + i
+            pltpu.make_async_copy(bufs[b].at[0], messages[k - 1].at[slot], sems.at[k - 1, slot]).wait()
+            return 0
+
+        lax.fori_loop(0, n, finish, 0)
+
+
+def messages_for(pairs, tile_cols, sources):
+    senders = pairs[0]
+    devices = lax.axis_size("veh")
+    vehicles, agents = senders.shape[0] // devices, senders.shape[1]
+    group = half_size()
+    capacity = tile_cols * max(1, vehicles * agents // devices)
+    ids = jnp.stack([lax.axis_index("veh")] + [d for d, _ in sources]).astype(jnp.int32)
+    shape = (len(sources) * capacity, *sources[0][1].shape[1:])
+    return pl.pallas_call(
+        functools.partial(
+            send_kernel, (vehicles, agents, tile_cols, group, capacity, len(sources))
+        ),
+        out_shape=[jax.ShapeDtypeStruct(shape, sources[0][1].dtype)] * (group - 1),
         grid_spec=pltpu.PrefetchScalarGridSpec(
-            num_scalar_prefetch=1,
+            num_scalar_prefetch=4,
             grid=(1,),
-            in_specs=[whole(maps.shape)],
-            out_specs=[whole(shape) for shape in shapes[:3]] + [pl.BlockSpec(memory_space=pl.ANY)],
-            scratch_shapes=[
-                pltpu.VMEM((rows * cols, channels), jnp.float32),
-                pltpu.SemaphoreType.DMA((count,)),
-            ],
+            in_specs=[pl.BlockSpec(memory_space=pl.ANY)] * len(sources),
+            out_specs=[pl.BlockSpec(memory_space=pl.ANY)] * (group - 1),
+            scratch_shapes=[pltpu.SemaphoreType.DMA((group - 1, shape[0]))],
         ),
         compiler_params=pltpu.CompilerParams(vmem_limit_bytes=VMEM_BYTES),
-        cost_estimate=pl.CostEstimate(flops=0, bytes_accessed=10 * maps.size, transcendentals=0),
-    )(chosen, maps)
-
-
-def pack_tiles(pieces, chosen):
-    count = chosen.shape[0]
-    return pl.pallas_call(
-        copy_tiles,
-        out_shape=jax.ShapeDtypeStruct((count, *pieces.shape[1:]), pieces.dtype),
-        grid_spec=pltpu.PrefetchScalarGridSpec(
-            num_scalar_prefetch=1,
-            grid=(1,),
-            in_specs=[pl.BlockSpec(pieces.shape, lambda i, *_: (0,) * pieces.ndim)],
-            out_specs=pl.BlockSpec(memory_space=pl.ANY),
-            scratch_shapes=[pltpu.SemaphoreType.DMA((count,))],
+        cost_estimate=pl.CostEstimate(
+            flops=0, bytes_accessed=4 * (group - 1) * math.prod(shape), transcendentals=0
         ),
+    )(*pairs, ids, *(x for _, x in sources))
+
+
+def place_kernel(sizes, senders, shifts, counts, ids, place, live, sent):
+    vehicles, agents, tile_cols, group, capacity = sizes
+    me = ids[0]
+    tiles_held = vehicles * tile_cols
+    rank = me % group
+
+    def clear(i, _):
+        sent[i] = 0
+        return 0
+
+    lax.fori_loop(0, sent.shape[0], clear, 0)
+
+    def pair(i, _):
+        v, a = i // agents, i % agents
+        r = me * vehicles + v
+        sender, shift = senders[r, a], shifts[r, a]
+        alive = a < counts[r]
+        source = sender // vehicles
+        n = sent[source]
+        k = (rank - source % group + group) % group
+        apart = jnp.where(source // group == me // group, 0, 1)
+        slot = jnp.where(
+            k == 0,
+            apart * tiles_held + sender % vehicles * tile_cols + jnp.maximum(shift, 0),
+            2 * tiles_held + ((k - 1) * 2 + apart) * capacity + n,
+        )
+        first = jnp.maximum(-shift, 0)
+        for t in range(tile_cols):
+            inside = alive & (t + shift >= 0) & (t + shift < tile_cols)
+            at = a * tiles_held + v * tile_cols + t
+            place[at] = jnp.where(inside, slot + t - first, 0)
+            live[at] = jnp.where(inside, 1, 0)
+        sent[source] = n + jnp.where(alive, tile_cols - jnp.abs(shift), 0)
+        return 0
+
+    lax.fori_loop(0, vehicles * agents, pair, 0)
+
+
+def places_of(pairs, tile_cols):
+    senders = pairs[0]
+    devices = lax.axis_size("veh")
+    vehicles, agents = senders.shape[0] // devices, senders.shape[1]
+    capacity = tile_cols * max(1, vehicles * agents // devices)
+    count = agents * vehicles * tile_cols
+    ids = lax.axis_index("veh").astype(jnp.int32).reshape(1)
+    place, live = pl.pallas_call(
+        functools.partial(place_kernel, (vehicles, agents, tile_cols, half_size(), capacity)),
+        out_shape=[jax.ShapeDtypeStruct((count,), jnp.int32)] * 2,
+        in_specs=[pl.BlockSpec(memory_space=pltpu.SMEM)] * 4,
+        out_specs=[pl.BlockSpec(memory_space=pltpu.SMEM)] * 2,
+        scratch_shapes=[pltpu.SMEM((devices,), jnp.int32)],
         compiler_params=pltpu.CompilerParams(vmem_limit_bytes=VMEM_BYTES),
-        cost_estimate=pl.CostEstimate(flops=0, bytes_accessed=8 * pieces.size, transcendentals=0),
-    )(chosen, pieces)
+    )(*pairs, ids)
+    return place, live.reshape(agents, -1)
 
 
 LANES = 128
 
 
-def join_kernel(steps, place, ego, arrived, present, wq, wkv, wout, scale, out, top_row, low_row, landed, joined, sems):
+def join_kernel(steps, starts, place, ego, *refs):
+    bufs, refs = refs[: len(starts)], refs[len(starts) :]
+    present, wq, wkv, wout, scale, out, top_row, low_row, landed, joined, sems = refs
     step = pl.program_id(0)
     agents, total, channels = landed.shape
     here = total // steps
-    cells = arrived.shape[1]
+    cells = bufs[0].shape[1]
     pieces = total // cells
     part = pieces // steps
 
     def copy(i, source):
         a, q = i // pieces, i % pieces
         start = pl.multiple_of(q * cells, 16)
-        return pltpu.make_async_copy(arrived.at[source], landed.at[a, pl.ds(start, cells), :], sems.at[i])
+        return pltpu.make_async_copy(source, landed.at[a, pl.ds(start, cells), :], sems.at[i])
+
+    def fetch(i, _):
+        at = place[i]
+        for buf, parts in zip(bufs, starts):
+            for first, size, offset in parts:
+
+                @pl.when((at >= first) & (at < first + size))
+                def _(buf=buf, first=first, offset=offset):
+                    copy(i, buf.at[at - first + offset]).start()
+
+        return 0
 
     @pl.when(step == 0)
     def _():
-        lax.fori_loop(0, agents * pieces, lambda i, _: (copy(i, place[i]).start(), 0)[1], 0)
+        lax.fori_loop(0, agents * pieces, fetch, 0)
 
     def wait(i, _):
-        copy(i // part * pieces + step * part + i % part, 0).wait()
+        copy(i // part * pieces + step * part + i % part, bufs[0].at[0]).wait()
         return 0
 
     lax.fori_loop(0, agents * part, wait, 0)
@@ -183,7 +275,7 @@
     low_row[...] = joined[pl.ds(rows - 1, here // rows, stride=rows), :].astype(jnp.bfloat16)
 
 
-def join_agents(pieces, arrived, place, live, wq, wkv, wout, scale):
+def join_agents(pieces, arrived, starts, place, live, wq, wkv, wout, scale):
     count, cols, rows, channels = pieces.shape
     agents = live.shape[0]
     cells = cols * rows
@@ -195,14 +287,14 @@
     present = jnp.repeat(live.astype(jnp.float32), cells, axis=1)
     like = lambda n: jax.ShapeDtypeStruct((n, channels), jnp.bfloat16)
     return pl.pallas_call(
-        functools.partial(join_kernel, steps),
+        functools.partial(join_kernel, steps, starts),
         out_shape=[like(total), like(total // rows), like(total // rows)],
         grid_spec=pltpu.PrefetchScalarGridSpec(
             num_scalar_prefetch=1,
             grid=(steps,),
             in_specs=[
                 block(total),
-                pl.BlockSpec(memory_space=pl.ANY),
+                *[pl.BlockSpec(memory_space=pl.ANY)] * len(arrived),
                 pl.BlockSpec((agents, total // steps), lambda r, *_: (0, r)),
             ]
             + [whole(w) for w in weights],
@@ -218,9 +310,9 @@
             flops=total * channels * channels * 40, bytes_accessed=total * channels * 12, transcendentals=total * 20
         ),
     )(
-        place.reshape(-1),
+        place,
         pieces.reshape(total, channels),
-        arrived.reshape(-1, cells, channels),
+        *(x.reshape(-1, cells, channels) for x in arrived),
         present,
         *weights,
     )
@@ -468,43 +560,6 @@
     return above, below
 
 
-def tables(vehicles_here, tile_cols, senders, shifts, counts):
-    agents = senders.shape[1]
-    devices = lax.axis_size("veh")
-    myself = lax.axis_index("veh")
-    pairs = vehicles_here * agents
-    capacity = tile_cols * max(1, pairs // devices)
-    send_all = senders.reshape(devices, pairs)
-    shift_all = shifts.reshape(devices, pairs)
-    live_all = (jnp.arange(agents)[None, :] < counts[:, None]).reshape(devices, pairs)
-    tiles_all = jnp.where(live_all, tile_cols - jnp.abs(shift_all), 0)
-    source_all = send_all // vehicles_here
-    same = source_all[:, :, None] == source_all[:, None, :]
-    before = jnp.arange(pairs)[None, :] < jnp.arange(pairs)[:, None]
-    start_all = jnp.sum(jnp.where(same & before[None], tiles_all[:, None, :], 0), axis=2)
-    step = jnp.arange(tile_cols, dtype=jnp.int32)
-    tile_of = (
-        (send_all % vehicles_here * tile_cols + jnp.maximum(shift_all, 0))[:, :, None] + step
-    ).reshape(devices, pairs * tile_cols)
-    slot_of = jnp.where(
-        ((source_all == myself)[:, :, None]) & (step < tiles_all[:, :, None]),
-        start_all[:, :, None] + step,
-        -1,
-    ).reshape(devices, pairs * tile_cols)
-    hit = slot_of[:, None, :] == jnp.arange(capacity)[None, :, None]
-    chosen = jnp.sum(jnp.where(hit, tile_of[:, None, :], 0), axis=2).reshape(-1)
-    shifted = step + shift_all[myself][:, None]
-    inside = (shifted >= 0) & (shifted < tile_cols) & live_all[myself][:, None]
-    place = (
-        (source_all[myself] * capacity + start_all[myself])[:, None]
-        + step
-        - jnp.maximum(-shift_all[myself], 0)[:, None]
-    )
-    place = jnp.where(inside, place, 0)
-    by_agent = lambda x: jnp.swapaxes(x.reshape(vehicles_here, agents, tile_cols), 0, 1).reshape(agents, -1)
-    return chosen.astype(jnp.int32), by_agent(place.astype(jnp.int32)), by_agent(inside)
-
-
 def on_device(
     bev_maps,
     senders,
@@ -525,25 +580,50 @@
 ):
     vehicles_here, rows, cols, channels = bev_maps.shape
     devices = lax.axis_size("veh")
-    chosen, place, live = tables(vehicles_here, cols // TILE, senders, shifts, counts)
-    turned, first, second, packed = turn_maps(bev_maps, chosen)
+    tile_cols = cols // TILE
+    tiles = vehicles_here * tile_cols
+    myself = lax.axis_index("veh")
+    group = half_size()
+    partner = (myself + group) % devices
+    capacity = tile_cols * max(1, vehicles_here * senders.shape[1] // devices)
+    pairs = (senders, shifts, counts)
+
+    turned, first, second = turn_maps(bev_maps)
+
+    def swap(x):
+        return lax.ppermute(x, "veh", [(i, (i + group) % devices) for i in range(devices)])
+
+    def send(messages):
+        return [
+            lax.ppermute(
+                x, "veh", [(i, i // group * group + (i + k + 1) % group) for i in range(devices)]
+            )
+            for k, x in enumerate(messages)
+        ]
+
+    far = swap(first)
+    near_tiles = send(messages_for(pairs, tile_cols, [(myself, first)]))
+    place, live = places_of(pairs, tile_cols)
     ego_edges = beside(bev_maps[:, rows - 1 :], bev_maps[:, :1])
-
-    def travel(x):
-        x = x.reshape(devices, -1, *x.shape[1:])
-        x = lax.all_to_all(x, "veh", 0, 0, tiled=True)
-        return x.reshape(-1, *x.shape[2:])
-
-    arrived = [travel(packed)]
-    later = pack_tiles(second, chosen)
-    arrived[0], later = lax.optimization_barrier((arrived[0], later))
-    arrived.append(travel(later))
+    far, second = lax.optimization_barrier((far, second))
+    far_tiles = send(messages_for(pairs, tile_cols, [(partner, far)]))
+    later = swap(second)
+    later_tiles = send(messages_for(pairs, tile_cols, [(myself, second), (partner, later)]))
+    arrived = [[first, far, *near_tiles, *far_tiles], [second, later, *later_tiles]]
+    slots = lambda n: 2 * tiles + n * capacity
+    whole_maps = [((0, tiles, 0),), ((tiles, tiles, 0),)]
+    starts = [
+        whole_maps
+        + [((slots(2 * k), capacity, 0),) for k in range(group - 1)]
+        + [((slots(2 * k + 1), capacity, 0),) for k in range(group - 1)],
+        whole_maps + [((slots(2 * k), 2 * capacity, 0),) for k in range(group - 1)],
+    ]
     result, pieces = None, []
     for phase, own in enumerate((first, second)):
         if phase:
             place, result = lax.optimization_barrier((place, result))
         joined, top, low = join_agents(
-            own, arrived[phase], place, live, agent_query, agent_keyvalue, agent_out, agent_scale
+            own, arrived[phase], starts[phase], place, live, agent_query, agent_keyvalue, agent_out, agent_scale
         )
         pieces.append((joined, *beside(low, top)))
         result = window_layer(

time: 175 us -> 168 us (0.960)
  waiting for transfers between devices: 55.3 us -> 19.6 us
  Pallas kernels: 68.6 us -> 91.2 us
  starting transfers between devices: 27 us -> 36.1 us
  local copies, waits for them, and re-layouts: 22 us -> 19 us
    all_to_all x2 -> x0, waiting for transfers between devices: 50.6 us -> none  [travel(): x = lax.all_to_all(x, 'veh', 0, 0, tiled=True)]
    pallas_call x4 -> x7, Pallas kernels: 30.3 us -> 53 us  [the longest x2 26.9 us: join_agents(): pl.pallas_call(functools.partial(join_kernel, steps, starts), out_shape=[...]
    ppermute x0 -> x11, starting transfers between devices: none -> 20.1 us  [the longest x9 13.7 us: send(): lax.ppermute(x, 'veh', [(i, i // group * group + (i + k + 1) % group) for...]
    ppermute x0 -> x11, waiting for transfers between devices: none -> 12.4 us  [the longest x2 12.3 us: swap(): lax.ppermute(x, 'veh', [(i, (i + group) % devices) for i in range(devices)])]
    all_to_all x2 -> x0, starting transfers between devices: 11.2 us -> none  [travel(): x = lax.all_to_all(x, 'veh', 0, 0, tiled=True)]
    ppermute x3, waiting for transfers between devices: 4.63 us -> 7.18 us  [beside(): below = lax.ppermute(first, 'row', [(i + 1, i) for i in range(count - 1)])]
    unnamed x56 -> x54, local copies, waits for them, and re-layouts: 16.2 us -> 15.5 us
  transfers between devices with their start and end apart: 8 -> 17, of which waited for: 3 -> 3; matrix products, arithmetic and copies ran while one was open for 4% -> 4% of each run, Pallas kernels for 20% -> 35%
where the time goes in v4:
time: 168 us; the launch traced here: 166 us
  Pallas kernels  91.2 us (54%)
  starting transfers between devices  36.1 us (21%)
  waiting for transfers between devices  19.6 us (12%)
  local copies, waits for them, and re-layouts  19 us (11%)
    pallas_call x2, Pallas kernels, window_layer(): pl.pallas_call(functools.partial(window_kernel, phase, rows), out_shape=j...  38.2 us
    pallas_call x2, Pallas kernels, join_agents(): pl.pallas_call(functools.partial(join_kernel, steps, starts), out_shape=[...  26.9 us
    pallas_call x3, Pallas kernels, messages_for(): pl.pallas_call(functools.partial(send_kernel, (vehicles, agents, tile_col...  21.7 us
    unnamed x54, local copies, waits for them, and re-layouts  15.5 us
    ppermute x9, starting transfers between devices, send(): lax.ppermute(x, 'veh', [(i, i // group * group + (i + k + 1) % group) for...  13.7 us
    ppermute x2, waiting for transfers between devices, swap(): lax.ppermute(x, 'veh', [(i, (i + group) % devices) for i in range(devices)])  12.3 us
    ppermute x3, starting transfers between devices, beside(): above = lax.ppermute(last, 'row', [(i, i + 1) for i in range(count - 1)])  8.56 us
    ppermute x3, starting transfers between devices, beside(): below = lax.ppermute(first, 'row', [(i + 1, i) for i in range(count - 1)])  7.41 us
  transfers between devices with their start and end apart: 17, of which 3 were waited for; matrix products, arithmetic and copies ran while one was open for 4% of the time, Pallas kernels for 35%

profile of v4, /device:TPU:1, one launch (start us, length us, event | category | flops | bytes accessed | tf_op | source)
XLA Modules:
  0.0 166.4 jit_solution(5275157297305387054)
XLA Ops:
  0.0 1.2 copy-done
  1.2 0.7 shard_map.154
  1.9 1.0 copy-done.3
  2.9 3.1 %collective-permute-start.2 = (bf16[16,18,8,128]{3,2,1,0:T(8,128)(2,1)S(1)}, bf16[16,18,8,128]{3,2,1,0:T(8,128)(2,1)S(1)}, u32[]{:S(2)}, u32[]{:S(2)}) collective-permute-start(bf16[16,18,8,128]{3,2,1,0:T(8,128)(2,1)S(1)} %get-tuple-element.31.refs_0_), channel_id=1, source_target_pairs={{0,16},{4,20},{8,24},{12,28},{16,0},{20,4},{24,8},{28,12},{1,17},{... | collective-permute-start | bytes 1769480 | tf_op jit(solution)/shard_map/ppermute | solution.py:594
  6.1 0.8 copy.34.senders
  6.8 0.8 copy.35.shifts
  7.7 0.7 copy-done.1
  8.3 6.2 %shard_map.156 = (bf16[8,18,8,128]{3,2,1,0:T(8,128)(2,1)S(1)}, bf16[8,18,8,128]{3,2,1,0:T(8,128)(2,1)S(1)}, bf16[8,18,8,128]{3,2,1,0:T(8,128)(2,1)}) custom-call(s32[64,4]{1,0:T(8,128)S(1)} %copy.34.senders, s32[64,4]{1,0:T(8,128)S(1)} %copy.35.shifts, s32[64]{0:T(128)S(1)} %copy-done.1, s32[2]{0:T(128)S(1)} %get-tuple-element.58.ids, ...), custom_call_target="tpu_custom_call" | custom-call | bytes 1769472 | tf_op jit(solution)/shard_map/pallas_call | solution.py:129
  14.5 1.0 collective-permute-start.3
  15.5 1.7 %collective-permute-start.4 = (bf16[8,18,8,128]{3,2,1,0:T(8,128)(2,1)S(1)}, bf16[8,18,8,128]{3,2,1,0:T(8,128)(2,1)S(1)}, u32[]{:S(2)}, u32[]{:S(2)}) collective-permute-start(bf16[8,18,8,128]{3,2,1,0:T(8,128)(2,1)S(1)} %get-tuple-element.35), channel_id=1, source_target_pairs={{0,8},{4,12},{8,0},{12,4},{16,24},{20,28},{24,16},{28,20},{1,9},{5... | collective-permute-start | bytes 884744 | tf_op jit(solution)/shard_map/ppermute | solution.py:598
  17.2 1.2 collective-permute-start.5
  18.4 1.1 fusion.1
  19.5 12.3 %collective-permute-done.2.refs_0_ = bf16[16,18,8,128]{3,2,1,0:T(8,128)(2,1)S(1)} collective-permute-done((bf16[16,18,8,128]{3,2,1,0:T(8,128)(2,1)S(1)}, bf16[16,18,8,128]{3,2,1,0:T(8,128)(2,1)S(1)}, u32[]{:S(2)}, u32[]{:S(2)}) %collective-permute-start.2) | collective-permute-done | bytes 589856 | tf_op jit(solution)/shard_map/ppermute | solution.py:594
  31.8 4.7 %shard_map.157 = (bf16[8,18,8,128]{3,2,1,0:T(8,128)(2,1)}, bf16[8,18,8,128]{3,2,1,0:T(8,128)(2,1)}, bf16[8,18,8,128]{3,2,1,0:T(8,128)(2,1)}) custom-call(s32[64,4]{1,0:T(8,128)S(1)} %copy.34.senders, s32[64,4]{1,0:T(8,128)S(1)} %copy.35.shifts, s32[64]{0:T(128)S(1)} %copy-done.1, s32[2]{0:T(128)S(1)} %get-tuple-element.59.ids, ...), custom_call_target="tpu_custom_call" | custom-call | bytes 1769472 | tf_op jit(solution)/shard_map/pallas_call | solution.py:129
  36.5 1.3 collective-permute-start.6
  37.8 1.5 collective-permute-start.7
  39.3 0.9 collective-permute-start.8
  40.2 3.7 %shard_map.155 = (s32[64]{0:T(128)S(1)}, s32[64]{0:T(128)S(1)}) custom-call(s32[64,4]{1,0:T(8,128)S(1)} %copy.34.senders, s32[64,4]{1,0:T(8,128)S(1)} %copy.35.shifts, s32[64]{0:T(128)S(1)} %copy-done.1, s32[1]{0:T(128)} %bitcast.ids), custom_call_target="tpu_custom_call" | custom-call | tf_op jit(solution)/shard_map/pallas_call | solution.py:193
  44.4 0.1 copy.40
  44.6 0.1 reshape.102.refs_8_
  44.7 1.0 copy.41
  45.9 3.2 %collective-permute-start.11 = (bf16[16,14,8,128]{3,2,1,0:T(8,128)(2,1)S(1)}, bf16[16,14,8,128]{3,2,1,0:T(8,128)(2,1)S(1)}, u32[]{:S(2)}, u32[]{:S(2)}) collective-permute-start(bf16[16,14,8,128]{3,2,1,0:T(8,128)(2,1)S(1)} %get-tuple-element.45.refs_0_), channel_id=1, source_target_pairs={{0,16},{4,20},{8,24},{12,28},{16,0},{20,4},{24,8},{28,12},{1,17},{... | collective-permute-start | bytes 1376264 | tf_op jit(solution)/shard_map/ppermute | solution.py:594
  49.1 1.7 %fusion = (bf16[8,1,64,128]{3,2,1,0:T(8,128)(2,1)}, bf16[8,1,64,128]{3,2,1,0:T(8,128)(2,1)}) fusion(bf16[8,8,64,128]{3,2,1,0:T(8,128)(2,1)} %maps.1), kind=kLoop, calls=%fused_computation.4 | loop fusion | bytes 524288 | tf_op jit(solution)/shard_map/slice | solution.py:607
  50.8 3.6 %collective-permute-start.1 = (bf16[8,1,64,128]{3,2,1,0:T(8,128)(2,1)}, bf16[8,1,64,128]{3,2,1,0:T(8,128)(2,1)}, u32[]{:S(2)}, u32[]{:S(2)}) collective-permute-start(bf16[8,1,64,128]{3,2,1,0:T(8,128)(2,1)} %get-tuple-element.53), channel_id=1, source_target_pairs={{1,0},{2,1},{3,2},{5,4},{6,5},{7,6},{9,8},{10,9},{11,10},{13,12},{... | collective-permute-start | bytes 393224 | tf_op jit(solution)/shard_map/ppermute | solution.py:559
  54.4 3.0 %collective-permute-start = (bf16[8,1,64,128]{3,2,1,0:T(8,128)(2,1)}, bf16[8,1,64,128]{3,2,1,0:T(8,128)(2,1)}, u32[]{:S(2)}, u32[]{:S(2)}) collective-permute-start(bf16[8,1,64,128]{3,2,1,0:T(8,128)(2,1)} %get-tuple-element.54), channel_id=1, source_target_pairs={{0,1},{1,2},{2,3},{4,5},{5,6},{6,7},{8,9},{9,10},{10,11},{12,13},{... | collective-permute-start | bytes 393224 | tf_op jit(solution)/shard_map/ppermute | solution.py:558
  57.4 0.7 copy-done.11
  58.2 14.3 %shard_map.158 = (bf16[2304,128]{1,0:T(8,128)(2,1)S(1)}, bf16[288,128]{1,0:T(8,128)(2,1)S(1)}, bf16[288,128]{1,0:T(8,128)(2,1)S(1)}) custom-call(s32[64]{0:T(128)S(1)} %get-tuple-element.44.place, bf16[2304,128]{1,0:T(8,128)(2,1)S(1)} %bitcast.29, bf16[16,144,128]{2,1,0:T(8,128)(2,1)S(1)} %bitcast.30, bf16[16,144,128]{2,1,0:T(8,128)(2,1)S(1)} %bitcast.31, ...), custom_call_target="tpu_custom_call" | custom-call | flops 1509949440 | bytes 3538944 | tf_op jit(solution)/shard_map/pallas_call | solution.py:289
  72.5 0.8 copy-done.15
  73.4 3.0 %collective-permute-start.9 = (bf16[288,128]{1,0:T(8,128)(2,1)S(1)}, bf16[288,128]{1,0:T(8,128)(2,1)S(1)}, u32[]{:S(2)}, u32[]{:S(2)}) collective-permute-start(bf16[288,128]{1,0:T(8,128)(2,1)S(1)} %get-tuple-element.42), channel_id=1, source_target_pairs={{0,1},{1,2},{2,3},{4,5},{5,6},{6,7},{8,9},{9,10},{10,11},{12,13},{... | collective-permute-start | bytes 221192 | tf_op jit(solution)/shard_map/ppermute | solution.py:558
  76.4 1.9 %collective-permute-start.10 = (bf16[288,128]{1,0:T(8,128)(2,1)S(1)}, bf16[288,128]{1,0:T(8,128)(2,1)S(1)}, u32[]{:S(2)}, u32[]{:S(2)}) collective-permute-start(bf16[288,128]{1,0:T(8,128)(2,1)S(1)} %get-tuple-element.43), channel_id=1, source_target_pairs={{1,0},{2,1},{3,2},{5,4},{6,5},{7,6},{9,8},{10,9},{11,10},{13,12},{... | collective-permute-start | bytes 221192 | tf_op jit(solution)/shard_map/ppermute | solution.py:559
  78.4 3.6 %collective-permute-done.10 = bf16[288,128]{1,0:T(8,128)(2,1)S(1)} collective-permute-done((bf16[288,128]{1,0:T(8,128)(2,1)S(1)}, bf16[288,128]{1,0:T(8,128)(2,1)S(1)}, u32[]{:S(2)}, u32[]{:S(2)}) %collective-permute-start.10) | collective-permute-done | bytes 73760 | tf_op jit(solution)/shard_map/ppermute | solution.py:559
  82.1 10.8 %shard_map.160 = (bf16[16,14,8,128]{3,2,1,0:T(8,128)(2,1)S(1)}, bf16[16,14,8,128]{3,2,1,0:T(8,128)(2,1)S(1)}, bf16[16,14,8,128]{3,2,1,0:T(8,128)(2,1)S(1)}) custom-call(s32[64,4]{1,0:T(8,128)S(1)} %copy.34.senders, s32[64,4]{1,0:T(8,128)S(1)} %copy.35.shifts, s32[64]{0:T(128)S(1)} %copy-done.2, s32[3]{0:T(128)S(1)} %pad_add_fusion.2.ids, ...), custom_call_target="tpu_custom_call" | custom-call | bytes 2752512 | tf_op jit(solution)/shard_map/pallas_call | solution.py:129
  92.9 4.9 %collective-permute-start.12 = (bf16[16,14,8,128]{3,2,1,0:T(8,128)(2,1)S(1)}, bf16[16,14,8,128]{3,2,1,0:T(8,128)(2,1)S(1)}, u32[]{:S(2)}, u32[]{:S(2)}) collective-permute-start(bf16[16,14,8,128]{3,2,1,0:T(8,128)(2,1)S(1)} %get-tuple-element.46), channel_id=1, source_target_pairs={{0,4},{4,8},{8,12},{12,0},{16,20},{20,24},{24,28},{28,16},{1,5},{5... | collective-permute-start | bytes 1376264 | tf_op jit(solution)/shard_map/ppermute | solution.py:598
  97.9 1.3 collective-permute-start.14
  99.2 1.2 copy-done.4
  100.4 0.9 copy-done.6
  101.3 0.9 copy-done.8
  102.3 1.1 copy-done.16
  103.3 19.1 %shard_map.159.refs_19_ = bf16[8,8,2,2,16,256]{5,4,3,2,1,0:T(8,128)(2,1)} custom-call(bf16[8,64,8,128]{3,2,1,0:T(8,128)(2,1)S(1)} %copy-done.4, bf16[8,1,64,128]{3,2,1,0:T(8,128)(2,1)} %collective-permute-done.refs_1_, bf16[8,1,64,128]{3,2,1,0:T(8,128)(2,1)} %collective-permute-done.1.refs_2_, bf16[8,288,128]{2,1,0:T(8,128)(2,1)S(1)} %bitcast.52, ...), custom_call_target="tpu_custom_call" | custom-call | flops 8053063680 | bytes 3145728 | tf_op jit(solution)/shard_map/pallas_call | solution.py:535
  122.5 12.6 %shard_map.161 = (bf16[1792,128]{1,0:T(8,128)(2,1)S(1)}, bf16[224,128]{1,0:T(8,128)(2,1)S(1)}, bf16[224,128]{1,0:T(8,128)(2,1)S(1)}) custom-call(s32[64]{0:T(128)S(1)} %get-tuple-element.44.place, bf16[1792,128]{1,0:T(8,128)(2,1)S(1)} %bitcast.32, bf16[16,112,128]{2,1,0:T(8,128)(2,1)S(1)} %bitcast.33, bf16[16,112,128]{2,1,0:T(8,128)(2,1)S(1)} %bitcast.34, ...), custom_call_target="tpu_custom_call" | custom-call | flops 1174405120 | bytes 2752512 | tf_op jit(solution)/shard_map/pallas_call | solution.py:289
  135.1 0.8 copy-done.18
  135.9 2.5 %collective-permute-start.15 = (bf16[224,128]{1,0:T(8,128)(2,1)S(1)}, bf16[224,128]{1,0:T(8,128)(2,1)S(1)}, u32[]{:S(2)}, u32[]{:S(2)}) collective-permute-start(bf16[224,128]{1,0:T(8,128)(2,1)S(1)} %get-tuple-element.50), channel_id=1, source_target_pairs={{0,1},{1,2},{2,3},{4,5},{5,6},{6,7},{8,9},{9,10},{10,11},{12,13},{... | collective-permute-start | bytes 172040 | tf_op jit(solution)/shard_map/ppermute | solution.py:558
  138.4 1.9 %collective-permute-start.16 = (bf16[224,128]{1,0:T(8,128)(2,1)S(1)}, bf16[224,128]{1,0:T(8,128)(2,1)S(1)}, u32[]{:S(2)}, u32[]{:S(2)}) collective-permute-start(bf16[224,128]{1,0:T(8,128)(2,1)S(1)} %get-tuple-element.51), channel_id=1, source_target_pairs={{1,0},{2,1},{3,2},{5,4},{6,5},{7,6},{9,8},{10,9},{11,10},{13,12},{... | collective-permute-start | bytes 172040 | tf_op jit(solution)/shard_map/ppermute | solution.py:559
  140.4 3.5 %collective-permute-done.16 = bf16[224,128]{1,0:T(8,128)(2,1)S(1)} collective-permute-done((bf16[224,128]{1,0:T(8,128)(2,1)S(1)}, bf16[224,128]{1,0:T(8,128)(2,1)S(1)}, u32[]{:S(2)}, u32[]{:S(2)}) %collective-permute-start.16) | collective-permute-done | bytes 57376 | tf_op jit(solution)/shard_map/ppermute | solution.py:559
  144.0 1.2 copy-done.5
  145.2 1.1 copy-done.17
  146.3 1.0 copy-done.19
  147.3 19.1 %shard_map.162 = bf16[8,8,2,2,16,256]{5,4,3,2,1,0:T(8,128)(2,1)} custom-call(bf16[8,64,8,128]{3,2,1,0:T(8,128)(2,1)S(1)} %copy-done.5, bf16[8,1,64,128]{3,2,1,0:T(8,128)(2,1)} %collective-permute-done.refs_1_, bf16[8,1,64,128]{3,2,1,0:T(8,128)(2,1)} %collective-permute-done.1.refs_2_, ...), custom_call_target="tpu_custom_call", output_to_operand_aliasing={{}: (19, {})} | custom-call | flops 8053063680 | bytes 3145728 | tf_op jit(solution)/shard_map/pallas_call | solution.py:535
  (67 shorter events, 1.0 us)
Async XLA Ops:
  0.0 1.2 copy-start
  1.2 39.0 %copy-start.23 = (f32[8]{0:T(128)S(1)}, f32[8]{0:T(128)}, u32[]{:S(2)}) copy-start(f32[8]{0:T(128)} %param.28) | copy-start | bytes 100
  1.2 42.7 %copy-start.22 = (f32[4]{0:T(128)S(1)}, f32[4]{0:T(128)}, u32[]{:S(2)}) copy-start(f32[4]{0:T(128)} %param.23) | copy-start | bytes 52
  1.2 42.8 %copy-start.21 = (f32[3,3,256]{2,1,0:T(4,128)S(1)}, f32[3,3,256]{2,1,0:T(4,128)}, u32[]{:S(2)}) copy-start(f32[3,3,256]{2,1,0:T(4,128)} %param.24) | copy-start | bytes 27652
  1.2 43.1 %copy-start.20 = (bf16[128,128]{1,0:T(8,128)(2,1)S(1)}, bf16[128,128]{1,0:T(8,128)(2,1)}, u32[]{:S(2)}) copy-start(bf16[128,128]{1,0:T(8,128)(2,1)} %param.20) | copy-start | bytes 98308
  1.9 1.0 copy-start.3
  2.9 28.9 %collective-permute-start.2 = (bf16[16,18,8,128]{3,2,1,0:T(8,128)(2,1)S(1)}, bf16[16,18,8,128]{3,2,1,0:T(8,128)(2,1)S(1)}, u32[]{:S(2)}, u32[]{:S(2)}) collective-permute-start(bf16[16,18,8,128]{3,2,1,0:T(8,128)(2,1)S(1)} %get-tuple-element.31.refs_0_), channel_id=1, source_target_pairs={{0,16},{4,20},{8,24},{12,28},{16,0},{20,4},{24,8},{28,12},{1,17},{... | collective-permute-start | bytes 1769480 | tf_op jit(solution)/shard_map/ppermute | solution.py:594
  7.7 0.7 copy-start.1
  14.5 24.8 %collective-permute-start.3 = (bf16[8,18,8,128]{3,2,1,0:T(8,128)(2,1)S(1)}, bf16[8,18,8,128]{3,2,1,0:T(8,128)(2,1)S(1)}, u32[]{:S(2)}, u32[]{:S(2)}) collective-permute-start(bf16[8,18,8,128]{3,2,1,0:T(8,128)(2,1)S(1)} %get-tuple-element.34), channel_id=1, source_target_pairs={{0,4},{4,8},{8,12},{12,0},{16,20},{20,24},{24,28},{28,16},{1,5},{5... | collective-permute-start | bytes 884744 | tf_op jit(solution)/shard_map/ppermute | solution.py:598
  15.5 30.4 %collective-permute-start.4 = (bf16[8,18,8,128]{3,2,1,0:T(8,128)(2,1)S(1)}, bf16[8,18,8,128]{3,2,1,0:T(8,128)(2,1)S(1)}, u32[]{:S(2)}, u32[]{:S(2)}) collective-permute-start(bf16[8,18,8,128]{3,2,1,0:T(8,128)(2,1)S(1)} %get-tuple-element.35), channel_id=1, source_target_pairs={{0,8},{4,12},{8,0},{12,4},{16,24},{20,28},{24,16},{28,20},{1,9},{5... | collective-permute-start | bytes 884744 | tf_op jit(solution)/shard_map/ppermute | solution.py:598
  17.2 33.6 %collective-permute-start.5 = (bf16[8,18,8,128]{3,2,1,0:T(8,128)(2,1)}, bf16[8,18,8,128]{3,2,1,0:T(8,128)(2,1)}, u32[]{:S(2)}, u32[]{:S(2)}) collective-permute-start(bf16[8,18,8,128]{3,2,1,0:T(8,128)(2,1)} %get-tuple-element.36), channel_id=1, source_target_pairs={{0,12},{4,0},{8,4},{12,8},{16,28},{20,16},{24,20},{28,24},{1,13},{... | collective-permute-start | bytes 884744 | tf_op jit(solution)/shard_map/ppermute | solution.py:598
  36.5 17.9 %collective-permute-start.6 = (bf16[8,18,8,128]{3,2,1,0:T(8,128)(2,1)}, bf16[8,18,8,128]{3,2,1,0:T(8,128)(2,1)}, u32[]{:S(2)}, u32[]{:S(2)}) collective-permute-start(bf16[8,18,8,128]{3,2,1,0:T(8,128)(2,1)} %get-tuple-element.37), channel_id=1, source_target_pairs={{0,4},{4,8},{8,12},{12,0},{16,20},{20,24},{24,28},{28,16},{1,5},{5... | collective-permute-start | bytes 884744 | tf_op jit(solution)/shard_map/ppermute | solution.py:598
  37.8 19.6 %collective-permute-start.7 = (bf16[8,18,8,128]{3,2,1,0:T(8,128)(2,1)}, bf16[8,18,8,128]{3,2,1,0:T(8,128)(2,1)}, u32[]{:S(2)}, u32[]{:S(2)}) collective-permute-start(bf16[8,18,8,128]{3,2,1,0:T(8,128)(2,1)} %get-tuple-element.38), channel_id=1, source_target_pairs={{0,8},{4,12},{8,0},{12,4},{16,24},{20,28},{24,16},{28,20},{1,9},{5... | collective-permute-start | bytes 884744 | tf_op jit(solution)/shard_map/ppermute | solution.py:598
  39.3 18.1 %collective-permute-start.8 = (bf16[8,18,8,128]{3,2,1,0:T(8,128)(2,1)}, bf16[8,18,8,128]{3,2,1,0:T(8,128)(2,1)}, u32[]{:S(2)}, u32[]{:S(2)}) collective-permute-start(bf16[8,18,8,128]{3,2,1,0:T(8,128)(2,1)} %get-tuple-element.39), channel_id=1, source_target_pairs={{0,12},{4,0},{8,4},{12,8},{16,28},{20,16},{24,20},{28,24},{1,13},{... | collective-permute-start | bytes 884744 | tf_op jit(solution)/shard_map/ppermute | solution.py:598
  45.9 36.2 %collective-permute-start.11 = (bf16[16,14,8,128]{3,2,1,0:T(8,128)(2,1)S(1)}, bf16[16,14,8,128]{3,2,1,0:T(8,128)(2,1)S(1)}, u32[]{:S(2)}, u32[]{:S(2)}) collective-permute-start(bf16[16,14,8,128]{3,2,1,0:T(8,128)(2,1)S(1)} %get-tuple-element.45.refs_0_), channel_id=1, source_target_pairs={{0,16},{4,20},{8,24},{12,28},{16,0},{20,4},{24,8},{28,12},{1,17},{... | collective-permute-start | bytes 1376264 | tf_op jit(solution)/shard_map/ppermute | solution.py:594
  50.8 48.3 %collective-permute-start.1 = (bf16[8,1,64,128]{3,2,1,0:T(8,128)(2,1)}, bf16[8,1,64,128]{3,2,1,0:T(8,128)(2,1)}, u32[]{:S(2)}, u32[]{:S(2)}) collective-permute-start(bf16[8,1,64,128]{3,2,1,0:T(8,128)(2,1)} %get-tuple-element.53), channel_id=1, source_target_pairs={{1,0},{2,1},{3,2},{5,4},{6,5},{7,6},{9,8},{10,9},{11,10},{13,12},{... | collective-permute-start | bytes 393224 | tf_op jit(solution)/shard_map/ppermute | solution.py:559
  54.4 44.8 %collective-permute-start = (bf16[8,1,64,128]{3,2,1,0:T(8,128)(2,1)}, bf16[8,1,64,128]{3,2,1,0:T(8,128)(2,1)}, u32[]{:S(2)}, u32[]{:S(2)}) collective-permute-start(bf16[8,1,64,128]{3,2,1,0:T(8,128)(2,1)} %get-tuple-element.54), channel_id=1, source_target_pairs={{0,1},{1,2},{2,3},{4,5},{5,6},{6,7},{8,9},{9,10},{10,11},{12,13},{... | collective-permute-start | bytes 393224 | tf_op jit(solution)/shard_map/ppermute | solution.py:558
  57.4 0.8 copy-start.11
  58.2 23.9 %copy-start.2 = (s32[64]{0:T(128)S(1)}, s32[64]{0:T(128)}, u32[]{:S(2)}) copy-start(s32[64]{0:T(128)} %counts.7) | copy-start | bytes 772
  58.2 40.9 %copy-start.10 = (bf16[256,256]{1,0:T(8,128)(2,1)S(1)}, bf16[256,256]{1,0:T(8,128)(2,1)}, u32[]{:S(2)}) copy-start(bf16[256,256]{1,0:T(8,128)(2,1)} %refs_14_.3) | copy-start | bytes 393220
  58.2 40.9 %copy-start.13 = (f32[256]{0:T(256)S(1)}, f32[256]{0:T(256)}, u32[]{:S(2)}) copy-start(f32[256]{0:T(256)} %param.25) | copy-start | bytes 3076
  58.2 41.0 %copy-start.14 = (f32[256]{0:T(256)S(1)}, f32[256]{0:T(256)}, u32[]{:S(2)}) copy-start(f32[256]{0:T(256)} %param.29) | copy-start | bytes 3076
  72.5 0.8 copy-start.15
  73.4 5.0 %collective-permute-start.9 = (bf16[288,128]{1,0:T(8,128)(2,1)S(1)}, bf16[288,128]{1,0:T(8,128)(2,1)S(1)}, u32[]{:S(2)}, u32[]{:S(2)}) collective-permute-start(bf16[288,128]{1,0:T(8,128)(2,1)S(1)} %get-tuple-element.42), channel_id=1, source_target_pairs={{0,1},{1,2},{2,3},{4,5},{5,6},{6,7},{8,9},{9,10},{10,11},{12,13},{... | collective-permute-start | bytes 221192 | tf_op jit(solution)/shard_map/ppermute | solution.py:558
  76.4 5.7 %collective-permute-start.10 = (bf16[288,128]{1,0:T(8,128)(2,1)S(1)}, bf16[288,128]{1,0:T(8,128)(2,1)S(1)}, u32[]{:S(2)}, u32[]{:S(2)}) collective-permute-start(bf16[288,128]{1,0:T(8,128)(2,1)S(1)} %get-tuple-element.43), channel_id=1, source_target_pairs={{1,0},{2,1},{3,2},{5,4},{6,5},{7,6},{9,8},{10,9},{11,10},{13,12},{... | collective-permute-start | bytes 221192 | tf_op jit(solution)/shard_map/ppermute | solution.py:559
  92.9 29.5 %collective-permute-start.12 = (bf16[16,14,8,128]{3,2,1,0:T(8,128)(2,1)S(1)}, bf16[16,14,8,128]{3,2,1,0:T(8,128)(2,1)S(1)}, u32[]{:S(2)}, u32[]{:S(2)}) collective-permute-start(bf16[16,14,8,128]{3,2,1,0:T(8,128)(2,1)S(1)} %get-tuple-element.46), channel_id=1, source_target_pairs={{0,4},{4,8},{8,12},{12,0},{16,20},{20,24},{24,28},{28,16},{1,5},{5... | collective-permute-start | bytes 1376264 | tf_op jit(solution)/shard_map/ppermute | solution.py:598
  97.9 24.6 %collective-permute-start.13 = (bf16[16,14,8,128]{3,2,1,0:T(8,128)(2,1)S(1)}, bf16[16,14,8,128]{3,2,1,0:T(8,128)(2,1)S(1)}, u32[]{:S(2)}, u32[]{:S(2)}) collective-permute-start(bf16[16,14,8,128]{3,2,1,0:T(8,128)(2,1)S(1)} %get-tuple-element.47), channel_id=1, source_target_pairs={{0,8},{4,12},{8,0},{12,4},{16,24},{20,28},{24,16},{28,20},{1,9},{5... | collective-permute-start | bytes 1376264 | tf_op jit(solution)/shard_map/ppermute | solution.py:598
  97.9 24.6 %collective-permute-start.14 = (bf16[16,14,8,128]{3,2,1,0:T(8,128)(2,1)S(1)}, bf16[16,14,8,128]{3,2,1,0:T(8,128)(2,1)S(1)}, u32[]{:S(2)}, u32[]{:S(2)}) collective-permute-start(bf16[16,14,8,128]{3,2,1,0:T(8,128)(2,1)S(1)} %get-tuple-element.48), channel_id=1, source_target_pairs={{0,12},{4,0},{8,4},{12,8},{16,28},{20,16},{24,20},{28,24},{1,13},{... | collective-permute-start | bytes 1376264 | tf_op jit(solution)/shard_map/ppermute | solution.py:598
  99.2 1.2 copy-start.4
  100.4 0.9 copy-start.6
  101.3 0.9 copy-start.8
  102.3 1.1 copy-start.16
  103.3 19.1 %copy-start.12 = (bf16[128,128]{1,0:T(8,128)(2,1)S(1)}, bf16[128,128]{1,0:T(8,128)(2,1)}, u32[]{:S(2)}) copy-start(bf16[128,128]{1,0:T(8,128)(2,1)} %refs_8_.1) | copy-start | bytes 98308
  122.5 21.5 %copy-start.7 = (bf16[256,512]{1,0:T(8,128)(2,1)S(1)}, bf16[256,512]{1,0:T(8,128)(2,1)}, u32[]{:S(2)}) copy-start(bf16[256,512]{1,0:T(8,128)(2,1)} %refs_17_.1) | copy-start | bytes 786436
  122.5 21.5 %copy-start.9 = (bf16[512,256]{1,0:T(8,128)(2,1)S(1)}, bf16[512,256]{1,0:T(8,128)(2,1)}, u32[]{:S(2)}) copy-start(bf16[512,256]{1,0:T(8,128)(2,1)} %refs_18_.1) | copy-start | bytes 786436
  135.1 0.8 copy-start.18
  135.9 4.5 %collective-permute-start.15 = (bf16[224,128]{1,0:T(8,128)(2,1)S(1)}, bf16[224,128]{1,0:T(8,128)(2,1)S(1)}, u32[]{:S(2)}, u32[]{:S(2)}) collective-permute-start(bf16[224,128]{1,0:T(8,128)(2,1)S(1)} %get-tuple-element.50), channel_id=1, source_target_pairs={{0,1},{1,2},{2,3},{4,5},{5,6},{6,7},{8,9},{9,10},{10,11},{12,13},{... | collective-permute-start | bytes 172040 | tf_op jit(solution)/shard_map/ppermute | solution.py:558
  138.4 5.5 %collective-permute-start.16 = (bf16[224,128]{1,0:T(8,128)(2,1)S(1)}, bf16[224,128]{1,0:T(8,128)(2,1)S(1)}, u32[]{:S(2)}, u32[]{:S(2)}) collective-permute-start(bf16[224,128]{1,0:T(8,128)(2,1)S(1)} %get-tuple-element.51), channel_id=1, source_target_pairs={{1,0},{2,1},{3,2},{5,4},{6,5},{7,6},{9,8},{10,9},{11,10},{13,12},{... | collective-permute-start | bytes 172040 | tf_op jit(solution)/shard_map/ppermute | solution.py:559
  144.0 1.2 copy-start.5
  145.2 1.1 copy-start.17
  146.3 1.0 copy-start.19

commit v5 on v4

--- a/solution.py
+++ b/solution.py
@@ -16,6 +16,7 @@
 unit_eps = 1e-06
 LOG2E = math.log2(math.e)
 VMEM_BYTES = 24 * 2**20
+WINDOW_VMEM_BYTES = 60 * 2**20
 PHASES = 2
 
 NN = (((1,), (0,)), ((), ()))
@@ -80,82 +81,50 @@
     )(maps)
 
 
-def send_kernel(sizes, senders, shifts, counts, ids, *refs):
-    vehicles, agents, tile_cols, group, capacity, sources = sizes
-    bufs, messages, sems = refs[:sources], refs[sources:-1], refs[-1]
-    me = ids[0]
-    base = me // group * group
-    filled = []
-    for k in range(1, group):
-        target = base + (me - base + k) % group
-        for b in range(sources):
-
-            def pair(i, n):
-                r, a = target * vehicles + i // agents, i % agents
-                sender, shift = senders[r, a], shifts[r, a]
-                tiles = tile_cols - jnp.abs(shift)
-                fits = (a < counts[r]) & (sender // vehicles == ids[b + 1]) & (n + tiles <= capacity)
-                tile = sender % vehicles * tile_cols + jnp.maximum(shift, 0)
-                for t in range(tile_cols):
-
-                    @pl.when(fits & (t < tiles))
-                    def _():
-                        slot = b * capacity + n + t
-                        pltpu.make_async_copy(
-                            bufs[b].at[tile + t], messages[k - 1].at[slot], sems.at[k - 1, slot]
-                        ).start()
-
-                return n + jnp.where(fits, tiles, 0)
-
-            filled.append((k, b, lax.fori_loop(0, vehicles * agents, pair, 0)))
-    for k, b, n in filled:
-
-        def finish(i, _):
-            slot = b * capacity + i
-            pltpu.make_async_copy(bufs[b].at[0], messages[k - 1].at[slot], sems.at[k - 1, slot]).wait()
-            return 0
-
-        lax.fori_loop(0, n, finish, 0)
-
-
-def messages_for(pairs, tile_cols, sources):
-    senders = pairs[0]
-    devices = lax.axis_size("veh")
-    vehicles, agents = senders.shape[0] // devices, senders.shape[1]
-    group = half_size()
-    capacity = tile_cols * max(1, vehicles * agents // devices)
-    ids = jnp.stack([lax.axis_index("veh")] + [d for d, _ in sources]).astype(jnp.int32)
-    shape = (len(sources) * capacity, *sources[0][1].shape[1:])
-    return pl.pallas_call(
-        functools.partial(
-            send_kernel, (vehicles, agents, tile_cols, group, capacity, len(sources))
-        ),
-        out_shape=[jax.ShapeDtypeStruct(shape, sources[0][1].dtype)] * (group - 1),
-        grid_spec=pltpu.PrefetchScalarGridSpec(
-            num_scalar_prefetch=4,
-            grid=(1,),
-            in_specs=[pl.BlockSpec(memory_space=pl.ANY)] * len(sources),
-            out_specs=[pl.BlockSpec(memory_space=pl.ANY)] * (group - 1),
-            scratch_shapes=[pltpu.SemaphoreType.DMA((group - 1, shape[0]))],
-        ),
-        compiler_params=pltpu.CompilerParams(vmem_limit_bytes=VMEM_BYTES),
-        cost_estimate=pl.CostEstimate(
-            flops=0, bytes_accessed=4 * (group - 1) * math.prod(shape), transcendentals=0
-        ),
-    )(*pairs, ids, *(x for _, x in sources))
-
-
-def place_kernel(sizes, senders, shifts, counts, ids, place, live, sent):
+def plan_kernel(sizes, senders, shifts, counts, ids, chosen, filled, place, live, sent):
     vehicles, agents, tile_cols, group, capacity = sizes
-    me = ids[0]
+    me, partner = ids[0], ids[1]
     tiles_held = vehicles * tile_cols
     rank = me % group
+    pairs = vehicles * agents
 
     def clear(i, _):
         sent[i] = 0
         return 0
 
     lax.fori_loop(0, sent.shape[0], clear, 0)
+
+    def target(k, _):
+        first = (me - rank + (rank + k + 1) % group) * vehicles
+
+        def pair(i, n):
+            r, a = first + i // agents, i % agents
+            sender, shift = senders[r, a], shifts[r, a]
+            tiles = tile_cols - jnp.abs(shift)
+            source = sender // vehicles
+            far = jnp.where(source == partner, 1, 0)
+            filled_here = jnp.where(far == 1, n[1], n[0])
+            fits = (a < counts[r]) & ((source == me) | (far == 1)) & (filled_here + tiles <= capacity)
+
+            @pl.when(fits)
+            def _():
+                at = (2 * k + far) * capacity + filled_here
+                tile = sender % vehicles * tile_cols + jnp.maximum(shift, 0)
+                for t in range(tile_cols):
+
+                    @pl.when(t < tiles)
+                    def _():
+                        chosen[at + t] = tile + t
+
+            more = jnp.where(fits, tiles, 0)
+            return n[0] + more * (1 - far), n[1] + more * far
+
+        near, far = lax.fori_loop(0, pairs, pair, (0, 0))
+        filled[2 * k] = near
+        filled[2 * k + 1] = far
+        return 0
+
+    lax.fori_loop(0, group - 1, target, 0)
 
     def pair(i, _):
         v, a = i // agents, i % agents
@@ -180,25 +149,67 @@
         sent[source] = n + jnp.where(alive, tile_cols - jnp.abs(shift), 0)
         return 0
 
-    lax.fori_loop(0, vehicles * agents, pair, 0)
-
-
-def places_of(pairs, tile_cols):
-    senders = pairs[0]
+    lax.fori_loop(0, pairs, pair, 0)
+
+
+def plan_of(senders, shifts, counts, tile_cols, capacity):
     devices = lax.axis_size("veh")
+    group = half_size()
     vehicles, agents = senders.shape[0] // devices, senders.shape[1]
-    capacity = tile_cols * max(1, vehicles * agents // devices)
-    count = agents * vehicles * tile_cols
-    ids = lax.axis_index("veh").astype(jnp.int32).reshape(1)
-    place, live = pl.pallas_call(
-        functools.partial(place_kernel, (vehicles, agents, tile_cols, half_size(), capacity)),
-        out_shape=[jax.ShapeDtypeStruct((count,), jnp.int32)] * 2,
-        in_specs=[pl.BlockSpec(memory_space=pltpu.SMEM)] * 4,
-        out_specs=[pl.BlockSpec(memory_space=pltpu.SMEM)] * 2,
+    me = lax.axis_index("veh").astype(jnp.int32)
+    ids = jnp.stack([me, (me + group) % devices])
+    sizes = [(group - 1) * 2 * capacity, (group - 1) * 2] + [agents * vehicles * tile_cols] * 2
+    smem = pl.BlockSpec(memory_space=pltpu.SMEM)
+    return pl.pallas_call(
+        functools.partial(plan_kernel, (vehicles, agents, tile_cols, group, capacity)),
+        out_shape=[jax.ShapeDtypeStruct((n,), jnp.int32) for n in sizes],
+        in_specs=[smem] * 4,
+        out_specs=[smem] * 4,
         scratch_shapes=[pltpu.SMEM((devices,), jnp.int32)],
         compiler_params=pltpu.CompilerParams(vmem_limit_bytes=VMEM_BYTES),
-    )(*pairs, ids)
-    return place, live.reshape(agents, -1)
+        cost_estimate=pl.CostEstimate(flops=0, bytes_accessed=20 * 2**20, transcendentals=0),
+    )(senders, shifts, counts, ids)
+
+
+def send_kernel(sources, capacity, chosen, filled, *refs):
+    bufs, messages, sems = refs[: len(sources)], refs[len(sources) : -1], refs[-1]
+    copies = []
+    for k, message in enumerate(messages):
+        for b, source in enumerate(sources):
+
+            def copy(i, tile, k=k, b=b, message=message):
+                slot = b * capacity + i
+                return pltpu.make_async_copy(bufs[b].at[tile], message.at[slot], sems.at[k, slot])
+
+            copies.append((2 * k + source, copy))
+    for at, copy in copies:
+        lax.fori_loop(
+            0, filled[at], lambda i, _: (copy(i, chosen[at * capacity + i]).start(), 0)[1], 0
+        )
+    for at, copy in copies:
+        lax.fori_loop(0, filled[at], lambda i, _: (copy(i, 0).wait(), 0)[1], 0)
+
+
+def messages_for(chosen, filled, capacity, sources):
+    first = next(iter(sources.values()))
+    count = filled.shape[0] // 2
+    shape = (len(sources) * capacity, *first.shape[1:])
+    anywhere = pl.BlockSpec(memory_space=pl.ANY)
+    return pl.pallas_call(
+        functools.partial(send_kernel, tuple(sources), capacity),
+        out_shape=[jax.ShapeDtypeStruct(shape, first.dtype)] * count,
+        grid_spec=pltpu.PrefetchScalarGridSpec(
+            num_scalar_prefetch=2,
+            grid=(1,),
+            in_specs=[anywhere] * len(sources),
+            out_specs=[anywhere] * count,
+            scratch_shapes=[pltpu.SemaphoreType.DMA((count, shape[0]))],
+        ),
+        compiler_params=pltpu.CompilerParams(vmem_limit_bytes=VMEM_BYTES),
+        cost_estimate=pl.CostEstimate(
+            flops=0, bytes_accessed=4 * count * math.prod(shape), transcendentals=0
+        ),
+    )(chosen, filled, *sources.values())
 
 
 LANES = 128
@@ -546,7 +557,7 @@
             pltpu.VMEM((2 * PHASES + 2, most, channels), jnp.float32),
         ],
         input_output_aliases=aliases,
-        compiler_params=pltpu.CompilerParams(vmem_limit_bytes=VMEM_BYTES),
+        compiler_params=pltpu.CompilerParams(vmem_limit_bytes=WINDOW_VMEM_BYTES),
         cost_estimate=pl.CostEstimate(
             flops=cells * width * width * 60, bytes_accessed=cells * width * 6, transcendentals=cells * width * 4
         ),
@@ -582,12 +593,8 @@
     devices = lax.axis_size("veh")
     tile_cols = cols // TILE
     tiles = vehicles_here * tile_cols
-    myself = lax.axis_index("veh")
     group = half_size()
-    partner = (myself + group) % devices
     capacity = tile_cols * max(1, vehicles_here * senders.shape[1] // devices)
-    pairs = (senders, shifts, counts)
-
     turned, first, second = turn_maps(bev_maps)
 
     def swap(x):
@@ -602,13 +609,14 @@
         ]
 
     far = swap(first)
-    near_tiles = send(messages_for(pairs, tile_cols, [(myself, first)]))
-    place, live = places_of(pairs, tile_cols)
+    chosen, filled, place, live = plan_of(senders, shifts, counts, tile_cols, capacity)
+    live = live.reshape(senders.shape[1], -1)
+    near_tiles = send(messages_for(chosen, filled, capacity, {0: first}))
     ego_edges = beside(bev_maps[:, rows - 1 :], bev_maps[:, :1])
     far, second = lax.optimization_barrier((far, second))
-    far_tiles = send(messages_for(pairs, tile_cols, [(partner, far)]))
+    far_tiles = send(messages_for(chosen, filled, capacity, {1: far}))
     later = swap(second)
-    later_tiles = send(messages_for(pairs, tile_cols, [(myself, second), (partner, later)]))
+    later_tiles = send(messages_for(chosen, filled, capacity, {0: second, 1: later}))
     arrived = [[first, far, *near_tiles, *far_tiles], [second, later, *later_tiles]]
     slots = lambda n: 2 * tiles + n * capacity
     whole_maps = [((0, tiles, 0),), ((tiles, tiles, 0),)]

time: 168 us -> 166 us (0.988)
  Pallas kernels: 91.2 us -> 82.7 us
  starting transfers between devices: 36.1 us -> 40.8 us
  waiting for transfers between devices: 19.6 us -> 23.8 us
    pallas_call x4, Pallas kernels: 25.4 us -> 13.3 us  [the longest x1 6.8 us: plan_of(): pl.pallas_call(functools.partial(plan_kernel, (vehicles, agents, tile_col...]
    ppermute x9, waiting for transfers between devices: 0.02 us -> 10.3 us  [send(): lax.ppermute(x, 'veh', [(i, i // group * group + (i + k + 1) % group) for...]
    unnamed x54 -> x28, local copies, waits for them, and re-layouts: 15.5 us -> 9.53 us
    ppermute x3, waiting for transfers between devices: 7.18 us -> 2.75 us  [beside(): below = lax.ppermute(first, 'row', [(i + 1, i) for i in range(count - 1)])]
    ppermute x3, starting transfers between devices: 8.56 us -> 12.7 us  [beside(): above = lax.ppermute(last, 'row', [(i, i + 1) for i in range(count - 1)])]
    reshape x4, local copies, waits for them, and re-layouts: 0.06 us -> 2.58 us  [window_layer(): x.reshape(vehicles, -1, channels)]
    pallas_call x2, Pallas kernels: 38.2 us -> 40.1 us  [window_layer(): pl.pallas_call(functools.partial(window_kernel, phase, rows), out_shape=j...]
    pallas_call x2, Pallas kernels: 26.9 us -> 28.7 us  [join_agents(): pl.pallas_call(functools.partial(join_kernel, steps, starts), out_shape=[...]
  transfers between devices with their start and end apart: 17 -> 17, of which waited for: 3 -> 5; matrix products, arithmetic and copies ran while one was open for 4% -> 8% of each run, Pallas kernels for 35% -> 30%
where the time goes in v5:
time: 166 us; the launch traced here: 165 us
  Pallas kernels  82.7 us (50%)
  starting transfers between devices  40.8 us (25%)
  waiting for transfers between devices  23.8 us (14%)
  local copies, waits for them, and re-layouts  17.4 us (10%)
    pallas_call x2, Pallas kernels, window_layer(): pl.pallas_call(functools.partial(window_kernel, phase, rows), out_shape=j...  40.1 us
    pallas_call x2, Pallas kernels, join_agents(): pl.pallas_call(functools.partial(join_kernel, steps, starts), out_shape=[...  28.7 us
    ppermute x9, starting transfers between devices, send(): lax.ppermute(x, 'veh', [(i, i // group * group + (i + k + 1) % group) for...  15.3 us
    ppermute x3, starting transfers between devices, beside(): above = lax.ppermute(last, 'row', [(i, i + 1) for i in range(count - 1)])  12.7 us
    ppermute x2, waiting for transfers between devices, swap(): lax.ppermute(x, 'veh', [(i, (i + group) % devices) for i in range(devices)])  10.7 us
    ppermute x9, waiting for transfers between devices, send(): lax.ppermute(x, 'veh', [(i, i // group * group + (i + k + 1) % group) for...  10.3 us
    unnamed x28, local copies, waits for them, and re-layouts  9.53 us
    ppermute x3, starting transfers between devices, beside(): below = lax.ppermute(first, 'row', [(i + 1, i) for i in range(count - 1)])  7.61 us
  transfers between devices with their start and end apart: 17, of which 5 were waited for; matrix products, arithmetic and copies ran while one was open for 8% of the time, Pallas kernels for 30%

profile of v5, /device:TPU:1, one launch (start us, length us, event | category | flops | bytes accessed | tf_op | source)
XLA Modules:
  0.0 165.2 jit_solution(11867022283674432547)
XLA Ops:
  0.0 1.2 copy-done
  1.2 0.7 shard_map.154
  1.9 1.0 copy-done.2
  2.9 3.1 %collective-permute-start.2 = (bf16[16,18,8,128]{3,2,1,0:T(8,128)(2,1)S(1)}, bf16[16,18,8,128]{3,2,1,0:T(8,128)(2,1)S(1)}, u32[]{:S(2)}, u32[]{:S(2)}) collective-permute-start(bf16[16,18,8,128]{3,2,1,0:T(8,128)(2,1)S(1)} %get-tuple-element.33.refs_0_), channel_id=1, source_target_pairs={{0,16},{4,20},{8,24},{12,28},{16,0},{20,4},{24,8},{28,12},{1,17},{... | collective-permute-start | bytes 1769480 | tf_op jit(solution)/shard_map/ppermute | solution.py:601
  6.1 0.8 copy.28.senders
  6.8 0.8 copy.29.shifts
  7.7 0.7 copy-done.1
  8.3 6.8 %shard_map.155 = (s32[48]{0:T(128)S(1)}, s32[6]{0:T(128)S(1)}, s32[64]{0:T(128)S(1)}, s32[64]{0:T(128)S(1)}) custom-call(s32[64,4]{1,0:T(8,128)S(1)} %copy.28.senders, s32[64,4]{1,0:T(8,128)S(1)} %copy.29.shifts, s32[64]{0:T(128)S(1)} %copy-done.1, s32[2]{0:T(128)S(1)} %pad_add_fusion.ids), custom_call_target="tpu_custom_call" | custom-call | bytes 20971520 | tf_op jit(solution)/shard_map/pallas_call | solution.py:163
  15.1 2.4 %shard_map.156 = (bf16[8,18,8,128]{3,2,1,0:T(8,128)(2,1)S(1)}, bf16[8,18,8,128]{3,2,1,0:T(8,128)(2,1)S(1)}, bf16[8,18,8,128]{3,2,1,0:T(8,128)(2,1)}) custom-call(s32[48]{0:T(128)S(1)} %get-tuple-element.36.chosen, s32[6]{0:T(128)S(1)} %get-tuple-element.37.filled, bf16[16,18,8,128]{3,2,1,0:T(8,128)(2,1)S(1)} %get-tuple-element.33.refs_0_), custom_call_target="tpu_custom_call" | custom-call | bytes 1769472 | tf_op jit(solution)/shard_map/pallas_call | solution.py:198
  17.5 1.2 collective-permute-start.3
  18.7 1.2 collective-permute-start.4
  19.9 1.2 collective-permute-start.5
  21.1 10.7 %collective-permute-done.2.refs_0_ = bf16[16,18,8,128]{3,2,1,0:T(8,128)(2,1)S(1)} collective-permute-done((bf16[16,18,8,128]{3,2,1,0:T(8,128)(2,1)S(1)}, bf16[16,18,8,128]{3,2,1,0:T(8,128)(2,1)S(1)}, u32[]{:S(2)}, u32[]{:S(2)}) %collective-permute-start.2) | collective-permute-done | bytes 589856 | tf_op jit(solution)/shard_map/ppermute | solution.py:601
  31.8 1.6 shard_map.157
  33.4 1.1 collective-permute-start.6
  34.5 1.4 collective-permute-start.7
  35.9 2.3 %collective-permute-done.3 = bf16[8,18,8,128]{3,2,1,0:T(8,128)(2,1)S(1)} collective-permute-done((bf16[8,18,8,128]{3,2,1,0:T(8,128)(2,1)S(1)}, bf16[8,18,8,128]{3,2,1,0:T(8,128)(2,1)S(1)}, u32[]{:S(2)}, u32[]{:S(2)}) %collective-permute-start.3) | collective-permute-done | bytes 294944 | tf_op jit(solution)/shard_map/ppermute | solution.py:605
  38.2 1.8 %fusion.1 = (bf16[256,256]{1,0:T(8,128)(2,1)}, bf16[256,256]{1,0:T(8,128)(2,1)}, bf16[256,256]{1,0:T(8,128)(2,1)}) fusion(bf16[256,768]{1,0:T(8,128)(2,1)} %param.26), kind=kLoop, calls=%fused_computation.3 | loop fusion | bytes 786432 | tf_op jit(solution)/shard_map/slice | solution.py:524
  40.0 2.0 %collective-permute-start.11 = (bf16[16,14,8,128]{3,2,1,0:T(8,128)(2,1)S(1)}, bf16[16,14,8,128]{3,2,1,0:T(8,128)(2,1)S(1)}, u32[]{:S(2)}, u32[]{:S(2)}) collective-permute-start(bf16[16,14,8,128]{3,2,1,0:T(8,128)(2,1)S(1)} %get-tuple-element.49.refs_0_), channel_id=1, source_target_pairs={{0,16},{4,20},{8,24},{12,28},{16,0},{20,4},{24,8},{28,12},{1,17},{... | collective-permute-start | bytes 1376264 | tf_op jit(solution)/shard_map/ppermute | solution.py:601
  42.0 1.7 %fusion = (bf16[8,1,64,128]{3,2,1,0:T(8,128)(2,1)}, bf16[8,1,64,128]{3,2,1,0:T(8,128)(2,1)}) fusion(bf16[8,8,64,128]{3,2,1,0:T(8,128)(2,1)} %maps.1), kind=kLoop, calls=%fused_computation.2 | loop fusion | bytes 524288 | tf_op jit(solution)/shard_map/slice | solution.py:615
  43.9 0.1 copy.30
  44.1 0.1 reshape.98.refs_8_
  44.3 3.6 %collective-permute-start.1 = (bf16[8,1,64,128]{3,2,1,0:T(8,128)(2,1)}, bf16[8,1,64,128]{3,2,1,0:T(8,128)(2,1)}, u32[]{:S(2)}, u32[]{:S(2)}) collective-permute-start(bf16[8,1,64,128]{3,2,1,0:T(8,128)(2,1)} %get-tuple-element.57), channel_id=1, source_target_pairs={{1,0},{2,1},{3,2},{5,4},{6,5},{7,6},{9,8},{10,9},{11,10},{13,12},{... | collective-permute-start | bytes 393224 | tf_op jit(solution)/shard_map/ppermute | solution.py:570
  47.9 7.4 %collective-permute-done.6 = bf16[8,18,8,128]{3,2,1,0:T(8,128)(2,1)S(1)} collective-permute-done((bf16[8,18,8,128]{3,2,1,0:T(8,128)(2,1)}, bf16[8,18,8,128]{3,2,1,0:T(8,128)(2,1)S(1)}, u32[]{:S(2)}, u32[]{:S(2)}) %collective-permute-start.6) | collective-permute-done | bytes 294944 | tf_op jit(solution)/shard_map/ppermute | solution.py:605
  55.4 4.9 %collective-permute-start = (bf16[8,1,64,128]{3,2,1,0:T(8,128)(2,1)}, bf16[8,1,64,128]{3,2,1,0:T(8,128)(2,1)}, u32[]{:S(2)}, u32[]{:S(2)}) collective-permute-start(bf16[8,1,64,128]{3,2,1,0:T(8,128)(2,1)} %get-tuple-element.58), channel_id=1, source_target_pairs={{0,1},{1,2},{2,3},{4,5},{5,6},{6,7},{8,9},{9,10},{10,11},{12,13},{... | collective-permute-start | bytes 393224 | tf_op jit(solution)/shard_map/ppermute | solution.py:569
  60.3 0.6 collective-permute-done.7
  60.9 16.0 %shard_map.158 = (bf16[2304,128]{1,0:T(8,128)(2,1)S(1)}, bf16[288,128]{1,0:T(8,128)(2,1)S(1)}, bf16[288,128]{1,0:T(8,128)(2,1)}) custom-call(s32[64]{0:T(128)S(1)} %get-tuple-element.48.place, bf16[2304,128]{1,0:T(8,128)(2,1)S(1)} %bitcast.29, bf16[16,144,128]{2,1,0:T(8,128)(2,1)S(1)} %bitcast.30, bf16[16,144,128]{2,1,0:T(8,128)(2,1)S(1)} %bitcast.31, ...), custom_call_target="tpu_custom_call" | custom-call | flops 1509949440 | bytes 3538944 | tf_op jit(solution)/shard_map/pallas_call | solution.py:300
  76.9 0.8 copy-done.4
  77.7 3.6 %collective-permute-start.9 = (bf16[288,128]{1,0:T(8,128)(2,1)}, bf16[288,128]{1,0:T(8,128)(2,1)S(1)}, u32[]{:S(2)}, u32[]{:S(2)}) collective-permute-start(bf16[288,128]{1,0:T(8,128)(2,1)} %get-tuple-element.46), channel_id=1, source_target_pairs={{0,1},{1,2},{2,3},{4,5},{5,6},{6,7},{8,9},{9,10},{10,11},{12,13},{... | collective-permute-start | bytes 221192 | tf_op jit(solution)/shard_map/ppermute | solution.py:569
  81.4 1.9 %collective-permute-start.10 = (bf16[288,128]{1,0:T(8,128)(2,1)S(1)}, bf16[288,128]{1,0:T(8,128)(2,1)S(1)}, u32[]{:S(2)}, u32[]{:S(2)}) collective-permute-start(bf16[288,128]{1,0:T(8,128)(2,1)S(1)} %get-tuple-element.47), channel_id=1, source_target_pairs={{1,0},{2,1},{3,2},{5,4},{6,5},{7,6},{9,8},{10,9},{11,10},{13,12},{... | collective-permute-start | bytes 221192 | tf_op jit(solution)/shard_map/ppermute | solution.py:570
  83.3 0.7 copy.35.refs_12_.refs_15_
  84.0 0.6 reshape.103.refs_6_.refs_9_
  84.8 1.7 %copy.39 = bf16[256,256]{0,1:T(8,128)(2,1)} copy(bf16[256,256]{1,0:T(8,128)(2,1)} %get-tuple-element.59) | data formatting | bytes 262144
  86.4 1.7 %copy.38 = bf16[256,256]{0,1:T(8,128)(2,1)} copy(bf16[256,256]{1,0:T(8,128)(2,1)} %get-tuple-element.60) | data formatting | bytes 262144
  88.1 0.6 reshape.101.refs_4_
  88.8 0.6 reshape.102.refs_5_
  89.4 2.5 %shard_map.160 = (bf16[16,14,8,128]{3,2,1,0:T(8,128)(2,1)}, bf16[16,14,8,128]{3,2,1,0:T(8,128)(2,1)S(1)}, bf16[16,14,8,128]{3,2,1,0:T(8,128)(2,1)S(1)}) custom-call(s32[48]{0:T(128)S(1)} %get-tuple-element.36.chosen, s32[6]{0:T(128)S(1)} %get-tuple-element.37.filled, bf16[16,14,8,128]{3,2,1,0:T(8,128)(2,1)S(1)} %get-tuple-element.49.refs_0_, ...), custom_call_target="tpu_custom_call" | custom-call | bytes 2752512 | tf_op jit(solution)/shard_map/pallas_call | solution.py:198
  92.0 8.0 %collective-permute-start.12 = (bf16[16,14,8,128]{3,2,1,0:T(8,128)(2,1)}, bf16[16,14,8,128]{3,2,1,0:T(8,128)(2,1)S(1)}, u32[]{:S(2)}, u32[]{:S(2)}) collective-permute-start(bf16[16,14,8,128]{3,2,1,0:T(8,128)(2,1)} %get-tuple-element.50), channel_id=1, source_target_pairs={{0,4},{4,8},{8,12},{12,0},{16,20},{20,24},{24,28},{28,16},{1,5},{5... | collective-permute-start | bytes 1376264 | tf_op jit(solution)/shard_map/ppermute | solution.py:605
  99.9 1.3 collective-permute-start.14
  101.2 20.0 %shard_map.159.refs_19_ = bf16[8,8,2,2,16,256]{5,4,3,2,1,0:T(8,128)(2,1)} custom-call(bf16[8,64,8,128]{3,2,1,0:T(8,128)(2,1)} %copy-done.2, bf16[8,1,64,128]{3,2,1,0:T(8,128)(2,1)} %collective-permute-done.refs_1_, bf16[8,1,64,128]{3,2,1,0:T(8,128)(2,1)} %collective-permute-done.1.refs_2_, bf16[8,288,128]{2,1,0:T(8,128)(2,1)} %bitcast.46, ...), custom_call_target="tpu_custom_call" | custom-call | flops 8053063680 | bytes 3145728 | tf_op jit(solution)/shard_map/pallas_call | solution.py:546
  121.2 12.6 %shard_map.161 = (bf16[1792,128]{1,0:T(8,128)(2,1)S(1)}, bf16[224,128]{1,0:T(8,128)(2,1)S(1)}, bf16[224,128]{1,0:T(8,128)(2,1)S(1)}) custom-call(s32[64]{0:T(128)S(1)} %get-tuple-element.48.place, bf16[1792,128]{1,0:T(8,128)(2,1)S(1)} %bitcast.32, bf16[16,112,128]{2,1,0:T(8,128)(2,1)S(1)} %bitcast.33, bf16[16,112,128]{2,1,0:T(8,128)(2,1)S(1)} %bitcast.34, ...), custom_call_target="tpu_custom_call" | custom-call | flops 1174405120 | bytes 2752512 | tf_op jit(solution)/shard_map/pallas_call | solution.py:300
  133.9 0.8 copy-done.5
  134.6 4.2 %collective-permute-start.15 = (bf16[224,128]{1,0:T(8,128)(2,1)S(1)}, bf16[224,128]{1,0:T(8,128)(2,1)S(1)}, u32[]{:S(2)}, u32[]{:S(2)}) collective-permute-start(bf16[224,128]{1,0:T(8,128)(2,1)S(1)} %get-tuple-element.54), channel_id=1, source_target_pairs={{0,1},{1,2},{2,3},{4,5},{5,6},{6,7},{8,9},{9,10},{10,11},{12,13},{... | collective-permute-start | bytes 172040 | tf_op jit(solution)/shard_map/ppermute | solution.py:569
  138.8 2.1 %collective-permute-start.16 = (bf16[224,128]{1,0:T(8,128)(2,1)S(1)}, bf16[224,128]{1,0:T(8,128)(2,1)S(1)}, u32[]{:S(2)}, u32[]{:S(2)}) collective-permute-start(bf16[224,128]{1,0:T(8,128)(2,1)S(1)} %get-tuple-element.55), channel_id=1, source_target_pairs={{1,0},{2,1},{3,2},{5,4},{6,5},{7,6},{9,8},{10,9},{11,10},{13,12},{... | collective-permute-start | bytes 172040 | tf_op jit(solution)/shard_map/ppermute | solution.py:570
  140.9 0.6 reshape.113.refs_7_
  141.6 2.7 %collective-permute-done.16 = bf16[224,128]{1,0:T(8,128)(2,1)S(1)} collective-permute-done((bf16[224,128]{1,0:T(8,128)(2,1)S(1)}, bf16[224,128]{1,0:T(8,128)(2,1)S(1)}, u32[]{:S(2)}, u32[]{:S(2)}) %collective-permute-start.16) | collective-permute-done | bytes 57376 | tf_op jit(solution)/shard_map/ppermute | solution.py:570
  144.3 0.7 reshape.114.refs_8_
  145.0 20.1 %shard_map.162 = bf16[8,8,2,2,16,256]{5,4,3,2,1,0:T(8,128)(2,1)} custom-call(bf16[8,64,8,128]{3,2,1,0:T(8,128)(2,1)} %copy-done.2, bf16[8,1,64,128]{3,2,1,0:T(8,128)(2,1)} %collective-permute-done.refs_1_, bf16[8,1,64,128]{3,2,1,0:T(8,128)(2,1)} %collective-permute-done.1.refs_2_, bf16[8,288,128]{2,1,0:T(8,128)(2,1)} %bitcast.47, ...), custom_call_target="tpu_custom_call", output_to_operand_aliasing={{}: (19, {})} | custom-call | flops 8053063680 | bytes 3145728 | tf_op jit(solution)/shard_map/pallas_call | solution.py:546
  (40 shorter events, 0.7 us)
Async XLA Ops:
  0.0 1.2 copy-start
  1.2 42.5 %copy-start.9 = (f32[4]{0:T(128)S(1)}, f32[4]{0:T(128)}, u32[]{:S(2)}) copy-start(f32[4]{0:T(128)} %param.23) | copy-start | bytes 52
  1.2 42.7 %copy-start.7 = (bf16[128,128]{1,0:T(8,128)(2,1)S(1)}, bf16[128,128]{1,0:T(8,128)(2,1)}, u32[]{:S(2)}) copy-start(bf16[128,128]{1,0:T(8,128)(2,1)} %param.20) | copy-start | bytes 98308
  1.2 43.0 %copy-start.6 = (bf16[128,256]{1,0:T(8,128)(2,1)S(1)}, bf16[128,256]{1,0:T(8,128)(2,1)}, u32[]{:S(2)}) copy-start(bf16[128,256]{1,0:T(8,128)(2,1)} %param.21) | copy-start | bytes 196612
  1.2 59.6 %copy-start.3 = (bf16[128,128]{1,0:T(8,128)(2,1)S(1)}, bf16[128,128]{1,0:T(8,128)(2,1)}, u32[]{:S(2)}) copy-start(bf16[128,128]{1,0:T(8,128)(2,1)} %refs_8_.1) | copy-start | bytes 98308
  1.9 1.0 copy-start.2
  2.9 28.9 %collective-permute-start.2 = (bf16[16,18,8,128]{3,2,1,0:T(8,128)(2,1)S(1)}, bf16[16,18,8,128]{3,2,1,0:T(8,128)(2,1)S(1)}, u32[]{:S(2)}, u32[]{:S(2)}) collective-permute-start(bf16[16,18,8,128]{3,2,1,0:T(8,128)(2,1)S(1)} %get-tuple-element.33.refs_0_), channel_id=1, source_target_pairs={{0,16},{4,20},{8,24},{12,28},{16,0},{20,4},{24,8},{28,12},{1,17},{... | collective-permute-start | bytes 1769480 | tf_op jit(solution)/shard_map/ppermute | solution.py:601
  7.7 0.7 copy-start.1
  17.5 20.7 %collective-permute-start.3 = (bf16[8,18,8,128]{3,2,1,0:T(8,128)(2,1)S(1)}, bf16[8,18,8,128]{3,2,1,0:T(8,128)(2,1)S(1)}, u32[]{:S(2)}, u32[]{:S(2)}) collective-permute-start(bf16[8,18,8,128]{3,2,1,0:T(8,128)(2,1)S(1)} %get-tuple-element.38), channel_id=1, source_target_pairs={{0,4},{4,8},{8,12},{12,0},{16,20},{20,24},{24,28},{28,16},{1,5},{5... | collective-permute-start | bytes 884744 | tf_op jit(solution)/shard_map/ppermute | solution.py:605
  18.7 21.3 %collective-permute-start.4 = (bf16[8,18,8,128]{3,2,1,0:T(8,128)(2,1)S(1)}, bf16[8,18,8,128]{3,2,1,0:T(8,128)(2,1)S(1)}, u32[]{:S(2)}, u32[]{:S(2)}) collective-permute-start(bf16[8,18,8,128]{3,2,1,0:T(8,128)(2,1)S(1)} %get-tuple-element.39), channel_id=1, source_target_pairs={{0,8},{4,12},{8,0},{12,4},{16,24},{20,28},{24,16},{28,20},{1,9},{5... | collective-permute-start | bytes 884744 | tf_op jit(solution)/shard_map/ppermute | solution.py:605
  19.9 24.4 %collective-permute-start.5 = (bf16[8,18,8,128]{3,2,1,0:T(8,128)(2,1)}, bf16[8,18,8,128]{3,2,1,0:T(8,128)(2,1)S(1)}, u32[]{:S(2)}, u32[]{:S(2)}) collective-permute-start(bf16[8,18,8,128]{3,2,1,0:T(8,128)(2,1)} %get-tuple-element.40), channel_id=1, source_target_pairs={{0,12},{4,0},{8,4},{12,8},{16,28},{20,16},{24,20},{28,24},{1,13},{... | collective-permute-start | bytes 884744 | tf_op jit(solution)/shard_map/ppermute | solution.py:605
  33.4 22.0 %collective-permute-start.6 = (bf16[8,18,8,128]{3,2,1,0:T(8,128)(2,1)}, bf16[8,18,8,128]{3,2,1,0:T(8,128)(2,1)S(1)}, u32[]{:S(2)}, u32[]{:S(2)}) collective-permute-start(bf16[8,18,8,128]{3,2,1,0:T(8,128)(2,1)} %get-tuple-element.41), channel_id=1, source_target_pairs={{0,4},{4,8},{8,12},{12,0},{16,20},{20,24},{24,28},{28,16},{1,5},{5... | collective-permute-start | bytes 884744 | tf_op jit(solution)/shard_map/ppermute | solution.py:605
  34.5 26.4 %collective-permute-start.7 = (bf16[8,18,8,128]{3,2,1,0:T(8,128)(2,1)}, bf16[8,18,8,128]{3,2,1,0:T(8,128)(2,1)}, u32[]{:S(2)}, u32[]{:S(2)}) collective-permute-start(bf16[8,18,8,128]{3,2,1,0:T(8,128)(2,1)} %get-tuple-element.42), channel_id=1, source_target_pairs={{0,8},{4,12},{8,0},{12,4},{16,24},{20,28},{24,16},{28,20},{1,9},{5... | collective-permute-start | bytes 884744 | tf_op jit(solution)/shard_map/ppermute | solution.py:605
  38.2 22.7 %collective-permute-start.8 = (bf16[8,18,8,128]{3,2,1,0:T(8,128)(2,1)}, bf16[8,18,8,128]{3,2,1,0:T(8,128)(2,1)}, u32[]{:S(2)}, u32[]{:S(2)}) collective-permute-start(bf16[8,18,8,128]{3,2,1,0:T(8,128)(2,1)} %get-tuple-element.43), channel_id=1, source_target_pairs={{0,12},{4,0},{8,4},{12,8},{16,28},{20,16},{24,20},{28,24},{1,13},{... | collective-permute-start | bytes 884744 | tf_op jit(solution)/shard_map/ppermute | solution.py:605
  40.0 49.4 %collective-permute-start.11 = (bf16[16,14,8,128]{3,2,1,0:T(8,128)(2,1)S(1)}, bf16[16,14,8,128]{3,2,1,0:T(8,128)(2,1)S(1)}, u32[]{:S(2)}, u32[]{:S(2)}) collective-permute-start(bf16[16,14,8,128]{3,2,1,0:T(8,128)(2,1)S(1)} %get-tuple-element.49.refs_0_), channel_id=1, source_target_pairs={{0,16},{4,20},{8,24},{12,28},{16,0},{20,4},{24,8},{28,12},{1,17},{... | collective-permute-start | bytes 1376264 | tf_op jit(solution)/shard_map/ppermute | solution.py:601
  44.3 56.8 %collective-permute-start.1 = (bf16[8,1,64,128]{3,2,1,0:T(8,128)(2,1)}, bf16[8,1,64,128]{3,2,1,0:T(8,128)(2,1)}, u32[]{:S(2)}, u32[]{:S(2)}) collective-permute-start(bf16[8,1,64,128]{3,2,1,0:T(8,128)(2,1)} %get-tuple-element.57), channel_id=1, source_target_pairs={{1,0},{2,1},{3,2},{5,4},{6,5},{7,6},{9,8},{10,9},{11,10},{13,12},{... | collective-permute-start | bytes 393224 | tf_op jit(solution)/shard_map/ppermute | solution.py:570
  55.4 45.8 %collective-permute-start = (bf16[8,1,64,128]{3,2,1,0:T(8,128)(2,1)}, bf16[8,1,64,128]{3,2,1,0:T(8,128)(2,1)}, u32[]{:S(2)}, u32[]{:S(2)}) collective-permute-start(bf16[8,1,64,128]{3,2,1,0:T(8,128)(2,1)} %get-tuple-element.58), channel_id=1, source_target_pairs={{0,1},{1,2},{2,3},{4,5},{5,6},{6,7},{8,9},{9,10},{10,11},{12,13},{... | collective-permute-start | bytes 393224 | tf_op jit(solution)/shard_map/ppermute | solution.py:569
  60.8 22.5 %copy-start.10 = (f32[8]{0:T(128)S(1)}, f32[8]{0:T(128)}, u32[]{:S(2)}) copy-start(f32[8]{0:T(128)} %param.28) | copy-start | bytes 100
  60.9 23.2 %copy-start.8 = (f32[3,3,256]{2,1,0:T(4,128)S(1)}, f32[3,3,256]{2,1,0:T(4,128)}, u32[]{:S(2)}) copy-start(f32[3,3,256]{2,1,0:T(4,128)} %param.24) | copy-start | bytes 27652
  76.9 0.8 copy-start.4
  77.7 10.4 %collective-permute-start.9 = (bf16[288,128]{1,0:T(8,128)(2,1)}, bf16[288,128]{1,0:T(8,128)(2,1)S(1)}, u32[]{:S(2)}, u32[]{:S(2)}) collective-permute-start(bf16[288,128]{1,0:T(8,128)(2,1)} %get-tuple-element.46), channel_id=1, source_target_pairs={{0,1},{1,2},{2,3},{4,5},{5,6},{6,7},{8,9},{9,10},{10,11},{12,13},{... | collective-permute-start | bytes 221192 | tf_op jit(solution)/shard_map/ppermute | solution.py:569
  81.4 7.4 %collective-permute-start.10 = (bf16[288,128]{1,0:T(8,128)(2,1)S(1)}, bf16[288,128]{1,0:T(8,128)(2,1)S(1)}, u32[]{:S(2)}, u32[]{:S(2)}) collective-permute-start(bf16[288,128]{1,0:T(8,128)(2,1)S(1)} %get-tuple-element.47), channel_id=1, source_target_pairs={{1,0},{2,1},{3,2},{5,4},{6,5},{7,6},{9,8},{10,9},{11,10},{13,12},{... | collective-permute-start | bytes 221192 | tf_op jit(solution)/shard_map/ppermute | solution.py:570
  92.0 29.3 %collective-permute-start.12 = (bf16[16,14,8,128]{3,2,1,0:T(8,128)(2,1)}, bf16[16,14,8,128]{3,2,1,0:T(8,128)(2,1)S(1)}, u32[]{:S(2)}, u32[]{:S(2)}) collective-permute-start(bf16[16,14,8,128]{3,2,1,0:T(8,128)(2,1)} %get-tuple-element.50), channel_id=1, source_target_pairs={{0,4},{4,8},{8,12},{12,0},{16,20},{20,24},{24,28},{28,16},{1,5},{5... | collective-permute-start | bytes 1376264 | tf_op jit(solution)/shard_map/ppermute | solution.py:605
  99.9 21.3 %collective-permute-start.13 = (bf16[16,14,8,128]{3,2,1,0:T(8,128)(2,1)S(1)}, bf16[16,14,8,128]{3,2,1,0:T(8,128)(2,1)S(1)}, u32[]{:S(2)}, u32[]{:S(2)}) collective-permute-start(bf16[16,14,8,128]{3,2,1,0:T(8,128)(2,1)S(1)} %get-tuple-element.51), channel_id=1, source_target_pairs={{0,8},{4,12},{8,0},{12,4},{16,24},{20,28},{24,16},{28,20},{1,9},{5... | collective-permute-start | bytes 1376264 | tf_op jit(solution)/shard_map/ppermute | solution.py:605
  99.9 21.3 %collective-permute-start.14 = (bf16[16,14,8,128]{3,2,1,0:T(8,128)(2,1)S(1)}, bf16[16,14,8,128]{3,2,1,0:T(8,128)(2,1)S(1)}, u32[]{:S(2)}, u32[]{:S(2)}) collective-permute-start(bf16[16,14,8,128]{3,2,1,0:T(8,128)(2,1)S(1)} %get-tuple-element.52), channel_id=1, source_target_pairs={{0,12},{4,0},{8,4},{12,8},{16,28},{20,16},{24,20},{28,24},{1,13},{... | collective-permute-start | bytes 1376264 | tf_op jit(solution)/shard_map/ppermute | solution.py:605
  133.9 0.8 copy-start.5
  134.6 6.3 %collective-permute-start.15 = (bf16[224,128]{1,0:T(8,128)(2,1)S(1)}, bf16[224,128]{1,0:T(8,128)(2,1)S(1)}, u32[]{:S(2)}, u32[]{:S(2)}) collective-permute-start(bf16[224,128]{1,0:T(8,128)(2,1)S(1)} %get-tuple-element.54), channel_id=1, source_target_pairs={{0,1},{1,2},{2,3},{4,5},{5,6},{6,7},{8,9},{9,10},{10,11},{12,13},{... | collective-permute-start | bytes 172040 | tf_op jit(solution)/shard_map/ppermute | solution.py:569
  138.8 5.5 %collective-permute-start.16 = (bf16[224,128]{1,0:T(8,128)(2,1)S(1)}, bf16[224,128]{1,0:T(8,128)(2,1)S(1)}, u32[]{:S(2)}, u32[]{:S(2)}) collective-permute-start(bf16[224,128]{1,0:T(8,128)(2,1)S(1)} %get-tuple-element.55), channel_id=1, source_target_pairs={{1,0},{2,1},{3,2},{5,4},{6,5},{7,6},{9,8},{10,9},{11,10},{13,12},{... | collective-permute-start | bytes 172040 | tf_op jit(solution)/shard_map/ppermute | solution.py:570

commit v6 on v5

--- a/solution.py
+++ b/solution.py
@@ -11,6 +11,7 @@
 TILE = 32
 WIN = 8
 HEAD = 32
+ENTRY_BITS = 10
 
 norm_eps = 1e-05
 unit_eps = 1e-06
@@ -81,7 +82,7 @@
     )(maps)
 
 
-def plan_kernel(sizes, senders, shifts, counts, ids, chosen, filled, place, live, sent):
+def plan_kernel(sizes, senders, shifts, counts, ids, chosen, filled, entries, listed, sizes_of, live, blank, sent):
     vehicles, agents, tile_cols, group, capacity = sizes
     me, partner = ids[0], ids[1]
     tiles_held = vehicles * tile_cols
@@ -92,7 +93,14 @@
         sent[i] = 0
         return 0
 
+    def clear_list(i, _):
+        listed[i] = 0
+        return 0
+
     lax.fori_loop(0, sent.shape[0], clear, 0)
+    lax.fori_loop(0, listed.shape[0], clear_list, 0)
+    last = blank.shape[0] - 1
+    blank[last] = 0
 
     def target(k, _):
         first = (me - rank + (rank + k + 1) % group) * vehicles
@@ -135,18 +143,29 @@
         n = sent[source]
         k = (rank - source % group + group) % group
         apart = jnp.where(source // group == me // group, 0, 1)
-        slot = jnp.where(
-            k == 0,
-            apart * tiles_held + sender % vehicles * tile_cols + jnp.maximum(shift, 0),
-            2 * tiles_held + ((k - 1) * 2 + apart) * capacity + n,
-        )
+        slot = jnp.where(k == 0, sender % vehicles * tile_cols + jnp.maximum(shift, 0), n)
+        origin = jnp.where(k == 0, 0, 2 * k) + apart
+        tiles = jnp.where(alive, tile_cols - jnp.abs(shift), 0)
+        base = a * tiles_held + v * tile_cols
         first = jnp.maximum(-shift, 0)
+
+        @pl.when(tiles > 0)
+        def _():
+            here = origin * tile_cols + tiles - 1
+            entries[here * pairs + listed[here]] = ((base + first) << ENTRY_BITS) + slot
+            listed[here] = listed[here] + 1
+
+        sizes_of[a * vehicles + v] = tiles
         for t in range(tile_cols):
-            inside = alive & (t + shift >= 0) & (t + shift < tile_cols)
-            at = a * tiles_held + v * tile_cols + t
-            place[at] = jnp.where(inside, slot + t - first, 0)
-            live[at] = jnp.where(inside, 1, 0)
-        sent[source] = n + jnp.where(alive, tile_cols - jnp.abs(shift), 0)
+            inside = (t >= first) & (t < first + tiles)
+            live[base + t] = jnp.where(inside, 1, 0)
+
+            @pl.when(jnp.logical_not(inside))
+            def _():
+                blank[blank[last]] = base + t
+                blank[last] = blank[last] + 1
+
+        sent[source] = n + tiles
         return 0
 
     lax.fori_loop(0, pairs, pair, 0)
@@ -158,13 +177,16 @@
     vehicles, agents = senders.shape[0] // devices, senders.shape[1]
     me = lax.axis_index("veh").astype(jnp.int32)
     ids = jnp.stack([me, (me + group) % devices])
-    sizes = [(group - 1) * 2 * capacity, (group - 1) * 2] + [agents * vehicles * tile_cols] * 2
+    pairs = agents * vehicles
+    places = 2 * group * tile_cols
+    sizes = [(group - 1) * 2 * capacity, (group - 1) * 2, places * pairs, places, pairs]
+    sizes += [pairs * tile_cols, pairs * tile_cols + 1]
     smem = pl.BlockSpec(memory_space=pltpu.SMEM)
     return pl.pallas_call(
         functools.partial(plan_kernel, (vehicles, agents, tile_cols, group, capacity)),
         out_shape=[jax.ShapeDtypeStruct((n,), jnp.int32) for n in sizes],
         in_specs=[smem] * 4,
-        out_specs=[smem] * 4,
+        out_specs=[smem] * 7,
         scratch_shapes=[pltpu.SMEM((devices,), jnp.int32)],
         compiler_params=pltpu.CompilerParams(vmem_limit_bytes=VMEM_BYTES),
         cost_estimate=pl.CostEstimate(flops=0, bytes_accessed=20 * 2**20, transcendentals=0),
@@ -212,47 +234,55 @@
     )(chosen, filled, *sources.values())
 
 
-LANES = 128
-
-
-def join_kernel(steps, starts, place, ego, *refs):
-    bufs, refs = refs[: len(starts)], refs[len(starts) :]
+LANES = 256
+
+
+def join_kernel(origins, tile_cols, entries, listed, sizes_of, blank, ego, *refs):
+    buffers = 1 + max(b for b, _ in origins)
+    bufs, refs = refs[:buffers], refs[buffers:]
     present, wq, wkv, wout, scale, out, top_row, low_row, landed, joined, sems = refs
-    step = pl.program_id(0)
-    agents, total, channels = landed.shape
-    here = total // steps
-    cells = bufs[0].shape[1]
-    pieces = total // cells
-    part = pieces // steps
-
-    def copy(i, source):
-        a, q = i // pieces, i % pieces
-        start = pl.multiple_of(q * cells, 16)
-        return pltpu.make_async_copy(source, landed.at[a, pl.ds(start, cells), :], sems.at[i])
-
-    def fetch(i, _):
-        at = place[i]
-        for buf, parts in zip(bufs, starts):
-            for first, size, offset in parts:
-
-                @pl.when((at >= first) & (at < first + size))
-                def _(buf=buf, first=first, offset=offset):
-                    copy(i, buf.at[at - first + offset]).start()
-
+    count, cells, channels = landed.shape
+    agents = present.shape[0]
+    pieces = count // agents
+    vehicles = pieces // tile_cols
+    total = pieces * cells
+    pairs = agents * vehicles
+
+    def copy(source, at, size, pair):
+        return pltpu.make_async_copy(source, landed.at[pl.ds(at, size)], sems.at[pair])
+
+    for origin, (b, offset) in enumerate(origins):
+        for size in range(tile_cols, 0, -1):
+            place = origin * tile_cols + size - 1
+
+            def fetch(i, _, b=b, offset=offset, size=size, place=place):
+                entry = entries[place * pairs + i]
+                at, tile = entry >> ENTRY_BITS, entry & ((1 << ENTRY_BITS) - 1)
+                copy(bufs[b].at[pl.ds(tile + offset, size)], at, size, at // tile_cols).start()
+                return 0
+
+            lax.fori_loop(0, listed[place], fetch, 0)
+
+    def clear(i, _):
+        landed[blank[i]] = jnp.zeros((cells, channels), landed.dtype)
         return 0
 
-    @pl.when(step == 0)
-    def _():
-        lax.fori_loop(0, agents * pieces, fetch, 0)
-
-    def wait(i, _):
-        copy(i // part * pieces + step * part + i % part, bufs[0].at[0]).wait()
-        return 0
-
-    lax.fori_loop(0, agents * part, wait, 0)
+    lax.fori_loop(0, blank[blank.shape[0] - 1], clear, 0)
+    arrived = 0
     heads = channels // HEAD
     scale_col = scale[...].reshape(heads, 1, 1)
-    for c in range(here // LANES):
+    landed_cells = landed.reshape(agents, total, channels)
+    for c in range(total // LANES):
+        while arrived * tile_cols * cells < (c + 1) * LANES:
+            for a in range(agents):
+                for size in range(1, tile_cols + 1):
+                    pair = a * vehicles + arrived
+
+                    @pl.when(sizes_of[pair] == size)
+                    def _(size=size, pair=pair):
+                        copy(bufs[0].at[pl.ds(0, size)], pair * tile_cols, size, pair).wait()
+
+            arrived += 1
         span = pl.ds(c * LANES, LANES)
         cells_here = ego[span, :]
         queries = dot(wq[...], cells_here, NT)
@@ -267,7 +297,7 @@
         scores, values = zip(
             agent(cells_here),
             *(
-                agent(landed[a, pl.ds(pl.multiple_of(step * here + c * LANES, LANES), LANES), :])
+                agent(landed_cells[a, span, :])
                 for a in range(agents)
             ),
         )
@@ -281,39 +311,37 @@
         mix = functools.reduce(jnp.add, [by_head(v, w * inverse) for w, v in zip(weights, values)])
         joined[span, :] = dot(mix.astype(jnp.bfloat16), wout[...], TN)
     out[...] = joined[...].astype(jnp.bfloat16)
-    rows = here // top_row.shape[0]
-    top_row[...] = joined[pl.ds(0, here // rows, stride=rows), :].astype(jnp.bfloat16)
-    low_row[...] = joined[pl.ds(rows - 1, here // rows, stride=rows), :].astype(jnp.bfloat16)
-
-
-def join_agents(pieces, arrived, starts, place, live, wq, wkv, wout, scale):
+    rows = total // top_row.shape[0]
+    top_row[...] = joined[pl.ds(0, total // rows, stride=rows), :].astype(jnp.bfloat16)
+    low_row[...] = joined[pl.ds(rows - 1, total // rows, stride=rows), :].astype(jnp.bfloat16)
+
+
+def join_agents(pieces, arrived, origins, tile_cols, plan, live, wq, wkv, wout, scale):
     count, cols, rows, channels = pieces.shape
     agents = live.shape[0]
     cells = cols * rows
     total = count * cells
-    steps = 2
-    whole = lambda x: pl.BlockSpec(x.shape, lambda r, *_: (0,) * x.ndim)
-    block = lambda n: pl.BlockSpec((n // steps, channels), lambda r, *_: (r, 0))
+    whole = lambda shape: pl.BlockSpec(shape, lambda r, *_: (0,) * len(shape))
     weights = (wq.T, wkv.T, wout, scale.reshape(-1, 1))
     present = jnp.repeat(live.astype(jnp.float32), cells, axis=1)
-    like = lambda n: jax.ShapeDtypeStruct((n, channels), jnp.bfloat16)
+    shapes = [(n, channels) for n in (total, total // rows, total // rows)]
     return pl.pallas_call(
-        functools.partial(join_kernel, steps, starts),
-        out_shape=[like(total), like(total // rows), like(total // rows)],
+        functools.partial(join_kernel, origins, tile_cols),
+        out_shape=[jax.ShapeDtypeStruct(shape, jnp.bfloat16) for shape in shapes],
         grid_spec=pltpu.PrefetchScalarGridSpec(
-            num_scalar_prefetch=1,
-            grid=(steps,),
+            num_scalar_prefetch=4,
+            grid=(1,),
             in_specs=[
-                block(total),
+                whole((total, channels)),
                 *[pl.BlockSpec(memory_space=pl.ANY)] * len(arrived),
-                pl.BlockSpec((agents, total // steps), lambda r, *_: (0, r)),
+                whole(present.shape),
             ]
-            + [whole(w) for w in weights],
-            out_specs=[block(total), block(total // rows), block(total // rows)],
+            + [whole(w.shape) for w in weights],
+            out_specs=[whole(shape) for shape in shapes],
             scratch_shapes=[
-                pltpu.VMEM((agents, total, channels), jnp.bfloat16),
-                pltpu.VMEM((total // steps, channels), jnp.float32),
-                pltpu.SemaphoreType.DMA((agents * count,)),
+                pltpu.VMEM((agents * count, cells, channels), jnp.bfloat16),
+                pltpu.VMEM((total, channels), jnp.float32),
+                pltpu.SemaphoreType.DMA((agents * count // tile_cols,)),
             ],
         ),
         compiler_params=pltpu.CompilerParams(vmem_limit_bytes=VMEM_BYTES),
@@ -321,7 +349,7 @@
             flops=total * channels * channels * 40, bytes_accessed=total * channels * 12, transcendentals=total * 20
         ),
     )(
-        place,
+        *plan,
         pieces.reshape(total, channels),
         *(x.reshape(-1, cells, channels) for x in arrived),
         present,
@@ -442,43 +470,42 @@
     blank = jnp.zeros((2 * HEAD, pair), jnp.bfloat16)
     blank_p = jnp.zeros((in_window, 4 * in_window), jnp.bfloat16)
     lane_head = lax.broadcasted_iota(jnp.int32, (HEAD, pair), 1) < in_window
-    attended = []
+    rights = []
     for p in range(windows // 2):
         straight = queries[:, p * pair : (p + 1) * pair]
         turned = pltpu.roll(straight, in_window, 1)
-        blocks = []
         for w in range(2):
             low, high = (straight, turned) if w == 0 else (turned, straight)
-            blocks.append(split(jnp.where(even, jnp.where(lane, low, 0.0), jnp.where(lane, 0.0, high))))
+            rights.append(split(jnp.where(even, jnp.where(lane, low, 0.0), jnp.where(lane, 0.0, high))))
+
+    def right(block, g):
+        block = block[g * group : (g + 1) * group]
+        return jnp.concatenate(
+            [
+                jnp.concatenate([block[: 2 * HEAD], blank], axis=1),
+                jnp.concatenate([blank, block[2 * HEAD :]], axis=1),
+            ],
+            axis=0,
+        )
+
+    groups = width // group
+    scores = []
+    for w in range(windows):
+        for g in range(groups):
+            span = slice(w * in_window, (w + 1) * in_window), slice(g * group, (g + 1) * group)
+            both = dot(jnp.concatenate([key_high[span], key_low[span]], axis=0), right(rights[w][0], g))
+            scores.append(both[:in_window] + both[in_window:] + dot(key_high[span], right(rights[w][1], g)))
+    probs = []
+    for score in scores:
+        weight = jnp.exp2(score - jnp.max(score, axis=0, keepdims=True))
+        probs.append((weight * (1.0 / jnp.sum(weight, axis=0, keepdims=True))).astype(jnp.bfloat16))
+    attended = []
+    for p in range(windows // 2):
         parts = []
-        for g in range(width // group):
-            channels_of = slice(g * group, (g + 1) * group)
-            probs = []
-            for w in range(2):
-                at = (2 * p + w) * in_window
-                k_high = key_high[at : at + in_window, channels_of]
-                k_low = key_low[at : at + in_window, channels_of]
-
-                def right(block):
-                    block = block[channels_of]
-                    return jnp.concatenate(
-                        [
-                            jnp.concatenate([block[: 2 * HEAD], blank], axis=1),
-                            jnp.concatenate([blank, block[2 * HEAD :]], axis=1),
-                        ],
-                        axis=0,
-                    )
-
-                first = dot(jnp.concatenate([k_high, k_low], axis=0), right(blocks[w][0]))
-                score = first[:in_window] + first[in_window:] + dot(k_high, right(blocks[w][1]))
-                weight = jnp.exp2(score - jnp.max(score, axis=0, keepdims=True))
-                weight = weight * (1.0 / jnp.sum(weight, axis=0, keepdims=True))
-                weight = weight.astype(jnp.bfloat16)
-                probs.append(
-                    jnp.concatenate([weight, blank_p] if w == 0 else [blank_p, weight], axis=0)
-                )
-            v = values[channels_of, p * pair : (p + 1) * pair]
-            first, second = dot(v, probs[0]), dot(v, probs[1])
+        for g in range(groups):
+            v = values[g * group : (g + 1) * group, p * pair : (p + 1) * pair]
+            first = dot(v, jnp.concatenate([probs[2 * p * groups + g], blank_p], axis=0))
+            second = dot(v, jnp.concatenate([blank_p, probs[(2 * p + 1) * groups + g]], axis=0))
             for h in range(4):
                 rows_of = slice(h * HEAD, (h + 1) * HEAD)
                 cols_of = slice((h // 2) * pair, (h // 2 + 1) * pair)
@@ -513,7 +540,7 @@
     width = 2 * channels
     tile_cols = cols // TILE
     run = TILE // PHASES
-    group = 2
+    group = 4
     whole = lambda x: pl.BlockSpec(x.shape, lambda r: (0,) * x.ndim)
     block = lambda *shape: pl.BlockSpec((group, *shape), lambda r: (r,) + (0,) * len(shape))
     weights = (
@@ -592,7 +619,6 @@
     vehicles_here, rows, cols, channels = bev_maps.shape
     devices = lax.axis_size("veh")
     tile_cols = cols // TILE
-    tiles = vehicles_here * tile_cols
     group = half_size()
     capacity = tile_cols * max(1, vehicles_here * senders.shape[1] // devices)
     turned, first, second = turn_maps(bev_maps)
@@ -609,7 +635,9 @@
         ]
 
     far = swap(first)
-    chosen, filled, place, live = plan_of(senders, shifts, counts, tile_cols, capacity)
+    chosen, filled, *plan = plan_of(senders, shifts, counts, tile_cols, capacity)
+    entries, listed, sizes_of, live, blank = plan
+    plan = (entries, listed, sizes_of, blank)
     live = live.reshape(senders.shape[1], -1)
     near_tiles = send(messages_for(chosen, filled, capacity, {0: first}))
     ego_edges = beside(bev_maps[:, rows - 1 :], bev_maps[:, :1])
@@ -618,20 +646,16 @@
     later = swap(second)
     later_tiles = send(messages_for(chosen, filled, capacity, {0: second, 1: later}))
     arrived = [[first, far, *near_tiles, *far_tiles], [second, later, *later_tiles]]
-    slots = lambda n: 2 * tiles + n * capacity
-    whole_maps = [((0, tiles, 0),), ((tiles, tiles, 0),)]
-    starts = [
-        whole_maps
-        + [((slots(2 * k), capacity, 0),) for k in range(group - 1)]
-        + [((slots(2 * k + 1), capacity, 0),) for k in range(group - 1)],
-        whole_maps + [((slots(2 * k), 2 * capacity, 0),) for k in range(group - 1)],
+    origins = [
+        [(0, 0), (1, 0)] + [(2 + k + part * (group - 1), 0) for k in range(group - 1) for part in (0, 1)],
+        [(0, 0), (1, 0)] + [(2 + k, part * capacity) for k in range(group - 1) for part in (0, 1)],
     ]
     result, pieces = None, []
     for phase, own in enumerate((first, second)):
         if phase:
-            place, result = lax.optimization_barrier((place, result))
+            plan, result = lax.optimization_barrier((plan, result))
         joined, top, low = join_agents(
-            own, arrived[phase], starts[phase], place, live, agent_query, agent_keyvalue, agent_out, agent_scale
+            own, arrived[phase], origins[phase], tile_cols, plan, live, agent_query, agent_keyvalue, agent_out, agent_scale
         )
         pieces.append((joined, *beside(low, top)))
         result = window_layer(

time: 166 us -> 149 us (0.90); the launches traced: 165 us -> 146 us
  Pallas kernels: 82.7 us -> 61.1 us
  waiting for transfers between devices: 23.8 us -> 27.5 us
    pallas_call x2, Pallas kernels: 40.1 us -> 27.3 us  [window_layer(): pl.pallas_call(functools.partial(window_kernel, phase, rows), out_shape=j...]
    pallas_call x2, Pallas kernels: 28.7 us -> 19.2 us  [join_agents(): pl.pallas_call(functools.partial(join_kernel, origins, tile_cols), out_sh...]
    ppermute x9, waiting for transfers between devices: 10.3 us -> 14.3 us  [send(): lax.ppermute(x, 'veh', [(i, i // group * group + (i + k + 1) % group) for...]
    unnamed x28 -> x26, local copies, waits for them, and re-layouts: 9.53 us -> 9.52 us
  transfers between devices with their start and end apart: 17 -> 17, of which waited for: 5 -> 6; matrix products, arithmetic and copies ran while one was open for 8% -> 9% of each run, Pallas kernels for 30% -> 26%
where the time goes in v6:
time: 149 us; the launch traced here: 146 us
  Pallas kernels  61.1 us (41%)
  starting transfers between devices  39.2 us (26%)
  waiting for transfers between devices  27.5 us (18%)
  local copies, waits for them, and re-layouts  18.1 us (12%)
    pallas_call x2, Pallas kernels, window_layer(): pl.pallas_call(functools.partial(window_kernel, phase, rows), out_shape=j...  27.3 us
    pallas_call x2, Pallas kernels, join_agents(): pl.pallas_call(functools.partial(join_kernel, origins, tile_cols), out_sh...  19.2 us
    ppermute x9, starting transfers between devices, send(): lax.ppermute(x, 'veh', [(i, i // group * group + (i + k + 1) % group) for...  14.5 us
    ppermute x9, waiting for transfers between devices, send(): lax.ppermute(x, 'veh', [(i, i // group * group + (i + k + 1) % group) for...  14.3 us
    ppermute x3, starting transfers between devices, beside(): above = lax.ppermute(last, 'row', [(i, i + 1) for i in range(count - 1)])  12.2 us
    ppermute x2, waiting for transfers between devices, swap(): lax.ppermute(x, 'veh', [(i, (i + group) % devices) for i in range(devices)])  10.5 us
    unnamed x26, local copies, waits for them, and re-layouts  9.52 us
    ppermute x3, starting transfers between devices, beside(): below = lax.ppermute(first, 'row', [(i + 1, i) for i in range(count - 1)])  7.65 us
  transfers between devices with their start and end apart: 17, of which 6 were waited for; matrix products, arithmetic and copies ran while one was open for 9% of the time, Pallas kernels for 26%

profile of v6, /device:TPU:1, one launch (start us, length us, event | category | flops | bytes accessed | tf_op | source)
XLA Modules:
  0.0 146.4 jit_solution(7527554566450326987)
XLA Ops:
  0.0 1.2 copy-done
  1.2 0.7 shard_map.154
  1.9 1.0 copy-done.2
  2.9 3.1 %collective-permute-start.2 = (bf16[16,18,8,128]{3,2,1,0:T(8,128)(2,1)S(1)}, bf16[16,18,8,128]{3,2,1,0:T(8,128)(2,1)S(1)}, u32[]{:S(2)}, u32[]{:S(2)}) collective-permute-start(bf16[16,18,8,128]{3,2,1,0:T(8,128)(2,1)S(1)} %get-tuple-element.42.refs_0_), channel_id=1, source_target_pairs={{0,16},{4,20},{8,24},{12,28},{16,0},{20,4},{24,8},{28,12},{1,17},{... | collective-permute-start | bytes 1769480 | tf_op jit(solution)/shard_map/ppermute | solution.py:627
  6.1 0.8 copy.28.senders
  6.8 0.8 copy.29.shifts
  7.7 0.7 copy-done.1
  8.3 7.3 %shard_map.155 = (s32[48]{0:T(128)S(1)}, s32[6]{0:T(128)S(1)}, s32[512]{0:T(512)S(1)}, s32[16]{0:T(128)S(1)}, s32[32]{0:T(128)S(1)}, /*index=5*/s32[64]{0:T(128)S(1)}, s32[65]{0:T(128)S(1)}) custom-call(s32[64,4]{1,0:T(8,128)S(1)} %copy.28.senders, s32[64,4]{1,0:T(8,128)S(1)} %copy.29.shifts, s32[64]{0:T(128)S(1)} %copy-done.1, s32[2]{0:T(128)S(1)} %pad_add_fusion.ids), custom_call_target="tpu_custom_call" | custom-call | bytes 20971520 | tf_op jit(solution)/shard_map/pallas_call | solution.py:185
  15.6 2.2 %shard_map.156 = (bf16[8,18,8,128]{3,2,1,0:T(8,128)(2,1)S(1)}, bf16[8,18,8,128]{3,2,1,0:T(8,128)(2,1)S(1)}, bf16[8,18,8,128]{3,2,1,0:T(8,128)(2,1)}) custom-call(s32[48]{0:T(128)S(1)} %get-tuple-element.45.chosen, s32[6]{0:T(128)S(1)} %get-tuple-element.46.filled, bf16[16,18,8,128]{3,2,1,0:T(8,128)(2,1)S(1)} %get-tuple-element.42.refs_0_), custom_call_target="tpu_custom_call" | custom-call | bytes 1769472 | tf_op jit(solution)/shard_map/pallas_call | solution.py:220
  17.8 1.2 collective-permute-start.3
  19.0 1.4 collective-permute-start.4
  20.4 0.9 collective-permute-start.5
  21.3 10.5 %collective-permute-done.2.refs_0_ = bf16[16,18,8,128]{3,2,1,0:T(8,128)(2,1)S(1)} collective-permute-done((bf16[16,18,8,128]{3,2,1,0:T(8,128)(2,1)S(1)}, bf16[16,18,8,128]{3,2,1,0:T(8,128)(2,1)S(1)}, u32[]{:S(2)}, u32[]{:S(2)}) %collective-permute-start.2) | collective-permute-done | bytes 589856 | tf_op jit(solution)/shard_map/ppermute | solution.py:627
  31.8 1.7 %shard_map.157 = (bf16[8,18,8,128]{3,2,1,0:T(8,128)(2,1)}, bf16[8,18,8,128]{3,2,1,0:T(8,128)(2,1)}, bf16[8,18,8,128]{3,2,1,0:T(8,128)(2,1)}) custom-call(s32[48]{0:T(128)S(1)} %get-tuple-element.45.chosen, s32[6]{0:T(128)S(1)} %get-tuple-element.46.filled, bf16[16,18,8,128]{3,2,1,0:T(8,128)(2,1)S(1)} %collective-permute-done.2.refs_0_), custom_call_target="tpu_custom_call" | custom-call | bytes 1769472 | tf_op jit(solution)/shard_map/pallas_call | solution.py:220
  33.5 1.0 collective-permute-start.6
  34.5 1.4 collective-permute-start.7
  35.9 2.6 %collective-permute-done.3 = bf16[8,18,8,128]{3,2,1,0:T(8,128)(2,1)S(1)} collective-permute-done((bf16[8,18,8,128]{3,2,1,0:T(8,128)(2,1)S(1)}, bf16[8,18,8,128]{3,2,1,0:T(8,128)(2,1)S(1)}, u32[]{:S(2)}, u32[]{:S(2)}) %collective-permute-start.3) | collective-permute-done | bytes 294944 | tf_op jit(solution)/shard_map/ppermute | solution.py:631
  38.5 1.8 %fusion.1 = (bf16[256,256]{1,0:T(8,128)(2,1)}, bf16[256,256]{1,0:T(8,128)(2,1)}, bf16[256,256]{1,0:T(8,128)(2,1)}) fusion(bf16[256,768]{1,0:T(8,128)(2,1)} %param.26), kind=kLoop, calls=%fused_computation.3 | loop fusion | bytes 786432 | tf_op jit(solution)/shard_map/slice | solution.py:551
  40.3 1.7 %collective-permute-start.11 = (bf16[16,14,8,128]{3,2,1,0:T(8,128)(2,1)S(1)}, bf16[16,14,8,128]{3,2,1,0:T(8,128)(2,1)S(1)}, u32[]{:S(2)}, u32[]{:S(2)}) collective-permute-start(bf16[16,14,8,128]{3,2,1,0:T(8,128)(2,1)S(1)} %get-tuple-element.61.refs_0_), channel_id=1, source_target_pairs={{0,16},{4,20},{8,24},{12,28},{16,0},{20,4},{24,8},{28,12},{1,17},{... | collective-permute-start | bytes 1376264 | tf_op jit(solution)/shard_map/ppermute | solution.py:627
  42.0 1.7 %fusion = (bf16[8,1,64,128]{3,2,1,0:T(8,128)(2,1)}, bf16[8,1,64,128]{3,2,1,0:T(8,128)(2,1)}) fusion(bf16[8,8,64,128]{3,2,1,0:T(8,128)(2,1)} %maps.1), kind=kLoop, calls=%fused_computation.2 | loop fusion | bytes 524288 | tf_op jit(solution)/shard_map/slice | solution.py:643
  44.1 0.1 reshape.98.refs_8_
  44.3 3.6 %collective-permute-start.1 = (bf16[8,1,64,128]{3,2,1,0:T(8,128)(2,1)}, bf16[8,1,64,128]{3,2,1,0:T(8,128)(2,1)}, u32[]{:S(2)}, u32[]{:S(2)}) collective-permute-start(bf16[8,1,64,128]{3,2,1,0:T(8,128)(2,1)} %get-tuple-element.69), channel_id=1, source_target_pairs={{1,0},{2,1},{3,2},{5,4},{6,5},{7,6},{9,8},{10,9},{11,10},{13,12},{... | collective-permute-start | bytes 393224 | tf_op jit(solution)/shard_map/ppermute | solution.py:597
  47.9 7.5 %collective-permute-done.6 = bf16[8,18,8,128]{3,2,1,0:T(8,128)(2,1)S(1)} collective-permute-done((bf16[8,18,8,128]{3,2,1,0:T(8,128)(2,1)}, bf16[8,18,8,128]{3,2,1,0:T(8,128)(2,1)S(1)}, u32[]{:S(2)}, u32[]{:S(2)}) %collective-permute-start.6) | collective-permute-done | bytes 294944 | tf_op jit(solution)/shard_map/ppermute | solution.py:631
  55.4 4.9 %collective-permute-start = (bf16[8,1,64,128]{3,2,1,0:T(8,128)(2,1)}, bf16[8,1,64,128]{3,2,1,0:T(8,128)(2,1)}, u32[]{:S(2)}, u32[]{:S(2)}) collective-permute-start(bf16[8,1,64,128]{3,2,1,0:T(8,128)(2,1)} %get-tuple-element.70), channel_id=1, source_target_pairs={{0,1},{1,2},{2,3},{4,5},{5,6},{6,7},{8,9},{9,10},{10,11},{12,13},{... | collective-permute-start | bytes 393224 | tf_op jit(solution)/shard_map/ppermute | solution.py:596
  60.4 0.2 collective-permute-done.7
  60.6 10.8 %shard_map.158 = (bf16[2304,128]{1,0:T(8,128)(2,1)S(1)}, bf16[288,128]{1,0:T(8,128)(2,1)S(1)}, bf16[288,128]{1,0:T(8,128)(2,1)}) custom-call(s32[512]{0:T(512)S(1)} %get-tuple-element.57.entries, s32[16]{0:T(128)S(1)} %get-tuple-element.58.listed, s32[32]{0:T(128)S(1)} %get-tuple-element.59.sizes_of, s32[65]{0:T(128)S(1)} %get-tuple-element.60.blank, ...), custom_call_target="tpu_custom_call" | custom-call | flops 1509949440 | bytes 3538944 | tf_op jit(solution)/shard_map/pallas_call | solution.py:328
  71.4 0.8 copy-done.4
  72.2 3.6 %collective-permute-start.9 = (bf16[288,128]{1,0:T(8,128)(2,1)}, bf16[288,128]{1,0:T(8,128)(2,1)S(1)}, u32[]{:S(2)}, u32[]{:S(2)}) collective-permute-start(bf16[288,128]{1,0:T(8,128)(2,1)} %get-tuple-element.55), channel_id=1, source_target_pairs={{0,1},{1,2},{2,3},{4,5},{5,6},{6,7},{8,9},{9,10},{10,11},{12,13},{... | collective-permute-start | bytes 221192 | tf_op jit(solution)/shard_map/ppermute | solution.py:596
  75.9 1.9 %collective-permute-start.10 = (bf16[288,128]{1,0:T(8,128)(2,1)S(1)}, bf16[288,128]{1,0:T(8,128)(2,1)S(1)}, u32[]{:S(2)}, u32[]{:S(2)}) collective-permute-start(bf16[288,128]{1,0:T(8,128)(2,1)S(1)} %get-tuple-element.56), channel_id=1, source_target_pairs={{1,0},{2,1},{3,2},{5,4},{6,5},{7,6},{9,8},{10,9},{11,10},{13,12},{... | collective-permute-start | bytes 221192 | tf_op jit(solution)/shard_map/ppermute | solution.py:597
  77.8 0.7 copy.35.refs_12_.refs_15_
  78.5 1.3 reshape.103.refs_6_.refs_9_
  80.0 1.7 %copy.39 = bf16[256,256]{0,1:T(8,128)(2,1)} copy(bf16[256,256]{1,0:T(8,128)(2,1)} %get-tuple-element.71) | data formatting | bytes 262144
  81.6 1.7 %copy.38 = bf16[256,256]{0,1:T(8,128)(2,1)} copy(bf16[256,256]{1,0:T(8,128)(2,1)} %get-tuple-element.72) | data formatting | bytes 262144
  83.3 0.6 reshape.101.refs_4_
  83.9 0.6 reshape.102.refs_5_
  84.6 2.7 %shard_map.160 = (bf16[16,14,8,128]{3,2,1,0:T(8,128)(2,1)}, bf16[16,14,8,128]{3,2,1,0:T(8,128)(2,1)S(1)}, bf16[16,14,8,128]{3,2,1,0:T(8,128)(2,1)S(1)}) custom-call(s32[48]{0:T(128)S(1)} %get-tuple-element.45.chosen, s32[6]{0:T(128)S(1)} %get-tuple-element.46.filled, bf16[16,14,8,128]{3,2,1,0:T(8,128)(2,1)S(1)} %get-tuple-element.61.refs_0_, ...), custom_call_target="tpu_custom_call" | custom-call | bytes 2752512 | tf_op jit(solution)/shard_map/pallas_call | solution.py:220
  87.3 7.4 %collective-permute-start.12 = (bf16[16,14,8,128]{3,2,1,0:T(8,128)(2,1)}, bf16[16,14,8,128]{3,2,1,0:T(8,128)(2,1)S(1)}, u32[]{:S(2)}, u32[]{:S(2)}) collective-permute-start(bf16[16,14,8,128]{3,2,1,0:T(8,128)(2,1)} %get-tuple-element.62), channel_id=1, source_target_pairs={{0,4},{4,8},{8,12},{12,0},{16,20},{20,24},{24,28},{28,16},{1,5},{5... | collective-permute-start | bytes 1376264 | tf_op jit(solution)/shard_map/ppermute | solution.py:631
  94.6 1.3 collective-permute-start.14
  95.9 13.6 %shard_map.159.refs_19_ = bf16[8,8,2,2,16,256]{5,4,3,2,1,0:T(8,128)(2,1)} custom-call(bf16[8,64,8,128]{3,2,1,0:T(8,128)(2,1)} %copy-done.2, bf16[8,1,64,128]{3,2,1,0:T(8,128)(2,1)} %collective-permute-done.refs_1_, bf16[8,1,64,128]{3,2,1,0:T(8,128)(2,1)} %collective-permute-done.1.refs_2_, bf16[8,288,128]{2,1,0:T(8,128)(2,1)} %bitcast.46, ...), custom_call_target="tpu_custom_call" | custom-call | flops 8053063680 | bytes 3145728 | tf_op jit(solution)/shard_map/pallas_call | solution.py:573
  109.5 4.0 %collective-permute-done.14 = bf16[16,14,8,128]{3,2,1,0:T(8,128)(2,1)S(1)} collective-permute-done((bf16[16,14,8,128]{3,2,1,0:T(8,128)(2,1)S(1)}, bf16[16,14,8,128]{3,2,1,0:T(8,128)(2,1)S(1)}, u32[]{:S(2)}, u32[]{:S(2)}) %collective-permute-start.14) | collective-permute-done | bytes 458784 | tf_op jit(solution)/shard_map/ppermute | solution.py:631
  113.5 8.4 %shard_map.161 = (bf16[1792,128]{1,0:T(8,128)(2,1)S(1)}, bf16[224,128]{1,0:T(8,128)(2,1)S(1)}, bf16[224,128]{1,0:T(8,128)(2,1)S(1)}) custom-call(s32[512]{0:T(512)S(1)} %get-tuple-element.57.entries, s32[16]{0:T(128)S(1)} %get-tuple-element.58.listed, s32[32]{0:T(128)S(1)} %get-tuple-element.59.sizes_of, s32[65]{0:T(128)S(1)} %get-tuple-element.60.blank, ...), custom_call_target="tpu_custom_call" | custom-call | flops 1174405120 | bytes 2752512 | tf_op jit(solution)/shard_map/pallas_call | solution.py:328
  122.0 0.8 copy-done.5
  122.7 3.6 %collective-permute-start.15 = (bf16[224,128]{1,0:T(8,128)(2,1)S(1)}, bf16[224,128]{1,0:T(8,128)(2,1)S(1)}, u32[]{:S(2)}, u32[]{:S(2)}) collective-permute-start(bf16[224,128]{1,0:T(8,128)(2,1)S(1)} %get-tuple-element.66), channel_id=1, source_target_pairs={{0,1},{1,2},{2,3},{4,5},{5,6},{6,7},{8,9},{9,10},{10,11},{12,13},{... | collective-permute-start | bytes 172040 | tf_op jit(solution)/shard_map/ppermute | solution.py:596
  126.3 2.1 %collective-permute-start.16 = (bf16[224,128]{1,0:T(8,128)(2,1)S(1)}, bf16[224,128]{1,0:T(8,128)(2,1)S(1)}, u32[]{:S(2)}, u32[]{:S(2)}) collective-permute-start(bf16[224,128]{1,0:T(8,128)(2,1)S(1)} %get-tuple-element.67), channel_id=1, source_target_pairs={{1,0},{2,1},{3,2},{5,4},{6,5},{7,6},{9,8},{10,9},{11,10},{13,12},{... | collective-permute-start | bytes 172040 | tf_op jit(solution)/shard_map/ppermute | solution.py:597
  128.5 0.6 reshape.113.refs_7_
  129.1 2.7 %collective-permute-done.16 = bf16[224,128]{1,0:T(8,128)(2,1)S(1)} collective-permute-done((bf16[224,128]{1,0:T(8,128)(2,1)S(1)}, bf16[224,128]{1,0:T(8,128)(2,1)S(1)}, u32[]{:S(2)}, u32[]{:S(2)}) %collective-permute-start.16) | collective-permute-done | bytes 57376 | tf_op jit(solution)/shard_map/ppermute | solution.py:597
  131.8 0.6 reshape.114.refs_8_
  132.5 13.7 %shard_map.162 = bf16[8,8,2,2,16,256]{5,4,3,2,1,0:T(8,128)(2,1)} custom-call(bf16[8,64,8,128]{3,2,1,0:T(8,128)(2,1)} %copy-done.2, bf16[8,1,64,128]{3,2,1,0:T(8,128)(2,1)} %collective-permute-done.refs_1_, bf16[8,1,64,128]{3,2,1,0:T(8,128)(2,1)} %collective-permute-done.1.refs_2_, bf16[8,288,128]{2,1,0:T(8,128)(2,1)} %bitcast.47, ...), custom_call_target="tpu_custom_call", output_to_operand_aliasing={{}: (19, {})} | custom-call | flops 8053063680 | bytes 3145728 | tf_op jit(solution)/shard_map/pallas_call | solution.py:573
  (38 shorter events, 0.8 us)
Async XLA Ops:
  0.0 1.2 copy-start
  1.2 42.5 %copy-start.8 = (f32[4]{0:T(128)S(1)}, f32[4]{0:T(128)}, u32[]{:S(2)}) copy-start(f32[4]{0:T(128)} %param.23) | copy-start | bytes 52
  1.2 42.7 %copy-start.7 = (bf16[128,128]{1,0:T(8,128)(2,1)S(1)}, bf16[128,128]{1,0:T(8,128)(2,1)}, u32[]{:S(2)}) copy-start(bf16[128,128]{1,0:T(8,128)(2,1)} %param.20) | copy-start | bytes 98308
  1.2 43.0 %copy-start.6 = (bf16[128,256]{1,0:T(8,128)(2,1)S(1)}, bf16[128,256]{1,0:T(8,128)(2,1)}, u32[]{:S(2)}) copy-start(bf16[128,256]{1,0:T(8,128)(2,1)} %param.21) | copy-start | bytes 196612
  1.2 59.3 %copy-start.3 = (bf16[128,128]{1,0:T(8,128)(2,1)S(1)}, bf16[128,128]{1,0:T(8,128)(2,1)}, u32[]{:S(2)}) copy-start(bf16[128,128]{1,0:T(8,128)(2,1)} %refs_8_.1) | copy-start | bytes 98308
  1.9 1.0 copy-start.2
  2.9 28.9 %collective-permute-start.2 = (bf16[16,18,8,128]{3,2,1,0:T(8,128)(2,1)S(1)}, bf16[16,18,8,128]{3,2,1,0:T(8,128)(2,1)S(1)}, u32[]{:S(2)}, u32[]{:S(2)}) collective-permute-start(bf16[16,18,8,128]{3,2,1,0:T(8,128)(2,1)S(1)} %get-tuple-element.42.refs_0_), channel_id=1, source_target_pairs={{0,16},{4,20},{8,24},{12,28},{16,0},{20,4},{24,8},{28,12},{1,17},{... | collective-permute-start | bytes 1769480 | tf_op jit(solution)/shard_map/ppermute | solution.py:627
  7.7 0.7 copy-start.1
  17.8 20.7 %collective-permute-start.3 = (bf16[8,18,8,128]{3,2,1,0:T(8,128)(2,1)S(1)}, bf16[8,18,8,128]{3,2,1,0:T(8,128)(2,1)S(1)}, u32[]{:S(2)}, u32[]{:S(2)}) collective-permute-start(bf16[8,18,8,128]{3,2,1,0:T(8,128)(2,1)S(1)} %get-tuple-element.47), channel_id=1, source_target_pairs={{0,4},{4,8},{8,12},{12,0},{16,20},{20,24},{24,28},{28,16},{1,5},{5... | collective-permute-start | bytes 884744 | tf_op jit(solution)/shard_map/ppermute | solution.py:631
  19.0 21.3 %collective-permute-start.4 = (bf16[8,18,8,128]{3,2,1,0:T(8,128)(2,1)S(1)}, bf16[8,18,8,128]{3,2,1,0:T(8,128)(2,1)S(1)}, u32[]{:S(2)}, u32[]{:S(2)}) collective-permute-start(bf16[8,18,8,128]{3,2,1,0:T(8,128)(2,1)S(1)} %get-tuple-element.48), channel_id=1, source_target_pairs={{0,8},{4,12},{8,0},{12,4},{16,24},{20,28},{24,16},{28,20},{1,9},{5... | collective-permute-start | bytes 884744 | tf_op jit(solution)/shard_map/ppermute | solution.py:631
  20.4 23.9 %collective-permute-start.5 = (bf16[8,18,8,128]{3,2,1,0:T(8,128)(2,1)}, bf16[8,18,8,128]{3,2,1,0:T(8,128)(2,1)S(1)}, u32[]{:S(2)}, u32[]{:S(2)}) collective-permute-start(bf16[8,18,8,128]{3,2,1,0:T(8,128)(2,1)} %get-tuple-element.49), channel_id=1, source_target_pairs={{0,12},{4,0},{8,4},{12,8},{16,28},{20,16},{24,20},{28,24},{1,13},{... | collective-permute-start | bytes 884744 | tf_op jit(solution)/shard_map/ppermute | solution.py:631
  33.5 22.0 %collective-permute-start.6 = (bf16[8,18,8,128]{3,2,1,0:T(8,128)(2,1)}, bf16[8,18,8,128]{3,2,1,0:T(8,128)(2,1)S(1)}, u32[]{:S(2)}, u32[]{:S(2)}) collective-permute-start(bf16[8,18,8,128]{3,2,1,0:T(8,128)(2,1)} %get-tuple-element.50), channel_id=1, source_target_pairs={{0,4},{4,8},{8,12},{12,0},{16,20},{20,24},{24,28},{28,16},{1,5},{5... | collective-permute-start | bytes 884744 | tf_op jit(solution)/shard_map/ppermute | solution.py:631
  34.5 26.1 %collective-permute-start.7 = (bf16[8,18,8,128]{3,2,1,0:T(8,128)(2,1)}, bf16[8,18,8,128]{3,2,1,0:T(8,128)(2,1)}, u32[]{:S(2)}, u32[]{:S(2)}) collective-permute-start(bf16[8,18,8,128]{3,2,1,0:T(8,128)(2,1)} %get-tuple-element.51), channel_id=1, source_target_pairs={{0,8},{4,12},{8,0},{12,4},{16,24},{20,28},{24,16},{28,20},{1,9},{5... | collective-permute-start | bytes 884744 | tf_op jit(solution)/shard_map/ppermute | solution.py:631
  38.5 22.1 %collective-permute-start.8 = (bf16[8,18,8,128]{3,2,1,0:T(8,128)(2,1)}, bf16[8,18,8,128]{3,2,1,0:T(8,128)(2,1)}, u32[]{:S(2)}, u32[]{:S(2)}) collective-permute-start(bf16[8,18,8,128]{3,2,1,0:T(8,128)(2,1)} %get-tuple-element.52), channel_id=1, source_target_pairs={{0,12},{4,0},{8,4},{12,8},{16,28},{20,16},{24,20},{28,24},{1,13},{... | collective-permute-start | bytes 884744 | tf_op jit(solution)/shard_map/ppermute | solution.py:631
  40.3 44.3 %collective-permute-start.11 = (bf16[16,14,8,128]{3,2,1,0:T(8,128)(2,1)S(1)}, bf16[16,14,8,128]{3,2,1,0:T(8,128)(2,1)S(1)}, u32[]{:S(2)}, u32[]{:S(2)}) collective-permute-start(bf16[16,14,8,128]{3,2,1,0:T(8,128)(2,1)S(1)} %get-tuple-element.61.refs_0_), channel_id=1, source_target_pairs={{0,16},{4,20},{8,24},{12,28},{16,0},{20,4},{24,8},{28,12},{1,17},{... | collective-permute-start | bytes 1376264 | tf_op jit(solution)/shard_map/ppermute | solution.py:627
  44.3 51.6 %collective-permute-start.1 = (bf16[8,1,64,128]{3,2,1,0:T(8,128)(2,1)}, bf16[8,1,64,128]{3,2,1,0:T(8,128)(2,1)}, u32[]{:S(2)}, u32[]{:S(2)}) collective-permute-start(bf16[8,1,64,128]{3,2,1,0:T(8,128)(2,1)} %get-tuple-element.69), channel_id=1, source_target_pairs={{1,0},{2,1},{3,2},{5,4},{6,5},{7,6},{9,8},{10,9},{11,10},{13,12},{... | collective-permute-start | bytes 393224 | tf_op jit(solution)/shard_map/ppermute | solution.py:597
  55.4 40.5 %collective-permute-start = (bf16[8,1,64,128]{3,2,1,0:T(8,128)(2,1)}, bf16[8,1,64,128]{3,2,1,0:T(8,128)(2,1)}, u32[]{:S(2)}, u32[]{:S(2)}) collective-permute-start(bf16[8,1,64,128]{3,2,1,0:T(8,128)(2,1)} %get-tuple-element.70), channel_id=1, source_target_pairs={{0,1},{1,2},{2,3},{4,5},{5,6},{6,7},{8,9},{9,10},{10,11},{12,13},{... | collective-permute-start | bytes 393224 | tf_op jit(solution)/shard_map/ppermute | solution.py:596
  60.6 17.2 %copy-start.9 = (f32[8]{0:T(128)S(1)}, f32[8]{0:T(128)}, u32[]{:S(2)}) copy-start(f32[8]{0:T(128)} %param.28) | copy-start | bytes 100
  71.4 0.8 copy-start.4
  72.2 11.1 %collective-permute-start.9 = (bf16[288,128]{1,0:T(8,128)(2,1)}, bf16[288,128]{1,0:T(8,128)(2,1)S(1)}, u32[]{:S(2)}, u32[]{:S(2)}) collective-permute-start(bf16[288,128]{1,0:T(8,128)(2,1)} %get-tuple-element.55), channel_id=1, source_target_pairs={{0,1},{1,2},{2,3},{4,5},{5,6},{6,7},{8,9},{9,10},{10,11},{12,13},{... | collective-permute-start | bytes 221192 | tf_op jit(solution)/shard_map/ppermute | solution.py:596
  75.9 8.1 %collective-permute-start.10 = (bf16[288,128]{1,0:T(8,128)(2,1)S(1)}, bf16[288,128]{1,0:T(8,128)(2,1)S(1)}, u32[]{:S(2)}, u32[]{:S(2)}) collective-permute-start(bf16[288,128]{1,0:T(8,128)(2,1)S(1)} %get-tuple-element.56), channel_id=1, source_target_pairs={{1,0},{2,1},{3,2},{5,4},{6,5},{7,6},{9,8},{10,9},{11,10},{13,12},{... | collective-permute-start | bytes 221192 | tf_op jit(solution)/shard_map/ppermute | solution.py:597
  87.3 22.2 %collective-permute-start.12 = (bf16[16,14,8,128]{3,2,1,0:T(8,128)(2,1)}, bf16[16,14,8,128]{3,2,1,0:T(8,128)(2,1)S(1)}, u32[]{:S(2)}, u32[]{:S(2)}) collective-permute-start(bf16[16,14,8,128]{3,2,1,0:T(8,128)(2,1)} %get-tuple-element.62), channel_id=1, source_target_pairs={{0,4},{4,8},{8,12},{12,0},{16,20},{20,24},{24,28},{28,16},{1,5},{5... | collective-permute-start | bytes 1376264 | tf_op jit(solution)/shard_map/ppermute | solution.py:631
  94.6 14.9 %collective-permute-start.13 = (bf16[16,14,8,128]{3,2,1,0:T(8,128)(2,1)S(1)}, bf16[16,14,8,128]{3,2,1,0:T(8,128)(2,1)S(1)}, u32[]{:S(2)}, u32[]{:S(2)}) collective-permute-start(bf16[16,14,8,128]{3,2,1,0:T(8,128)(2,1)S(1)} %get-tuple-element.63), channel_id=1, source_target_pairs={{0,8},{4,12},{8,0},{12,4},{16,24},{20,28},{24,16},{28,20},{1,9},{5... | collective-permute-start | bytes 1376264 | tf_op jit(solution)/shard_map/ppermute | solution.py:631
  94.6 18.9 %collective-permute-start.14 = (bf16[16,14,8,128]{3,2,1,0:T(8,128)(2,1)S(1)}, bf16[16,14,8,128]{3,2,1,0:T(8,128)(2,1)S(1)}, u32[]{:S(2)}, u32[]{:S(2)}) collective-permute-start(bf16[16,14,8,128]{3,2,1,0:T(8,128)(2,1)S(1)} %get-tuple-element.64), channel_id=1, source_target_pairs={{0,12},{4,0},{8,4},{12,8},{16,28},{20,16},{24,20},{28,24},{1,13},{... | collective-permute-start | bytes 1376264 | tf_op jit(solution)/shard_map/ppermute | solution.py:631
  122.0 0.8 copy-start.5
  122.7 5.7 %collective-permute-start.15 = (bf16[224,128]{1,0:T(8,128)(2,1)S(1)}, bf16[224,128]{1,0:T(8,128)(2,1)S(1)}, u32[]{:S(2)}, u32[]{:S(2)}) collective-permute-start(bf16[224,128]{1,0:T(8,128)(2,1)S(1)} %get-tuple-element.66), channel_id=1, source_target_pairs={{0,1},{1,2},{2,3},{4,5},{5,6},{6,7},{8,9},{9,10},{10,11},{12,13},{... | collective-permute-start | bytes 172040 | tf_op jit(solution)/shard_map/ppermute | solution.py:596
  126.3 5.5 %collective-permute-start.16 = (bf16[224,128]{1,0:T(8,128)(2,1)S(1)}, bf16[224,128]{1,0:T(8,128)(2,1)S(1)}, u32[]{:S(2)}, u32[]{:S(2)}) collective-permute-start(bf16[224,128]{1,0:T(8,128)(2,1)S(1)} %get-tuple-element.67), channel_id=1, source_target_pairs={{1,0},{2,1},{3,2},{5,4},{6,5},{7,6},{9,8},{10,9},{11,10},{13,12},{... | collective-permute-start | bytes 172040 | tf_op jit(solution)/shard_map/ppermute | solution.py:597

commit v7 on v6

--- a/solution.py
+++ b/solution.py
@@ -17,6 +17,7 @@
 unit_eps = 1e-06
 LOG2E = math.log2(math.e)
 VMEM_BYTES = 24 * 2**20
+COST = pl.CostEstimate(flops=0, bytes_accessed=2**16, transcendentals=0)
 WINDOW_VMEM_BYTES = 60 * 2**20
 PHASES = 2
 
@@ -78,7 +79,7 @@
         out_specs=[block(n) for n in blocks],
         scratch_shapes=[pltpu.VMEM((rows * cols, channels), jnp.float32)],
         compiler_params=pltpu.CompilerParams(vmem_limit_bytes=VMEM_BYTES),
-        cost_estimate=pl.CostEstimate(flops=0, bytes_accessed=10 * maps.size, transcendentals=0),
+        cost_estimate=COST,
     )(maps)
 
 
@@ -189,7 +190,7 @@
         out_specs=[smem] * 7,
         scratch_shapes=[pltpu.SMEM((devices,), jnp.int32)],
         compiler_params=pltpu.CompilerParams(vmem_limit_bytes=VMEM_BYTES),
-        cost_estimate=pl.CostEstimate(flops=0, bytes_accessed=20 * 2**20, transcendentals=0),
+        cost_estimate=COST,
     )(senders, shifts, counts, ids)
 
 
@@ -228,9 +229,7 @@
             scratch_shapes=[pltpu.SemaphoreType.DMA((count, shape[0]))],
         ),
         compiler_params=pltpu.CompilerParams(vmem_limit_bytes=VMEM_BYTES),
-        cost_estimate=pl.CostEstimate(
-            flops=0, bytes_accessed=4 * count * math.prod(shape), transcendentals=0
-        ),
+        cost_estimate=COST,
     )(chosen, filled, *sources.values())
 
 
@@ -311,20 +310,29 @@
         mix = functools.reduce(jnp.add, [by_head(v, w * inverse) for w, v in zip(weights, values)])
         joined[span, :] = dot(mix.astype(jnp.bfloat16), wout[...], TN)
     out[...] = joined[...].astype(jnp.bfloat16)
-    rows = total // top_row.shape[0]
-    top_row[...] = joined[pl.ds(0, total // rows, stride=rows), :].astype(jnp.bfloat16)
-    low_row[...] = joined[pl.ds(rows - 1, total // rows, stride=rows), :].astype(jnp.bfloat16)
-
-
-def join_agents(pieces, arrived, origins, tile_cols, plan, live, wq, wkv, wout, scale):
+    edge = top_row.shape[1]
+    rows = total // (vehicles * edge)
+    for v in range(vehicles):
+        start = v * edge * rows
+        top_row[v] = joined[pl.ds(start, edge, stride=rows), :].astype(jnp.bfloat16)
+        low_row[v] = joined[pl.ds(start + rows - 1, edge, stride=rows), :].astype(jnp.bfloat16)
+
+
+def join_weights(wq, wkv, wout, scale):
+    return wq.T, wkv.T, wout, scale.reshape(-1, 1)
+
+
+def present_cells(live, phase, rows):
+    return jnp.repeat(live.astype(jnp.float32), len(phase_columns(phase)) * rows, axis=1)
+
+
+def join_agents(pieces, arrived, origins, tile_cols, plan, present, weights):
     count, cols, rows, channels = pieces.shape
-    agents = live.shape[0]
+    agents = present.shape[0]
     cells = cols * rows
     total = count * cells
     whole = lambda shape: pl.BlockSpec(shape, lambda r, *_: (0,) * len(shape))
-    weights = (wq.T, wkv.T, wout, scale.reshape(-1, 1))
-    present = jnp.repeat(live.astype(jnp.float32), cells, axis=1)
-    shapes = [(n, channels) for n in (total, total // rows, total // rows)]
+    shapes = [(total, channels)] + [(count // tile_cols, tile_cols * cols, channels)] * 2
     return pl.pallas_call(
         functools.partial(join_kernel, origins, tile_cols),
         out_shape=[jax.ShapeDtypeStruct(shape, jnp.bfloat16) for shape in shapes],
@@ -345,9 +353,7 @@
             ],
         ),
         compiler_params=pltpu.CompilerParams(vmem_limit_bytes=VMEM_BYTES),
-        cost_estimate=pl.CostEstimate(
-            flops=total * channels * channels * 40, bytes_accessed=total * channels * 12, transcendentals=total * 20
-        ),
+        cost_estimate=COST,
     )(
         *plan,
         pieces.reshape(total, channels),
@@ -534,16 +540,9 @@
                     out[v, i, t, :, lanes] = line.astype(jnp.bfloat16)
 
 
-def window_layer(phase, turned, ego_edges, pieces, before, conv_weight, gain_first, window_in, window_out,
-                 window_scale, gain_second, hidden_up, hidden_down):
-    vehicles, cols, rows, channels = turned.shape
-    width = 2 * channels
-    tile_cols = cols // TILE
-    run = TILE // PHASES
-    group = 4
-    whole = lambda x: pl.BlockSpec(x.shape, lambda r: (0,) * x.ndim)
-    block = lambda *shape: pl.BlockSpec((group, *shape), lambda r: (r,) + (0,) * len(shape))
-    weights = (
+def window_weights(conv_weight, gain_first, window_in, window_out, window_scale, gain_second, hidden_up, hidden_down):
+    width = conv_weight.shape[-1]
+    return (
         conv_weight.reshape(9, width),
         gain_first[None],
         window_in[:, :width].T,
@@ -555,6 +554,16 @@
         hidden_up,
         hidden_down,
     )
+
+
+def window_layer(phase, turned, ego_edges, pieces, before, weights):
+    vehicles, cols, rows, channels = turned.shape
+    width = 2 * channels
+    tile_cols = cols // TILE
+    run = TILE // PHASES
+    group = 4
+    whole = lambda x: pl.BlockSpec(x.shape, lambda r: (0,) * x.ndim)
+    block = lambda *shape: pl.BlockSpec((group, *shape), lambda r: (r,) + (0,) * len(shape))
     pieces = [x.reshape(vehicles, -1, channels) for three in pieces for x in three]
     cells = vehicles * rows * tile_cols * run
     most = cols * rows
@@ -585,9 +594,7 @@
         ],
         input_output_aliases=aliases,
         compiler_params=pltpu.CompilerParams(vmem_limit_bytes=WINDOW_VMEM_BYTES),
-        cost_estimate=pl.CostEstimate(
-            flops=cells * width * width * 60, bytes_accessed=cells * width * 6, transcendentals=cells * width * 4
-        ),
+        cost_estimate=COST,
     )(*operands)
 
 
@@ -641,10 +648,19 @@
     live = live.reshape(senders.shape[1], -1)
     near_tiles = send(messages_for(chosen, filled, capacity, {0: first}))
     ego_edges = beside(bev_maps[:, rows - 1 :], bev_maps[:, :1])
-    far, second = lax.optimization_barrier((far, second))
+    join_all = join_weights(agent_query, agent_keyvalue, agent_out, agent_scale)
+    present = [present_cells(live, p, rows) for p in range(PHASES)]
+    window_all = window_weights(
+        conv_weight, gain_first, window_in, window_out, window_scale, gain_second, hidden_up, hidden_down
+    )
+    far, near_tiles, second, join_all, present, window_all, ego_edges = lax.optimization_barrier(
+        (far, near_tiles, second, join_all, present, window_all, ego_edges)
+    )
     far_tiles = send(messages_for(chosen, filled, capacity, {1: far}))
     later = swap(second)
-    later_tiles = send(messages_for(chosen, filled, capacity, {0: second, 1: later}))
+    later_messages = messages_for(chosen, filled, capacity, {0: second, 1: later})
+    plan, later_messages = lax.optimization_barrier((plan, later_messages))
+    later_tiles = send(later_messages)
     arrived = [[first, far, *near_tiles, *far_tiles], [second, later, *later_tiles]]
     origins = [
         [(0, 0), (1, 0)] + [(2 + k + part * (group - 1), 0) for k in range(group - 1) for part in (0, 1)],
@@ -655,24 +671,10 @@
         if phase:
             plan, result = lax.optimization_barrier((plan, result))
         joined, top, low = join_agents(
-            own, arrived[phase], origins[phase], tile_cols, plan, live, agent_query, agent_keyvalue, agent_out, agent_scale
+            own, arrived[phase], origins[phase], tile_cols, plan, present[phase], join_all
         )
         pieces.append((joined, *beside(low, top)))
-        result = window_layer(
-            phase,
-            turned,
-            ego_edges,
-            pieces,
-            result,
-            conv_weight,
-            gain_first,
-            window_in,
-            window_out,
-            window_scale,
-            gain_second,
-            hidden_up,
-            hidden_down,
-        )
+        result = window_layer(phase, turned, ego_edges, pieces, result, window_all)
     return result.reshape(vehicles_here, rows, cols, 2 * channels)
 
 

time: 149 us -> 180 us (1.21)
  waiting for transfers between devices: 27.5 us -> 56.8 us
  local copies, waits for them, and re-layouts: 18.1 us -> 29.5 us
  starting transfers between devices: 39.2 us -> 31.1 us
    ppermute x9, waiting for transfers between devices: 14.3 us -> 28.1 us  [send(): lax.ppermute(x, 'veh', [(i, i // group * group + (i + k + 1) % group) for...]
    unnamed x26 -> x68, local copies, waits for them, and re-layouts: 9.52 us -> 20.2 us
    ppermute x2, waiting for transfers between devices: 10.5 us -> 19.2 us  [swap(): lax.ppermute(x, 'veh', [(i, (i + group) % devices) for i in range(devices)])]
    ppermute x3, waiting for transfers between devices: 2.71 us -> 9.55 us  [beside(): below = lax.ppermute(first, 'row', [(i + 1, i) for i in range(count - 1)])]
    ppermute x9, starting transfers between devices: 14.5 us -> 9.53 us  [send(): lax.ppermute(x, 'veh', [(i, i // group * group + (i + k + 1) % group) for...]
    optimization_barrier x0 -> x2, local copies, waits for them, and re-layouts: none -> 2.03 us  [on_device(): lax.optimization_barrier((far, near_tiles, second, join_all, present, win...]
    reshape x9 -> x3, local copies, waits for them, and re-layouts: 4.85 us -> 2.88 us  [the longest x2 2.27 us: present_cells(): jnp.repeat(live.astype(jnp.float32), len(phase_columns(phase)) * rows, ax...]
  transfers between devices with their start and end apart: 17 -> 17, of which waited for: 6 -> 6; matrix products, arithmetic and copies ran while one was open for 9% -> 9% of each run, Pallas kernels for 26% -> 21%
where the time goes in v7:
time: 180 us; the launch traced here: 178 us
  Pallas kernels  59.7 us (33%)
  waiting for transfers between devices  56.8 us (32%)
  starting transfers between devices  31.1 us (17%)
  local copies, waits for them, and re-layouts  29.5 us (16%)
    ppermute x9, waiting for transfers between devices, send(): lax.ppermute(x, 'veh', [(i, i // group * group + (i + k + 1) % group) for...  28.1 us
    pallas_call x2, Pallas kernels, window_layer(): pl.pallas_call(functools.partial(window_kernel, phase, rows), out_shape=j...  27.3 us
    unnamed x68, local copies, waits for them, and re-layouts  20.2 us
    pallas_call x2, Pallas kernels, join_agents(): pl.pallas_call(functools.partial(join_kernel, origins, tile_cols), out_sh...  19.2 us
    ppermute x2, waiting for transfers between devices, swap(): lax.ppermute(x, 'veh', [(i, (i + group) % devices) for i in range(devices)])  19.2 us
    ppermute x3, starting transfers between devices, beside(): above = lax.ppermute(last, 'row', [(i, i + 1) for i in range(count - 1)])  11.1 us
    ppermute x3, waiting for transfers between devices, beside(): below = lax.ppermute(first, 'row', [(i + 1, i) for i in range(count - 1)])  9.55 us
    ppermute x9, starting transfers between devices, send(): lax.ppermute(x, 'veh', [(i, i // group * group + (i + k + 1) % group) for...  9.53 us
  transfers between devices with their start and end apart: 17, of which 6 were waited for; matrix products, arithmetic and copies ran while one was open for 9% of the time, Pallas kernels for 21%

profile of v7, /device:TPU:1, one launch (start us, length us, event | category | flops | bytes accessed | tf_op | source)
XLA Modules:
  0.0 178.2 jit_solution(15245079436253477644)
XLA Ops:
  0.0 1.2 copy-done.2
  1.9 1.0 copy-done
  2.9 3.1 %collective-permute-start = (bf16[16,18,8,128]{3,2,1,0:T(8,128)(2,1)S(1)}, bf16[16,18,8,128]{3,2,1,0:T(8,128)(2,1)S(1)}, u32[]{:S(2)}, u32[]{:S(2)}) collective-permute-start(bf16[16,18,8,128]{3,2,1,0:T(8,128)(2,1)S(1)} %get-tuple-element.66.refs_0_), channel_id=1, source_target_pairs={{0,16},{4,20},{8,24},{12,28},{16,0},{20,4},{24,8},{28,12},{1,17},{... | collective-permute-start | bytes 1769480 | tf_op jit(solution)/shard_map/ppermute | solution.py:634
  6.1 0.8 copy.18.senders
  6.8 0.8 copy.19.shifts
  8.3 7.3 %shard_map.155 = (s32[48]{0:T(128)S(1)}, s32[6]{0:T(128)S(1)}, s32[512]{0:T(512)S(1)}, s32[16]{0:T(128)S(1)}, s32[32]{0:T(128)S(1)}, /*index=5*/s32[64]{0:T(128)S(1)}, s32[65]{0:T(128)S(1)}) custom-call(s32[64,4]{1,0:T(8,128)S(1)} %copy.18.senders, s32[64,4]{1,0:T(8,128)S(1)} %copy.19.shifts, s32[64]{0:T(128)S(1)} %copy-done.21, s32[2]{0:T(128)S(1)} %pad_add_fusion.ids), custom_call_target="tpu_custom_call" | custom-call | bytes 65536 | tf_op jit(solution)/shard_map/pallas_call | solution.py:186
  16.2 1.5 shard_map.156
  17.7 1.4 collective-permute-start.1
  19.2 1.0 collective-permute-start.2
  20.2 1.2 collective-permute-start.3
  21.4 1.7 fusion
  23.1 4.8 %collective-permute-start.4 = (bf16[8,1,64,128]{3,2,1,0:T(8,128)(2,1)}, bf16[8,1,64,128]{3,2,1,0:T(8,128)(2,1)S(1)}, u32[]{:S(2)}, u32[]{:S(2)}) collective-permute-start(bf16[8,1,64,128]{3,2,1,0:T(8,128)(2,1)} %get-tuple-element.126), channel_id=1, source_target_pairs={{0,1},{1,2},{2,3},{4,5},{5,6},{6,7},{8,9},{9,10},{10,11},{12,13},{... | collective-permute-start | bytes 393224 | tf_op jit(solution)/shard_map/ppermute | solution.py:603
  27.9 1.8 fusion.1
  30.4 0.9 copy.21
  32.2 1.6 reshape.73.refs_8_
  35.1 1.7 copy.28
  36.8 0.8 copy.29
  37.6 1.9 %collective-permute-start.5 = (bf16[8,1,64,128]{3,2,1,0:T(8,128)(2,1)}, bf16[8,1,64,128]{3,2,1,0:T(8,128)(2,1)S(1)}, u32[]{:S(2)}, u32[]{:S(2)}) collective-permute-start(bf16[8,1,64,128]{3,2,1,0:T(8,128)(2,1)} %get-tuple-element.125), channel_id=1, source_target_pairs={{1,0},{2,1},{3,2},{5,4},{6,5},{7,6},{9,8},{10,9},{11,10},{13,12},{... | collective-permute-start | bytes 393224 | tf_op jit(solution)/shard_map/ppermute | solution.py:604
  40.0 4.0 %collective-permute-done.5.refs_2_ = bf16[8,1,64,128]{3,2,1,0:T(8,128)(2,1)S(1)} collective-permute-done((bf16[8,1,64,128]{3,2,1,0:T(8,128)(2,1)}, bf16[8,1,64,128]{3,2,1,0:T(8,128)(2,1)S(1)}, u32[]{:S(2)}, u32[]{:S(2)}) %collective-permute-start.5) | collective-permute-done | bytes 131104 | tf_op jit(solution)/shard_map/ppermute | solution.py:604
  45.6 1.7 shard_map.158
  47.3 0.8 collective-permute-start.7
  48.2 19.2 %collective-permute-done.6.refs_1_ = bf16[16,14,8,128]{3,2,1,0:T(8,128)(2,1)S(1)} collective-permute-done((bf16[16,14,8,128]{3,2,1,0:T(8,128)(2,1)S(1)}, bf16[16,14,8,128]{3,2,1,0:T(8,128)(2,1)S(1)}, u32[]{:S(2)}, u32[]{:S(2)}) %collective-permute-start.6) | collective-permute-done | bytes 458784 | tf_op jit(solution)/shard_map/ppermute | solution.py:634
  67.4 1.9 %shard_map.157 = (bf16[16,14,8,128]{3,2,1,0:T(8,128)(2,1)}, bf16[16,14,8,128]{3,2,1,0:T(8,128)(2,1)}, bf16[16,14,8,128]{3,2,1,0:T(8,128)(2,1)}) custom-call(s32[48]{0:T(128)S(1)} %get-tuple-element.67.chosen, s32[6]{0:T(128)S(1)} %get-tuple-element.68.filled, bf16[16,14,8,128]{3,2,1,0:T(8,128)(2,1)S(1)} %get-tuple-element.80.refs_0_, ...), custom_call_target="tpu_custom_call" | custom-call | bytes 65536 | tf_op jit(solution)/shard_map/pallas_call | solution.py:221
  69.3 2.3 %collective-permute-start.12 = (bf16[16,14,8,128]{3,2,1,0:T(8,128)(2,1)}, bf16[16,14,8,128]{3,2,1,0:T(8,128)(2,1)S(1)}, u32[]{:S(2)}, u32[]{:S(2)}) collective-permute-start(bf16[16,14,8,128]{3,2,1,0:T(8,128)(2,1)} %get-tuple-element.117), channel_id=1, source_target_pairs={{0,4},{4,8},{8,12},{12,0},{16,20},{20,24},{24,28},{28,16},{1,5},{5... | collective-permute-start | bytes 1376264 | tf_op jit(solution)/shard_map/ppermute | solution.py:638
  71.6 1.3 collective-permute-start.14
  73.9 1.1 collective-permute-start.9
  75.7 23.6 %collective-permute-done.8 = bf16[8,18,8,128]{3,2,1,0:T(8,128)(2,1)} collective-permute-done((bf16[8,18,8,128]{3,2,1,0:T(8,128)(2,1)}, bf16[8,18,8,128]{3,2,1,0:T(8,128)(2,1)}, u32[]{:S(2)}, u32[]{:S(2)}) %collective-permute-start.8) | collective-permute-done | bytes 294944 | tf_op jit(solution)/shard_map/ppermute | solution.py:638
  99.3 4.4 %collective-permute-done.9 = bf16[8,18,8,128]{3,2,1,0:T(8,128)(2,1)} collective-permute-done((bf16[8,18,8,128]{3,2,1,0:T(8,128)(2,1)}, bf16[8,18,8,128]{3,2,1,0:T(8,128)(2,1)}, u32[]{:S(2)}, u32[]{:S(2)}) %collective-permute-start.9) | collective-permute-done | bytes 294944 | tf_op jit(solution)/shard_map/ppermute | solution.py:638
  103.8 0.8 copy-done.4
  104.5 1.0 copy-done.7
  105.5 1.0 copy-done.9
  106.5 1.0 copy-done.11
  107.4 1.0 copy-done.13
  108.4 0.8 copy-done.14
  109.2 0.8 copy-done.15
  110.6 10.6 %shard_map.159 = (bf16[2304,128]{1,0:T(8,128)(2,1)S(1)}, bf16[8,36,128]{2,1,0:T(8,128)(2,1)}, bf16[8,36,128]{2,1,0:T(8,128)(2,1)}) custom-call(s32[512]{0:T(512)S(1)} %get-tuple-element.113.entries, s32[16]{0:T(128)S(1)} %get-tuple-element.114.listed, s32[32]{0:T(128)S(1)} %get-tuple-element.115.sizes_of, s32[65]{0:T(128)S(1)} %copy-done.19, ...), custom_call_target="tpu_custom_call" | custom-call | bytes 65536 | tf_op jit(solution)/shard_map/pallas_call | solution.py:336
  121.2 0.8 copy-done.1
  122.0 4.4 %collective-permute-start.10 = (bf16[8,36,128]{2,1,0:T(8,128)(2,1)}, bf16[8,36,128]{2,1,0:T(8,128)(2,1)S(1)}, u32[]{:S(2)}, u32[]{:S(2)}) collective-permute-start(bf16[8,36,128]{2,1,0:T(8,128)(2,1)} %get-tuple-element.101), channel_id=1, source_target_pairs={{0,1},{1,2},{2,3},{4,5},{5,6},{6,7},{8,9},{9,10},{10,11},{12,13},{... | collective-permute-start | bytes 221192 | tf_op jit(solution)/shard_map/ppermute | solution.py:603
  126.3 2.1 %collective-permute-start.11 = (bf16[8,36,128]{2,1,0:T(8,128)(2,1)}, bf16[8,36,128]{2,1,0:T(8,128)(2,1)S(1)}, u32[]{:S(2)}, u32[]{:S(2)}) collective-permute-start(bf16[8,36,128]{2,1,0:T(8,128)(2,1)} %get-tuple-element.102), channel_id=1, source_target_pairs={{1,0},{2,1},{3,2},{5,4},{6,5},{7,6},{9,8},{10,9},{11,10},{13,12},{... | collective-permute-start | bytes 221192 | tf_op jit(solution)/shard_map/ppermute | solution.py:604
  128.4 1.3 copy.25.refs_12_.refs_15_
  129.7 2.6 %collective-permute-done.11.refs_5_ = bf16[8,36,128]{2,1,0:T(8,128)(2,1)S(1)} collective-permute-done((bf16[8,36,128]{2,1,0:T(8,128)(2,1)}, bf16[8,36,128]{2,1,0:T(8,128)(2,1)S(1)}, u32[]{:S(2)}, u32[]{:S(2)}) %collective-permute-start.11) | collective-permute-done | bytes 73760 | tf_op jit(solution)/shard_map/ppermute | solution.py:604
  132.9 13.6 %shard_map.160.refs_19_ = bf16[8,8,2,2,16,256]{5,4,3,2,1,0:T(8,128)(2,1)} custom-call(bf16[8,64,8,128]{3,2,1,0:T(8,128)(2,1)} %copy-done, bf16[8,1,64,128]{3,2,1,0:T(8,128)(2,1)} %copy-done.22, bf16[8,1,64,128]{3,2,1,0:T(8,128)(2,1)} %copy-done.23, bf16[8,288,128]{2,1,0:T(8,128)(2,1)} %bitcast.33, bf16[8,36,128]{2,1,0:T(8,128)(2,1)} %copy-done.24, ...), custom_call_target="tpu_custom_call" | custom-call | bytes 65536 | tf_op jit(solution)/shard_map/pallas_call | solution.py:582
  146.6 8.7 %shard_map.161 = (bf16[1792,128]{1,0:T(8,128)(2,1)S(1)}, bf16[8,28,128]{2,1,0:T(8,128)(2,1)S(1)}, bf16[8,28,128]{2,1,0:T(8,128)(2,1)S(1)}) custom-call(s32[512]{0:T(512)S(1)} %get-tuple-element.113.entries, s32[16]{0:T(128)S(1)} %get-tuple-element.114.listed, s32[32]{0:T(128)S(1)} %get-tuple-element.115.sizes_of, s32[65]{0:T(128)S(1)} %copy-done.20, ...), custom_call_target="tpu_custom_call" | custom-call | bytes 65536 | tf_op jit(solution)/shard_map/pallas_call | solution.py:336
  155.3 0.8 copy-done.3
  156.1 1.9 %collective-permute-start.15 = (bf16[8,28,128]{2,1,0:T(8,128)(2,1)S(1)}, bf16[8,28,128]{2,1,0:T(8,128)(2,1)S(1)}, u32[]{:S(2)}, u32[]{:S(2)}) collective-permute-start(bf16[8,28,128]{2,1,0:T(8,128)(2,1)S(1)} %get-tuple-element.122), channel_id=1, source_target_pairs={{0,1},{1,2},{2,3},{4,5},{5,6},{6,7},{8,9},{9,10},{10,11},{12,13},{... | collective-permute-start | bytes 172040 | tf_op jit(solution)/shard_map/ppermute | solution.py:603
  158.0 2.6 %collective-permute-start.16 = (bf16[8,28,128]{2,1,0:T(8,128)(2,1)S(1)}, bf16[8,28,128]{2,1,0:T(8,128)(2,1)S(1)}, u32[]{:S(2)}, u32[]{:S(2)}) collective-permute-start(bf16[8,28,128]{2,1,0:T(8,128)(2,1)S(1)} %get-tuple-element.123), channel_id=1, source_target_pairs={{1,0},{2,1},{3,2},{5,4},{6,5},{7,6},{9,8},{10,9},{11,10},{13,12},{... | collective-permute-start | bytes 172040 | tf_op jit(solution)/shard_map/ppermute | solution.py:604
  160.7 3.0 %collective-permute-done.16.refs_8_ = bf16[8,28,128]{2,1,0:T(8,128)(2,1)S(1)} collective-permute-done((bf16[8,28,128]{2,1,0:T(8,128)(2,1)S(1)}, bf16[8,28,128]{2,1,0:T(8,128)(2,1)S(1)}, u32[]{:S(2)}, u32[]{:S(2)}) %collective-permute-start.16) | collective-permute-done | bytes 57376 | tf_op jit(solution)/shard_map/ppermute | solution.py:604
  164.3 13.7 %shard_map.162 = bf16[8,8,2,2,16,256]{5,4,3,2,1,0:T(8,128)(2,1)} custom-call(bf16[8,64,8,128]{3,2,1,0:T(8,128)(2,1)} %copy-done, bf16[8,1,64,128]{3,2,1,0:T(8,128)(2,1)} %copy-done.22, bf16[8,1,64,128]{3,2,1,0:T(8,128)(2,1)} %copy-done.23, bf16[8,288,128]{2,1,0:T(8,128)(2,1)} %bitcast.34, ...), custom_call_target="tpu_custom_call", output_to_operand_aliasing={{}: (19, {})} | custom-call | bytes 65536 | tf_op jit(solution)/shard_map/pallas_call | solution.py:582
  (76 shorter events, 10.6 us)
Async XLA Ops:
  0.0 1.2 copy-start.2
  1.2 28.5 %copy-start.28 = (bf16[128,128]{1,0:T(8,128)(2,1)S(1)}, bf16[128,128]{1,0:T(8,128)(2,1)}, u32[]{:S(2)}) copy-start(bf16[128,128]{1,0:T(8,128)(2,1)} %param.20) | copy-start | bytes 98308
  1.2 33.3 %copy-start.29 = (f32[3,3,256]{2,1,0:T(4,128)S(1)}, f32[3,3,256]{2,1,0:T(4,128)}, u32[]{:S(2)}) copy-start(f32[3,3,256]{2,1,0:T(4,128)} %param.24) | copy-start | bytes 27652
  1.2 38.3 %copy-start.30 = (f32[8]{0:T(128)S(1)}, f32[8]{0:T(128)}, u32[]{:S(2)}) copy-start(f32[8]{0:T(128)} %param.28) | copy-start | bytes 100
  1.9 1.0 copy-start
  2.9 41.9 %collective-permute-start = (bf16[16,18,8,128]{3,2,1,0:T(8,128)(2,1)S(1)}, bf16[16,18,8,128]{3,2,1,0:T(8,128)(2,1)S(1)}, u32[]{:S(2)}, u32[]{:S(2)}) collective-permute-start(bf16[16,18,8,128]{3,2,1,0:T(8,128)(2,1)S(1)} %get-tuple-element.66.refs_0_), channel_id=1, source_target_pairs={{0,16},{4,20},{8,24},{12,28},{16,0},{20,4},{24,8},{28,12},{1,17},{... | collective-permute-start | bytes 1769480 | tf_op jit(solution)/shard_map/ppermute | solution.py:634
  7.7 0.7 copy-start.21
  15.6 0.6 copy-start.18
  17.7 26.4 %collective-permute-start.1 = (bf16[8,18,8,128]{3,2,1,0:T(8,128)(2,1)}, bf16[8,18,8,128]{3,2,1,0:T(8,128)(2,1)S(1)}, u32[]{:S(2)}, u32[]{:S(2)}) collective-permute-start(bf16[8,18,8,128]{3,2,1,0:T(8,128)(2,1)} %get-tuple-element.69), channel_id=1, source_target_pairs={{0,4},{4,8},{8,12},{12,0},{16,20},{20,24},{24,28},{28,16},{1,5},{5... | collective-permute-start | bytes 884744 | tf_op jit(solution)/shard_map/ppermute | solution.py:638
  19.2 25.7 %collective-permute-start.2 = (bf16[8,18,8,128]{3,2,1,0:T(8,128)(2,1)S(1)}, bf16[8,18,8,128]{3,2,1,0:T(8,128)(2,1)S(1)}, u32[]{:S(2)}, u32[]{:S(2)}) collective-permute-start(bf16[8,18,8,128]{3,2,1,0:T(8,128)(2,1)S(1)} %get-tuple-element.70), channel_id=1, source_target_pairs={{0,8},{4,12},{8,0},{12,4},{16,24},{20,28},{24,16},{28,20},{1,9},{5... | collective-permute-start | bytes 884744 | tf_op jit(solution)/shard_map/ppermute | solution.py:638
  20.2 24.6 %collective-permute-start.3 = (bf16[8,18,8,128]{3,2,1,0:T(8,128)(2,1)S(1)}, bf16[8,18,8,128]{3,2,1,0:T(8,128)(2,1)S(1)}, u32[]{:S(2)}, u32[]{:S(2)}) collective-permute-start(bf16[8,18,8,128]{3,2,1,0:T(8,128)(2,1)S(1)} %get-tuple-element.71), channel_id=1, source_target_pairs={{0,12},{4,0},{8,4},{12,8},{16,28},{20,16},{24,20},{28,24},{1,13},{... | collective-permute-start | bytes 884744 | tf_op jit(solution)/shard_map/ppermute | solution.py:638
  23.1 14.4 %collective-permute-start.4 = (bf16[8,1,64,128]{3,2,1,0:T(8,128)(2,1)}, bf16[8,1,64,128]{3,2,1,0:T(8,128)(2,1)S(1)}, u32[]{:S(2)}, u32[]{:S(2)}) collective-permute-start(bf16[8,1,64,128]{3,2,1,0:T(8,128)(2,1)} %get-tuple-element.126), channel_id=1, source_target_pairs={{0,1},{1,2},{2,3},{4,5},{5,6},{6,7},{8,9},{9,10},{10,11},{12,13},{... | collective-permute-start | bytes 393224 | tf_op jit(solution)/shard_map/ppermute | solution.py:603
  37.6 7.3 %copy-start.22 = (bf16[8,1,64,128]{3,2,1,0:T(8,128)(2,1)}, bf16[8,1,64,128]{3,2,1,0:T(8,128)(2,1)S(1)}, u32[]{:S(2)}) copy-start(bf16[8,1,64,128]{3,2,1,0:T(8,128)(2,1)S(1)} %collective-permute-done.4.refs_1_) | copy-start | bytes 393220
  37.6 6.5 %collective-permute-start.5 = (bf16[8,1,64,128]{3,2,1,0:T(8,128)(2,1)}, bf16[8,1,64,128]{3,2,1,0:T(8,128)(2,1)S(1)}, u32[]{:S(2)}, u32[]{:S(2)}) collective-permute-start(bf16[8,1,64,128]{3,2,1,0:T(8,128)(2,1)} %get-tuple-element.125), channel_id=1, source_target_pairs={{1,0},{2,1},{3,2},{5,4},{6,5},{7,6},{9,8},{10,9},{11,10},{13,12},{... | collective-permute-start | bytes 393224 | tf_op jit(solution)/shard_map/ppermute | solution.py:604
  44.1 27.6 %copy-start.23 = (bf16[8,1,64,128]{3,2,1,0:T(8,128)(2,1)}, bf16[8,1,64,128]{3,2,1,0:T(8,128)(2,1)S(1)}, u32[]{:S(2)}) copy-start(bf16[8,1,64,128]{3,2,1,0:T(8,128)(2,1)S(1)} %collective-permute-done.5.refs_2_) | copy-start | bytes 393220
  44.1 0.8 copy-start.6
  44.8 24.5 %copy-start.8 = (bf16[8,18,8,128]{3,2,1,0:T(8,128)(2,1)}, bf16[8,18,8,128]{3,2,1,0:T(8,128)(2,1)S(1)}, u32[]{:S(2)}) copy-start(bf16[8,18,8,128]{3,2,1,0:T(8,128)(2,1)S(1)} %collective-permute-done.2) | copy-start | bytes 884740
  44.8 24.5 %copy-start.10 = (bf16[8,18,8,128]{3,2,1,0:T(8,128)(2,1)}, bf16[8,18,8,128]{3,2,1,0:T(8,128)(2,1)S(1)}, u32[]{:S(2)}) copy-start(bf16[8,18,8,128]{3,2,1,0:T(8,128)(2,1)S(1)} %collective-permute-done.3) | copy-start | bytes 884740
  44.9 22.5 %collective-permute-start.6 = (bf16[16,14,8,128]{3,2,1,0:T(8,128)(2,1)S(1)}, bf16[16,14,8,128]{3,2,1,0:T(8,128)(2,1)S(1)}, u32[]{:S(2)}, u32[]{:S(2)}) collective-permute-start(bf16[16,14,8,128]{3,2,1,0:T(8,128)(2,1)S(1)} %get-tuple-element.80.refs_0_), channel_id=1, source_target_pairs={{0,16},{4,20},{8,24},{12,28},{16,0},{20,4},{24,8},{28,12},{1,17},{... | collective-permute-start | bytes 1376264 | tf_op jit(solution)/shard_map/ppermute | solution.py:634
  47.3 25.9 %collective-permute-start.7 = (bf16[8,18,8,128]{3,2,1,0:T(8,128)(2,1)S(1)}, bf16[8,18,8,128]{3,2,1,0:T(8,128)(2,1)S(1)}, u32[]{:S(2)}, u32[]{:S(2)}) collective-permute-start(bf16[8,18,8,128]{3,2,1,0:T(8,128)(2,1)S(1)} %get-tuple-element.92), channel_id=1, source_target_pairs={{0,4},{4,8},{8,12},{12,0},{16,20},{20,24},{24,28},{28,16},{1,5},{5... | collective-permute-start | bytes 884744 | tf_op jit(solution)/shard_map/ppermute | solution.py:638
  69.3 77.3 %collective-permute-start.12 = (bf16[16,14,8,128]{3,2,1,0:T(8,128)(2,1)}, bf16[16,14,8,128]{3,2,1,0:T(8,128)(2,1)S(1)}, u32[]{:S(2)}, u32[]{:S(2)}) collective-permute-start(bf16[16,14,8,128]{3,2,1,0:T(8,128)(2,1)} %get-tuple-element.117), channel_id=1, source_target_pairs={{0,4},{4,8},{8,12},{12,0},{16,20},{20,24},{24,28},{28,16},{1,5},{5... | collective-permute-start | bytes 1376264 | tf_op jit(solution)/shard_map/ppermute | solution.py:638
  71.6 75.0 %collective-permute-start.13 = (bf16[16,14,8,128]{3,2,1,0:T(8,128)(2,1)}, bf16[16,14,8,128]{3,2,1,0:T(8,128)(2,1)S(1)}, u32[]{:S(2)}, u32[]{:S(2)}) collective-permute-start(bf16[16,14,8,128]{3,2,1,0:T(8,128)(2,1)} %get-tuple-element.118), channel_id=1, source_target_pairs={{0,8},{4,12},{8,0},{12,4},{16,24},{20,28},{24,16},{28,20},{1,9},{5... | collective-permute-start | bytes 1376264 | tf_op jit(solution)/shard_map/ppermute | solution.py:638
  71.6 75.0 %collective-permute-start.14 = (bf16[16,14,8,128]{3,2,1,0:T(8,128)(2,1)}, bf16[16,14,8,128]{3,2,1,0:T(8,128)(2,1)S(1)}, u32[]{:S(2)}, u32[]{:S(2)}) collective-permute-start(bf16[16,14,8,128]{3,2,1,0:T(8,128)(2,1)} %get-tuple-element.119), channel_id=1, source_target_pairs={{0,12},{4,0},{8,4},{12,8},{16,28},{20,16},{24,20},{28,24},{1,13},{... | collective-permute-start | bytes 1376264 | tf_op jit(solution)/shard_map/ppermute | solution.py:638
  72.9 26.5 %collective-permute-start.8 = (bf16[8,18,8,128]{3,2,1,0:T(8,128)(2,1)}, bf16[8,18,8,128]{3,2,1,0:T(8,128)(2,1)}, u32[]{:S(2)}, u32[]{:S(2)}) collective-permute-start(bf16[8,18,8,128]{3,2,1,0:T(8,128)(2,1)} %get-tuple-element.93), channel_id=1, source_target_pairs={{0,8},{4,12},{8,0},{12,4},{16,24},{20,28},{24,16},{28,20},{1,9},{5... | collective-permute-start | bytes 884744 | tf_op jit(solution)/shard_map/ppermute | solution.py:638
  73.2 0.7 copy-start.12
  73.9 29.9 %collective-permute-start.9 = (bf16[8,18,8,128]{3,2,1,0:T(8,128)(2,1)}, bf16[8,18,8,128]{3,2,1,0:T(8,128)(2,1)}, u32[]{:S(2)}, u32[]{:S(2)}) collective-permute-start(bf16[8,18,8,128]{3,2,1,0:T(8,128)(2,1)} %get-tuple-element.94), channel_id=1, source_target_pairs={{0,12},{4,0},{8,4},{12,8},{16,28},{20,16},{24,20},{28,24},{1,13},{... | collective-permute-start | bytes 884744 | tf_op jit(solution)/shard_map/ppermute | solution.py:638
  103.8 0.8 copy-start.4
  104.5 1.0 copy-start.7
  105.5 1.0 copy-start.9
  106.5 1.0 copy-start.11
  107.4 1.0 copy-start.13
  108.4 0.8 copy-start.14
  109.2 0.8 copy-start.15
  109.9 0.7 copy-start.19
  121.2 0.8 copy-start.1
  122.0 7.8 %collective-permute-start.10 = (bf16[8,36,128]{2,1,0:T(8,128)(2,1)}, bf16[8,36,128]{2,1,0:T(8,128)(2,1)S(1)}, u32[]{:S(2)}, u32[]{:S(2)}) collective-permute-start(bf16[8,36,128]{2,1,0:T(8,128)(2,1)} %get-tuple-element.101), channel_id=1, source_target_pairs={{0,1},{1,2},{2,3},{4,5},{5,6},{6,7},{8,9},{9,10},{10,11},{12,13},{... | collective-permute-start | bytes 221192 | tf_op jit(solution)/shard_map/ppermute | solution.py:603
  126.3 6.0 %collective-permute-start.11 = (bf16[8,36,128]{2,1,0:T(8,128)(2,1)}, bf16[8,36,128]{2,1,0:T(8,128)(2,1)S(1)}, u32[]{:S(2)}, u32[]{:S(2)}) collective-permute-start(bf16[8,36,128]{2,1,0:T(8,128)(2,1)} %get-tuple-element.102), channel_id=1, source_target_pairs={{1,0},{2,1},{3,2},{5,4},{6,5},{7,6},{9,8},{10,9},{11,10},{13,12},{... | collective-permute-start | bytes 221192 | tf_op jit(solution)/shard_map/ppermute | solution.py:604
  129.7 2.6 %copy-start.24 = (bf16[8,36,128]{2,1,0:T(8,128)(2,1)}, bf16[8,36,128]{2,1,0:T(8,128)(2,1)S(1)}, u32[]{:S(2)}) copy-start(bf16[8,36,128]{2,1,0:T(8,128)(2,1)S(1)} %collective-permute-done.10.refs_4_) | copy-start | bytes 221188
  132.3 0.6 copy-start.25
  132.9 13.7 %copy-start.5 = (bf16[128,128]{0,1:T(8,128)(2,1)S(1)}, bf16[128,128]{0,1:T(8,128)(2,1)}, u32[]{:S(2)}) copy-start(bf16[128,128]{0,1:T(8,128)(2,1)} %copy.20) | copy-start | bytes 98308
  132.9 13.7 %copy-start.16 = (bf16[128,128]{1,0:T(8,128)(2,1)S(1)}, bf16[128,128]{1,0:T(8,128)(2,1)}, u32[]{:S(2)}) copy-start(bf16[128,128]{1,0:T(8,128)(2,1)} %refs_8_) | copy-start | bytes 98308
  132.9 13.7 %copy-start.17 = (f32[4,1792]{1,0:T(4,128)S(1)}, f32[4,1792]{1,0:T(4,128)}, u32[]{:S(2)}) copy-start(f32[4,1792]{1,0:T(4,128)} %reshape.74.refs_5_) | copy-start | bytes 86020
  132.9 13.7 %copy-start.20 = (s32[65]{0:T(128)S(1)}, s32[65]{0:T(128)}, u32[]{:S(2)}) copy-start(s32[65]{0:T(128)} %copy-done.18) | copy-start | bytes 784
  155.3 0.8 copy-start.3
  156.1 4.6 %collective-permute-start.15 = (bf16[8,28,128]{2,1,0:T(8,128)(2,1)S(1)}, bf16[8,28,128]{2,1,0:T(8,128)(2,1)S(1)}, u32[]{:S(2)}, u32[]{:S(2)}) collective-permute-start(bf16[8,28,128]{2,1,0:T(8,128)(2,1)S(1)} %get-tuple-element.122), channel_id=1, source_target_pairs={{0,1},{1,2},{2,3},{4,5},{5,6},{6,7},{8,9},{9,10},{10,11},{12,13},{... | collective-permute-start | bytes 172040 | tf_op jit(solution)/shard_map/ppermute | solution.py:603
  158.0 5.6 %collective-permute-start.16 = (bf16[8,28,128]{2,1,0:T(8,128)(2,1)S(1)}, bf16[8,28,128]{2,1,0:T(8,128)(2,1)S(1)}, u32[]{:S(2)}, u32[]{:S(2)}) collective-permute-start(bf16[8,28,128]{2,1,0:T(8,128)(2,1)S(1)} %get-tuple-element.123), channel_id=1, source_target_pairs={{1,0},{2,1},{3,2},{5,4},{6,5},{7,6},{9,8},{10,9},{11,10},{13,12},{... | collective-permute-start | bytes 172040 | tf_op jit(solution)/shard_map/ppermute | solution.py:604
  160.6 3.0 %copy-start.26 = (bf16[8,28,128]{2,1,0:T(8,128)(2,1)}, bf16[8,28,128]{2,1,0:T(8,128)(2,1)S(1)}, u32[]{:S(2)}) copy-start(bf16[8,28,128]{2,1,0:T(8,128)(2,1)S(1)} %collective-permute-done.15.refs_7_) | copy-start | bytes 172036
  163.6 0.6 copy-start.27

commit v8 on v7

--- a/solution.py
+++ b/solution.py
@@ -17,8 +17,7 @@
 unit_eps = 1e-06
 LOG2E = math.log2(math.e)
 VMEM_BYTES = 24 * 2**20
-COST = pl.CostEstimate(flops=0, bytes_accessed=2**16, transcendentals=0)
-WINDOW_VMEM_BYTES = 60 * 2**20
+WINDOW_VMEM_BYTES = 40 * 2**20
 PHASES = 2
 
 NN = (((1,), (0,)), ((), ()))
@@ -79,7 +78,7 @@
         out_specs=[block(n) for n in blocks],
         scratch_shapes=[pltpu.VMEM((rows * cols, channels), jnp.float32)],
         compiler_params=pltpu.CompilerParams(vmem_limit_bytes=VMEM_BYTES),
-        cost_estimate=COST,
+        cost_estimate=pl.CostEstimate(flops=0, bytes_accessed=10 * maps.size, transcendentals=0),
     )(maps)
 
 
@@ -98,10 +97,11 @@
         listed[i] = 0
         return 0
 
+    spare = chosen.shape[0] - 1
     lax.fori_loop(0, sent.shape[0], clear, 0)
     lax.fori_loop(0, listed.shape[0], clear_list, 0)
     last = blank.shape[0] - 1
-    blank[last] = 0
+    nowhere = listed.shape[0] - 1
 
     def target(k, _):
         first = (me - rank + (rank + k + 1) % group) * vehicles
@@ -115,16 +115,10 @@
             filled_here = jnp.where(far == 1, n[1], n[0])
             fits = (a < counts[r]) & ((source == me) | (far == 1)) & (filled_here + tiles <= capacity)
 
-            @pl.when(fits)
-            def _():
-                at = (2 * k + far) * capacity + filled_here
-                tile = sender % vehicles * tile_cols + jnp.maximum(shift, 0)
-                for t in range(tile_cols):
-
-                    @pl.when(t < tiles)
-                    def _():
-                        chosen[at + t] = tile + t
-
+            at = (2 * k + far) * capacity + filled_here
+            tile = sender % vehicles * tile_cols + jnp.maximum(shift, 0)
+            for t in range(tile_cols):
+                chosen[jnp.where(fits & (t < tiles), at + t, spare)] = tile + t
             more = jnp.where(fits, tiles, 0)
             return n[0] + more * (1 - far), n[1] + more * far
 
@@ -135,7 +129,7 @@
 
     lax.fori_loop(0, group - 1, target, 0)
 
-    def pair(i, _):
+    def pair(i, bare):
         v, a = i // agents, i % agents
         r = me * vehicles + v
         sender, shift = senders[r, a], shifts[r, a]
@@ -150,26 +144,21 @@
         base = a * tiles_held + v * tile_cols
         first = jnp.maximum(-shift, 0)
 
-        @pl.when(tiles > 0)
-        def _():
-            here = origin * tile_cols + tiles - 1
-            entries[here * pairs + listed[here]] = ((base + first) << ENTRY_BITS) + slot
-            listed[here] = listed[here] + 1
-
+        here = jnp.where(tiles > 0, origin * tile_cols + tiles - 1, nowhere)
+        entries[here * pairs + listed[here]] = ((base + first) << ENTRY_BITS) + slot
+        listed[here] = listed[here] + 1
         sizes_of[a * vehicles + v] = tiles
         for t in range(tile_cols):
             inside = (t >= first) & (t < first + tiles)
             live[base + t] = jnp.where(inside, 1, 0)
 
-            @pl.when(jnp.logical_not(inside))
-            def _():
-                blank[blank[last]] = base + t
-                blank[last] = blank[last] + 1
+            blank[jnp.where(inside, last, bare)] = base + t
+            bare = bare + jnp.where(inside, 0, 1)
 
         sent[source] = n + tiles
-        return 0
-
-    lax.fori_loop(0, pairs, pair, 0)
+        return bare
+
+    blank[last] = lax.fori_loop(0, pairs, pair, 0)
 
 
 def plan_of(senders, shifts, counts, tile_cols, capacity):
@@ -180,7 +169,7 @@
     ids = jnp.stack([me, (me + group) % devices])
     pairs = agents * vehicles
     places = 2 * group * tile_cols
-    sizes = [(group - 1) * 2 * capacity, (group - 1) * 2, places * pairs, places, pairs]
+    sizes = [(group - 1) * 2 * capacity + 1, (group - 1) * 2, (places + 1) * pairs, places + 1, pairs]
     sizes += [pairs * tile_cols, pairs * tile_cols + 1]
     smem = pl.BlockSpec(memory_space=pltpu.SMEM)
     return pl.pallas_call(
@@ -190,7 +179,7 @@
         out_specs=[smem] * 7,
         scratch_shapes=[pltpu.SMEM((devices,), jnp.int32)],
         compiler_params=pltpu.CompilerParams(vmem_limit_bytes=VMEM_BYTES),
-        cost_estimate=COST,
+        cost_estimate=pl.CostEstimate(flops=0, bytes_accessed=20 * 2**20, transcendentals=0),
     )(senders, shifts, counts, ids)
 
 
@@ -229,7 +218,9 @@
             scratch_shapes=[pltpu.SemaphoreType.DMA((count, shape[0]))],
         ),
         compiler_params=pltpu.CompilerParams(vmem_limit_bytes=VMEM_BYTES),
-        cost_estimate=COST,
+        cost_estimate=pl.CostEstimate(
+            flops=0, bytes_accessed=4 * count * math.prod(shape), transcendentals=0
+        ),
     )(chosen, filled, *sources.values())
 
 
@@ -353,7 +344,9 @@
             ],
         ),
         compiler_params=pltpu.CompilerParams(vmem_limit_bytes=VMEM_BYTES),
-        cost_estimate=COST,
+        cost_estimate=pl.CostEstimate(
+            flops=total * channels * channels * 40, bytes_accessed=total * channels * 12, transcendentals=total * 20
+        ),
     )(
         *plan,
         pieces.reshape(total, channels),
@@ -594,7 +587,9 @@
         ],
         input_output_aliases=aliases,
         compiler_params=pltpu.CompilerParams(vmem_limit_bytes=WINDOW_VMEM_BYTES),
-        cost_estimate=COST,
+        cost_estimate=pl.CostEstimate(
+            flops=cells * width * width * 60, bytes_accessed=cells * width * 6, transcendentals=cells * width * 4
+        ),
     )(*operands)
 
 
@@ -646,20 +641,20 @@
     entries, listed, sizes_of, live, blank = plan
     plan = (entries, listed, sizes_of, blank)
     live = live.reshape(senders.shape[1], -1)
-    near_tiles = send(messages_for(chosen, filled, capacity, {0: first}))
+    near_messages = messages_for(chosen, filled, capacity, {0: first})
+    near_tiles = send(near_messages)
     ego_edges = beside(bev_maps[:, rows - 1 :], bev_maps[:, :1])
     join_all = join_weights(agent_query, agent_keyvalue, agent_out, agent_scale)
     present = [present_cells(live, p, rows) for p in range(PHASES)]
     window_all = window_weights(
         conv_weight, gain_first, window_in, window_out, window_scale, gain_second, hidden_up, hidden_down
     )
-    far, near_tiles, second, join_all, present, window_all, ego_edges = lax.optimization_barrier(
-        (far, near_tiles, second, join_all, present, window_all, ego_edges)
+    far, second, join_all, present, window_all, _ = lax.optimization_barrier(
+        (far, second, join_all, present, window_all, near_messages)
     )
     far_tiles = send(messages_for(chosen, filled, capacity, {1: far}))
     later = swap(second)
     later_messages = messages_for(chosen, filled, capacity, {0: second, 1: later})
-    plan, later_messages = lax.optimization_barrier((plan, later_messages))
     later_tiles = send(later_messages)
     arrived = [[first, far, *near_tiles, *far_tiles], [second, later, *later_tiles]]
     origins = [

time: 180 us -> 142 us (0.79)
  waiting for transfers between devices: 56.8 us -> 26 us
  local copies, waits for them, and re-layouts: 29.5 us -> 15.3 us
  starting transfers between devices: 31.1 us -> 38.8 us
    ppermute x9, waiting for transfers between devices: 28.1 us -> 14.3 us  [send(): lax.ppermute(x, 'veh', [(i, i // group * group + (i + k + 1) % group) for...]
    ppermute x2, waiting for transfers between devices: 19.2 us -> 8.23 us  [swap(): lax.ppermute(x, 'veh', [(i, (i + group) % devices) for i in range(devices)])]
    unnamed x68 -> x52, local copies, waits for them, and re-layouts: 20.2 us -> 11.2 us
    ppermute x3, waiting for transfers between devices: 9.55 us -> 3.43 us  [beside(): below = lax.ppermute(first, 'row', [(i + 1, i) for i in range(count - 1)])]
    ppermute x9, starting transfers between devices: 9.53 us -> 14.4 us  [send(): lax.ppermute(x, 'veh', [(i, i // group * group + (i + k + 1) % group) for...]
    reshape x2, local copies, waits for them, and re-layouts: 2.27 us -> 0.22 us  [present_cells(): jnp.repeat(live.astype(jnp.float32), len(phase_columns(phase)) * rows, ax...]
  transfers between devices with their start and end apart: 17 -> 17, of which waited for: 6 -> 7; matrix products, arithmetic and copies ran while one was open for 9% -> 5% of each run, Pallas kernels for 21% -> 26%
where the time goes in v8:
time: 142 us; the launch traced here: 140 us
  Pallas kernels  59.1 us (42%)
  starting transfers between devices  38.8 us (27%)
  waiting for transfers between devices  26 us (18%)
  local copies, waits for them, and re-layouts  15.3 us (11%)
    pallas_call x2, Pallas kernels, window_layer(): pl.pallas_call(functools.partial(window_kernel, phase, rows), out_shape=j...  25.7 us
    pallas_call x2, Pallas kernels, join_agents(): pl.pallas_call(functools.partial(join_kernel, origins, tile_cols), out_sh...  18.7 us
    ppermute x9, starting transfers between devices, send(): lax.ppermute(x, 'veh', [(i, i // group * group + (i + k + 1) % group) for...  14.4 us
    ppermute x9, waiting for transfers between devices, send(): lax.ppermute(x, 'veh', [(i, i // group * group + (i + k + 1) % group) for...  14.3 us
    ppermute x3, starting transfers between devices, beside(): above = lax.ppermute(last, 'row', [(i, i + 1) for i in range(count - 1)])  12.2 us
    unnamed x52, local copies, waits for them, and re-layouts  11.2 us
    ppermute x2, waiting for transfers between devices, swap(): lax.ppermute(x, 'veh', [(i, (i + group) % devices) for i in range(devices)])  8.23 us
    ppermute x3, starting transfers between devices, beside(): below = lax.ppermute(first, 'row', [(i + 1, i) for i in range(count - 1)])  7.63 us
  transfers between devices with their start and end apart: 17, of which 7 were waited for; matrix products, arithmetic and copies ran while one was open for 5% of the time, Pallas kernels for 26%

profile of v8, /device:TPU:1, one launch (start us, length us, event | category | flops | bytes accessed | tf_op | source)
XLA Modules:
  0.0 140.2 jit_solution(16481737707512830805)
XLA Ops:
  0.0 1.2 copy-done
  1.2 0.7 shard_map.154
  1.9 1.0 copy-done.2
  2.9 3.1 %collective-permute-start.2 = (bf16[16,18,8,128]{3,2,1,0:T(8,128)(2,1)S(1)}, bf16[16,18,8,128]{3,2,1,0:T(8,128)(2,1)S(1)}, u32[]{:S(2)}, u32[]{:S(2)}) collective-permute-start(bf16[16,18,8,128]{3,2,1,0:T(8,128)(2,1)S(1)} %get-tuple-element.58.refs_0_), channel_id=1, source_target_pairs={{0,16},{4,20},{8,24},{12,28},{16,0},{20,4},{24,8},{28,12},{1,17},{... | collective-permute-start | bytes 1769480 | tf_op jit(solution)/shard_map/ppermute | solution.py:629
  6.0 0.8 copy.18.senders
  6.8 0.8 copy.19.shifts
  7.7 0.7 copy-done.1
  8.3 7.1 %shard_map.155 = (s32[49]{0:T(128)S(1)}, s32[6]{0:T(128)S(1)}, s32[544]{0:T(1024)S(1)}, s32[17]{0:T(128)S(1)}, s32[32]{0:T(128)S(1)}, /*index=5*/s32[64]{0:T(128)S(1)}, s32[65]{0:T(128)S(1)}) custom-call(s32[64,4]{1,0:T(8,128)S(1)} %copy.18.senders, s32[64,4]{1,0:T(8,128)S(1)} %copy.19.shifts, s32[64]{0:T(128)S(1)} %copy-done.1, s32[2]{0:T(128)S(1)} %pad_add_fusion.ids), custom_call_target="tpu_custom_call" | custom-call | bytes 20971520 | tf_op jit(solution)/shard_map/pallas_call | solution.py:175
  15.5 2.0 %shard_map.156 = (bf16[8,18,8,128]{3,2,1,0:T(8,128)(2,1)}, bf16[8,18,8,128]{3,2,1,0:T(8,128)(2,1)S(1)}, bf16[8,18,8,128]{3,2,1,0:T(8,128)(2,1)}) custom-call(s32[49]{0:T(128)S(1)} %get-tuple-element.61.chosen, s32[6]{0:T(128)S(1)} %get-tuple-element.62.filled, bf16[16,18,8,128]{3,2,1,0:T(8,128)(2,1)S(1)} %get-tuple-element.58.refs_0_), custom_call_target="tpu_custom_call" | custom-call | bytes 1769472 | tf_op jit(solution)/shard_map/pallas_call | solution.py:210
  17.5 1.2 collective-permute-start.3
  18.7 1.3 collective-permute-start.4
  20.0 0.9 collective-permute-start.5
  20.9 1.1 fusion.1
  22.5 0.1 reshape.75.refs_8_
  23.0 0.6 multiply_bitcast_fusion
  23.6 8.2 %collective-permute-done.2.refs_0_ = bf16[16,18,8,128]{3,2,1,0:T(8,128)(2,1)S(1)} collective-permute-done((bf16[16,18,8,128]{3,2,1,0:T(8,128)(2,1)S(1)}, bf16[16,18,8,128]{3,2,1,0:T(8,128)(2,1)S(1)}, u32[]{:S(2)}, u32[]{:S(2)}) %collective-permute-start.2) | collective-permute-done | bytes 589856 | tf_op jit(solution)/shard_map/ppermute | solution.py:629
  31.8 1.7 %shard_map.157 = (bf16[8,18,8,128]{3,2,1,0:T(8,128)(2,1)}, bf16[8,18,8,128]{3,2,1,0:T(8,128)(2,1)}, bf16[8,18,8,128]{3,2,1,0:T(8,128)(2,1)}) custom-call(s32[49]{0:T(128)S(1)} %get-tuple-element.61.chosen, s32[6]{0:T(128)S(1)} %get-tuple-element.62.filled, bf16[16,18,8,128]{3,2,1,0:T(8,128)(2,1)S(1)} %collective-permute-done.2.refs_0_), custom_call_target="tpu_custom_call" | custom-call | bytes 1769472 | tf_op jit(solution)/shard_map/pallas_call | solution.py:210
  33.4 1.0 collective-permute-start.6
  34.5 1.5 %collective-permute-start.7 = (bf16[8,18,8,128]{3,2,1,0:T(8,128)(2,1)}, bf16[8,18,8,128]{3,2,1,0:T(8,128)(2,1)}, u32[]{:S(2)}, u32[]{:S(2)}) collective-permute-start(bf16[8,18,8,128]{3,2,1,0:T(8,128)(2,1)} %get-tuple-element.68), channel_id=1, source_target_pairs={{0,8},{4,12},{8,0},{12,4},{16,24},{20,28},{24,16},{28,20},{1,9},{5... | collective-permute-start | bytes 884744 | tf_op jit(solution)/shard_map/ppermute | solution.py:633
  36.0 2.3 %collective-permute-done.3 = bf16[8,18,8,128]{3,2,1,0:T(8,128)(2,1)S(1)} collective-permute-done((bf16[8,18,8,128]{3,2,1,0:T(8,128)(2,1)}, bf16[8,18,8,128]{3,2,1,0:T(8,128)(2,1)S(1)}, u32[]{:S(2)}, u32[]{:S(2)}) %collective-permute-start.3) | collective-permute-done | bytes 294944 | tf_op jit(solution)/shard_map/ppermute | solution.py:633
  38.3 0.5 collective-permute-done.4
  38.8 1.4 collective-permute-start.11
  40.2 1.7 %fusion = (bf16[8,1,64,128]{3,2,1,0:T(8,128)(2,1)}, bf16[8,1,64,128]{3,2,1,0:T(8,128)(2,1)}) fusion(bf16[8,8,64,128]{3,2,1,0:T(8,128)(2,1)} %maps.1), kind=kLoop, calls=%fused_computation.2 | loop fusion | bytes 524288 | tf_op jit(solution)/shard_map/slice | solution.py:646
  42.0 3.6 %collective-permute-start.1 = (bf16[8,1,64,128]{3,2,1,0:T(8,128)(2,1)}, bf16[8,1,64,128]{3,2,1,0:T(8,128)(2,1)}, u32[]{:S(2)}, u32[]{:S(2)}) collective-permute-start(bf16[8,1,64,128]{3,2,1,0:T(8,128)(2,1)} %get-tuple-element.101), channel_id=1, source_target_pairs={{1,0},{2,1},{3,2},{5,4},{6,5},{7,6},{9,8},{10,9},{11,10},{13,12},{... | collective-permute-start | bytes 393224 | tf_op jit(solution)/shard_map/ppermute | solution.py:599
  45.6 9.8 %collective-permute-done.6 = bf16[8,18,8,128]{3,2,1,0:T(8,128)(2,1)} collective-permute-done((bf16[8,18,8,128]{3,2,1,0:T(8,128)(2,1)}, bf16[8,18,8,128]{3,2,1,0:T(8,128)(2,1)}, u32[]{:S(2)}, u32[]{:S(2)}) %collective-permute-start.6) | collective-permute-done | bytes 294944 | tf_op jit(solution)/shard_map/ppermute | solution.py:633
  55.4 4.9 %collective-permute-start = (bf16[8,1,64,128]{3,2,1,0:T(8,128)(2,1)}, bf16[8,1,64,128]{3,2,1,0:T(8,128)(2,1)}, u32[]{:S(2)}, u32[]{:S(2)}) collective-permute-start(bf16[8,1,64,128]{3,2,1,0:T(8,128)(2,1)} %get-tuple-element.102), channel_id=1, source_target_pairs={{0,1},{1,2},{2,3},{4,5},{5,6},{6,7},{8,9},{9,10},{10,11},{12,13},{... | collective-permute-start | bytes 393224 | tf_op jit(solution)/shard_map/ppermute | solution.py:598
  60.3 1.1 collective-permute-done.7
  61.4 0.8 copy-done.9
  62.2 0.7 copy-done.14
  62.9 10.3 %shard_map.158 = (bf16[2304,128]{1,0:T(8,128)(2,1)S(1)}, bf16[8,36,128]{2,1,0:T(8,128)(2,1)}, bf16[8,36,128]{2,1,0:T(8,128)(2,1)}) custom-call(s32[544]{0:T(1024)S(1)} %get-tuple-element.88.entries, s32[17]{0:T(128)S(1)} %get-tuple-element.89.listed, s32[32]{0:T(128)S(1)} %get-tuple-element.90.sizes_of, s32[65]{0:T(128)S(1)} %copy-done.14, ...), custom_call_target="tpu_custom_call" | custom-call | flops 1509949440 | bytes 3538944 | tf_op jit(solution)/shard_map/pallas_call | solution.py:327
  73.2 0.8 copy-done.16
  74.0 3.6 %collective-permute-start.9 = (bf16[8,36,128]{2,1,0:T(8,128)(2,1)}, bf16[8,36,128]{2,1,0:T(8,128)(2,1)S(1)}, u32[]{:S(2)}, u32[]{:S(2)}) collective-permute-start(bf16[8,36,128]{2,1,0:T(8,128)(2,1)} %get-tuple-element.76), channel_id=1, source_target_pairs={{0,1},{1,2},{2,3},{4,5},{5,6},{6,7},{8,9},{9,10},{10,11},{12,13},{... | collective-permute-start | bytes 221192 | tf_op jit(solution)/shard_map/ppermute | solution.py:598
  77.7 1.9 %collective-permute-start.10 = (bf16[8,36,128]{2,1,0:T(8,128)(2,1)}, bf16[8,36,128]{2,1,0:T(8,128)(2,1)S(1)}, u32[]{:S(2)}, u32[]{:S(2)}) collective-permute-start(bf16[8,36,128]{2,1,0:T(8,128)(2,1)} %get-tuple-element.77), channel_id=1, source_target_pairs={{1,0},{2,1},{3,2},{5,4},{6,5},{7,6},{9,8},{10,9},{11,10},{13,12},{... | collective-permute-start | bytes 221192 | tf_op jit(solution)/shard_map/ppermute | solution.py:599
  79.6 0.8 copy.25.refs_12_.refs_15_
  80.4 3.2 %shard_map.160 = (bf16[16,14,8,128]{3,2,1,0:T(8,128)(2,1)S(1)}, bf16[16,14,8,128]{3,2,1,0:T(8,128)(2,1)S(1)}, bf16[16,14,8,128]{3,2,1,0:T(8,128)(2,1)S(1)}) custom-call(s32[49]{0:T(128)S(1)} %get-tuple-element.61.chosen, s32[6]{0:T(128)S(1)} %get-tuple-element.62.filled, bf16[16,14,8,128]{3,2,1,0:T(8,128)(2,1)S(1)} %get-tuple-element.92.refs_0_, ...), custom_call_target="tpu_custom_call" | custom-call | bytes 2752512 | tf_op jit(solution)/shard_map/pallas_call | solution.py:210
  83.6 7.2 %collective-permute-start.12 = (bf16[16,14,8,128]{3,2,1,0:T(8,128)(2,1)S(1)}, bf16[16,14,8,128]{3,2,1,0:T(8,128)(2,1)S(1)}, u32[]{:S(2)}, u32[]{:S(2)}) collective-permute-start(bf16[16,14,8,128]{3,2,1,0:T(8,128)(2,1)S(1)} %get-tuple-element.93), channel_id=1, source_target_pairs={{0,4},{4,8},{8,12},{12,0},{16,20},{20,24},{24,28},{28,16},{1,5},{5... | collective-permute-start | bytes 1376264 | tf_op jit(solution)/shard_map/ppermute | solution.py:633
  90.8 1.3 collective-permute-start.14
  92.1 1.2 copy-done.3
  93.3 0.9 copy-done.5
  94.2 0.9 copy-done.7
  95.1 1.1 copy-done.17
  96.2 12.8 %shard_map.159.refs_19_ = bf16[8,8,2,2,16,256]{5,4,3,2,1,0:T(8,128)(2,1)} custom-call(bf16[8,64,8,128]{3,2,1,0:T(8,128)(2,1)S(1)} %copy-done.3, bf16[8,1,64,128]{3,2,1,0:T(8,128)(2,1)} %collective-permute-done.refs_1_, bf16[8,1,64,128]{3,2,1,0:T(8,128)(2,1)} %collective-permute-done.1.refs_2_, bf16[8,288,128]{2,1,0:T(8,128)(2,1)S(1)} %bitcast.52, ...), custom_call_target="tpu_custom_call" | custom-call | flops 8053063680 | bytes 3145728 | tf_op jit(solution)/shard_map/pallas_call | solution.py:575
  109.0 0.6 collective-permute-done.14
  109.6 8.4 %shard_map.161 = (bf16[1792,128]{1,0:T(8,128)(2,1)S(1)}, bf16[8,28,128]{2,1,0:T(8,128)(2,1)S(1)}, bf16[8,28,128]{2,1,0:T(8,128)(2,1)S(1)}) custom-call(s32[544]{0:T(1024)S(1)} %get-tuple-element.88.entries, s32[17]{0:T(128)S(1)} %get-tuple-element.89.listed, s32[32]{0:T(128)S(1)} %get-tuple-element.90.sizes_of, s32[65]{0:T(128)S(1)} %copy-done.15, ...), custom_call_target="tpu_custom_call" | custom-call | flops 1174405120 | bytes 2752512 | tf_op jit(solution)/shard_map/pallas_call | solution.py:327
  118.0 3.7 %collective-permute-start.15 = (bf16[8,28,128]{2,1,0:T(8,128)(2,1)S(1)}, bf16[8,28,128]{2,1,0:T(8,128)(2,1)S(1)}, u32[]{:S(2)}, u32[]{:S(2)}) collective-permute-start(bf16[8,28,128]{2,1,0:T(8,128)(2,1)S(1)} %get-tuple-element.98), channel_id=1, source_target_pairs={{0,1},{1,2},{2,3},{4,5},{5,6},{6,7},{8,9},{9,10},{10,11},{12,13},{... | collective-permute-start | bytes 172040 | tf_op jit(solution)/shard_map/ppermute | solution.py:598
  121.7 2.1 %collective-permute-start.16 = (bf16[8,28,128]{2,1,0:T(8,128)(2,1)S(1)}, bf16[8,28,128]{2,1,0:T(8,128)(2,1)S(1)}, u32[]{:S(2)}, u32[]{:S(2)}) collective-permute-start(bf16[8,28,128]{2,1,0:T(8,128)(2,1)S(1)} %get-tuple-element.99), channel_id=1, source_target_pairs={{1,0},{2,1},{3,2},{5,4},{6,5},{7,6},{9,8},{10,9},{11,10},{13,12},{... | collective-permute-start | bytes 172040 | tf_op jit(solution)/shard_map/ppermute | solution.py:599
  123.9 3.4 %collective-permute-done.16.refs_8_ = bf16[8,28,128]{2,1,0:T(8,128)(2,1)S(1)} collective-permute-done((bf16[8,28,128]{2,1,0:T(8,128)(2,1)S(1)}, bf16[8,28,128]{2,1,0:T(8,128)(2,1)S(1)}, u32[]{:S(2)}, u32[]{:S(2)}) %collective-permute-start.16) | collective-permute-done | bytes 57376 | tf_op jit(solution)/shard_map/ppermute | solution.py:599
  127.3 12.9 %shard_map.162 = bf16[8,8,2,2,16,256]{5,4,3,2,1,0:T(8,128)(2,1)} custom-call(bf16[8,64,8,128]{3,2,1,0:T(8,128)(2,1)S(1)} %copy-done.3, bf16[8,1,64,128]{3,2,1,0:T(8,128)(2,1)} %collective-permute-done.refs_1_, bf16[8,1,64,128]{3,2,1,0:T(8,128)(2,1)} %collective-permute-done.1.refs_2_, ...), custom_call_target="tpu_custom_call", output_to_operand_aliasing={{}: (19, {})} | custom-call | flops 8053063680 | bytes 3145728 | tf_op jit(solution)/shard_map/pallas_call | solution.py:575
  (60 shorter events, 1.0 us)
Async XLA Ops:
  0.0 1.2 copy-start
  1.2 20.8 %copy-start.20 = (f32[3,3,256]{2,1,0:T(4,128)S(1)}, f32[3,3,256]{2,1,0:T(4,128)}, u32[]{:S(2)}) copy-start(f32[3,3,256]{2,1,0:T(4,128)} %param.24) | copy-start | bytes 27652
  1.2 21.1 %copy-start.19 = (bf16[128,128]{1,0:T(8,128)(2,1)S(1)}, bf16[128,128]{1,0:T(8,128)(2,1)}, u32[]{:S(2)}) copy-start(bf16[128,128]{1,0:T(8,128)(2,1)} %param.20) | copy-start | bytes 98308
  1.2 21.4 %copy-start.18 = (bf16[128,256]{1,0:T(8,128)(2,1)S(1)}, bf16[128,256]{1,0:T(8,128)(2,1)}, u32[]{:S(2)}) copy-start(bf16[128,256]{1,0:T(8,128)(2,1)} %param.21) | copy-start | bytes 196612
  1.2 21.7 %copy-start.22 = (f32[8]{0:T(128)S(1)}, f32[8]{0:T(128)}, u32[]{:S(2)}) copy-start(f32[8]{0:T(128)} %param.28) | copy-start | bytes 100
  1.9 1.0 copy-start.2
  2.9 39.0 %copy-start.21 = (f32[4]{0:T(128)S(1)}, f32[4]{0:T(128)}, u32[]{:S(2)}) copy-start(f32[4]{0:T(128)} %param.23) | copy-start | bytes 52
  2.9 28.9 %collective-permute-start.2 = (bf16[16,18,8,128]{3,2,1,0:T(8,128)(2,1)S(1)}, bf16[16,18,8,128]{3,2,1,0:T(8,128)(2,1)S(1)}, u32[]{:S(2)}, u32[]{:S(2)}) collective-permute-start(bf16[16,18,8,128]{3,2,1,0:T(8,128)(2,1)S(1)} %get-tuple-element.58.refs_0_), channel_id=1, source_target_pairs={{0,16},{4,20},{8,24},{12,28},{16,0},{20,4},{24,8},{28,12},{1,17},{... | collective-permute-start | bytes 1769480 | tf_op jit(solution)/shard_map/ppermute | solution.py:629
  7.7 0.7 copy-start.1
  15.5 46.0 %copy-start.13 = (s32[65]{0:T(128)}, s32[65]{0:T(128)S(1)}, u32[]{:S(2)}) copy-start(s32[65]{0:T(128)S(1)} %get-tuple-element.91.blank) | copy-start | bytes 784
  17.5 20.8 %collective-permute-start.3 = (bf16[8,18,8,128]{3,2,1,0:T(8,128)(2,1)}, bf16[8,18,8,128]{3,2,1,0:T(8,128)(2,1)S(1)}, u32[]{:S(2)}, u32[]{:S(2)}) collective-permute-start(bf16[8,18,8,128]{3,2,1,0:T(8,128)(2,1)} %get-tuple-element.63), channel_id=1, source_target_pairs={{0,4},{4,8},{8,12},{12,0},{16,20},{20,24},{24,28},{28,16},{1,5},{5... | collective-permute-start | bytes 884744 | tf_op jit(solution)/shard_map/ppermute | solution.py:633
  18.7 20.1 %collective-permute-start.4 = (bf16[8,18,8,128]{3,2,1,0:T(8,128)(2,1)S(1)}, bf16[8,18,8,128]{3,2,1,0:T(8,128)(2,1)S(1)}, u32[]{:S(2)}, u32[]{:S(2)}) collective-permute-start(bf16[8,18,8,128]{3,2,1,0:T(8,128)(2,1)S(1)} %get-tuple-element.64), channel_id=1, source_target_pairs={{0,8},{4,12},{8,0},{12,4},{16,24},{20,28},{24,16},{28,20},{1,9},{5... | collective-permute-start | bytes 884744 | tf_op jit(solution)/shard_map/ppermute | solution.py:633
  20.0 22.0 %collective-permute-start.5 = (bf16[8,18,8,128]{3,2,1,0:T(8,128)(2,1)}, bf16[8,18,8,128]{3,2,1,0:T(8,128)(2,1)}, u32[]{:S(2)}, u32[]{:S(2)}) collective-permute-start(bf16[8,18,8,128]{3,2,1,0:T(8,128)(2,1)} %get-tuple-element.65), channel_id=1, source_target_pairs={{0,12},{4,0},{8,4},{12,8},{16,28},{20,16},{24,20},{28,24},{1,13},{... | collective-permute-start | bytes 884744 | tf_op jit(solution)/shard_map/ppermute | solution.py:633
  33.4 21.9 %collective-permute-start.6 = (bf16[8,18,8,128]{3,2,1,0:T(8,128)(2,1)}, bf16[8,18,8,128]{3,2,1,0:T(8,128)(2,1)}, u32[]{:S(2)}, u32[]{:S(2)}) collective-permute-start(bf16[8,18,8,128]{3,2,1,0:T(8,128)(2,1)} %get-tuple-element.67), channel_id=1, source_target_pairs={{0,4},{4,8},{8,12},{12,0},{16,20},{20,24},{24,28},{28,16},{1,5},{5... | collective-permute-start | bytes 884744 | tf_op jit(solution)/shard_map/ppermute | solution.py:633
  34.5 26.9 %collective-permute-start.7 = (bf16[8,18,8,128]{3,2,1,0:T(8,128)(2,1)}, bf16[8,18,8,128]{3,2,1,0:T(8,128)(2,1)}, u32[]{:S(2)}, u32[]{:S(2)}) collective-permute-start(bf16[8,18,8,128]{3,2,1,0:T(8,128)(2,1)} %get-tuple-element.68), channel_id=1, source_target_pairs={{0,8},{4,12},{8,0},{12,4},{16,24},{20,28},{24,16},{28,20},{1,9},{5... | collective-permute-start | bytes 884744 | tf_op jit(solution)/shard_map/ppermute | solution.py:633
  38.3 23.1 %collective-permute-start.8 = (bf16[8,18,8,128]{3,2,1,0:T(8,128)(2,1)}, bf16[8,18,8,128]{3,2,1,0:T(8,128)(2,1)}, u32[]{:S(2)}, u32[]{:S(2)}) collective-permute-start(bf16[8,18,8,128]{3,2,1,0:T(8,128)(2,1)} %get-tuple-element.69), channel_id=1, source_target_pairs={{0,12},{4,0},{8,4},{12,8},{16,28},{20,16},{24,20},{28,24},{1,13},{... | collective-permute-start | bytes 884744 | tf_op jit(solution)/shard_map/ppermute | solution.py:633
  38.8 41.6 %collective-permute-start.11 = (bf16[16,14,8,128]{3,2,1,0:T(8,128)(2,1)S(1)}, bf16[16,14,8,128]{3,2,1,0:T(8,128)(2,1)S(1)}, u32[]{:S(2)}, u32[]{:S(2)}) collective-permute-start(bf16[16,14,8,128]{3,2,1,0:T(8,128)(2,1)S(1)} %get-tuple-element.92.refs_0_), channel_id=1, source_target_pairs={{0,16},{4,20},{8,24},{12,28},{16,0},{20,4},{24,8},{28,12},{1,17},{... | collective-permute-start | bytes 1376264 | tf_op jit(solution)/shard_map/ppermute | solution.py:629
  42.0 48.8 %collective-permute-start.1 = (bf16[8,1,64,128]{3,2,1,0:T(8,128)(2,1)}, bf16[8,1,64,128]{3,2,1,0:T(8,128)(2,1)}, u32[]{:S(2)}, u32[]{:S(2)}) collective-permute-start(bf16[8,1,64,128]{3,2,1,0:T(8,128)(2,1)} %get-tuple-element.101), channel_id=1, source_target_pairs={{1,0},{2,1},{3,2},{5,4},{6,5},{7,6},{9,8},{10,9},{11,10},{13,12},{... | collective-permute-start | bytes 393224 | tf_op jit(solution)/shard_map/ppermute | solution.py:599
  55.4 35.4 %collective-permute-start = (bf16[8,1,64,128]{3,2,1,0:T(8,128)(2,1)}, bf16[8,1,64,128]{3,2,1,0:T(8,128)(2,1)}, u32[]{:S(2)}, u32[]{:S(2)}) collective-permute-start(bf16[8,1,64,128]{3,2,1,0:T(8,128)(2,1)} %get-tuple-element.102), channel_id=1, source_target_pairs={{0,1},{1,2},{2,3},{4,5},{5,6},{6,7},{8,9},{9,10},{10,11},{12,13},{... | collective-permute-start | bytes 393224 | tf_op jit(solution)/shard_map/ppermute | solution.py:598
  61.4 0.8 copy-start.9
  62.2 0.7 copy-start.14
  62.9 29.2 %copy-start.4 = (bf16[256,512]{1,0:T(8,128)(2,1)S(1)}, bf16[256,512]{1,0:T(8,128)(2,1)}, u32[]{:S(2)}) copy-start(bf16[256,512]{1,0:T(8,128)(2,1)} %refs_17_) | copy-start | bytes 786436
  62.9 29.2 %copy-start.11 = (f32[256]{0:T(256)S(1)}, f32[256]{0:T(256)}, u32[]{:S(2)}) copy-start(f32[256]{0:T(256)} %param.25) | copy-start | bytes 3076
  62.9 29.2 %copy-start.12 = (f32[256]{0:T(256)S(1)}, f32[256]{0:T(256)}, u32[]{:S(2)}) copy-start(f32[256]{0:T(256)} %param.29) | copy-start | bytes 3076
  73.2 0.8 copy-start.16
  74.0 18.0 %collective-permute-start.9 = (bf16[8,36,128]{2,1,0:T(8,128)(2,1)}, bf16[8,36,128]{2,1,0:T(8,128)(2,1)S(1)}, u32[]{:S(2)}, u32[]{:S(2)}) collective-permute-start(bf16[8,36,128]{2,1,0:T(8,128)(2,1)} %get-tuple-element.76), channel_id=1, source_target_pairs={{0,1},{1,2},{2,3},{4,5},{5,6},{6,7},{8,9},{9,10},{10,11},{12,13},{... | collective-permute-start | bytes 221192 | tf_op jit(solution)/shard_map/ppermute | solution.py:598
  77.7 14.4 %collective-permute-start.10 = (bf16[8,36,128]{2,1,0:T(8,128)(2,1)}, bf16[8,36,128]{2,1,0:T(8,128)(2,1)S(1)}, u32[]{:S(2)}, u32[]{:S(2)}) collective-permute-start(bf16[8,36,128]{2,1,0:T(8,128)(2,1)} %get-tuple-element.77), channel_id=1, source_target_pairs={{1,0},{2,1},{3,2},{5,4},{6,5},{7,6},{9,8},{10,9},{11,10},{13,12},{... | collective-permute-start | bytes 221192 | tf_op jit(solution)/shard_map/ppermute | solution.py:599
  83.6 25.5 %collective-permute-start.12 = (bf16[16,14,8,128]{3,2,1,0:T(8,128)(2,1)S(1)}, bf16[16,14,8,128]{3,2,1,0:T(8,128)(2,1)S(1)}, u32[]{:S(2)}, u32[]{:S(2)}) collective-permute-start(bf16[16,14,8,128]{3,2,1,0:T(8,128)(2,1)S(1)} %get-tuple-element.93), channel_id=1, source_target_pairs={{0,4},{4,8},{8,12},{12,0},{16,20},{20,24},{24,28},{28,16},{1,5},{5... | collective-permute-start | bytes 1376264 | tf_op jit(solution)/shard_map/ppermute | solution.py:633
  90.8 18.3 %collective-permute-start.13 = (bf16[16,14,8,128]{3,2,1,0:T(8,128)(2,1)S(1)}, bf16[16,14,8,128]{3,2,1,0:T(8,128)(2,1)S(1)}, u32[]{:S(2)}, u32[]{:S(2)}) collective-permute-start(bf16[16,14,8,128]{3,2,1,0:T(8,128)(2,1)S(1)} %get-tuple-element.94), channel_id=1, source_target_pairs={{0,8},{4,12},{8,0},{12,4},{16,24},{20,28},{24,16},{28,20},{1,9},{5... | collective-permute-start | bytes 1376264 | tf_op jit(solution)/shard_map/ppermute | solution.py:633
  90.8 18.9 %collective-permute-start.14 = (bf16[16,14,8,128]{3,2,1,0:T(8,128)(2,1)S(1)}, bf16[16,14,8,128]{3,2,1,0:T(8,128)(2,1)S(1)}, u32[]{:S(2)}, u32[]{:S(2)}) collective-permute-start(bf16[16,14,8,128]{3,2,1,0:T(8,128)(2,1)S(1)} %get-tuple-element.95), channel_id=1, source_target_pairs={{0,12},{4,0},{8,4},{12,8},{16,28},{20,16},{24,20},{28,24},{1,13},{... | collective-permute-start | bytes 1376264 | tf_op jit(solution)/shard_map/ppermute | solution.py:633
  92.1 1.2 copy-start.3
  93.3 0.9 copy-start.5
  94.2 0.9 copy-start.7
  95.1 1.1 copy-start.17
  96.2 13.4 %copy-start.10 = (bf16[128,128]{1,0:T(8,128)(2,1)S(1)}, bf16[128,128]{1,0:T(8,128)(2,1)}, u32[]{:S(2)}) copy-start(bf16[128,128]{1,0:T(8,128)(2,1)} %refs_8_) | copy-start | bytes 98308
  96.2 13.4 %copy-start.15 = (s32[65]{0:T(128)S(1)}, s32[65]{0:T(128)}, u32[]{:S(2)}) copy-start(s32[65]{0:T(128)} %copy-done.13) | copy-start | bytes 784
  109.6 17.7 %copy-start.6 = (bf16[512,256]{1,0:T(8,128)(2,1)S(1)}, bf16[512,256]{1,0:T(8,128)(2,1)}, u32[]{:S(2)}) copy-start(bf16[512,256]{1,0:T(8,128)(2,1)} %refs_18_) | copy-start | bytes 786436
  109.6 17.7 %copy-start.8 = (bf16[256,256]{1,0:T(8,128)(2,1)S(1)}, bf16[256,256]{1,0:T(8,128)(2,1)}, u32[]{:S(2)}) copy-start(bf16[256,256]{1,0:T(8,128)(2,1)} %refs_14_.1) | copy-start | bytes 393220
  118.0 5.8 %collective-permute-start.15 = (bf16[8,28,128]{2,1,0:T(8,128)(2,1)S(1)}, bf16[8,28,128]{2,1,0:T(8,128)(2,1)S(1)}, u32[]{:S(2)}, u32[]{:S(2)}) collective-permute-start(bf16[8,28,128]{2,1,0:T(8,128)(2,1)S(1)} %get-tuple-element.98), channel_id=1, source_target_pairs={{0,1},{1,2},{2,3},{4,5},{5,6},{6,7},{8,9},{9,10},{10,11},{12,13},{... | collective-permute-start | bytes 172040 | tf_op jit(solution)/shard_map/ppermute | solution.py:598
  121.7 5.6 %collective-permute-start.16 = (bf16[8,28,128]{2,1,0:T(8,128)(2,1)S(1)}, bf16[8,28,128]{2,1,0:T(8,128)(2,1)S(1)}, u32[]{:S(2)}, u32[]{:S(2)}) collective-permute-start(bf16[8,28,128]{2,1,0:T(8,128)(2,1)S(1)} %get-tuple-element.99), channel_id=1, source_target_pairs={{1,0},{2,1},{3,2},{5,4},{6,5},{7,6},{9,8},{10,9},{11,10},{13,12},{... | collective-permute-start | bytes 172040 | tf_op jit(solution)/shard_map/ppermute | solution.py:599

commit v9 on v8

--- a/solution.py
+++ b/solution.py
@@ -554,7 +554,7 @@
     width = 2 * channels
     tile_cols = cols // TILE
     run = TILE // PHASES
-    group = 4
+    group = vehicles
     whole = lambda x: pl.BlockSpec(x.shape, lambda r: (0,) * x.ndim)
     block = lambda *shape: pl.BlockSpec((group, *shape), lambda r: (r,) + (0,) * len(shape))
     pieces = [x.reshape(vehicles, -1, channels) for three in pieces for x in three]

time: 142 us -> 142 us (level)
    pallas_call x2, Pallas kernels: 25.7 us -> 24.1 us  [window_layer(): pl.pallas_call(functools.partial(window_kernel, phase, rows), out_shape=j...]
where the time goes in v9:
time: 142 us; the launch traced here: 141 us
  Pallas kernels  58.2 us (41%)
  starting transfers between devices  39.3 us (28%)
  waiting for transfers between devices  26.9 us (19%)
  local copies, waits for them, and re-layouts  15.3 us (11%)
    pallas_call x2, Pallas kernels, window_layer(): pl.pallas_call(functools.partial(window_kernel, phase, rows), out_shape=j...  24.1 us
    pallas_call x2, Pallas kernels, join_agents(): pl.pallas_call(functools.partial(join_kernel, origins, tile_cols), out_sh...  19.5 us
    ppermute x9, starting transfers between devices, send(): lax.ppermute(x, 'veh', [(i, i // group * group + (i + k + 1) % group) for...  15.3 us
    ppermute x9, waiting for transfers between devices, send(): lax.ppermute(x, 'veh', [(i, i // group * group + (i + k + 1) % group) for...  15.2 us
    ppermute x3, starting transfers between devices, beside(): above = lax.ppermute(last, 'row', [(i, i + 1) for i in range(count - 1)])  12.1 us
    unnamed x52, local copies, waits for them, and re-layouts  11.2 us
    ppermute x2, waiting for transfers between devices, swap(): lax.ppermute(x, 'veh', [(i, (i + group) % devices) for i in range(devices)])  8.03 us
    ppermute x3, starting transfers between devices, beside(): below = lax.ppermute(first, 'row', [(i + 1, i) for i in range(count - 1)])  7.41 us
  transfers between devices with their start and end apart: 17, of which 7 were waited for; matrix products, arithmetic and copies ran while one was open for 5% of the time, Pallas kernels for 26%

profile of v9, /device:TPU:1, one launch (start us, length us, event | category | flops | bytes accessed | tf_op | source)
XLA Modules:
  0.0 140.7 jit_solution(1306876466244619142)
XLA Ops:
  0.0 1.2 copy-done
  1.2 0.7 shard_map.154
  1.9 1.0 copy-done.2
  2.9 3.1 %collective-permute-start.2 = (bf16[16,18,8,128]{3,2,1,0:T(8,128)(2,1)S(1)}, bf16[16,18,8,128]{3,2,1,0:T(8,128)(2,1)S(1)}, u32[]{:S(2)}, u32[]{:S(2)}) collective-permute-start(bf16[16,18,8,128]{3,2,1,0:T(8,128)(2,1)S(1)} %get-tuple-element.58.refs_0_), channel_id=1, source_target_pairs={{0,16},{4,20},{8,24},{12,28},{16,0},{20,4},{24,8},{28,12},{1,17},{... | collective-permute-start | bytes 1769480 | tf_op jit(solution)/shard_map/ppermute | solution.py:629
  6.0 0.8 copy.18.senders
  6.8 0.8 copy.19.shifts
  7.7 0.7 copy-done.1
  8.3 7.1 %shard_map.155 = (s32[49]{0:T(128)S(1)}, s32[6]{0:T(128)S(1)}, s32[544]{0:T(1024)S(1)}, s32[17]{0:T(128)S(1)}, s32[32]{0:T(128)S(1)}, /*index=5*/s32[64]{0:T(128)S(1)}, s32[65]{0:T(128)S(1)}) custom-call(s32[64,4]{1,0:T(8,128)S(1)} %copy.18.senders, s32[64,4]{1,0:T(8,128)S(1)} %copy.19.shifts, s32[64]{0:T(128)S(1)} %copy-done.1, s32[2]{0:T(128)S(1)} %pad_add_fusion.ids), custom_call_target="tpu_custom_call" | custom-call | bytes 20971520 | tf_op jit(solution)/shard_map/pallas_call | solution.py:175
  15.5 1.9 %shard_map.156 = (bf16[8,18,8,128]{3,2,1,0:T(8,128)(2,1)}, bf16[8,18,8,128]{3,2,1,0:T(8,128)(2,1)S(1)}, bf16[8,18,8,128]{3,2,1,0:T(8,128)(2,1)}) custom-call(s32[49]{0:T(128)S(1)} %get-tuple-element.61.chosen, s32[6]{0:T(128)S(1)} %get-tuple-element.62.filled, bf16[16,18,8,128]{3,2,1,0:T(8,128)(2,1)S(1)} %get-tuple-element.58.refs_0_), custom_call_target="tpu_custom_call" | custom-call | bytes 1769472 | tf_op jit(solution)/shard_map/pallas_call | solution.py:210
  17.4 1.3 collective-permute-start.3
  18.8 1.2 collective-permute-start.4
  20.0 1.2 collective-permute-start.5
  21.1 1.1 fusion.1
  22.7 0.1 reshape.75.refs_8_
  23.2 0.6 multiply_bitcast_fusion
  23.8 8.0 %collective-permute-done.2.refs_0_ = bf16[16,18,8,128]{3,2,1,0:T(8,128)(2,1)S(1)} collective-permute-done((bf16[16,18,8,128]{3,2,1,0:T(8,128)(2,1)S(1)}, bf16[16,18,8,128]{3,2,1,0:T(8,128)(2,1)S(1)}, u32[]{:S(2)}, u32[]{:S(2)}) %collective-permute-start.2) | collective-permute-done | bytes 589856 | tf_op jit(solution)/shard_map/ppermute | solution.py:629
  31.8 1.6 %shard_map.157 = (bf16[8,18,8,128]{3,2,1,0:T(8,128)(2,1)}, bf16[8,18,8,128]{3,2,1,0:T(8,128)(2,1)}, bf16[8,18,8,128]{3,2,1,0:T(8,128)(2,1)}) custom-call(s32[49]{0:T(128)S(1)} %get-tuple-element.61.chosen, s32[6]{0:T(128)S(1)} %get-tuple-element.62.filled, bf16[16,18,8,128]{3,2,1,0:T(8,128)(2,1)S(1)} %collective-permute-done.2.refs_0_), custom_call_target="tpu_custom_call" | custom-call | bytes 1769472 | tf_op jit(solution)/shard_map/pallas_call | solution.py:210
  33.4 1.1 collective-permute-start.6
  34.5 1.4 %collective-permute-start.7 = (bf16[8,18,8,128]{3,2,1,0:T(8,128)(2,1)}, bf16[8,18,8,128]{3,2,1,0:T(8,128)(2,1)}, u32[]{:S(2)}, u32[]{:S(2)}) collective-permute-start(bf16[8,18,8,128]{3,2,1,0:T(8,128)(2,1)} %get-tuple-element.68), channel_id=1, source_target_pairs={{0,8},{4,12},{8,0},{12,4},{16,24},{20,28},{24,16},{28,20},{1,9},{5... | collective-permute-start | bytes 884744 | tf_op jit(solution)/shard_map/ppermute | solution.py:633
  35.9 2.4 %collective-permute-done.3 = bf16[8,18,8,128]{3,2,1,0:T(8,128)(2,1)S(1)} collective-permute-done((bf16[8,18,8,128]{3,2,1,0:T(8,128)(2,1)}, bf16[8,18,8,128]{3,2,1,0:T(8,128)(2,1)S(1)}, u32[]{:S(2)}, u32[]{:S(2)}) %collective-permute-start.3) | collective-permute-done | bytes 294944 | tf_op jit(solution)/shard_map/ppermute | solution.py:633
  38.3 0.5 collective-permute-done.4
  38.8 1.4 collective-permute-start.11
  40.2 1.7 %fusion = (bf16[8,1,64,128]{3,2,1,0:T(8,128)(2,1)}, bf16[8,1,64,128]{3,2,1,0:T(8,128)(2,1)}) fusion(bf16[8,8,64,128]{3,2,1,0:T(8,128)(2,1)} %maps.1), kind=kLoop, calls=%fused_computation.2 | loop fusion | bytes 524288 | tf_op jit(solution)/shard_map/slice | solution.py:646
  42.0 3.6 %collective-permute-start.1 = (bf16[8,1,64,128]{3,2,1,0:T(8,128)(2,1)}, bf16[8,1,64,128]{3,2,1,0:T(8,128)(2,1)}, u32[]{:S(2)}, u32[]{:S(2)}) collective-permute-start(bf16[8,1,64,128]{3,2,1,0:T(8,128)(2,1)} %get-tuple-element.101), channel_id=1, source_target_pairs={{1,0},{2,1},{3,2},{5,4},{6,5},{7,6},{9,8},{10,9},{11,10},{13,12},{... | collective-permute-start | bytes 393224 | tf_op jit(solution)/shard_map/ppermute | solution.py:599
  45.5 9.9 %collective-permute-done.6 = bf16[8,18,8,128]{3,2,1,0:T(8,128)(2,1)} collective-permute-done((bf16[8,18,8,128]{3,2,1,0:T(8,128)(2,1)}, bf16[8,18,8,128]{3,2,1,0:T(8,128)(2,1)}, u32[]{:S(2)}, u32[]{:S(2)}) %collective-permute-start.6) | collective-permute-done | bytes 294944 | tf_op jit(solution)/shard_map/ppermute | solution.py:633
  55.4 4.9 %collective-permute-start = (bf16[8,1,64,128]{3,2,1,0:T(8,128)(2,1)}, bf16[8,1,64,128]{3,2,1,0:T(8,128)(2,1)}, u32[]{:S(2)}, u32[]{:S(2)}) collective-permute-start(bf16[8,1,64,128]{3,2,1,0:T(8,128)(2,1)} %get-tuple-element.102), channel_id=1, source_target_pairs={{0,1},{1,2},{2,3},{4,5},{5,6},{6,7},{8,9},{9,10},{10,11},{12,13},{... | collective-permute-start | bytes 393224 | tf_op jit(solution)/shard_map/ppermute | solution.py:598
  60.3 1.1 collective-permute-done.7
  61.4 0.8 copy-done.9
  62.2 0.7 copy-done.14
  62.9 10.5 %shard_map.158 = (bf16[2304,128]{1,0:T(8,128)(2,1)S(1)}, bf16[8,36,128]{2,1,0:T(8,128)(2,1)}, bf16[8,36,128]{2,1,0:T(8,128)(2,1)}) custom-call(s32[544]{0:T(1024)S(1)} %get-tuple-element.88.entries, s32[17]{0:T(128)S(1)} %get-tuple-element.89.listed, s32[32]{0:T(128)S(1)} %get-tuple-element.90.sizes_of, s32[65]{0:T(128)S(1)} %copy-done.14, ...), custom_call_target="tpu_custom_call" | custom-call | flops 1509949440 | bytes 3538944 | tf_op jit(solution)/shard_map/pallas_call | solution.py:327
  73.3 0.8 copy-done.16
  74.2 3.6 %collective-permute-start.9 = (bf16[8,36,128]{2,1,0:T(8,128)(2,1)}, bf16[8,36,128]{2,1,0:T(8,128)(2,1)S(1)}, u32[]{:S(2)}, u32[]{:S(2)}) collective-permute-start(bf16[8,36,128]{2,1,0:T(8,128)(2,1)} %get-tuple-element.76), channel_id=1, source_target_pairs={{0,1},{1,2},{2,3},{4,5},{5,6},{6,7},{8,9},{9,10},{10,11},{12,13},{... | collective-permute-start | bytes 221192 | tf_op jit(solution)/shard_map/ppermute | solution.py:598
  77.8 1.9 %collective-permute-start.10 = (bf16[8,36,128]{2,1,0:T(8,128)(2,1)}, bf16[8,36,128]{2,1,0:T(8,128)(2,1)S(1)}, u32[]{:S(2)}, u32[]{:S(2)}) collective-permute-start(bf16[8,36,128]{2,1,0:T(8,128)(2,1)} %get-tuple-element.77), channel_id=1, source_target_pairs={{1,0},{2,1},{3,2},{5,4},{6,5},{7,6},{9,8},{10,9},{11,10},{13,12},{... | collective-permute-start | bytes 221192 | tf_op jit(solution)/shard_map/ppermute | solution.py:599
  79.7 0.8 copy.25.refs_12_.refs_15_
  80.5 3.2 %shard_map.160 = (bf16[16,14,8,128]{3,2,1,0:T(8,128)(2,1)S(1)}, bf16[16,14,8,128]{3,2,1,0:T(8,128)(2,1)S(1)}, bf16[16,14,8,128]{3,2,1,0:T(8,128)(2,1)S(1)}) custom-call(s32[49]{0:T(128)S(1)} %get-tuple-element.61.chosen, s32[6]{0:T(128)S(1)} %get-tuple-element.62.filled, bf16[16,14,8,128]{3,2,1,0:T(8,128)(2,1)S(1)} %get-tuple-element.92.refs_0_, ...), custom_call_target="tpu_custom_call" | custom-call | bytes 2752512 | tf_op jit(solution)/shard_map/pallas_call | solution.py:210
  83.7 7.8 %collective-permute-start.12 = (bf16[16,14,8,128]{3,2,1,0:T(8,128)(2,1)S(1)}, bf16[16,14,8,128]{3,2,1,0:T(8,128)(2,1)S(1)}, u32[]{:S(2)}, u32[]{:S(2)}) collective-permute-start(bf16[16,14,8,128]{3,2,1,0:T(8,128)(2,1)S(1)} %get-tuple-element.93), channel_id=1, source_target_pairs={{0,4},{4,8},{8,12},{12,0},{16,20},{20,24},{24,28},{28,16},{1,5},{5... | collective-permute-start | bytes 1376264 | tf_op jit(solution)/shard_map/ppermute | solution.py:633
  91.6 1.3 collective-permute-start.14
  92.9 1.2 copy-done.3
  94.1 0.9 copy-done.5
  95.1 0.9 copy-done.7
  96.0 1.1 copy-done.17
  97.0 12.0 %shard_map.159.refs_19_ = bf16[8,8,2,2,16,256]{5,4,3,2,1,0:T(8,128)(2,1)} custom-call(bf16[8,64,8,128]{3,2,1,0:T(8,128)(2,1)S(1)} %copy-done.3, bf16[8,1,64,128]{3,2,1,0:T(8,128)(2,1)} %collective-permute-done.refs_1_, bf16[8,1,64,128]{3,2,1,0:T(8,128)(2,1)} %collective-permute-done.1.refs_2_, bf16[8,288,128]{2,1,0:T(8,128)(2,1)S(1)} %bitcast.52, ...), custom_call_target="tpu_custom_call" | custom-call | flops 8053063680 | bytes 3145728 | tf_op jit(solution)/shard_map/pallas_call | solution.py:575
  109.1 1.4 collective-permute-done.14
  110.5 9.0 %shard_map.161 = (bf16[1792,128]{1,0:T(8,128)(2,1)S(1)}, bf16[8,28,128]{2,1,0:T(8,128)(2,1)S(1)}, bf16[8,28,128]{2,1,0:T(8,128)(2,1)S(1)}) custom-call(s32[544]{0:T(1024)S(1)} %get-tuple-element.88.entries, s32[17]{0:T(128)S(1)} %get-tuple-element.89.listed, s32[32]{0:T(128)S(1)} %get-tuple-element.90.sizes_of, s32[65]{0:T(128)S(1)} %copy-done.15, ...), custom_call_target="tpu_custom_call" | custom-call | flops 1174405120 | bytes 2752512 | tf_op jit(solution)/shard_map/pallas_call | solution.py:327
  119.5 3.6 %collective-permute-start.15 = (bf16[8,28,128]{2,1,0:T(8,128)(2,1)S(1)}, bf16[8,28,128]{2,1,0:T(8,128)(2,1)S(1)}, u32[]{:S(2)}, u32[]{:S(2)}) collective-permute-start(bf16[8,28,128]{2,1,0:T(8,128)(2,1)S(1)} %get-tuple-element.98), channel_id=1, source_target_pairs={{0,1},{1,2},{2,3},{4,5},{5,6},{6,7},{8,9},{9,10},{10,11},{12,13},{... | collective-permute-start | bytes 172040 | tf_op jit(solution)/shard_map/ppermute | solution.py:598
  123.1 1.9 %collective-permute-start.16 = (bf16[8,28,128]{2,1,0:T(8,128)(2,1)S(1)}, bf16[8,28,128]{2,1,0:T(8,128)(2,1)S(1)}, u32[]{:S(2)}, u32[]{:S(2)}) collective-permute-start(bf16[8,28,128]{2,1,0:T(8,128)(2,1)S(1)} %get-tuple-element.99), channel_id=1, source_target_pairs={{1,0},{2,1},{3,2},{5,4},{6,5},{7,6},{9,8},{10,9},{11,10},{13,12},{... | collective-permute-start | bytes 172040 | tf_op jit(solution)/shard_map/ppermute | solution.py:599
  125.0 3.6 %collective-permute-done.16.refs_8_ = bf16[8,28,128]{2,1,0:T(8,128)(2,1)S(1)} collective-permute-done((bf16[8,28,128]{2,1,0:T(8,128)(2,1)S(1)}, bf16[8,28,128]{2,1,0:T(8,128)(2,1)S(1)}, u32[]{:S(2)}, u32[]{:S(2)}) %collective-permute-start.16) | collective-permute-done | bytes 57376 | tf_op jit(solution)/shard_map/ppermute | solution.py:599
  128.7 12.0 %shard_map.162 = bf16[8,8,2,2,16,256]{5,4,3,2,1,0:T(8,128)(2,1)} custom-call(bf16[8,64,8,128]{3,2,1,0:T(8,128)(2,1)S(1)} %copy-done.3, bf16[8,1,64,128]{3,2,1,0:T(8,128)(2,1)} %collective-permute-done.refs_1_, bf16[8,1,64,128]{3,2,1,0:T(8,128)(2,1)} %collective-permute-done.1.refs_2_, ...), custom_call_target="tpu_custom_call", output_to_operand_aliasing={{}: (19, {})} | custom-call | flops 8053063680 | bytes 3145728 | tf_op jit(solution)/shard_map/pallas_call | solution.py:575
  (60 shorter events, 1.0 us)
Async XLA Ops:
  0.0 1.2 copy-start
  1.2 21.0 %copy-start.20 = (f32[3,3,256]{2,1,0:T(4,128)S(1)}, f32[3,3,256]{2,1,0:T(4,128)}, u32[]{:S(2)}) copy-start(f32[3,3,256]{2,1,0:T(4,128)} %param.24) | copy-start | bytes 27652
  1.2 21.3 %copy-start.19 = (bf16[128,128]{1,0:T(8,128)(2,1)S(1)}, bf16[128,128]{1,0:T(8,128)(2,1)}, u32[]{:S(2)}) copy-start(bf16[128,128]{1,0:T(8,128)(2,1)} %param.20) | copy-start | bytes 98308
  1.2 21.6 %copy-start.18 = (bf16[128,256]{1,0:T(8,128)(2,1)S(1)}, bf16[128,256]{1,0:T(8,128)(2,1)}, u32[]{:S(2)}) copy-start(bf16[128,256]{1,0:T(8,128)(2,1)} %param.21) | copy-start | bytes 196612
  1.2 21.9 %copy-start.22 = (f32[8]{0:T(128)S(1)}, f32[8]{0:T(128)}, u32[]{:S(2)}) copy-start(f32[8]{0:T(128)} %param.28) | copy-start | bytes 100
  1.9 1.0 copy-start.2
  2.9 39.0 %copy-start.21 = (f32[4]{0:T(128)S(1)}, f32[4]{0:T(128)}, u32[]{:S(2)}) copy-start(f32[4]{0:T(128)} %param.23) | copy-start | bytes 52
  2.9 28.9 %collective-permute-start.2 = (bf16[16,18,8,128]{3,2,1,0:T(8,128)(2,1)S(1)}, bf16[16,18,8,128]{3,2,1,0:T(8,128)(2,1)S(1)}, u32[]{:S(2)}, u32[]{:S(2)}) collective-permute-start(bf16[16,18,8,128]{3,2,1,0:T(8,128)(2,1)S(1)} %get-tuple-element.58.refs_0_), channel_id=1, source_target_pairs={{0,16},{4,20},{8,24},{12,28},{16,0},{20,4},{24,8},{28,12},{1,17},{... | collective-permute-start | bytes 1769480 | tf_op jit(solution)/shard_map/ppermute | solution.py:629
  7.7 0.7 copy-start.1
  15.5 46.0 %copy-start.13 = (s32[65]{0:T(128)}, s32[65]{0:T(128)S(1)}, u32[]{:S(2)}) copy-start(s32[65]{0:T(128)S(1)} %get-tuple-element.91.blank) | copy-start | bytes 784
  17.4 20.9 %collective-permute-start.3 = (bf16[8,18,8,128]{3,2,1,0:T(8,128)(2,1)}, bf16[8,18,8,128]{3,2,1,0:T(8,128)(2,1)S(1)}, u32[]{:S(2)}, u32[]{:S(2)}) collective-permute-start(bf16[8,18,8,128]{3,2,1,0:T(8,128)(2,1)} %get-tuple-element.63), channel_id=1, source_target_pairs={{0,4},{4,8},{8,12},{12,0},{16,20},{20,24},{24,28},{28,16},{1,5},{5... | collective-permute-start | bytes 884744 | tf_op jit(solution)/shard_map/ppermute | solution.py:633
  18.8 20.0 %collective-permute-start.4 = (bf16[8,18,8,128]{3,2,1,0:T(8,128)(2,1)S(1)}, bf16[8,18,8,128]{3,2,1,0:T(8,128)(2,1)S(1)}, u32[]{:S(2)}, u32[]{:S(2)}) collective-permute-start(bf16[8,18,8,128]{3,2,1,0:T(8,128)(2,1)S(1)} %get-tuple-element.64), channel_id=1, source_target_pairs={{0,8},{4,12},{8,0},{12,4},{16,24},{20,28},{24,16},{28,20},{1,9},{5... | collective-permute-start | bytes 884744 | tf_op jit(solution)/shard_map/ppermute | solution.py:633
  20.0 22.0 %collective-permute-start.5 = (bf16[8,18,8,128]{3,2,1,0:T(8,128)(2,1)}, bf16[8,18,8,128]{3,2,1,0:T(8,128)(2,1)}, u32[]{:S(2)}, u32[]{:S(2)}) collective-permute-start(bf16[8,18,8,128]{3,2,1,0:T(8,128)(2,1)} %get-tuple-element.65), channel_id=1, source_target_pairs={{0,12},{4,0},{8,4},{12,8},{16,28},{20,16},{24,20},{28,24},{1,13},{... | collective-permute-start | bytes 884744 | tf_op jit(solution)/shard_map/ppermute | solution.py:633
  33.4 22.0 %collective-permute-start.6 = (bf16[8,18,8,128]{3,2,1,0:T(8,128)(2,1)}, bf16[8,18,8,128]{3,2,1,0:T(8,128)(2,1)}, u32[]{:S(2)}, u32[]{:S(2)}) collective-permute-start(bf16[8,18,8,128]{3,2,1,0:T(8,128)(2,1)} %get-tuple-element.67), channel_id=1, source_target_pairs={{0,4},{4,8},{8,12},{12,0},{16,20},{20,24},{24,28},{28,16},{1,5},{5... | collective-permute-start | bytes 884744 | tf_op jit(solution)/shard_map/ppermute | solution.py:633
  34.5 26.9 %collective-permute-start.7 = (bf16[8,18,8,128]{3,2,1,0:T(8,128)(2,1)}, bf16[8,18,8,128]{3,2,1,0:T(8,128)(2,1)}, u32[]{:S(2)}, u32[]{:S(2)}) collective-permute-start(bf16[8,18,8,128]{3,2,1,0:T(8,128)(2,1)} %get-tuple-element.68), channel_id=1, source_target_pairs={{0,8},{4,12},{8,0},{12,4},{16,24},{20,28},{24,16},{28,20},{1,9},{5... | collective-permute-start | bytes 884744 | tf_op jit(solution)/shard_map/ppermute | solution.py:633
  38.3 23.1 %collective-permute-start.8 = (bf16[8,18,8,128]{3,2,1,0:T(8,128)(2,1)}, bf16[8,18,8,128]{3,2,1,0:T(8,128)(2,1)}, u32[]{:S(2)}, u32[]{:S(2)}) collective-permute-start(bf16[8,18,8,128]{3,2,1,0:T(8,128)(2,1)} %get-tuple-element.69), channel_id=1, source_target_pairs={{0,12},{4,0},{8,4},{12,8},{16,28},{20,16},{24,20},{28,24},{1,13},{... | collective-permute-start | bytes 884744 | tf_op jit(solution)/shard_map/ppermute | solution.py:633
  38.8 41.7 %collective-permute-start.11 = (bf16[16,14,8,128]{3,2,1,0:T(8,128)(2,1)S(1)}, bf16[16,14,8,128]{3,2,1,0:T(8,128)(2,1)S(1)}, u32[]{:S(2)}, u32[]{:S(2)}) collective-permute-start(bf16[16,14,8,128]{3,2,1,0:T(8,128)(2,1)S(1)} %get-tuple-element.92.refs_0_), channel_id=1, source_target_pairs={{0,16},{4,20},{8,24},{12,28},{16,0},{20,4},{24,8},{28,12},{1,17},{... | collective-permute-start | bytes 1376264 | tf_op jit(solution)/shard_map/ppermute | solution.py:629
  42.0 49.6 %collective-permute-start.1 = (bf16[8,1,64,128]{3,2,1,0:T(8,128)(2,1)}, bf16[8,1,64,128]{3,2,1,0:T(8,128)(2,1)}, u32[]{:S(2)}, u32[]{:S(2)}) collective-permute-start(bf16[8,1,64,128]{3,2,1,0:T(8,128)(2,1)} %get-tuple-element.101), channel_id=1, source_target_pairs={{1,0},{2,1},{3,2},{5,4},{6,5},{7,6},{9,8},{10,9},{11,10},{13,12},{... | collective-permute-start | bytes 393224 | tf_op jit(solution)/shard_map/ppermute | solution.py:599
  55.4 36.1 %collective-permute-start = (bf16[8,1,64,128]{3,2,1,0:T(8,128)(2,1)}, bf16[8,1,64,128]{3,2,1,0:T(8,128)(2,1)}, u32[]{:S(2)}, u32[]{:S(2)}) collective-permute-start(bf16[8,1,64,128]{3,2,1,0:T(8,128)(2,1)} %get-tuple-element.102), channel_id=1, source_target_pairs={{0,1},{1,2},{2,3},{4,5},{5,6},{6,7},{8,9},{9,10},{10,11},{12,13},{... | collective-permute-start | bytes 393224 | tf_op jit(solution)/shard_map/ppermute | solution.py:598
  61.4 0.8 copy-start.9
  62.2 0.7 copy-start.14
  62.9 30.0 %copy-start.4 = (bf16[256,512]{1,0:T(8,128)(2,1)S(1)}, bf16[256,512]{1,0:T(8,128)(2,1)}, u32[]{:S(2)}) copy-start(bf16[256,512]{1,0:T(8,128)(2,1)} %refs_17_) | copy-start | bytes 786436
  62.9 30.0 %copy-start.11 = (f32[256]{0:T(256)S(1)}, f32[256]{0:T(256)}, u32[]{:S(2)}) copy-start(f32[256]{0:T(256)} %param.25) | copy-start | bytes 3076
  62.9 30.0 %copy-start.12 = (f32[256]{0:T(256)S(1)}, f32[256]{0:T(256)}, u32[]{:S(2)}) copy-start(f32[256]{0:T(256)} %param.29) | copy-start | bytes 3076
  73.3 0.8 copy-start.16
  74.2 18.7 %collective-permute-start.9 = (bf16[8,36,128]{2,1,0:T(8,128)(2,1)}, bf16[8,36,128]{2,1,0:T(8,128)(2,1)S(1)}, u32[]{:S(2)}, u32[]{:S(2)}) collective-permute-start(bf16[8,36,128]{2,1,0:T(8,128)(2,1)} %get-tuple-element.76), channel_id=1, source_target_pairs={{0,1},{1,2},{2,3},{4,5},{5,6},{6,7},{8,9},{9,10},{10,11},{12,13},{... | collective-permute-start | bytes 221192 | tf_op jit(solution)/shard_map/ppermute | solution.py:598
  77.8 15.1 %collective-permute-start.10 = (bf16[8,36,128]{2,1,0:T(8,128)(2,1)}, bf16[8,36,128]{2,1,0:T(8,128)(2,1)S(1)}, u32[]{:S(2)}, u32[]{:S(2)}) collective-permute-start(bf16[8,36,128]{2,1,0:T(8,128)(2,1)} %get-tuple-element.77), channel_id=1, source_target_pairs={{1,0},{2,1},{3,2},{5,4},{6,5},{7,6},{9,8},{10,9},{11,10},{13,12},{... | collective-permute-start | bytes 221192 | tf_op jit(solution)/shard_map/ppermute | solution.py:599
  83.7 25.3 %collective-permute-start.12 = (bf16[16,14,8,128]{3,2,1,0:T(8,128)(2,1)S(1)}, bf16[16,14,8,128]{3,2,1,0:T(8,128)(2,1)S(1)}, u32[]{:S(2)}, u32[]{:S(2)}) collective-permute-start(bf16[16,14,8,128]{3,2,1,0:T(8,128)(2,1)S(1)} %get-tuple-element.93), channel_id=1, source_target_pairs={{0,4},{4,8},{8,12},{12,0},{16,20},{20,24},{24,28},{28,16},{1,5},{5... | collective-permute-start | bytes 1376264 | tf_op jit(solution)/shard_map/ppermute | solution.py:633
  91.6 17.5 %collective-permute-start.13 = (bf16[16,14,8,128]{3,2,1,0:T(8,128)(2,1)S(1)}, bf16[16,14,8,128]{3,2,1,0:T(8,128)(2,1)S(1)}, u32[]{:S(2)}, u32[]{:S(2)}) collective-permute-start(bf16[16,14,8,128]{3,2,1,0:T(8,128)(2,1)S(1)} %get-tuple-element.94), channel_id=1, source_target_pairs={{0,8},{4,12},{8,0},{12,4},{16,24},{20,28},{24,16},{28,20},{1,9},{5... | collective-permute-start | bytes 1376264 | tf_op jit(solution)/shard_map/ppermute | solution.py:633
  91.6 18.9 %collective-permute-start.14 = (bf16[16,14,8,128]{3,2,1,0:T(8,128)(2,1)S(1)}, bf16[16,14,8,128]{3,2,1,0:T(8,128)(2,1)S(1)}, u32[]{:S(2)}, u32[]{:S(2)}) collective-permute-start(bf16[16,14,8,128]{3,2,1,0:T(8,128)(2,1)S(1)} %get-tuple-element.95), channel_id=1, source_target_pairs={{0,12},{4,0},{8,4},{12,8},{16,28},{20,16},{24,20},{28,24},{1,13},{... | collective-permute-start | bytes 1376264 | tf_op jit(solution)/shard_map/ppermute | solution.py:633
  92.9 1.2 copy-start.3
  94.1 0.9 copy-start.5
  95.1 0.9 copy-start.7
  96.0 1.1 copy-start.17
  97.0 13.4 %copy-start.10 = (bf16[128,128]{1,0:T(8,128)(2,1)S(1)}, bf16[128,128]{1,0:T(8,128)(2,1)}, u32[]{:S(2)}) copy-start(bf16[128,128]{1,0:T(8,128)(2,1)} %refs_8_) | copy-start | bytes 98308
  97.0 13.4 %copy-start.15 = (s32[65]{0:T(128)S(1)}, s32[65]{0:T(128)}, u32[]{:S(2)}) copy-start(s32[65]{0:T(128)} %copy-done.13) | copy-start | bytes 784
  110.5 18.2 %copy-start.6 = (bf16[512,256]{1,0:T(8,128)(2,1)S(1)}, bf16[512,256]{1,0:T(8,128)(2,1)}, u32[]{:S(2)}) copy-start(bf16[512,256]{1,0:T(8,128)(2,1)} %refs_18_) | copy-start | bytes 786436
  110.5 18.2 %copy-start.8 = (bf16[256,256]{1,0:T(8,128)(2,1)S(1)}, bf16[256,256]{1,0:T(8,128)(2,1)}, u32[]{:S(2)}) copy-start(bf16[256,256]{1,0:T(8,128)(2,1)} %refs_14_.1) | copy-start | bytes 393220
  119.5 5.5 %collective-permute-start.15 = (bf16[8,28,128]{2,1,0:T(8,128)(2,1)S(1)}, bf16[8,28,128]{2,1,0:T(8,128)(2,1)S(1)}, u32[]{:S(2)}, u32[]{:S(2)}) collective-permute-start(bf16[8,28,128]{2,1,0:T(8,128)(2,1)S(1)} %get-tuple-element.98), channel_id=1, source_target_pairs={{0,1},{1,2},{2,3},{4,5},{5,6},{6,7},{8,9},{9,10},{10,11},{12,13},{... | collective-permute-start | bytes 172040 | tf_op jit(solution)/shard_map/ppermute | solution.py:598
  123.1 5.6 %collective-permute-start.16 = (bf16[8,28,128]{2,1,0:T(8,128)(2,1)S(1)}, bf16[8,28,128]{2,1,0:T(8,128)(2,1)S(1)}, u32[]{:S(2)}, u32[]{:S(2)}) collective-permute-start(bf16[8,28,128]{2,1,0:T(8,128)(2,1)S(1)} %get-tuple-element.99), channel_id=1, source_target_pairs={{1,0},{2,1},{3,2},{5,4},{6,5},{7,6},{9,8},{10,9},{11,10},{13,12},{... | collective-permute-start | bytes 172040 | tf_op jit(solution)/shard_map/ppermute | solution.py:599

commit v10 on v9

--- a/solution.py
+++ b/solution.py
@@ -17,7 +17,7 @@
 unit_eps = 1e-06
 LOG2E = math.log2(math.e)
 VMEM_BYTES = 24 * 2**20
-WINDOW_VMEM_BYTES = 40 * 2**20
+WINDOW_VMEM_BYTES = 60 * 2**20
 PHASES = 2
 
 NN = (((1,), (0,)), ((), ()))

time: 142 us -> 141 us (level)
    ppermute x2, waiting for transfers between devices: 8.03 us -> 4.43 us  [swap(): lax.ppermute(x, 'veh', [(i, (i + group) % devices) for i in range(devices)])]
    ppermute x9, waiting for transfers between devices: 15.2 us -> 17.9 us  [send(): lax.ppermute(x, 'veh', [(i, i // group * group + (i + k + 1) % group) for...]
    pallas_call x2, Pallas kernels: 24.1 us -> 25.9 us  [window_layer(): pl.pallas_call(functools.partial(window_kernel, phase, rows), out_shape=j...]
    unnamed x52 -> x34, local copies, waits for them, and re-layouts: 11.2 us -> 10.7 us
  transfers between devices with their start and end apart: 17 -> 17, of which waited for: 7 -> 7; matrix products, arithmetic and copies ran while one was open for 5% -> 7% of each run, Pallas kernels for 26% -> 25%
where the time goes in v10:
time: 141 us; the launch traced here: 140 us
  Pallas kernels  57.4 us (41%)
  starting transfers between devices  40.1 us (28%)
  waiting for transfers between devices  26 us (18%)
  local copies, waits for them, and re-layouts  16 us (11%)
    pallas_call x2, Pallas kernels, window_layer(): pl.pallas_call(functools.partial(window_kernel, phase, rows), out_shape=j...  25.9 us
    pallas_call x2, Pallas kernels, join_agents(): pl.pallas_call(functools.partial(join_kernel, origins, tile_cols), out_sh...  18.1 us
    ppermute x9, waiting for transfers between devices, send(): lax.ppermute(x, 'veh', [(i, i // group * group + (i + k + 1) % group) for...  17.9 us
    ppermute x9, starting transfers between devices, send(): lax.ppermute(x, 'veh', [(i, i // group * group + (i + k + 1) % group) for...  15.9 us
    ppermute x3, starting transfers between devices, beside(): above = lax.ppermute(last, 'row', [(i, i + 1) for i in range(count - 1)])  12.2 us
    unnamed x34, local copies, waits for them, and re-layouts  10.7 us
    ppermute x3, starting transfers between devices, beside(): below = lax.ppermute(first, 'row', [(i + 1, i) for i in range(count - 1)])  7.42 us
    pallas_call x1, Pallas kernels, plan_of(): pl.pallas_call(functools.partial(plan_kernel, (vehicles, agents, tile_col...  7.13 us
  transfers between devices with their start and end apart: 17, of which 7 were waited for; matrix products, arithmetic and copies ran while one was open for 7% of the time, Pallas kernels for 25%

profile of v10, /device:TPU:1, one launch (start us, length us, event | category | flops | bytes accessed | tf_op | source)
XLA Modules:
  0.0 139.8 jit_solution(9035530924027981157)
XLA Ops:
  0.0 1.2 copy-done
  1.2 0.7 shard_map.154
  1.9 1.0 copy-done.2
  2.9 3.1 %collective-permute-start.2 = (bf16[16,18,8,128]{3,2,1,0:T(8,128)(2,1)S(1)}, bf16[16,18,8,128]{3,2,1,0:T(8,128)(2,1)S(1)}, u32[]{:S(2)}, u32[]{:S(2)}) collective-permute-start(bf16[16,18,8,128]{3,2,1,0:T(8,128)(2,1)S(1)} %get-tuple-element.58.refs_0_), channel_id=1, source_target_pairs={{0,16},{4,20},{8,24},{12,28},{16,0},{20,4},{24,8},{28,12},{1,17},{... | collective-permute-start | bytes 1769480 | tf_op jit(solution)/shard_map/ppermute | solution.py:629
  6.0 0.8 copy.18.senders
  6.8 0.8 copy.19.shifts
  7.7 0.7 copy-done.1
  8.3 7.1 %shard_map.155 = (s32[49]{0:T(128)S(1)}, s32[6]{0:T(128)S(1)}, s32[544]{0:T(1024)S(1)}, s32[17]{0:T(128)S(1)}, s32[32]{0:T(128)S(1)}, /*index=5*/s32[64]{0:T(128)S(1)}, s32[65]{0:T(128)S(1)}) custom-call(s32[64,4]{1,0:T(8,128)S(1)} %copy.18.senders, s32[64,4]{1,0:T(8,128)S(1)} %copy.19.shifts, s32[64]{0:T(128)S(1)} %copy-done.1, s32[2]{0:T(128)S(1)} %pad_add_fusion.ids), custom_call_target="tpu_custom_call" | custom-call | bytes 20971520 | tf_op jit(solution)/shard_map/pallas_call | solution.py:175
  15.4 1.7 %shard_map.156 = (bf16[8,18,8,128]{3,2,1,0:T(8,128)(2,1)}, bf16[8,18,8,128]{3,2,1,0:T(8,128)(2,1)S(1)}, bf16[8,18,8,128]{3,2,1,0:T(8,128)(2,1)S(1)}) custom-call(s32[49]{0:T(128)S(1)} %get-tuple-element.61.chosen, s32[6]{0:T(128)S(1)} %get-tuple-element.62.filled, bf16[16,18,8,128]{3,2,1,0:T(8,128)(2,1)S(1)} %get-tuple-element.58.refs_0_), custom_call_target="tpu_custom_call" | custom-call | bytes 1769472 | tf_op jit(solution)/shard_map/pallas_call | solution.py:210
  17.2 1.1 collective-permute-start.3
  18.2 1.6 %collective-permute-start.4 = (bf16[8,18,8,128]{3,2,1,0:T(8,128)(2,1)S(1)}, bf16[8,18,8,128]{3,2,1,0:T(8,128)(2,1)S(1)}, u32[]{:S(2)}, u32[]{:S(2)}) collective-permute-start(bf16[8,18,8,128]{3,2,1,0:T(8,128)(2,1)S(1)} %get-tuple-element.64), channel_id=1, source_target_pairs={{0,8},{4,12},{8,0},{12,4},{16,24},{20,28},{24,16},{28,20},{1,9},{5... | collective-permute-start | bytes 884744 | tf_op jit(solution)/shard_map/ppermute | solution.py:633
  19.9 1.1 collective-permute-start.5
  21.0 1.8 %fusion.1 = (bf16[256,256]{1,0:T(8,128)(2,1)}, bf16[256,256]{1,0:T(8,128)(2,1)S(1)}, bf16[256,256]{1,0:T(8,128)(2,1)}) fusion(bf16[256,768]{1,0:T(8,128)(2,1)} %param.26), kind=kLoop, calls=%fused_computation.3 | loop fusion | bytes 786432 | tf_op jit(solution)/shard_map/slice | solution.py:543
  22.8 0.6 reshape.77.refs_6_.refs_9_
  23.8 0.1 reshape.75.refs_8_
  23.9 1.0 copy.21
  24.9 1.7 %copy.29 = bf16[256,256]{0,1:T(8,128)(2,1)} copy(bf16[256,256]{1,0:T(8,128)(2,1)} %get-tuple-element.103) | data formatting | bytes 262144
  26.6 0.8 copy.28
  27.3 4.4 %collective-permute-done.2.refs_0_ = bf16[16,18,8,128]{3,2,1,0:T(8,128)(2,1)S(1)} collective-permute-done((bf16[16,18,8,128]{3,2,1,0:T(8,128)(2,1)S(1)}, bf16[16,18,8,128]{3,2,1,0:T(8,128)(2,1)S(1)}, u32[]{:S(2)}, u32[]{:S(2)}) %collective-permute-start.2) | collective-permute-done | bytes 589856 | tf_op jit(solution)/shard_map/ppermute | solution.py:629
  31.8 1.6 %shard_map.157 = (bf16[8,18,8,128]{3,2,1,0:T(8,128)(2,1)}, bf16[8,18,8,128]{3,2,1,0:T(8,128)(2,1)}, bf16[8,18,8,128]{3,2,1,0:T(8,128)(2,1)}) custom-call(s32[49]{0:T(128)S(1)} %get-tuple-element.61.chosen, s32[6]{0:T(128)S(1)} %get-tuple-element.62.filled, bf16[16,18,8,128]{3,2,1,0:T(8,128)(2,1)S(1)} %collective-permute-done.2.refs_0_), custom_call_target="tpu_custom_call" | custom-call | bytes 1769472 | tf_op jit(solution)/shard_map/pallas_call | solution.py:210
  33.4 1.1 collective-permute-start.6
  34.4 1.5 %collective-permute-start.7 = (bf16[8,18,8,128]{3,2,1,0:T(8,128)(2,1)}, bf16[8,18,8,128]{3,2,1,0:T(8,128)(2,1)}, u32[]{:S(2)}, u32[]{:S(2)}) collective-permute-start(bf16[8,18,8,128]{3,2,1,0:T(8,128)(2,1)} %get-tuple-element.68), channel_id=1, source_target_pairs={{0,8},{4,12},{8,0},{12,4},{16,24},{20,28},{24,16},{28,20},{1,9},{5... | collective-permute-start | bytes 884744 | tf_op jit(solution)/shard_map/ppermute | solution.py:633
  35.9 2.2 %collective-permute-done.3 = bf16[8,18,8,128]{3,2,1,0:T(8,128)(2,1)S(1)} collective-permute-done((bf16[8,18,8,128]{3,2,1,0:T(8,128)(2,1)}, bf16[8,18,8,128]{3,2,1,0:T(8,128)(2,1)S(1)}, u32[]{:S(2)}, u32[]{:S(2)}) %collective-permute-start.3) | collective-permute-done | bytes 294944 | tf_op jit(solution)/shard_map/ppermute | solution.py:633
  38.1 0.7 collective-permute-done.4
  38.8 1.4 collective-permute-start.11
  40.2 1.7 %fusion = (bf16[8,1,64,128]{3,2,1,0:T(8,128)(2,1)}, bf16[8,1,64,128]{3,2,1,0:T(8,128)(2,1)}) fusion(bf16[8,8,64,128]{3,2,1,0:T(8,128)(2,1)} %maps.1), kind=kLoop, calls=%fused_computation.2 | loop fusion | bytes 524288 | tf_op jit(solution)/shard_map/slice | solution.py:646
  41.9 3.6 %collective-permute-start.1 = (bf16[8,1,64,128]{3,2,1,0:T(8,128)(2,1)}, bf16[8,1,64,128]{3,2,1,0:T(8,128)(2,1)}, u32[]{:S(2)}, u32[]{:S(2)}) collective-permute-start(bf16[8,1,64,128]{3,2,1,0:T(8,128)(2,1)} %get-tuple-element.101), channel_id=1, source_target_pairs={{1,0},{2,1},{3,2},{5,4},{6,5},{7,6},{9,8},{10,9},{11,10},{13,12},{... | collective-permute-start | bytes 393224 | tf_op jit(solution)/shard_map/ppermute | solution.py:599
  45.5 9.9 %collective-permute-done.6 = bf16[8,18,8,128]{3,2,1,0:T(8,128)(2,1)} collective-permute-done((bf16[8,18,8,128]{3,2,1,0:T(8,128)(2,1)}, bf16[8,18,8,128]{3,2,1,0:T(8,128)(2,1)}, u32[]{:S(2)}, u32[]{:S(2)}) %collective-permute-start.6) | collective-permute-done | bytes 294944 | tf_op jit(solution)/shard_map/ppermute | solution.py:633
  55.4 5.0 %collective-permute-start = (bf16[8,1,64,128]{3,2,1,0:T(8,128)(2,1)}, bf16[8,1,64,128]{3,2,1,0:T(8,128)(2,1)}, u32[]{:S(2)}, u32[]{:S(2)}) collective-permute-start(bf16[8,1,64,128]{3,2,1,0:T(8,128)(2,1)} %get-tuple-element.102), channel_id=1, source_target_pairs={{0,1},{1,2},{2,3},{4,5},{5,6},{6,7},{8,9},{9,10},{10,11},{12,13},{... | collective-permute-start | bytes 393224 | tf_op jit(solution)/shard_map/ppermute | solution.py:598
  60.3 1.1 collective-permute-done.7
  61.4 9.5 %shard_map.158 = (bf16[2304,128]{1,0:T(8,128)(2,1)S(1)}, bf16[8,36,128]{2,1,0:T(8,128)(2,1)S(1)}, bf16[8,36,128]{2,1,0:T(8,128)(2,1)S(1)}) custom-call(s32[544]{0:T(1024)S(1)} %get-tuple-element.88.entries, s32[17]{0:T(128)S(1)} %get-tuple-element.89.listed, s32[32]{0:T(128)S(1)} %get-tuple-element.90.sizes_of, s32[65]{0:T(128)S(1)} %get-tuple-element.91.blank, ...), custom_call_target="tpu_custom_call" | custom-call | flops 1509949440 | bytes 3538944 | tf_op jit(solution)/shard_map/pallas_call | solution.py:327
  71.0 0.8 copy-done.4
  71.8 3.6 %collective-permute-start.9 = (bf16[8,36,128]{2,1,0:T(8,128)(2,1)S(1)}, bf16[8,36,128]{2,1,0:T(8,128)(2,1)S(1)}, u32[]{:S(2)}, u32[]{:S(2)}) collective-permute-start(bf16[8,36,128]{2,1,0:T(8,128)(2,1)S(1)} %get-tuple-element.76), channel_id=1, source_target_pairs={{0,1},{1,2},{2,3},{4,5},{5,6},{6,7},{8,9},{9,10},{10,11},{12,13},{... | collective-permute-start | bytes 221192 | tf_op jit(solution)/shard_map/ppermute | solution.py:598
  75.4 1.9 %collective-permute-start.10 = (bf16[8,36,128]{2,1,0:T(8,128)(2,1)S(1)}, bf16[8,36,128]{2,1,0:T(8,128)(2,1)S(1)}, u32[]{:S(2)}, u32[]{:S(2)}) collective-permute-start(bf16[8,36,128]{2,1,0:T(8,128)(2,1)S(1)} %get-tuple-element.77), channel_id=1, source_target_pairs={{1,0},{2,1},{3,2},{5,4},{6,5},{7,6},{9,8},{10,9},{11,10},{13,12},{... | collective-permute-start | bytes 221192 | tf_op jit(solution)/shard_map/ppermute | solution.py:599
  77.4 0.7 copy.25.refs_12_.refs_15_
  78.0 2.3 %shard_map.160 = (bf16[16,14,8,128]{3,2,1,0:T(8,128)(2,1)}, bf16[16,14,8,128]{3,2,1,0:T(8,128)(2,1)S(1)}, bf16[16,14,8,128]{3,2,1,0:T(8,128)(2,1)S(1)}) custom-call(s32[49]{0:T(128)S(1)} %get-tuple-element.61.chosen, s32[6]{0:T(128)S(1)} %get-tuple-element.62.filled, bf16[16,14,8,128]{3,2,1,0:T(8,128)(2,1)S(1)} %get-tuple-element.92.refs_0_, ...), custom_call_target="tpu_custom_call" | custom-call | bytes 2752512 | tf_op jit(solution)/shard_map/pallas_call | solution.py:210
  80.4 8.3 %collective-permute-start.12 = (bf16[16,14,8,128]{3,2,1,0:T(8,128)(2,1)}, bf16[16,14,8,128]{3,2,1,0:T(8,128)(2,1)S(1)}, u32[]{:S(2)}, u32[]{:S(2)}) collective-permute-start(bf16[16,14,8,128]{3,2,1,0:T(8,128)(2,1)} %get-tuple-element.93), channel_id=1, source_target_pairs={{0,4},{4,8},{8,12},{12,0},{16,20},{20,24},{24,28},{28,16},{1,5},{5... | collective-permute-start | bytes 1376264 | tf_op jit(solution)/shard_map/ppermute | solution.py:633
  88.7 1.3 collective-permute-start.14
  90.0 0.6 copy-done.9
  90.6 12.8 %shard_map.159.refs_19_ = bf16[8,8,2,2,16,256]{5,4,3,2,1,0:T(8,128)(2,1)} custom-call(bf16[8,64,8,128]{3,2,1,0:T(8,128)(2,1)} %copy-done.2, bf16[8,1,64,128]{3,2,1,0:T(8,128)(2,1)} %collective-permute-done.refs_1_, bf16[8,1,64,128]{3,2,1,0:T(8,128)(2,1)} %collective-permute-done.1.refs_2_, bf16[8,288,128]{2,1,0:T(8,128)(2,1)} %bitcast.45, ...), custom_call_target="tpu_custom_call" | custom-call | flops 8053063680 | bytes 3145728 | tf_op jit(solution)/shard_map/pallas_call | solution.py:575
  103.5 4.1 %collective-permute-done.14 = bf16[16,14,8,128]{3,2,1,0:T(8,128)(2,1)S(1)} collective-permute-done((bf16[16,14,8,128]{3,2,1,0:T(8,128)(2,1)S(1)}, bf16[16,14,8,128]{3,2,1,0:T(8,128)(2,1)S(1)}, u32[]{:S(2)}, u32[]{:S(2)}) %collective-permute-start.14) | collective-permute-done | bytes 458784 | tf_op jit(solution)/shard_map/ppermute | solution.py:633
  107.6 8.6 %shard_map.161 = (bf16[1792,128]{1,0:T(8,128)(2,1)S(1)}, bf16[8,28,128]{2,1,0:T(8,128)(2,1)S(1)}, bf16[8,28,128]{2,1,0:T(8,128)(2,1)S(1)}) custom-call(s32[544]{0:T(1024)S(1)} %get-tuple-element.88.entries, s32[17]{0:T(128)S(1)} %get-tuple-element.89.listed, s32[32]{0:T(128)S(1)} %get-tuple-element.90.sizes_of, s32[65]{0:T(128)S(1)} %get-tuple-element.91.blank, ...), custom_call_target="tpu_custom_call" | custom-call | flops 1174405120 | bytes 2752512 | tf_op jit(solution)/shard_map/pallas_call | solution.py:327
  116.2 0.8 copy-done.5
  117.0 3.6 %collective-permute-start.15 = (bf16[8,28,128]{2,1,0:T(8,128)(2,1)S(1)}, bf16[8,28,128]{2,1,0:T(8,128)(2,1)S(1)}, u32[]{:S(2)}, u32[]{:S(2)}) collective-permute-start(bf16[8,28,128]{2,1,0:T(8,128)(2,1)S(1)} %get-tuple-element.98), channel_id=1, source_target_pairs={{0,1},{1,2},{2,3},{4,5},{5,6},{6,7},{8,9},{9,10},{10,11},{12,13},{... | collective-permute-start | bytes 172040 | tf_op jit(solution)/shard_map/ppermute | solution.py:598
  120.6 1.9 %collective-permute-start.16 = (bf16[8,28,128]{2,1,0:T(8,128)(2,1)S(1)}, bf16[8,28,128]{2,1,0:T(8,128)(2,1)S(1)}, u32[]{:S(2)}, u32[]{:S(2)}) collective-permute-start(bf16[8,28,128]{2,1,0:T(8,128)(2,1)S(1)} %get-tuple-element.99), channel_id=1, source_target_pairs={{1,0},{2,1},{3,2},{5,4},{6,5},{7,6},{9,8},{10,9},{11,10},{13,12},{... | collective-permute-start | bytes 172040 | tf_op jit(solution)/shard_map/ppermute | solution.py:599
  122.5 3.6 %collective-permute-done.16.refs_8_ = bf16[8,28,128]{2,1,0:T(8,128)(2,1)S(1)} collective-permute-done((bf16[8,28,128]{2,1,0:T(8,128)(2,1)S(1)}, bf16[8,28,128]{2,1,0:T(8,128)(2,1)S(1)}, u32[]{:S(2)}, u32[]{:S(2)}) %collective-permute-start.16) | collective-permute-done | bytes 57376 | tf_op jit(solution)/shard_map/ppermute | solution.py:599
  126.2 0.6 copy-done.12
  126.8 13.0 %shard_map.162 = bf16[8,8,2,2,16,256]{5,4,3,2,1,0:T(8,128)(2,1)} custom-call(bf16[8,64,8,128]{3,2,1,0:T(8,128)(2,1)} %copy-done.2, bf16[8,1,64,128]{3,2,1,0:T(8,128)(2,1)} %collective-permute-done.refs_1_, bf16[8,1,64,128]{3,2,1,0:T(8,128)(2,1)} %collective-permute-done.1.refs_2_, bf16[8,288,128]{2,1,0:T(8,128)(2,1)} %bitcast.46, ...), custom_call_target="tpu_custom_call", output_to_operand_aliasing={{}: (19, {})} | custom-call | flops 8053063680 | bytes 3145728 | tf_op jit(solution)/shard_map/pallas_call | solution.py:575
  (42 shorter events, 0.7 us)
Async XLA Ops:
  0.0 1.2 copy-start
  1.2 21.5 %copy-start.7 = (f32[3,3,256]{2,1,0:T(4,128)S(1)}, f32[3,3,256]{2,1,0:T(4,128)}, u32[]{:S(2)}) copy-start(f32[3,3,256]{2,1,0:T(4,128)} %param.24) | copy-start | bytes 27652
  1.2 22.4 %copy-start.6 = (bf16[128,128]{1,0:T(8,128)(2,1)S(1)}, bf16[128,128]{1,0:T(8,128)(2,1)}, u32[]{:S(2)}) copy-start(bf16[128,128]{1,0:T(8,128)(2,1)} %param.20) | copy-start | bytes 98308
  1.2 26.1 %copy-start.13 = (f32[8]{0:T(128)S(1)}, f32[8]{0:T(128)}, u32[]{:S(2)}) copy-start(f32[8]{0:T(128)} %param.28) | copy-start | bytes 100
  1.9 1.0 copy-start.2
  2.9 38.9 %copy-start.8 = (f32[4]{0:T(128)S(1)}, f32[4]{0:T(128)}, u32[]{:S(2)}) copy-start(f32[4]{0:T(128)} %param.23) | copy-start | bytes 52
  2.9 58.5 %copy-start.3 = (bf16[128,128]{1,0:T(8,128)(2,1)S(1)}, bf16[128,128]{1,0:T(8,128)(2,1)}, u32[]{:S(2)}) copy-start(bf16[128,128]{1,0:T(8,128)(2,1)} %refs_8_) | copy-start | bytes 98308
  2.9 28.9 %collective-permute-start.2 = (bf16[16,18,8,128]{3,2,1,0:T(8,128)(2,1)S(1)}, bf16[16,18,8,128]{3,2,1,0:T(8,128)(2,1)S(1)}, u32[]{:S(2)}, u32[]{:S(2)}) collective-permute-start(bf16[16,18,8,128]{3,2,1,0:T(8,128)(2,1)S(1)} %get-tuple-element.58.refs_0_), channel_id=1, source_target_pairs={{0,16},{4,20},{8,24},{12,28},{16,0},{20,4},{24,8},{28,12},{1,17},{... | collective-permute-start | bytes 1769480 | tf_op jit(solution)/shard_map/ppermute | solution.py:629
  7.7 0.7 copy-start.1
  17.2 21.0 %collective-permute-start.3 = (bf16[8,18,8,128]{3,2,1,0:T(8,128)(2,1)}, bf16[8,18,8,128]{3,2,1,0:T(8,128)(2,1)S(1)}, u32[]{:S(2)}, u32[]{:S(2)}) collective-permute-start(bf16[8,18,8,128]{3,2,1,0:T(8,128)(2,1)} %get-tuple-element.63), channel_id=1, source_target_pairs={{0,4},{4,8},{8,12},{12,0},{16,20},{20,24},{24,28},{28,16},{1,5},{5... | collective-permute-start | bytes 884744 | tf_op jit(solution)/shard_map/ppermute | solution.py:633
  18.2 20.6 %collective-permute-start.4 = (bf16[8,18,8,128]{3,2,1,0:T(8,128)(2,1)S(1)}, bf16[8,18,8,128]{3,2,1,0:T(8,128)(2,1)S(1)}, u32[]{:S(2)}, u32[]{:S(2)}) collective-permute-start(bf16[8,18,8,128]{3,2,1,0:T(8,128)(2,1)S(1)} %get-tuple-element.64), channel_id=1, source_target_pairs={{0,8},{4,12},{8,0},{12,4},{16,24},{20,28},{24,16},{28,20},{1,9},{5... | collective-permute-start | bytes 884744 | tf_op jit(solution)/shard_map/ppermute | solution.py:633
  19.9 22.1 %collective-permute-start.5 = (bf16[8,18,8,128]{3,2,1,0:T(8,128)(2,1)S(1)}, bf16[8,18,8,128]{3,2,1,0:T(8,128)(2,1)S(1)}, u32[]{:S(2)}, u32[]{:S(2)}) collective-permute-start(bf16[8,18,8,128]{3,2,1,0:T(8,128)(2,1)S(1)} %get-tuple-element.65), channel_id=1, source_target_pairs={{0,12},{4,0},{8,4},{12,8},{16,28},{20,16},{24,20},{28,24},{1,13},{... | collective-permute-start | bytes 884744 | tf_op jit(solution)/shard_map/ppermute | solution.py:633
  33.4 22.0 %collective-permute-start.6 = (bf16[8,18,8,128]{3,2,1,0:T(8,128)(2,1)}, bf16[8,18,8,128]{3,2,1,0:T(8,128)(2,1)}, u32[]{:S(2)}, u32[]{:S(2)}) collective-permute-start(bf16[8,18,8,128]{3,2,1,0:T(8,128)(2,1)} %get-tuple-element.67), channel_id=1, source_target_pairs={{0,4},{4,8},{8,12},{12,0},{16,20},{20,24},{24,28},{28,16},{1,5},{5... | collective-permute-start | bytes 884744 | tf_op jit(solution)/shard_map/ppermute | solution.py:633
  34.4 27.0 %collective-permute-start.7 = (bf16[8,18,8,128]{3,2,1,0:T(8,128)(2,1)}, bf16[8,18,8,128]{3,2,1,0:T(8,128)(2,1)}, u32[]{:S(2)}, u32[]{:S(2)}) collective-permute-start(bf16[8,18,8,128]{3,2,1,0:T(8,128)(2,1)} %get-tuple-element.68), channel_id=1, source_target_pairs={{0,8},{4,12},{8,0},{12,4},{16,24},{20,28},{24,16},{28,20},{1,9},{5... | collective-permute-start | bytes 884744 | tf_op jit(solution)/shard_map/ppermute | solution.py:633
  38.1 23.3 %collective-permute-start.8 = (bf16[8,18,8,128]{3,2,1,0:T(8,128)(2,1)}, bf16[8,18,8,128]{3,2,1,0:T(8,128)(2,1)}, u32[]{:S(2)}, u32[]{:S(2)}) collective-permute-start(bf16[8,18,8,128]{3,2,1,0:T(8,128)(2,1)} %get-tuple-element.69), channel_id=1, source_target_pairs={{0,12},{4,0},{8,4},{12,8},{16,28},{20,16},{24,20},{28,24},{1,13},{... | collective-permute-start | bytes 884744 | tf_op jit(solution)/shard_map/ppermute | solution.py:633
  38.8 39.2 %collective-permute-start.11 = (bf16[16,14,8,128]{3,2,1,0:T(8,128)(2,1)S(1)}, bf16[16,14,8,128]{3,2,1,0:T(8,128)(2,1)S(1)}, u32[]{:S(2)}, u32[]{:S(2)}) collective-permute-start(bf16[16,14,8,128]{3,2,1,0:T(8,128)(2,1)S(1)} %get-tuple-element.92.refs_0_), channel_id=1, source_target_pairs={{0,16},{4,20},{8,24},{12,28},{16,0},{20,4},{24,8},{28,12},{1,17},{... | collective-permute-start | bytes 1376264 | tf_op jit(solution)/shard_map/ppermute | solution.py:629
  41.9 46.8 %collective-permute-start.1 = (bf16[8,1,64,128]{3,2,1,0:T(8,128)(2,1)}, bf16[8,1,64,128]{3,2,1,0:T(8,128)(2,1)}, u32[]{:S(2)}, u32[]{:S(2)}) collective-permute-start(bf16[8,1,64,128]{3,2,1,0:T(8,128)(2,1)} %get-tuple-element.101), channel_id=1, source_target_pairs={{1,0},{2,1},{3,2},{5,4},{6,5},{7,6},{9,8},{10,9},{11,10},{13,12},{... | collective-permute-start | bytes 393224 | tf_op jit(solution)/shard_map/ppermute | solution.py:599
  55.4 33.3 %collective-permute-start = (bf16[8,1,64,128]{3,2,1,0:T(8,128)(2,1)}, bf16[8,1,64,128]{3,2,1,0:T(8,128)(2,1)}, u32[]{:S(2)}, u32[]{:S(2)}) collective-permute-start(bf16[8,1,64,128]{3,2,1,0:T(8,128)(2,1)} %get-tuple-element.102), channel_id=1, source_target_pairs={{0,1},{1,2},{2,3},{4,5},{5,6},{6,7},{8,9},{9,10},{10,11},{12,13},{... | collective-permute-start | bytes 393224 | tf_op jit(solution)/shard_map/ppermute | solution.py:598
  71.0 0.8 copy-start.4
  71.8 18.2 %collective-permute-start.9 = (bf16[8,36,128]{2,1,0:T(8,128)(2,1)S(1)}, bf16[8,36,128]{2,1,0:T(8,128)(2,1)S(1)}, u32[]{:S(2)}, u32[]{:S(2)}) collective-permute-start(bf16[8,36,128]{2,1,0:T(8,128)(2,1)S(1)} %get-tuple-element.76), channel_id=1, source_target_pairs={{0,1},{1,2},{2,3},{4,5},{5,6},{6,7},{8,9},{9,10},{10,11},{12,13},{... | collective-permute-start | bytes 221192 | tf_op jit(solution)/shard_map/ppermute | solution.py:598
  75.4 14.5 %collective-permute-start.10 = (bf16[8,36,128]{2,1,0:T(8,128)(2,1)S(1)}, bf16[8,36,128]{2,1,0:T(8,128)(2,1)S(1)}, u32[]{:S(2)}, u32[]{:S(2)}) collective-permute-start(bf16[8,36,128]{2,1,0:T(8,128)(2,1)S(1)} %get-tuple-element.77), channel_id=1, source_target_pairs={{1,0},{2,1},{3,2},{5,4},{6,5},{7,6},{9,8},{10,9},{11,10},{13,12},{... | collective-permute-start | bytes 221192 | tf_op jit(solution)/shard_map/ppermute | solution.py:599
  80.4 23.1 %collective-permute-start.12 = (bf16[16,14,8,128]{3,2,1,0:T(8,128)(2,1)}, bf16[16,14,8,128]{3,2,1,0:T(8,128)(2,1)S(1)}, u32[]{:S(2)}, u32[]{:S(2)}) collective-permute-start(bf16[16,14,8,128]{3,2,1,0:T(8,128)(2,1)} %get-tuple-element.93), channel_id=1, source_target_pairs={{0,4},{4,8},{8,12},{12,0},{16,20},{20,24},{24,28},{28,16},{1,5},{5... | collective-permute-start | bytes 1376264 | tf_op jit(solution)/shard_map/ppermute | solution.py:633
  88.7 14.8 %collective-permute-start.13 = (bf16[16,14,8,128]{3,2,1,0:T(8,128)(2,1)S(1)}, bf16[16,14,8,128]{3,2,1,0:T(8,128)(2,1)S(1)}, u32[]{:S(2)}, u32[]{:S(2)}) collective-permute-start(bf16[16,14,8,128]{3,2,1,0:T(8,128)(2,1)S(1)} %get-tuple-element.94), channel_id=1, source_target_pairs={{0,8},{4,12},{8,0},{12,4},{16,24},{20,28},{24,16},{28,20},{1,9},{5... | collective-permute-start | bytes 1376264 | tf_op jit(solution)/shard_map/ppermute | solution.py:633
  88.7 18.9 %collective-permute-start.14 = (bf16[16,14,8,128]{3,2,1,0:T(8,128)(2,1)S(1)}, bf16[16,14,8,128]{3,2,1,0:T(8,128)(2,1)S(1)}, u32[]{:S(2)}, u32[]{:S(2)}) collective-permute-start(bf16[16,14,8,128]{3,2,1,0:T(8,128)(2,1)S(1)} %get-tuple-element.95), channel_id=1, source_target_pairs={{0,12},{4,0},{8,4},{12,8},{16,28},{20,16},{24,20},{28,24},{1,13},{... | collective-permute-start | bytes 1376264 | tf_op jit(solution)/shard_map/ppermute | solution.py:633
  90.0 0.6 copy-start.9
  90.0 0.6 copy-start.10
  116.2 0.8 copy-start.5
  117.0 5.5 %collective-permute-start.15 = (bf16[8,28,128]{2,1,0:T(8,128)(2,1)S(1)}, bf16[8,28,128]{2,1,0:T(8,128)(2,1)S(1)}, u32[]{:S(2)}, u32[]{:S(2)}) collective-permute-start(bf16[8,28,128]{2,1,0:T(8,128)(2,1)S(1)} %get-tuple-element.98), channel_id=1, source_target_pairs={{0,1},{1,2},{2,3},{4,5},{5,6},{6,7},{8,9},{9,10},{10,11},{12,13},{... | collective-permute-start | bytes 172040 | tf_op jit(solution)/shard_map/ppermute | solution.py:598
  120.6 5.6 %collective-permute-start.16 = (bf16[8,28,128]{2,1,0:T(8,128)(2,1)S(1)}, bf16[8,28,128]{2,1,0:T(8,128)(2,1)S(1)}, u32[]{:S(2)}, u32[]{:S(2)}) collective-permute-start(bf16[8,28,128]{2,1,0:T(8,128)(2,1)S(1)} %get-tuple-element.99), channel_id=1, source_target_pairs={{1,0},{2,1},{3,2},{5,4},{6,5},{7,6},{9,8},{10,9},{11,10},{13,12},{... | collective-permute-start | bytes 172040 | tf_op jit(solution)/shard_map/ppermute | solution.py:599
  122.5 3.7 %copy-start.11 = (bf16[8,28,128]{2,1,0:T(8,128)(2,1)}, bf16[8,28,128]{2,1,0:T(8,128)(2,1)S(1)}, u32[]{:S(2)}) copy-start(bf16[8,28,128]{2,1,0:T(8,128)(2,1)S(1)} %collective-permute-done.15.refs_7_) | copy-start | bytes 172036
  126.1 0.6 copy-start.12

commit v11 on v9

--- a/solution.py
+++ b/solution.py
@@ -260,7 +260,7 @@
     lax.fori_loop(0, blank[blank.shape[0] - 1], clear, 0)
     arrived = 0
     heads = channels // HEAD
-    scale_col = scale[...].reshape(heads, 1, 1)
+    scale_col = scale[:, :1].reshape(heads, 1, 1)
     landed_cells = landed.reshape(agents, total, channels)
     for c in range(total // LANES):
         while arrived * tile_cols * cells < (c + 1) * LANES:
@@ -310,7 +310,7 @@
 
 
 def join_weights(wq, wkv, wout, scale):
-    return wq.T, wkv.T, wout, scale.reshape(-1, 1)
+    return wq.T, wkv.T, wout, jnp.broadcast_to(scale[:, None], (scale.shape[0], 128))
 
 
 def present_cells(live, phase, rows):
@@ -452,7 +452,7 @@
     queries = dot(wq[...], hidden, NT)
     values = dot(wv[...], hidden, NT).astype(jnp.bfloat16)
     keys = dot(hidden, wk[...])
-    factor = lax.rsqrt(head_sums(queries * queries) + unit_eps) * scale[...].reshape(heads, 1, 1)
+    factor = lax.rsqrt(head_sums(queries * queries) + unit_eps) * scale[:, :1].reshape(heads, 1, 1)
     queries = by_head(queries, factor)
     member = (
         lax.broadcasted_iota(jnp.int32, (width, width), 0) // HEAD
@@ -542,7 +542,7 @@
         window_in[:, width : 2 * width],
         window_in[:, 2 * width :].T,
         window_out,
-        (window_scale * LOG2E).reshape(-1, 1),
+        jnp.broadcast_to((window_scale * LOG2E)[:, None], (window_scale.shape[0], 128)),
         gain_second[None],
         hidden_up,
         hidden_down,

time: 142 us -> 136 us (0.958)
  local copies, waits for them, and re-layouts: 15.3 us -> 6.54 us
  waiting for transfers between devices: 26.9 us -> 33 us
  Pallas kernels: 58.2 us -> 54.3 us
    unnamed x52 -> x32, local copies, waits for them, and re-layouts: 11.2 us -> 3.9 us
    ppermute x9, waiting for transfers between devices: 15.2 us -> 20.3 us  [send(): lax.ppermute(x, 'veh', [(i, i // group * group + (i + k + 1) % group) for...]
    pallas_call x2, Pallas kernels: 24.1 us -> 21.9 us  [window_layer(): pl.pallas_call(functools.partial(window_kernel, phase, rows), out_shape=j...]
    pallas_call x2, Pallas kernels: 19.5 us -> 17.8 us  [join_agents(): pl.pallas_call(functools.partial(join_kernel, origins, tile_cols), out_sh...]
  transfers between devices with their start and end apart: 17 -> 17, of which waited for: 7 -> 8; matrix products, arithmetic and copies ran while one was open for 5% -> 4% of each run, Pallas kernels for 26% -> 25%
where the time goes in v11:
time: 136 us; the launch traced here: 134 us
  Pallas kernels  54.3 us (40%)
  starting transfers between devices  39.5 us (29%)
  waiting for transfers between devices  33 us (24%)
  local copies, waits for them, and re-layouts  6.54 us (5%)
    pallas_call x2, Pallas kernels, window_layer(): pl.pallas_call(functools.partial(window_kernel, phase, rows), out_shape=j...  21.9 us
    ppermute x9, waiting for transfers between devices, send(): lax.ppermute(x, 'veh', [(i, i // group * group + (i + k + 1) % group) for...  20.3 us
    pallas_call x2, Pallas kernels, join_agents(): pl.pallas_call(functools.partial(join_kernel, origins, tile_cols), out_sh...  17.8 us
    ppermute x9, starting transfers between devices, send(): lax.ppermute(x, 'veh', [(i, i // group * group + (i + k + 1) % group) for...  14.8 us
    ppermute x3, starting transfers between devices, beside(): above = lax.ppermute(last, 'row', [(i, i + 1) for i in range(count - 1)])  12.2 us
    ppermute x2, waiting for transfers between devices, swap(): lax.ppermute(x, 'veh', [(i, (i + group) % devices) for i in range(devices)])  9.06 us
    ppermute x3, starting transfers between devices, beside(): below = lax.ppermute(first, 'row', [(i + 1, i) for i in range(count - 1)])  7.32 us
    pallas_call x1, Pallas kernels, plan_of(): pl.pallas_call(functools.partial(plan_kernel, (vehicles, agents, tile_col...  7.13 us
  transfers between devices with their start and end apart: 17, of which 8 were waited for; matrix products, arithmetic and copies ran while one was open for 4% of the time, Pallas kernels for 25%

profile of v11, /device:TPU:1, one launch (start us, length us, event | category | flops | bytes accessed | tf_op | source)
XLA Modules:
  0.0 133.9 jit_solution(9040643070309333450)
XLA Ops:
  0.0 1.2 copy-done
  1.2 0.7 shard_map.154
  2.0 3.2 %collective-permute-start.2 = (bf16[16,18,8,128]{3,2,1,0:T(8,128)(2,1)S(1)}, bf16[16,18,8,128]{3,2,1,0:T(8,128)(2,1)S(1)}, u32[]{:S(2)}, u32[]{:S(2)}) collective-permute-start(bf16[16,18,8,128]{3,2,1,0:T(8,128)(2,1)S(1)} %get-tuple-element.58.refs_0_), channel_id=1, source_target_pairs={{0,16},{4,20},{8,24},{12,28},{16,0},{20,4},{24,8},{28,12},{1,17},{... | collective-permute-start | bytes 1769480 | tf_op jit(solution)/shard_map/ppermute | solution.py:629
  5.2 0.8 copy.18.senders
  5.9 0.8 copy.19.shifts
  6.7 0.1 pad_add_fusion.ids
  6.8 0.7 copy-done.1
  7.4 7.1 %shard_map.155 = (s32[49]{0:T(128)S(1)}, s32[6]{0:T(128)S(1)}, s32[544]{0:T(1024)S(1)}, s32[17]{0:T(128)S(1)}, s32[32]{0:T(128)S(1)}, /*index=5*/s32[64]{0:T(128)S(1)}, s32[65]{0:T(128)S(1)}) custom-call(s32[64,4]{1,0:T(8,128)S(1)} %copy.18.senders, s32[64,4]{1,0:T(8,128)S(1)} %copy.19.shifts, s32[64]{0:T(128)S(1)} %copy-done.1, s32[2]{0:T(128)S(1)} %pad_add_fusion.ids), custom_call_target="tpu_custom_call" | custom-call | bytes 20971520 | tf_op jit(solution)/shard_map/pallas_call | solution.py:175
  14.6 1.6 %shard_map.156 = (bf16[8,18,8,128]{3,2,1,0:T(8,128)(2,1)}, bf16[8,18,8,128]{3,2,1,0:T(8,128)(2,1)}, bf16[8,18,8,128]{3,2,1,0:T(8,128)(2,1)}) custom-call(s32[49]{0:T(128)S(1)} %get-tuple-element.61.chosen, s32[6]{0:T(128)S(1)} %get-tuple-element.62.filled, bf16[16,18,8,128]{3,2,1,0:T(8,128)(2,1)S(1)} %get-tuple-element.58.refs_0_), custom_call_target="tpu_custom_call" | custom-call | bytes 1769472 | tf_op jit(solution)/shard_map/pallas_call | solution.py:210
  16.2 1.2 collective-permute-start.3
  17.4 1.3 collective-permute-start.4
  18.7 1.2 collective-permute-start.5
  19.9 1.1 fusion.1
  21.0 0.1 convert_element_type.8
  21.1 0.1 broadcast_in_dim.26
  21.2 0.1 reshape.71.refs_5_
  21.3 0.1 copy.20
  21.4 0.1 broadcast_in_dim.25
  21.5 0.1 reshape.70.refs_8_
  21.6 0.1 copy.21
  21.7 0.1 copy.25
  21.8 0.1 copy.24
  21.9 9.1 %collective-permute-done.2.refs_0_ = bf16[16,18,8,128]{3,2,1,0:T(8,128)(2,1)S(1)} collective-permute-done((bf16[16,18,8,128]{3,2,1,0:T(8,128)(2,1)S(1)}, bf16[16,18,8,128]{3,2,1,0:T(8,128)(2,1)S(1)}, u32[]{:S(2)}, u32[]{:S(2)}) %collective-permute-start.2) | collective-permute-done | bytes 589856 | tf_op jit(solution)/shard_map/ppermute | solution.py:629
  31.1 1.9 %shard_map.157 = (bf16[8,18,8,128]{3,2,1,0:T(8,128)(2,1)S(1)}, bf16[8,18,8,128]{3,2,1,0:T(8,128)(2,1)S(1)}, bf16[8,18,8,128]{3,2,1,0:T(8,128)(2,1)S(1)}) custom-call(s32[49]{0:T(128)S(1)} %get-tuple-element.61.chosen, s32[6]{0:T(128)S(1)} %get-tuple-element.62.filled, bf16[16,18,8,128]{3,2,1,0:T(8,128)(2,1)S(1)} %collective-permute-done.2.refs_0_), custom_call_target="tpu_custom_call" | custom-call | bytes 1769472 | tf_op jit(solution)/shard_map/pallas_call | solution.py:210
  33.1 0.9 collective-permute-start.6
  34.0 1.2 collective-permute-start.7
  35.3 2.0 %collective-permute-done.3 = bf16[8,18,8,128]{3,2,1,0:T(8,128)(2,1)} collective-permute-done((bf16[8,18,8,128]{3,2,1,0:T(8,128)(2,1)}, bf16[8,18,8,128]{3,2,1,0:T(8,128)(2,1)}, u32[]{:S(2)}, u32[]{:S(2)}) %collective-permute-start.3) | collective-permute-done | bytes 294944 | tf_op jit(solution)/shard_map/ppermute | solution.py:633
  37.3 0.7 collective-permute-done.4
  38.0 2.0 %collective-permute-start.11 = (bf16[16,14,8,128]{3,2,1,0:T(8,128)(2,1)S(1)}, bf16[16,14,8,128]{3,2,1,0:T(8,128)(2,1)S(1)}, u32[]{:S(2)}, u32[]{:S(2)}) collective-permute-start(bf16[16,14,8,128]{3,2,1,0:T(8,128)(2,1)S(1)} %get-tuple-element.92.refs_0_), channel_id=1, source_target_pairs={{0,16},{4,20},{8,24},{12,28},{16,0},{20,4},{24,8},{28,12},{1,17},{... | collective-permute-start | bytes 1376264 | tf_op jit(solution)/shard_map/ppermute | solution.py:629
  40.0 1.0 fusion
  41.0 3.5 %collective-permute-start.1 = (bf16[8,1,64,128]{3,2,1,0:T(8,128)(2,1)S(1)}, bf16[8,1,64,128]{3,2,1,0:T(8,128)(2,1)S(1)}, u32[]{:S(2)}, u32[]{:S(2)}) collective-permute-start(bf16[8,1,64,128]{3,2,1,0:T(8,128)(2,1)S(1)} %get-tuple-element.101), channel_id=1, source_target_pairs={{1,0},{2,1},{3,2},{5,4},{6,5},{7,6},{9,8},{10,9},{11,10},{13,12},{... | collective-permute-start | bytes 393224 | tf_op jit(solution)/shard_map/ppermute | solution.py:599
  44.5 9.9 %collective-permute-done.6 = bf16[8,18,8,128]{3,2,1,0:T(8,128)(2,1)S(1)} collective-permute-done((bf16[8,18,8,128]{3,2,1,0:T(8,128)(2,1)S(1)}, bf16[8,18,8,128]{3,2,1,0:T(8,128)(2,1)S(1)}, u32[]{:S(2)}, u32[]{:S(2)}) %collective-permute-start.6) | collective-permute-done | bytes 294944 | tf_op jit(solution)/shard_map/ppermute | solution.py:633
  54.4 4.9 %collective-permute-start = (bf16[8,1,64,128]{3,2,1,0:T(8,128)(2,1)S(1)}, bf16[8,1,64,128]{3,2,1,0:T(8,128)(2,1)S(1)}, u32[]{:S(2)}, u32[]{:S(2)}) collective-permute-start(bf16[8,1,64,128]{3,2,1,0:T(8,128)(2,1)S(1)} %get-tuple-element.102), channel_id=1, source_target_pairs={{0,1},{1,2},{2,3},{4,5},{5,6},{6,7},{8,9},{9,10},{10,11},{12,13},{... | collective-permute-start | bytes 393224 | tf_op jit(solution)/shard_map/ppermute | solution.py:598
  59.4 1.1 collective-permute-done.7
  60.5 9.2 %shard_map.158 = (bf16[2304,128]{1,0:T(8,128)(2,1)S(1)}, bf16[8,36,128]{2,1,0:T(8,128)(2,1)S(1)}, bf16[8,36,128]{2,1,0:T(8,128)(2,1)S(1)}) custom-call(s32[544]{0:T(1024)S(1)} %get-tuple-element.88.entries, s32[17]{0:T(128)S(1)} %get-tuple-element.89.listed, s32[32]{0:T(128)S(1)} %get-tuple-element.90.sizes_of, s32[65]{0:T(128)S(1)} %get-tuple-element.91.blank, ...), custom_call_target="tpu_custom_call" | custom-call | flops 1509949440 | bytes 3538944 | tf_op jit(solution)/shard_map/pallas_call | solution.py:327
  69.7 3.6 %collective-permute-start.9 = (bf16[8,36,128]{2,1,0:T(8,128)(2,1)S(1)}, bf16[8,36,128]{2,1,0:T(8,128)(2,1)S(1)}, u32[]{:S(2)}, u32[]{:S(2)}) collective-permute-start(bf16[8,36,128]{2,1,0:T(8,128)(2,1)S(1)} %get-tuple-element.76), channel_id=1, source_target_pairs={{0,1},{1,2},{2,3},{4,5},{5,6},{6,7},{8,9},{9,10},{10,11},{12,13},{... | collective-permute-start | bytes 221192 | tf_op jit(solution)/shard_map/ppermute | solution.py:598
  73.3 1.9 %collective-permute-start.10 = (bf16[8,36,128]{2,1,0:T(8,128)(2,1)S(1)}, bf16[8,36,128]{2,1,0:T(8,128)(2,1)S(1)}, u32[]{:S(2)}, u32[]{:S(2)}) collective-permute-start(bf16[8,36,128]{2,1,0:T(8,128)(2,1)S(1)} %get-tuple-element.77), channel_id=1, source_target_pairs={{1,0},{2,1},{3,2},{5,4},{6,5},{7,6},{9,8},{10,9},{11,10},{13,12},{... | collective-permute-start | bytes 221192 | tf_op jit(solution)/shard_map/ppermute | solution.py:599
  75.2 3.2 %shard_map.160 = (bf16[16,14,8,128]{3,2,1,0:T(8,128)(2,1)S(1)}, bf16[16,14,8,128]{3,2,1,0:T(8,128)(2,1)S(1)}, bf16[16,14,8,128]{3,2,1,0:T(8,128)(2,1)S(1)}) custom-call(s32[49]{0:T(128)S(1)} %get-tuple-element.61.chosen, s32[6]{0:T(128)S(1)} %get-tuple-element.62.filled, bf16[16,14,8,128]{3,2,1,0:T(8,128)(2,1)S(1)} %get-tuple-element.92.refs_0_, ...), custom_call_target="tpu_custom_call" | custom-call | bytes 2752512 | tf_op jit(solution)/shard_map/pallas_call | solution.py:210
  78.4 7.7 %collective-permute-start.12 = (bf16[16,14,8,128]{3,2,1,0:T(8,128)(2,1)S(1)}, bf16[16,14,8,128]{3,2,1,0:T(8,128)(2,1)S(1)}, u32[]{:S(2)}, u32[]{:S(2)}) collective-permute-start(bf16[16,14,8,128]{3,2,1,0:T(8,128)(2,1)S(1)} %get-tuple-element.93), channel_id=1, source_target_pairs={{0,4},{4,8},{8,12},{12,0},{16,20},{20,24},{24,28},{28,16},{1,5},{5... | collective-permute-start | bytes 1376264 | tf_op jit(solution)/shard_map/ppermute | solution.py:633
  86.2 1.3 collective-permute-start.14
  87.5 11.0 %shard_map.159.refs_19_ = bf16[8,8,2,2,16,256]{5,4,3,2,1,0:T(8,128)(2,1)} custom-call(bf16[8,64,8,128]{3,2,1,0:T(8,128)(2,1)S(1)} %get-tuple-element.53.refs_0_, bf16[8,1,64,128]{3,2,1,0:T(8,128)(2,1)S(1)} %collective-permute-done.refs_1_, bf16[8,1,64,128]{3,2,1,0:T(8,128)(2,1)S(1)} %collective-permute-done.1.refs_2_, bf16[8,288,128]{2,1,0:T(8,128)(2,1)S(1)} %bitcast.50, ...), custom_call_target="tpu_custom_call" | custom-call | flops 8053063680 | bytes 3145728 | tf_op jit(solution)/shard_map/pallas_call | solution.py:575
  98.4 0.2 collective-permute-done.13
  98.7 6.3 %collective-permute-done.14 = bf16[16,14,8,128]{3,2,1,0:T(8,128)(2,1)S(1)} collective-permute-done((bf16[16,14,8,128]{3,2,1,0:T(8,128)(2,1)S(1)}, bf16[16,14,8,128]{3,2,1,0:T(8,128)(2,1)S(1)}, u32[]{:S(2)}, u32[]{:S(2)}) %collective-permute-start.14) | collective-permute-done | bytes 458784 | tf_op jit(solution)/shard_map/ppermute | solution.py:633
  105.0 8.7 %shard_map.161 = (bf16[1792,128]{1,0:T(8,128)(2,1)S(1)}, bf16[8,28,128]{2,1,0:T(8,128)(2,1)S(1)}, bf16[8,28,128]{2,1,0:T(8,128)(2,1)S(1)}) custom-call(s32[544]{0:T(1024)S(1)} %get-tuple-element.88.entries, s32[17]{0:T(128)S(1)} %get-tuple-element.89.listed, s32[32]{0:T(128)S(1)} %get-tuple-element.90.sizes_of, s32[65]{0:T(128)S(1)} %get-tuple-element.91.blank, ...), custom_call_target="tpu_custom_call" | custom-call | flops 1174405120 | bytes 2752512 | tf_op jit(solution)/shard_map/pallas_call | solution.py:327
  113.7 3.6 %collective-permute-start.15 = (bf16[8,28,128]{2,1,0:T(8,128)(2,1)S(1)}, bf16[8,28,128]{2,1,0:T(8,128)(2,1)S(1)}, u32[]{:S(2)}, u32[]{:S(2)}) collective-permute-start(bf16[8,28,128]{2,1,0:T(8,128)(2,1)S(1)} %get-tuple-element.98), channel_id=1, source_target_pairs={{0,1},{1,2},{2,3},{4,5},{5,6},{6,7},{8,9},{9,10},{10,11},{12,13},{... | collective-permute-start | bytes 172040 | tf_op jit(solution)/shard_map/ppermute | solution.py:598
  117.3 1.9 %collective-permute-start.16 = (bf16[8,28,128]{2,1,0:T(8,128)(2,1)S(1)}, bf16[8,28,128]{2,1,0:T(8,128)(2,1)S(1)}, u32[]{:S(2)}, u32[]{:S(2)}) collective-permute-start(bf16[8,28,128]{2,1,0:T(8,128)(2,1)S(1)} %get-tuple-element.99), channel_id=1, source_target_pairs={{1,0},{2,1},{3,2},{5,4},{6,5},{7,6},{9,8},{10,9},{11,10},{13,12},{... | collective-permute-start | bytes 172040 | tf_op jit(solution)/shard_map/ppermute | solution.py:599
  119.2 3.6 %collective-permute-done.16.refs_8_ = bf16[8,28,128]{2,1,0:T(8,128)(2,1)S(1)} collective-permute-done((bf16[8,28,128]{2,1,0:T(8,128)(2,1)S(1)}, bf16[8,28,128]{2,1,0:T(8,128)(2,1)S(1)}, u32[]{:S(2)}, u32[]{:S(2)}) %collective-permute-start.16) | collective-permute-done | bytes 57376 | tf_op jit(solution)/shard_map/ppermute | solution.py:599
  122.9 11.0 %shard_map.162 = bf16[8,8,2,2,16,256]{5,4,3,2,1,0:T(8,128)(2,1)} custom-call(bf16[8,64,8,128]{3,2,1,0:T(8,128)(2,1)S(1)} %get-tuple-element.53.refs_0_, bf16[8,1,64,128]{3,2,1,0:T(8,128)(2,1)S(1)} %collective-permute-done.refs_1_, bf16[8,1,64,128]{3,2,1,0:T(8,128)(2,1)S(1)} %collective-permute-done.1.refs_2_, ...), custom_call_target="tpu_custom_call", output_to_operand_aliasing={{}: (19, {})} | custom-call | flops 8053063680 | bytes 3145728 | tf_op jit(solution)/shard_map/pallas_call | solution.py:575
  (40 shorter events, 0.2 us)
Async XLA Ops:
  0.0 1.2 copy-start
  1.2 19.7 %copy-start.10 = (f32[3,3,256]{2,1,0:T(4,128)S(1)}, f32[3,3,256]{2,1,0:T(4,128)}, u32[]{:S(2)}) copy-start(f32[3,3,256]{2,1,0:T(4,128)} %param.24) | copy-start | bytes 27652
  1.2 20.0 %copy-start.9 = (bf16[128,128]{1,0:T(8,128)(2,1)S(1)}, bf16[128,128]{1,0:T(8,128)(2,1)}, u32[]{:S(2)}) copy-start(bf16[128,128]{1,0:T(8,128)(2,1)} %param.20) | copy-start | bytes 98308
  1.2 20.3 %copy-start.8 = (bf16[128,256]{1,0:T(8,128)(2,1)S(1)}, bf16[128,256]{1,0:T(8,128)(2,1)}, u32[]{:S(2)}) copy-start(bf16[128,256]{1,0:T(8,128)(2,1)} %param.21) | copy-start | bytes 196612
  1.2 20.7 %copy-start.12 = (f32[8]{0:T(128)S(1)}, f32[8]{0:T(128)}, u32[]{:S(2)}) copy-start(f32[8]{0:T(128)} %param.28) | copy-start | bytes 100
  1.2 29.8 %copy-start.11 = (f32[4]{0:T(128)S(1)}, f32[4]{0:T(128)}, u32[]{:S(2)}) copy-start(f32[4]{0:T(128)} %param.23) | copy-start | bytes 52
  1.9 58.5 %copy-start.5 = (bf16[128,128]{1,0:T(8,128)(2,1)S(1)}, bf16[128,128]{1,0:T(8,128)(2,1)}, u32[]{:S(2)}) copy-start(bf16[128,128]{1,0:T(8,128)(2,1)} %refs_8_) | copy-start | bytes 98308
  2.0 29.0 %collective-permute-start.2 = (bf16[16,18,8,128]{3,2,1,0:T(8,128)(2,1)S(1)}, bf16[16,18,8,128]{3,2,1,0:T(8,128)(2,1)S(1)}, u32[]{:S(2)}, u32[]{:S(2)}) collective-permute-start(bf16[16,18,8,128]{3,2,1,0:T(8,128)(2,1)S(1)} %get-tuple-element.58.refs_0_), channel_id=1, source_target_pairs={{0,16},{4,20},{8,24},{12,28},{16,0},{20,4},{24,8},{28,12},{1,17},{... | collective-permute-start | bytes 1769480 | tf_op jit(solution)/shard_map/ppermute | solution.py:629
  6.8 0.7 copy-start.1
  16.2 21.0 %collective-permute-start.3 = (bf16[8,18,8,128]{3,2,1,0:T(8,128)(2,1)}, bf16[8,18,8,128]{3,2,1,0:T(8,128)(2,1)}, u32[]{:S(2)}, u32[]{:S(2)}) collective-permute-start(bf16[8,18,8,128]{3,2,1,0:T(8,128)(2,1)} %get-tuple-element.63), channel_id=1, source_target_pairs={{0,4},{4,8},{8,12},{12,0},{16,20},{20,24},{24,28},{28,16},{1,5},{5... | collective-permute-start | bytes 884744 | tf_op jit(solution)/shard_map/ppermute | solution.py:633
  17.4 20.6 %collective-permute-start.4 = (bf16[8,18,8,128]{3,2,1,0:T(8,128)(2,1)}, bf16[8,18,8,128]{3,2,1,0:T(8,128)(2,1)}, u32[]{:S(2)}, u32[]{:S(2)}) collective-permute-start(bf16[8,18,8,128]{3,2,1,0:T(8,128)(2,1)} %get-tuple-element.64), channel_id=1, source_target_pairs={{0,8},{4,12},{8,0},{12,4},{16,24},{20,28},{24,16},{28,20},{1,9},{5... | collective-permute-start | bytes 884744 | tf_op jit(solution)/shard_map/ppermute | solution.py:633
  18.7 22.3 %collective-permute-start.5 = (bf16[8,18,8,128]{3,2,1,0:T(8,128)(2,1)}, bf16[8,18,8,128]{3,2,1,0:T(8,128)(2,1)}, u32[]{:S(2)}, u32[]{:S(2)}) collective-permute-start(bf16[8,18,8,128]{3,2,1,0:T(8,128)(2,1)} %get-tuple-element.65), channel_id=1, source_target_pairs={{0,12},{4,0},{8,4},{12,8},{16,28},{20,16},{24,20},{28,24},{1,13},{... | collective-permute-start | bytes 884744 | tf_op jit(solution)/shard_map/ppermute | solution.py:633
  33.1 21.3 %collective-permute-start.6 = (bf16[8,18,8,128]{3,2,1,0:T(8,128)(2,1)S(1)}, bf16[8,18,8,128]{3,2,1,0:T(8,128)(2,1)S(1)}, u32[]{:S(2)}, u32[]{:S(2)}) collective-permute-start(bf16[8,18,8,128]{3,2,1,0:T(8,128)(2,1)S(1)} %get-tuple-element.67), channel_id=1, source_target_pairs={{0,4},{4,8},{8,12},{12,0},{16,20},{20,24},{24,28},{28,16},{1,5},{5... | collective-permute-start | bytes 884744 | tf_op jit(solution)/shard_map/ppermute | solution.py:633
  34.0 26.4 %collective-permute-start.7 = (bf16[8,18,8,128]{3,2,1,0:T(8,128)(2,1)S(1)}, bf16[8,18,8,128]{3,2,1,0:T(8,128)(2,1)S(1)}, u32[]{:S(2)}, u32[]{:S(2)}) collective-permute-start(bf16[8,18,8,128]{3,2,1,0:T(8,128)(2,1)S(1)} %get-tuple-element.68), channel_id=1, source_target_pairs={{0,8},{4,12},{8,0},{12,4},{16,24},{20,28},{24,16},{28,20},{1,9},{5... | collective-permute-start | bytes 884744 | tf_op jit(solution)/shard_map/ppermute | solution.py:633
  37.3 23.2 %collective-permute-start.8 = (bf16[8,18,8,128]{3,2,1,0:T(8,128)(2,1)S(1)}, bf16[8,18,8,128]{3,2,1,0:T(8,128)(2,1)S(1)}, u32[]{:S(2)}, u32[]{:S(2)}) collective-permute-start(bf16[8,18,8,128]{3,2,1,0:T(8,128)(2,1)S(1)} %get-tuple-element.69), channel_id=1, source_target_pairs={{0,12},{4,0},{8,4},{12,8},{16,28},{20,16},{24,20},{28,24},{1,13},{... | collective-permute-start | bytes 884744 | tf_op jit(solution)/shard_map/ppermute | solution.py:633
  38.0 37.2 %collective-permute-start.11 = (bf16[16,14,8,128]{3,2,1,0:T(8,128)(2,1)S(1)}, bf16[16,14,8,128]{3,2,1,0:T(8,128)(2,1)S(1)}, u32[]{:S(2)}, u32[]{:S(2)}) collective-permute-start(bf16[16,14,8,128]{3,2,1,0:T(8,128)(2,1)S(1)} %get-tuple-element.92.refs_0_), channel_id=1, source_target_pairs={{0,16},{4,20},{8,24},{12,28},{16,0},{20,4},{24,8},{28,12},{1,17},{... | collective-permute-start | bytes 1376264 | tf_op jit(solution)/shard_map/ppermute | solution.py:629
  41.0 45.1 %collective-permute-start.1 = (bf16[8,1,64,128]{3,2,1,0:T(8,128)(2,1)S(1)}, bf16[8,1,64,128]{3,2,1,0:T(8,128)(2,1)S(1)}, u32[]{:S(2)}, u32[]{:S(2)}) collective-permute-start(bf16[8,1,64,128]{3,2,1,0:T(8,128)(2,1)S(1)} %get-tuple-element.101), channel_id=1, source_target_pairs={{1,0},{2,1},{3,2},{5,4},{6,5},{7,6},{9,8},{10,9},{11,10},{13,12},{... | collective-permute-start | bytes 393224 | tf_op jit(solution)/shard_map/ppermute | solution.py:599
  54.4 31.7 %collective-permute-start = (bf16[8,1,64,128]{3,2,1,0:T(8,128)(2,1)S(1)}, bf16[8,1,64,128]{3,2,1,0:T(8,128)(2,1)S(1)}, u32[]{:S(2)}, u32[]{:S(2)}) collective-permute-start(bf16[8,1,64,128]{3,2,1,0:T(8,128)(2,1)S(1)} %get-tuple-element.102), channel_id=1, source_target_pairs={{0,1},{1,2},{2,3},{4,5},{5,6},{6,7},{8,9},{9,10},{10,11},{12,13},{... | collective-permute-start | bytes 393224 | tf_op jit(solution)/shard_map/ppermute | solution.py:598
  60.4 27.0 %copy-start.2 = (bf16[256,512]{1,0:T(8,128)(2,1)S(1)}, bf16[256,512]{1,0:T(8,128)(2,1)}, u32[]{:S(2)}) copy-start(bf16[256,512]{1,0:T(8,128)(2,1)} %refs_17_) | copy-start | bytes 786436
  60.4 27.0 %copy-start.3 = (bf16[512,256]{1,0:T(8,128)(2,1)S(1)}, bf16[512,256]{1,0:T(8,128)(2,1)}, u32[]{:S(2)}) copy-start(bf16[512,256]{1,0:T(8,128)(2,1)} %refs_18_) | copy-start | bytes 786436
  60.5 27.0 %copy-start.4 = (bf16[256,256]{1,0:T(8,128)(2,1)S(1)}, bf16[256,256]{1,0:T(8,128)(2,1)}, u32[]{:S(2)}) copy-start(bf16[256,256]{1,0:T(8,128)(2,1)} %refs_14_.1) | copy-start | bytes 393220
  60.5 27.0 %copy-start.6 = (f32[256]{0:T(256)S(1)}, f32[256]{0:T(256)}, u32[]{:S(2)}) copy-start(f32[256]{0:T(256)} %param.25) | copy-start | bytes 3076
  60.5 27.0 %copy-start.7 = (f32[256]{0:T(256)S(1)}, f32[256]{0:T(256)}, u32[]{:S(2)}) copy-start(f32[256]{0:T(256)} %param.29) | copy-start | bytes 3076
  69.7 17.8 %collective-permute-start.9 = (bf16[8,36,128]{2,1,0:T(8,128)(2,1)S(1)}, bf16[8,36,128]{2,1,0:T(8,128)(2,1)S(1)}, u32[]{:S(2)}, u32[]{:S(2)}) collective-permute-start(bf16[8,36,128]{2,1,0:T(8,128)(2,1)S(1)} %get-tuple-element.76), channel_id=1, source_target_pairs={{0,1},{1,2},{2,3},{4,5},{5,6},{6,7},{8,9},{9,10},{10,11},{12,13},{... | collective-permute-start | bytes 221192 | tf_op jit(solution)/shard_map/ppermute | solution.py:598
  73.3 14.1 %collective-permute-start.10 = (bf16[8,36,128]{2,1,0:T(8,128)(2,1)S(1)}, bf16[8,36,128]{2,1,0:T(8,128)(2,1)S(1)}, u32[]{:S(2)}, u32[]{:S(2)}) collective-permute-start(bf16[8,36,128]{2,1,0:T(8,128)(2,1)S(1)} %get-tuple-element.77), channel_id=1, source_target_pairs={{1,0},{2,1},{3,2},{5,4},{6,5},{7,6},{9,8},{10,9},{11,10},{13,12},{... | collective-permute-start | bytes 221192 | tf_op jit(solution)/shard_map/ppermute | solution.py:599
  78.4 20.0 %collective-permute-start.12 = (bf16[16,14,8,128]{3,2,1,0:T(8,128)(2,1)S(1)}, bf16[16,14,8,128]{3,2,1,0:T(8,128)(2,1)S(1)}, u32[]{:S(2)}, u32[]{:S(2)}) collective-permute-start(bf16[16,14,8,128]{3,2,1,0:T(8,128)(2,1)S(1)} %get-tuple-element.93), channel_id=1, source_target_pairs={{0,4},{4,8},{8,12},{12,0},{16,20},{20,24},{24,28},{28,16},{1,5},{5... | collective-permute-start | bytes 1376264 | tf_op jit(solution)/shard_map/ppermute | solution.py:633
  86.2 12.5 %collective-permute-start.13 = (bf16[16,14,8,128]{3,2,1,0:T(8,128)(2,1)S(1)}, bf16[16,14,8,128]{3,2,1,0:T(8,128)(2,1)S(1)}, u32[]{:S(2)}, u32[]{:S(2)}) collective-permute-start(bf16[16,14,8,128]{3,2,1,0:T(8,128)(2,1)S(1)} %get-tuple-element.94), channel_id=1, source_target_pairs={{0,8},{4,12},{8,0},{12,4},{16,24},{20,28},{24,16},{28,20},{1,9},{5... | collective-permute-start | bytes 1376264 | tf_op jit(solution)/shard_map/ppermute | solution.py:633
  86.2 18.9 %collective-permute-start.14 = (bf16[16,14,8,128]{3,2,1,0:T(8,128)(2,1)S(1)}, bf16[16,14,8,128]{3,2,1,0:T(8,128)(2,1)S(1)}, u32[]{:S(2)}, u32[]{:S(2)}) collective-permute-start(bf16[16,14,8,128]{3,2,1,0:T(8,128)(2,1)S(1)} %get-tuple-element.95), channel_id=1, source_target_pairs={{0,12},{4,0},{8,4},{12,8},{16,28},{20,16},{24,20},{28,24},{1,13},{... | collective-permute-start | bytes 1376264 | tf_op jit(solution)/shard_map/ppermute | solution.py:633
  113.7 5.5 %collective-permute-start.15 = (bf16[8,28,128]{2,1,0:T(8,128)(2,1)S(1)}, bf16[8,28,128]{2,1,0:T(8,128)(2,1)S(1)}, u32[]{:S(2)}, u32[]{:S(2)}) collective-permute-start(bf16[8,28,128]{2,1,0:T(8,128)(2,1)S(1)} %get-tuple-element.98), channel_id=1, source_target_pairs={{0,1},{1,2},{2,3},{4,5},{5,6},{6,7},{8,9},{9,10},{10,11},{12,13},{... | collective-permute-start | bytes 172040 | tf_op jit(solution)/shard_map/ppermute | solution.py:598
  117.3 5.6 %collective-permute-start.16 = (bf16[8,28,128]{2,1,0:T(8,128)(2,1)S(1)}, bf16[8,28,128]{2,1,0:T(8,128)(2,1)S(1)}, u32[]{:S(2)}, u32[]{:S(2)}) collective-permute-start(bf16[8,28,128]{2,1,0:T(8,128)(2,1)S(1)} %get-tuple-element.99), channel_id=1, source_target_pairs={{1,0},{2,1},{3,2},{5,4},{6,5},{7,6},{9,8},{10,9},{11,10},{13,12},{... | collective-permute-start | bytes 172040 | tf_op jit(solution)/shard_map/ppermute | solution.py:599
